TPU v7x, 256 devices: a whole 4x4x8 slice. The times are simulated.
256 devices in a mesh: tm: 64 (over x, z, core), chan: 4 (over y).
Axes of the slice: x: 4, y: 4, z: 8, core: 2. Of those that a mesh axis runs over, the one named last changes fastest.
Arguments:
- features: bfloat16 [393216, 512], P('tm', 'chan'), may hold values from -6 to 6
- snake_alpha: float32 [512], P('chan'), may hold values from 0.5 to 3
- down_weight: bfloat16 [512, 16, 1024], P(None, None, 'chan'), may hold values from -0.0625 to 0.0625
- grad_out: bfloat16 [49152, 1024], P('tm', 'chan'), may hold values from -6 to 6
Outputs:
- encoded: bfloat16 [49152, 1024], P('tm', 'chan')
- grad_features: bfloat16 [393216, 512], P('tm', 'chan')
- grad_down: bfloat16 [1024, 16, 512], P('tm', None, 'chan')
All inputs are finite; a program needn't handle non-finite values.
Results may differ from a plain program's by a relative error of at most 0.0049.
Values may be sent and summed in bfloat16 or wider, within the bound.
No kernel may reach another device: no remote copies, remote signals or barrier semaphores. Data moves between devices by JAX's collectives and lax.ppermute only.
A program may use at most 128 MiB of HBM per device.

v0:
```python
import math

import jax
import jax.numpy as jnp
from jax import lax
from jax.sharding import PartitionSpec as P

STRIDE = 8


def with_halo(block, sides, width):
    for axis, dim in sides:
        count = lax.axis_size(axis)
        forward = [(i, i + 1) for i in range(count - 1)]
        backward = [(target, source) for source, target in forward]
        low = lax.ppermute(
            lax.slice_in_dim(block, block.shape[dim] - width, None, axis=dim), axis, forward
        )
        high = lax.ppermute(lax.slice_in_dim(block, 0, width, axis=dim), axis, backward)
        block = jnp.concatenate([low, block, high], axis=dim)
    return block


def snake(values, alpha):
    return values + jnp.sin(alpha * values) ** 2 / alpha


def shards(features, snake_alpha, down_weight, grad_out):
    frames = features.shape[0]
    local_chans = features.shape[1]
    blocks_out = frames // STRIDE
    offset = STRIDE // 2
    wide = features.astype(jnp.float32)
    snaked = snake(wide, snake_alpha).astype(jnp.bfloat16)
    padded = with_halo(snaked, (("tm", 0),), offset)
    local_tiled = padded.reshape(blocks_out + 1, STRIDE, local_chans)
    full_cols = lax.all_gather(padded, "chan", axis=1, tiled=True)
    tiled = full_cols.reshape(blocks_out + 1, STRIDE, full_cols.shape[1])
    encoded = (
        jnp.einsum(
            "ujr,rjp->up", tiled[:-1], down_weight[:, :STRIDE], preferred_element_type=jnp.float32
        )
        + jnp.einsum(
            "ujr,rjp->up", tiled[1:], down_weight[:, STRIDE:], preferred_element_type=jnp.float32
        )
    ).astype(jnp.bfloat16)
    grad_pad = with_halo(grad_out, (("tm", 0),), 1)
    grad_full = lax.all_gather(grad_pad, "chan", axis=1, tiled=True)
    spread = jnp.einsum(
        "up,rjp->ujr", grad_pad[1:], down_weight[:, :STRIDE], preferred_element_type=jnp.float32
    ) + jnp.einsum(
        "up,rjp->ujr", grad_pad[:-1], down_weight[:, STRIDE:], preferred_element_type=jnp.float32
    )
    partial_terms = spread.reshape(frames + STRIDE, down_weight.shape[0])[offset : offset + frames]
    grad_snaked = lax.psum_scatter(partial_terms, "chan", scatter_dimension=1, tiled=True)
    grad_features = (grad_snaked * (1.0 + jnp.sin(2.0 * snake_alpha * wide))).astype(jnp.bfloat16)
    grad_inner = grad_full[1:-1]
    scale = 1.0 / math.sqrt(blocks_out * lax.axis_size("tm"))
    lower = jnp.einsum(
        "ujr,up->pjr", local_tiled[:-1], grad_inner, preferred_element_type=jnp.float32
    )
    upper = jnp.einsum(
        "ujr,up->pjr", local_tiled[1:], grad_inner, preferred_element_type=jnp.float32
    )
    summed = lax.psum_scatter(
        jnp.concatenate([lower, upper], axis=1), "tm", scatter_dimension=0, tiled=True
    )
    grad_down = (summed * scale).astype(jnp.bfloat16)
    return (encoded, grad_features, grad_down)


def solution(mesh):
    placed = (P("tm", "chan"), P("chan"), P(None, None, "chan"), P("tm", "chan"))
    return jax.shard_map(
        shards,
        mesh=mesh,
        in_specs=placed,
        out_specs=(P("tm", "chan"), P("tm", "chan"), P("tm", None, "chan")),
        check_vma=False,
    )
```

profile of v0, /device:TPU:2, one launch (start us, length us, event | category | flops | bytes accessed | tf_op | source)
XLA Modules:
  0.0 449.4 jit_solution(14186953188106699410)
XLA Ops:
  7.2 0.0 reduce-scatter.3.cloned.1.call-start
  7.2 0.7 fusion.51
  7.9 1.9 collective-permute-start.3
  9.8 0.0 copy-start.4
  9.9 7.3 %collective-permute-start.2 = (bf16[1,256]{1,0:T(2,128)(2,1)S(1)}, bf16[1,256]{1,0:T(2,128)(2,1)S(1)}, u32[]{:S(2)}, u32[]{:S(2)}) collective-permute-start(bf16[1,256]{1,0:T(2,128)(2,1)S(1)} %get-tuple-element.19), channel_id=1, source_target_pairs={{4,0},{8,4},{12,8},{16,12},{20,16},{24,20},{28,24},{32,28},{36,32}... | collective-permute-start | bytes 1544 | tf_op jit(solution)/shard_map/ppermute | solution.py:19
  17.2 2.5 fusion.49
  19.7 0.0 copy-start
  19.7 0.0 copy-start.2
  19.7 0.0 collective-permute-done.3
  19.7 0.0 copy-done.4
  19.7 1.9 fusion.12
  21.6 0.0 copy-done
  21.6 0.0 collective-permute-done.2
  21.6 0.1 copy-done.2
  21.7 6.7 %add_bitcast_fusion = f32[769,8,512]{2,0,1:T(8,128)} fusion(f32[769,512,8]{1,0,2:T(8,128)S(1)} %fusion.12, bf16[512,8,256]{2,1,0:T(8,128)(2,1)S(1)} %get-tuple-element.11, bf16[1,256]{1,0:T(2,128)(2,1)S(1)} %collective-permute-done.2, bf16[768,256]{1,0:T(8,128)(2,1)S(1)} %copy-done.4), kind=kOutput, calls=%fused_computation | convolution fusion | flops 1616647168 | bytes 27689472 | tf_op jit(solution)/shard_map/up,rjp->ujr/dot_general | solution.py:49
  28.4 16.4 %copy.59 = f32[769,8,512]{2,1,0:T(8,128)} copy(f32[769,8,512]{2,0,1:T(8,128)} %add_bitcast_fusion) | data formatting | bytes 25198592 | tf_op jit(solution)/shard_map/add | solution.py:49
  44.8 10.9 %slice.76 = f32[6144,512]{1,0:T(8,128)} slice(f32[6152,512]{1,0:T(8,128)} %bitcast.31), slice={[4:6148], [0:512]} | slice | bytes 25165824 | tf_op jit(solution)/shard_map/slice | solution.py:54
  55.7 0.0 copy-start.6
  55.7 0.0 reduce-scatter.3.cloned.1.call-update
  55.7 0.0 copy-start.5
  55.7 0.0 all-gather.5.cloned.1.call-start
  55.8 0.2 copy.19
  56.0 0.1 copy.18
  56.1 0.1 copy.20
  56.3 1.0 pad_maximum_fusion.3
  57.3 0.0 all-gather.5.cloned.1.call-update
  57.3 0.0 all-gather.3.cloned.1.call-start
  57.3 0.0 copy-done.6
  57.4 116.2 %reduce-scatter.3.cloned.1.call-done = f32[6144,128]{1,0:T(8,128)} async-done(((f32[6144,512]{1,0:T(8,128)}), f32[6144,128]{1,0:T(8,128)}) %reduce-scatter.3.cloned.1.call-update) | async-done | bytes 3145744 | tf_op jit(solution)/shard_map/reduce_scatter | solution.py:55
  173.6 0.0 copy-done.5
  173.6 23.1 %fusion.11 = (bf16[6144,128]{1,0:T(8,128)(2,1)}, bf16[6144,128]{1,0:T(8,128)(2,1)S(1)}) fusion(f32[6144,128]{1,0:T(8,128)} %reduce-scatter.3.cloned.1.call-done, bf16[6144,128]{1,0:T(8,128)(2,1)S(1)} %copy-done.5, f32[128]{0:T(128)S(1)} %broadcast_multiply_fusion, f32[128]{0:T(128)S(1)} %copy-done.6), kind=kLoop, calls=%fused_computation.19 | loop fusion | flops 7864320 | bytes 7865344 | tf_op jit(solution)/shard_map/convert_element_type | solution.py:56
  196.6 1.9 collective-permute-start
  198.6 5.8 %collective-permute-start.1 = (bf16[4,128]{1,0:T(4,128)(2,1)S(1)}, bf16[4,128]{1,0:T(4,128)(2,1)S(1)}, u32[]{:S(2)}, u32[]{:S(2)}) collective-permute-start(bf16[4,128]{1,0:T(4,128)(2,1)S(1)} %get-tuple-element.17), channel_id=1, source_target_pairs={{4,0},{8,4},{12,8},{16,12},{20,16},{24,20},{28,24},{32,28},{36,32}... | collective-permute-start | bytes 3080 | tf_op jit(solution)/shard_map/ppermute | solution.py:19
  204.3 0.0 collective-permute-done
  204.3 1.3 collective-permute-done.1
  205.6 8.7 %concatenate.21 = bf16[6152,128]{1,0:T(8,128)(2,1)} concatenate(bf16[4,128]{1,0:T(4,128)(2,1)S(1)} %collective-permute-done, bf16[6144,128]{1,0:T(8,128)(2,1)S(1)} %get-tuple-element.16, bf16[4,128]{1,0:T(4,128)(2,1)S(1)} %collective-permute-done.1), dimensions={0} | concatenate | bytes 3149824 | tf_op jit(solution)/shard_map/concatenate | solution.py:20
  214.3 0.0 all-gather.3.cloned.1.call-update
  214.3 0.0 reduce-scatter.5.cloned.1.call-start
  214.4 1.6 fusion.18
  215.9 0.0 all-gather.5.cloned.1.call-done
  215.9 0.0 copy-start.7
  215.9 3.9 fusion.21
  219.9 0.0 copy-done.7
  219.9 1.8 fusion.19
  221.7 3.8 pad_maximum_fusion
  225.6 0.0 reduce-scatter.5.cloned.1.call-update
  225.6 0.0 copy-start.1
  225.6 60.4 %all-gather.3.cloned.1.call-done = bf16[6152,512]{1,0:T(8,128)(2,1)} async-done(((bf16[6152,128]{1,0:T(8,128)(2,1)}), bf16[6152,512]{1,0:T(8,128)(2,1)}) %all-gather.3.cloned.1.call-update) | async-done | bytes 6299664 | tf_op jit(solution)/shard_map/all_gather | solution.py:37
  286.0 5.3 %slice_bitcast_fusion.1 = (bf16[768,8,512]{2,1,0:T(8,128)(2,1)S(1)}, bf16[768,8,512]{2,1,0:T(8,128)(2,1)S(1)}) fusion(bf16[6152,512]{1,0:T(8,128)(2,1)} %all-gather.3.cloned.1.call-done), kind=kLoop, calls=%fused_computation.4 | loop fusion | bytes 25165824 | tf_op jit(solution)/shard_map/slice | solution.py:41
  291.3 0.0 copy-done.1
  291.3 0.0 copy-start.3
  291.3 3.9 fusion.28
  295.2 0.0 copy-done.3
  295.2 4.7 %fusion.38 = bf16[768,256]{1,0:T(8,128)(2,1)} fusion(f32[768,256]{1,0:T(8,128)S(1)} %fusion.28, bf16[512,8,256]{2,1,0:T(8,128)(2,1)S(1)} %copy-done.3, bf16[768,8,512]{2,1,0:T(8,128)(2,1)S(1)} %get-tuple-element.9), kind=kOutput, calls=%fused_computation.37 | convolution fusion | flops 1611005952 | bytes 9568256 | tf_op jit(solution)/shard_map/ujr,rjp->up/dot_general | solution.py:40
  299.9 141.3 %reduce-scatter.5.cloned.1.call-done = f32[16,16,128]{2,0,1:T(8,128)} async-done(((f32[1024,16,128]{2,0,1:T(8,128)}), f32[16,16,128]{2,0,1:T(8,128)}) %reduce-scatter.5.cloned.1.call-update) | async-done | bytes 131088 | tf_op jit(solution)/shard_map/reduce_scatter | solution.py:65
  441.3 0.9 multiply_convert_fusion
  442.2 0.6 copy.23
  (2 shorter events, 0.0 us)
Async XLA Ops:
  7.2 166.4 %reduce-scatter.3.cloned.1.call-start = ((), (), s32[]{:S(2)}) async-start(), calls=%async_computation.3 | async-start | bytes 15728640 | tf_op jit(solution)/shard_map/reduce_scatter | solution.py:55
  7.9 11.8 %collective-permute-start.3 = (bf16[1,256]{1,0:T(2,128)(2,1)S(1)}, bf16[1,256]{1,0:T(2,128)(2,1)S(1)}, u32[]{:S(2)}, u32[]{:S(2)}) collective-permute-start(bf16[1,256]{1,0:T(2,128)(2,1)S(1)} %get-tuple-element.20), channel_id=1, source_target_pairs={{0,4},{4,8},{8,12},{12,16},{16,20},{20,24},{24,28},{28,32},{32,36}... | collective-permute-start | bytes 1544 | tf_op jit(solution)/shard_map/ppermute | solution.py:16
  9.8 9.9 %copy-start.4 = (bf16[768,256]{1,0:T(8,128)(2,1)S(1)}, bf16[768,256]{1,0:T(8,128)(2,1)}, u32[]{:S(2)}) copy-start(bf16[768,256]{1,0:T(8,128)(2,1)} %param.7) | copy-start | bytes 1179652
  9.9 11.7 %collective-permute-start.2 = (bf16[1,256]{1,0:T(2,128)(2,1)S(1)}, bf16[1,256]{1,0:T(2,128)(2,1)S(1)}, u32[]{:S(2)}, u32[]{:S(2)}) collective-permute-start(bf16[1,256]{1,0:T(2,128)(2,1)S(1)} %get-tuple-element.19), channel_id=1, source_target_pairs={{4,0},{8,4},{12,8},{16,12},{20,16},{24,20},{28,24},{32,28},{36,32}... | collective-permute-start | bytes 1544 | tf_op jit(solution)/shard_map/ppermute | solution.py:19
  19.7 1.9 copy-start
  19.7 2.0 copy-start.2
  55.7 1.6 copy-start.6
  55.7 117.8 %copy-start.5 = (bf16[6144,128]{1,0:T(8,128)(2,1)S(1)}, bf16[6144,128]{1,0:T(8,128)(2,1)}, u32[]{:S(2)}) copy-start(bf16[6144,128]{1,0:T(8,128)(2,1)} %param.4) | copy-start | bytes 4718596
  55.7 160.2 %all-gather.5.cloned.1.call-start = ((), (), s32[]{:S(2)}) async-start(), calls=%async_computation.4 | async-start | bytes 2293760 | tf_op jit(solution)/shard_map/all_gather | solution.py:48
  57.3 228.7 %all-gather.3.cloned.1.call-start = ((), (), s32[]{:S(2)}) async-start(), calls=%async_computation.2 | async-start | bytes 7874560 | tf_op jit(solution)/shard_map/all_gather | solution.py:37
  196.6 7.7 %collective-permute-start = (bf16[4,128]{1,0:T(4,128)(2,1)S(1)}, bf16[4,128]{1,0:T(4,128)(2,1)S(1)}, u32[]{:S(2)}, u32[]{:S(2)}) collective-permute-start(bf16[4,128]{1,0:T(4,128)(2,1)S(1)} %get-tuple-element.18), channel_id=1, source_target_pairs={{0,4},{4,8},{8,12},{12,16},{16,20},{20,24},{24,28},{28,32},{32,36}... | collective-permute-start | bytes 3080 | tf_op jit(solution)/shard_map/ppermute | solution.py:16
  198.6 7.0 %collective-permute-start.1 = (bf16[4,128]{1,0:T(4,128)(2,1)S(1)}, bf16[4,128]{1,0:T(4,128)(2,1)S(1)}, u32[]{:S(2)}, u32[]{:S(2)}) collective-permute-start(bf16[4,128]{1,0:T(4,128)(2,1)S(1)} %get-tuple-element.17), channel_id=1, source_target_pairs={{4,0},{8,4},{12,8},{16,12},{20,16},{24,20},{28,24},{32,28},{36,32}... | collective-permute-start | bytes 3080 | tf_op jit(solution)/shard_map/ppermute | solution.py:19
  214.3 226.9 %reduce-scatter.5.cloned.1.call-start = ((), (), s32[]{:S(2)}) async-start(), calls=%async_computation.5 | async-start | bytes 8519680 | tf_op jit(solution)/shard_map/reduce_scatter | solution.py:65
  215.9 3.9 copy-start.7
  225.6 65.7 %copy-start.1 = (bf16[512,8,256]{2,1,0:T(8,128)(2,1)S(1)}, bf16[512,8,256]{2,1,0:T(8,128)(2,1)}, u32[]{:S(2)}) copy-start(bf16[512,8,256]{2,1,0:T(8,128)(2,1)} %copy-done) | copy-start | bytes 6291460
  291.3 3.9 copy-start.3
Sparse Core Ops, SparseCore 0:
  55.9 117.6 reduce-scatter.2
  175.4 31.0 all-gather.4
  214.4 71.4 all-gather.2
  290.0 151.1 reduce-scatter.4
where the time goes:
time: 451 us; the launch traced here: 449 us
  waiting for transfers between devices  319 us (71%)
  local copies, waits for them, and re-layouts  45.7 us (10%)
  other arithmetic  30.4 us (7%)
  matrix products  23 us (5%)
  starting transfers between devices  17.1 us (4%)
  between operations  14 us (3%)
    reduce_scatter x1, waiting for transfers between devices, shards(): lax.psum_scatter(jnp.concatenate([lower, upper], axis=1), 'tm', scatter_d...  141 us
    reduce_scatter x1, waiting for transfers between devices, shards(): lax.psum_scatter(partial_terms, 'chan', scatter_dimension=1, tiled=True)  116 us
    all_gather x1, waiting for transfers between devices, shards(): full_cols = lax.all_gather(padded, 'chan', axis=1, tiled=True)  60.4 us
    convert_element_type x1, other arithmetic, shards(): (grad_snaked * (1.0 + jnp.sin(2.0 * snake_alpha * wide))).astype(jnp.bflo...  23.1 us
    add x1, local copies, waits for them, and re-layouts, shards(): jnp.einsum('up,rjp->ujr', grad_pad[1:], down_weight[:, :STRIDE], preferre...  16.4 us
    ppermute x2, starting transfers between devices, with_halo(): lax.ppermute(lax.slice_in_dim(block, 0, width, axis=dim), axis, backward)  13.1 us
    slice x1, local copies, waits for them, and re-layouts, shards(): spread.reshape(frames + STRIDE, down_weight.shape[0])  10.9 us
  transfers between devices with their start and end apart: 8, of which 4 were waited for; matrix products, arithmetic and copies ran while one was open for 14% of the time, Pallas kernels for 0%

commit v1 on v0

v1 whole, which is shorter than its diff:
```python
import functools
import math

import jax
import jax.numpy as jnp
from jax import lax
from jax.experimental import pallas as pl
from jax.experimental.pallas import tpu as pltpu
from jax.sharding import Mesh
from jax.sharding import PartitionSpec as P

STRIDE = 8
TAPS = 16
BF = jnp.bfloat16
F32 = jnp.float32
TM = ("x", "z", "core")
SIN = (1.0, -1.66666666e-01, 8.33333079e-03, -1.98408371e-04, 2.75240247e-06, -2.38669497e-08)
COS = (
    1.0,
    -0.5,
    4.16666665e-02,
    -1.38888838e-03,
    2.48010074e-05,
    -2.75233926e-07,
    1.98888297e-09,
)
PI_A = 3.140625
PI_B = math.pi - PI_A
VMEM = pl.BlockSpec(memory_space=pltpu.VMEM)
SMEM = pl.BlockSpec(memory_space=pltpu.SMEM)
ANY = pl.BlockSpec(memory_space=pl.ANY)
LIMIT = 56 * 2**20


def params():
    return pltpu.CompilerParams(vmem_limit_bytes=LIMIT)


def cost(flops, moved):
    return pl.CostEstimate(flops=int(flops), bytes_accessed=int(moved), transcendentals=0)


def poly(coefs, z):
    out = jnp.full_like(z, coefs[-1])
    for c in coefs[-2::-1]:
        out = out * z + c
    return out


def sincos(theta):
    n = jnp.floor(theta * (1.0 / math.pi) + 0.5)
    r = (theta - n * PI_A) - n * PI_B
    z = r * r
    return r * poly(SIN, z), poly(COS, z)


def prep_kernel(feat, low, high, alpha, taps, factor, rows):
    frames = feat.shape[0]
    outs = frames // STRIDE
    a = alpha[...]
    inv = 1.0 / a

    def snake(values):
        wide = values.astype(F32)
        s, c = sincos(a * wide)
        return (wide + s * s * inv).astype(BF).astype(F32), 1.0 + 2.0 * s * c

    rows[0:8, :] = snake(low[8:16, :])[0]
    rows[frames + 8 : frames + 16, :] = snake(high[0:8, :])[0]
    step = 256

    def body(at, carry):
        here = pl.multiple_of(at * step, step)
        act, fac = snake(feat[pl.ds(here, step), :])
        rows[pl.ds(here + 8, step), :] = act
        factor[pl.ds(here, step), :] = fac
        return carry

    lax.fori_loop(0, frames // step, body, 0)
    for k in range(TAPS):
        taps[:, k * 128 : (k + 1) * 128] = rows[pl.ds(4 + k, outs, stride=STRIDE), :].astype(BF)


def prep(feat, low, high, alpha):
    frames, chans = feat.shape
    return pl.pallas_call(
        prep_kernel,
        out_shape=(
            jax.ShapeDtypeStruct((frames // STRIDE, TAPS * chans), BF),
            jax.ShapeDtypeStruct((frames, chans), F32),
        ),
        in_specs=[VMEM] * 4,
        out_specs=(VMEM, VMEM),
        scratch_shapes=[pltpu.VMEM((frames + 16, chans), F32)],
        compiler_params=params(),
        cost_estimate=cost(frames * chans * 60, frames * chans * 10),
        name="prep",
    )(feat, low, high, alpha)


def kernel_grad_kernel(which, taps, g0, g1, g2, g3, out):
    cols = g0.shape[1]
    half = cols // 2
    row = lax.broadcasted_iota(jnp.int32, (half, cols), 0)
    col = lax.broadcasted_iota(jnp.int32, (half, cols), 1)
    want = (row // 16) * 32 + which[0] * 16 + row % 16
    pick = jnp.where(col == want, 1.0, 0.0).astype(BF)
    for d, g in enumerate((g0, g1, g2, g3)):
        lhs = lax.dot_general(
            pick, g[...], (((1,), (1,)), ((), ())), preferred_element_type=F32
        ).astype(BF)
        for n in range(0, taps.shape[1], 512):
            out[d * half : (d + 1) * half, n : n + 512] = jnp.dot(
                lhs, taps[:, n : n + 512], preferred_element_type=F32
            ).astype(out.dtype)


def kernel_grad(which, taps, gs, dtype, name):
    rows = 2 * gs[0].shape[1]
    return pl.pallas_call(
        kernel_grad_kernel,
        out_shape=jax.ShapeDtypeStruct((rows, taps.shape[1]), dtype),
        in_specs=[SMEM] + [VMEM] * 5,
        out_specs=VMEM,
        compiler_params=params(),
        cost_estimate=cost(2 * rows * taps.shape[0] * taps.shape[1], 9e6),
        name=name,
    )(which, taps, *gs)


def encode_kernel(place, taps, own_w, *refs):
    pieces, (out, weights, sem) = refs[:8], refs[8:]
    copies = []

    def copy(src, row, size, d):
        c = pltpu.make_async_copy(
            src,
            weights.at[pl.ds(row, size), d * 256 : (d + 1) * 256],
            sem.at[len(copies)],
        )
        c.start()
        copies.append(c)

    copy(own_w, 0, 2048, 0)
    for n, piece in enumerate(pieces):
        row = pl.multiple_of(place[n] * 256, 256)
        for d in range(3):
            copy(piece.at[d], row, 256, d + 1)
    for c in copies:
        c.wait()
    for n in range(1024 // 256):
        for m in range(0, 768, 256):
            out[n, m : m + 256, :] = jnp.dot(
                taps[m : m + 256, :],
                weights[:, n * 256 : (n + 1) * 256],
                preferred_element_type=F32,
            ).astype(BF)


def encode(place, taps, own_w, pieces):
    return pl.pallas_call(
        encode_kernel,
        out_shape=(
            jax.ShapeDtypeStruct((4, 768, 256), BF),
            jax.ShapeDtypeStruct((2048, 1024), BF),
        ),
        in_specs=[SMEM, VMEM] + [ANY] * 9,
        out_specs=(VMEM, VMEM),
        scratch_shapes=[pltpu.SemaphoreType.DMA((25,))],
        compiler_params=params(),
        cost_estimate=cost(2 * 768 * 2048 * 1024, 13e6),
        name="encode",
    )(place, taps, own_w, *pieces)


def input_grad_kernel(g0, g1, g2, g3, edge, weights, factor, out, full, rows):
    outs = g0.shape[0]
    frames = out.shape[0]
    for d, g in enumerate((g0, g1, g2, g3)):
        full[0:outs, d * 256 : (d + 1) * 256] = g[...]
    full[outs : outs + 16, :] = edge[...]
    rows[frames : frames + 16, :] = jnp.zeros((16, 128), F32)
    for pair in range(TAPS // 2):
        res = lax.dot_general(
            full[...],
            weights[pair * 256 : (pair + 1) * 256, :],
            (((1,), (1,)), ((), ())),
            preferred_element_type=F32,
        )
        for side in range(2):
            k = 2 * pair + side
            part = res[:, side * 128 : (side + 1) * 128]
            at = pl.ds(4 + k, outs, stride=STRIDE)
            if k < STRIDE:
                rows[at, :] = part[:outs]
                if k < 4:
                    rows[frames + 4 + k : frames + 5 + k, :] = part[outs + 8 : outs + 9]
            else:
                if k < 12:
                    rows[at, :] = rows[at, :] + part[:outs]
                else:
                    rows[k - 4 : k - 3, :] = rows[k - 4 : k - 3, :] + part[outs : outs + 1]
                    rows[at, :] = rows[at, :] + part[:outs]
    step = 512
    for at in range(0, frames, step):
        out[at : at + step, :] = (
            rows[at + 8 : at + 8 + step, :] * factor[at : at + step, :]
        ).astype(BF)


def input_grad(gs, edge, weights, factor):
    frames, chans = factor.shape
    return pl.pallas_call(
        input_grad_kernel,
        out_shape=jax.ShapeDtypeStruct((frames, chans), BF),
        in_specs=[VMEM] * 7,
        out_specs=VMEM,
        scratch_shapes=[
            pltpu.VMEM((frames // STRIDE + 16, 1024), BF),
            pltpu.VMEM((frames + 16, chans), F32),
        ],
        compiler_params=params(),
        cost_estimate=cost(2 * 784 * 2048 * 1024, 13e6),
        name="input_grad",
    )(*gs, edge, weights, factor)


def turn(value, axis, by):
    count = lax.axis_size(axis)
    return lax.ppermute(value, axis, [(i, (i + by) % count) for i in range(count)])


def beside(value, by):
    count = math.prod(lax.axis_size(a) for a in TM)
    pairs = [(i, i + by) for i in range(count) if 0 <= i + by < count]
    return lax.ppermute(value, TM, pairs)


def shards(features, snake_alpha, down_weight, grad_out):
    x, z, core, y = (lax.axis_index(a) for a in ("x", "z", "core", "chan"))

    from_left = turn(grad_out, "chan", 1)
    from_right = turn(grad_out, "chan", -1)
    from_far = turn(grad_out, "chan", 2)
    gs = (grad_out, from_right, from_far, from_left)

    pair = x * 2 + core
    mine = lax.dynamic_slice(down_weight, (0, 2 * pair, 0), (512, 2, 256))
    mine = mine.reshape(4, 128, 2, 256).transpose(0, 2, 1, 3).reshape(4, 256, 256)

    def for_block(s):
        return lax.dynamic_index_in_dim(mine, (y + s) % 4, 0, keepdims=False)

    w3 = turn(for_block(1), "chan", 1)
    w1 = turn(for_block(3), "chan", -1)
    w2 = turn(for_block(2), "chan", 2)
    base = jnp.stack([w1, w2, w3])

    low = beside(features[-16:], 1)
    high = beside(features[:16], -1)
    taps, factor = prep(features, low, high, snake_alpha.reshape(1, -1))

    pieces = [base, turn(base, "x", -1), turn(base, "x", 1), turn(base, "x", 2)]
    places = [pair, ((x + 1) % 4) * 2 + core, ((x + 3) % 4) * 2 + core, ((x + 2) % 4) * 2 + core]
    pieces = pieces + [turn(p, "core", 1) for p in pieces]
    places = places + [p + 1 - 2 * core for p in places]

    own_w = lax.dynamic_slice(down_weight, (128 * y, 0, 0), (128, 16, 256))
    own_w = own_w.transpose(1, 0, 2).reshape(2048, 256)

    send = kernel_grad((1 - core).reshape(1), taps, gs, BF, "kernel_grad_send")
    got = turn(send, "core", 1)
    keep = kernel_grad(core.reshape(1), taps, gs, F32, "kernel_grad_keep")

    def for_x(e):
        at = ((x + e + 4 - y) % 4) * 128
        return lax.dynamic_slice(keep, (at, 0), (128, 2048)) + lax.dynamic_slice(
            got, (at, 0), (128, 2048)
        ).astype(F32)

    right = turn(for_x(1).astype(BF), "x", 1)
    left = turn(for_x(3).astype(BF), "x", -1)
    far = turn(for_x(2).astype(BF), "x", 2)

    partial, weights = encode(jnp.stack(places).astype(jnp.int32), taps, own_w, pieces)
    e3 = turn(partial[1], "chan", 1)
    e1 = turn(partial[3], "chan", -1)
    e2 = turn(partial[2], "chan", 2)

    last = jnp.concatenate([g[-1:] for g in gs], axis=1)
    first = jnp.concatenate([g[:1] for g in gs], axis=1)
    fill = jnp.zeros((7, 1024), BF)
    edge = jnp.concatenate([beside(last, 1), fill, beside(first, -1), fill])
    grad_features = input_grad(gs, edge, weights, factor)

    encoded = (
        partial[0].astype(F32) + e1.astype(F32) + e2.astype(F32) + e3.astype(F32)
    ).astype(BF)

    lines = (for_x(0) + right.astype(F32) + left.astype(F32) + far.astype(F32)).astype(BF)
    spread = lax.all_to_all(lines.reshape(8, 16, 2048), "z", 0, 0)
    scale = 1.0 / math.sqrt(features.shape[0] // STRIDE * 64)
    summed = jnp.sum(spread.astype(F32), axis=0) * scale
    grad_down = summed.astype(BF).reshape(16, 16, 128)
    return (encoded, grad_features, grad_down)


def solution(mesh):
    tm, chan = mesh.shape["tm"], mesh.shape["chan"]
    fine = Mesh(mesh.devices.reshape(4, tm // 8, 2, chan), (*TM, "chan"))
    placed = (P(TM, "chan"), P("chan"), P(None, None, "chan"), P(TM, "chan"))
    return jax.shard_map(
        shards,
        mesh=fine,
        in_specs=placed,
        out_specs=(P(TM, "chan"), P(TM, "chan"), P(TM, None, "chan")),
        check_vma=False,
    )
```

time: 451 us -> 139 us (0.31)
  waiting for transfers between devices: 319 us -> 20.7 us
  Pallas kernels: 0 us -> 40.1 us
  starting transfers between devices: 17.1 us -> 55.1 us
  local copies, waits for them, and re-layouts: 45.7 us -> 12.6 us
  matrix products: 23 us -> 0 us
  other arithmetic: 30.4 us -> 7.63 us
  between operations: 14 us -> 0.98 us
    reduce_scatter x2 -> x0, waiting for transfers between devices: 258 us -> none  [the longest x1 141 us: shards(): lax.psum_scatter(jnp.concatenate([lower, upper], axis=1), 'tm', scatter_d...]
    all_gather x2 -> x0, waiting for transfers between devices: 60.4 us -> none  [the longest x1 60.4 us: shards(): full_cols = lax.all_gather(padded, 'chan', axis=1, tiled=True)]
    pallas_call x0 -> x5, Pallas kernels: none -> 40.1 us  [the longest x2 13 us: kernel_grad(): pl.pallas_call(kernel_grad_kernel, out_shape=jax.ShapeDtypeStruct((rows,...]
    ppermute x4 -> x24, starting transfers between devices: 16.9 us -> 48.3 us  [the longest x20 33.1 us: turn(): lax.ppermute(value, axis, [(i, (i + by) % count) for i in range(count)])]
    dot_general x6 -> x0, matrix products: 23 us -> none  [the longest x1 6.72 us: shards(): jnp.einsum('up,rjp->ujr', grad_pad[1:], down_weight[:, :STRIDE], preferre...]
    ppermute x4 -> x24, waiting for transfers between devices: 1.27 us -> 20.7 us  [the longest x20 19.4 us: turn(): lax.ppermute(value, axis, [(i, (i + by) % count) for i in range(count)])]
    convert_element_type x2 -> x3, other arithmetic: 24 us -> 6.84 us  [the longest x1 2.51 us: shards(): right = turn(for_x(1).astype(BF), 'x', 1)]
    add x1 -> x0, local copies, waits for them, and re-layouts: 16.4 us -> none  [shards(): jnp.einsum('up,rjp->ujr', grad_pad[1:], down_weight[:, :STRIDE], preferre...]
  transfers between devices with their start and end apart: 8 -> 25, of which waited for: 4 -> 7; matrix products, arithmetic and copies ran while one was open for 14% -> 13% of each run, Pallas kernels for 0% -> 25%
where the time goes in v1:
time: 139 us; the launch traced here: 137 us
  starting transfers between devices  55.1 us (40%)
  Pallas kernels  40.1 us (29%)
  waiting for transfers between devices  20.7 us (15%)
  local copies, waits for them, and re-layouts  12.6 us (9%)
  other arithmetic  7.63 us (5%)
    ppermute x20, starting transfers between devices, turn(): lax.ppermute(value, axis, [(i, (i + by) % count) for i in range(count)])  33.1 us
    ppermute x20, waiting for transfers between devices, turn(): lax.ppermute(value, axis, [(i, (i + by) % count) for i in range(count)])  19.4 us
    ppermute x4, starting transfers between devices, beside(): return lax.ppermute(value, TM, pairs)  15.2 us
    pallas_call x2, Pallas kernels, kernel_grad(): pl.pallas_call(kernel_grad_kernel, out_shape=jax.ShapeDtypeStruct((rows,...  13 us
    pallas_call x1, Pallas kernels, input_grad(): pl.pallas_call(input_grad_kernel, out_shape=jax.ShapeDtypeStruct((frames,...  9.22 us
    pallas_call x1, Pallas kernels, prep(): pl.pallas_call(prep_kernel, out_shape=(jax.ShapeDtypeStruct((frames // ST...  9.11 us
    pallas_call x1, Pallas kernels, encode(): pl.pallas_call(encode_kernel, out_shape=(jax.ShapeDtypeStruct((4, 768, 25...  8.8 us
    all_to_all x1, starting transfers between devices, shards(): spread = lax.all_to_all(lines.reshape(8, 16, 2048), 'z', 0, 0)  6.75 us
  transfers between devices with their start and end apart: 25, of which 7 were waited for; matrix products, arithmetic and copies ran while one was open for 13% of the time, Pallas kernels for 25%

profile of v1, /device:TPU:2, one launch (start us, length us, event | category | flops | bytes accessed | tf_op | source)
XLA Modules:
  0.0 137.1 jit_solution(1137562625887989349)
XLA Ops:
  0.6 3.1 %collective-permute-start.15 = (bf16[768,256]{1,0:T(8,128)(2,1)}, bf16[768,256]{1,0:T(8,128)(2,1)S(1)}, u32[]{:S(2)}, u32[]{:S(2)}) collective-permute-start(bf16[768,256]{1,0:T(8,128)(2,1)} %g0.5), channel_id=1, source_target_pairs={{0,3},{1,0},{2,1},{3,2},{4,7},{5,4},{6,5},{7,6},{8,11},{9,8},{10,9... | collective-permute-start | bytes 1179656 | tf_op jit(solution)/shard_map/ppermute | solution.py:230
  3.7 0.6 collective-permute-start.16
  4.4 1.0 collective-permute-start.17
  5.3 0.7 fusion.4
  6.0 1.9 %collective-permute-start = (bf16[16,128]{1,0:T(8,128)(2,1)S(1)}, bf16[16,128]{1,0:T(8,128)(2,1)S(1)}, u32[]{:S(2)}, u32[]{:S(2)}) collective-permute-start(bf16[16,128]{1,0:T(8,128)(2,1)S(1)} %get-tuple-element.18), channel_id=1, source_target_pairs={{0,4},{4,8},{8,12},{12,16},{16,20},{20,24},{24,28},{28,32},{32,36}... | collective-permute-start | bytes 12296 | tf_op jit(solution)/shard_map/ppermute | solution.py:236
  7.9 6.3 %collective-permute-start.1 = (bf16[16,128]{1,0:T(8,128)(2,1)S(1)}, bf16[16,128]{1,0:T(8,128)(2,1)S(1)}, u32[]{:S(2)}, u32[]{:S(2)}) collective-permute-start(bf16[16,128]{1,0:T(8,128)(2,1)S(1)} %get-tuple-element.17), channel_id=1, source_target_pairs={{4,0},{8,4},{12,8},{16,12},{20,16},{24,20},{28,24},{32,28},{36,32}... | collective-permute-start | bytes 12296 | tf_op jit(solution)/shard_map/ppermute | solution.py:236
  14.3 0.0 collective-permute-done.low
  14.3 0.0 copy-start.4
  14.3 1.3 collective-permute-done.1.high
  15.6 0.6 copy-done.5
  16.2 9.1 %prep.1 = (bf16[768,2048]{1,0:T(8,128)(2,1)}, f32[6144,128]{1,0:T(8,128)}) custom-call(bf16[6144,128]{1,0:T(8,128)(2,1)} %feat.1, bf16[16,128]{1,0:T(8,128)(2,1)} %copy-done.4, bf16[16,128]{1,0:T(8,128)(2,1)} %copy-done.5, f32[1,128]{1,0:T(1,128)} %bitcast.47), custom_call_target="tpu_custom_call" | custom-call | flops 47185920 | bytes 7864320 | tf_op jit(solution)/shard_map/prep/pallas_call | solution.py:86
  25.3 0.0 collective-permute-done.16.g2
  25.3 0.7 copy-done
  26.0 0.2 copy-done.1
  26.2 0.1 copy-done.2
  26.3 6.2 %kernel_grad_send.1 = bf16[512,2048]{1,0:T(8,128)(2,1)} custom-call(s32[1]{0:T(128)} %bitcast.25.which, bf16[768,2048]{1,0:T(8,128)(2,1)} %get-tuple-element.7.taps, bf16[768,256]{1,0:T(8,128)(2,1)} %g0.5, bf16[768,256]{1,0:T(8,128)(2,1)} %copy-done, bf16[768,256]{1,0:T(8,128)(2,1)} %copy-done.1, bf16[768,256]{1,0:T(8,128)(2,1)} %copy-done.2), custom_call_target="tpu_custom_call" | custom-call | flops 1610612736 | bytes 9000000 | tf_op jit(solution)/shard_map/kernel_grad_send/pallas_call | solution.py:120
  32.5 0.0 collective-permute-start.20
  32.5 2.1 %constant_dynamic-slice_fusion = bf16[512,2,256]{2,1,0:T(2,128)(2,1)S(1)} fusion(bf16[512,16,256]{2,1,0:T(8,128)(2,1)} %param.6, s32[]{:T(128)S(6)} %select_n.79), kind=kLoop, calls=%fused_computation.22 | loop fusion | bytes 1048580 | tf_op jit(solution)/shard_map/dynamic_slice | solution.py:248
  34.6 0.1 copy.13
  34.8 2.0 %collective-permute-start.4 = (bf16[256,256]{1,0:T(8,128)(2,1)S(1)}, bf16[256,256]{1,0:T(8,128)(2,1)S(1)}, u32[]{:S(2)}, u32[]{:S(2)}) collective-permute-start(bf16[256,256]{1,0:T(8,128)(2,1)S(1)} %get-tuple-element.20), channel_id=1, source_target_pairs={{0,1},{1,2},{2,3},{3,0},{4,5},{5,6},{6,7},{7,4},{8,9},{9,10},{10,1... | collective-permute-start | bytes 393224 | tf_op jit(solution)/shard_map/ppermute | solution.py:230
  36.8 1.8 %collective-permute-start.3 = (bf16[256,256]{1,0:T(8,128)(2,1)S(1)}, bf16[256,256]{1,0:T(8,128)(2,1)S(1)}, u32[]{:S(2)}, u32[]{:S(2)}) collective-permute-start(bf16[256,256]{1,0:T(8,128)(2,1)S(1)} %get-tuple-element.21), channel_id=1, source_target_pairs={{0,2},{1,3},{2,0},{3,1},{4,6},{5,7},{6,4},{7,5},{8,10},{9,11},{10,... | collective-permute-start | bytes 393224 | tf_op jit(solution)/shard_map/ppermute | solution.py:230
  38.6 1.1 collective-permute-start.2
  39.7 1.3 dynamic-slice_bitcast_fusion
  41.0 1.3 copy.10
  42.3 0.6 stack.47.place
  43.0 0.7 fusion.5
  43.7 1.6 %collective-permute-done.3 = bf16[256,256]{1,0:T(8,128)(2,1)S(1)} collective-permute-done((bf16[256,256]{1,0:T(8,128)(2,1)S(1)}, bf16[256,256]{1,0:T(8,128)(2,1)S(1)}, u32[]{:S(2)}, u32[]{:S(2)}) %collective-permute-start.3) | collective-permute-done | bytes 131104 | tf_op jit(solution)/shard_map/ppermute | solution.py:230
  45.3 0.1 collective-permute-done.2
  45.4 0.0 copy-start.3
  45.5 0.1 collective-permute-start.5
  45.5 2.0 %collective-permute-start.6 = (bf16[3,256,256]{2,1,0:T(8,128)(2,1)S(1)}, bf16[3,256,256]{2,1,0:T(8,128)(2,1)S(1)}, u32[]{:S(2)}, u32[]{:S(2)}) collective-permute-start(bf16[3,256,256]{2,1,0:T(8,128)(2,1)S(1)} %pad_maximum_fusion.refs_0_), channel_id=1, source_target_pairs={{0,64},{64,128},{128,192},{192,0},{1,65},{65,129},{129,193},{193,1... | collective-permute-start | bytes 1179656 | tf_op jit(solution)/shard_map/ppermute | solution.py:230
  47.6 3.6 %collective-permute-start.7 = (bf16[3,256,256]{2,1,0:T(8,128)(2,1)S(1)}, bf16[3,256,256]{2,1,0:T(8,128)(2,1)S(1)}, u32[]{:S(2)}, u32[]{:S(2)}) collective-permute-start(bf16[3,256,256]{2,1,0:T(8,128)(2,1)S(1)} %pad_maximum_fusion.refs_0_), channel_id=1, source_target_pairs={{0,128},{64,192},{128,0},{192,64},{1,129},{65,193},{129,1},{193,65... | collective-permute-start | bytes 1179656 | tf_op jit(solution)/shard_map/ppermute | solution.py:230
  51.2 0.7 fusion.8
  51.9 0.7 fusion.7
  52.6 0.7 fusion.6
  53.2 3.4 %collective-permute-done.5.refs_1_ = bf16[3,256,256]{2,1,0:T(8,128)(2,1)S(1)} collective-permute-done((bf16[3,256,256]{2,1,0:T(8,128)(2,1)S(1)}, bf16[3,256,256]{2,1,0:T(8,128)(2,1)S(1)}, u32[]{:S(2)}, u32[]{:S(2)}) %collective-permute-start.5) | collective-permute-done | bytes 393248 | tf_op jit(solution)/shard_map/ppermute | solution.py:230
  56.6 0.0 collective-permute-start.9
  56.6 6.9 %kernel_grad_keep.1 = f32[512,2048]{1,0:T(8,128)} custom-call(s32[1]{0:T(128)} %bitcast.24.which, bf16[768,2048]{1,0:T(8,128)(2,1)} %get-tuple-element.7.taps, bf16[768,256]{1,0:T(8,128)(2,1)} %g0.5, bf16[768,256]{1,0:T(8,128)(2,1)} %copy-done, bf16[768,256]{1,0:T(8,128)(2,1)} %copy-done.1, bf16[768,256]{1,0:T(8,128)(2,1)} %copy-done.2), custom_call_target="tpu_custom_call" | custom-call | flops 1610612736 | bytes 9000000 | tf_op jit(solution)/shard_map/kernel_grad_keep/pallas_call | solution.py:120
  63.5 0.5 collective-permute-start.10
  64.0 1.5 %collective-permute-done.7.refs_3_ = bf16[3,256,256]{2,1,0:T(8,128)(2,1)S(1)} collective-permute-done((bf16[3,256,256]{2,1,0:T(8,128)(2,1)S(1)}, bf16[3,256,256]{2,1,0:T(8,128)(2,1)S(1)}, u32[]{:S(2)}, u32[]{:S(2)}) %collective-permute-start.7) | collective-permute-done | bytes 393248 | tf_op jit(solution)/shard_map/ppermute | solution.py:230
  65.5 0.0 collective-permute-start.11
  65.5 0.0 collective-permute-done.20
  65.6 2.5 %add_convert_fusion.3 = (bf16[128,2048]{1,0:T(8,128)(2,1)S(1)}, bf16[128,2048]{1,0:T(8,128)(2,1)S(1)}, bf16[128,2048]{1,0:T(8,128)(2,1)S(1)}) fusion(f32[512,2048]{1,0:T(8,128)} %kernel_grad_keep.1, s32[]{:T(128)S(6)} %select_n.89, bf16[512,2048]{1,0:T(8,128)(2,1)S(1)} %collective-permute-done.20, s32[]{:T(128)S(6)} %select_n.93, s32[]{:T(128)S(6)} %select_n.91), kind=kLoop, calls=%fused_computation.4 | loop fusion | flops 2359296 | bytes 6291468 | tf_op jit(solution)/shard_map/convert_element_type | solution.py:281
  68.1 10.1 %collective-permute-start.23 = (bf16[128,2048]{1,0:T(8,128)(2,1)S(1)}, bf16[128,2048]{1,0:T(8,128)(2,1)S(1)}, u32[]{:S(2)}, u32[]{:S(2)}) collective-permute-start(bf16[128,2048]{1,0:T(8,128)(2,1)S(1)} %get-tuple-element.12), channel_id=1, source_target_pairs={{0,128},{64,192},{128,0},{192,64},{1,129},{65,193},{129,1},{193,65... | collective-permute-start | bytes 1572872 | tf_op jit(solution)/shard_map/ppermute | solution.py:230
  78.2 0.0 collective-permute-done.8.refs_4_
  78.2 0.0 collective-permute-start.22
  78.3 2.0 %collective-permute-start.21 = (bf16[128,2048]{1,0:T(8,128)(2,1)S(1)}, bf16[128,2048]{1,0:T(8,128)(2,1)S(1)}, u32[]{:S(2)}, u32[]{:S(2)}) collective-permute-start(bf16[128,2048]{1,0:T(8,128)(2,1)S(1)} %get-tuple-element.11), channel_id=1, source_target_pairs={{0,64},{64,128},{128,192},{192,0},{1,65},{65,129},{129,193},{193,1... | collective-permute-start | bytes 1572872 | tf_op jit(solution)/shard_map/ppermute | solution.py:230
  80.3 0.0 collective-permute-done.10.refs_6_
  80.3 5.1 %collective-permute-start.19 = (bf16[1,1024]{1,0:T(2,128)(2,1)S(1)}, bf16[1,1024]{1,0:T(2,128)(2,1)S(1)}, u32[]{:S(2)}, u32[]{:S(2)}) collective-permute-start(bf16[1,1024]{1,0:T(2,128)(2,1)S(1)} %pad_maximum_fusion.3), channel_id=1, source_target_pairs={{4,0},{8,4},{12,8},{16,12},{20,16},{24,20},{28,24},{32,28},{36,32}... | collective-permute-start | bytes 6152 | tf_op jit(solution)/shard_map/ppermute | solution.py:236
  85.4 1.9 %collective-permute-start.18 = (bf16[1,1024]{1,0:T(2,128)(2,1)S(1)}, bf16[1,1024]{1,0:T(2,128)(2,1)S(1)}, u32[]{:S(2)}, u32[]{:S(2)}) collective-permute-start(bf16[1,1024]{1,0:T(2,128)(2,1)S(1)} %pad_maximum_fusion.2), channel_id=1, source_target_pairs={{0,4},{4,8},{8,12},{12,16},{16,20},{20,24},{24,28},{28,32},{32,36}... | collective-permute-start | bytes 6152 | tf_op jit(solution)/shard_map/ppermute | solution.py:236
  87.4 8.8 %encode.1 = (bf16[4,768,256]{2,1,0:T(8,128)(2,1)}, bf16[2048,1024]{1,0:T(8,128)(2,1)}) custom-call(s32[8]{0:T(128)} %stack.47.place, bf16[768,2048]{1,0:T(8,128)(2,1)} %get-tuple-element.7.taps, bf16[2048,256]{1,0:T(8,128)(2,1)} %bitcast.42, bf16[3,256,256]{2,1,0:T(8,128)(2,1)} %copy-done.3, bf16[3,256,256]{2,1,0:T(8,128)(2,1)} %copy-done.6, ...), custom_call_target="tpu_custom_call" | custom-call | flops 3221225472 | bytes 13000000 | tf_op jit(solution)/shard_map/encode/pallas_call | solution.py:161
  96.2 5.7 %collective-permute-done.22 = bf16[128,2048]{1,0:T(8,128)(2,1)S(1)} collective-permute-done((bf16[128,2048]{1,0:T(8,128)(2,1)S(1)}, bf16[128,2048]{1,0:T(8,128)(2,1)S(1)}, u32[]{:S(2)}, u32[]{:S(2)}) %collective-permute-start.22) | collective-permute-done | bytes 524320 | tf_op jit(solution)/shard_map/ppermute | solution.py:230
  101.9 2.4 %add_convert_fusion = bf16[128,2048]{1,0:T(8,128)(2,1)} fusion(bf16[128,2048]{1,0:T(8,128)(2,1)S(1)} %collective-permute-done.23, bf16[128,2048]{1,0:T(8,128)(2,1)S(1)} %collective-permute-done.22, bf16[128,2048]{1,0:T(8,128)(2,1)S(1)} %collective-permute-done.21, f32[512,2048]{1,0:T(8,128)} %kernel_grad_keep.1, s32[]{:T(128)S(6)} %select_n.87, ...), kind=kLoop, calls=%fused_computation.1 | loop fusion | flops 2359296 | bytes 3670020 | tf_op jit(solution)/shard_map/convert_element_type | solution.py:300
  104.3 6.8 %all-to-all-start = ((bf16[8,16,2048]{2,1,0:T(8,128)(2,1)}), bf16[8,16,2048]{2,1,0:T(8,128)(2,1)S(1)}, u32[]{:S(2)}, u32[]{:S(2)}) async-start(bf16[8,16,2048]{2,1,0:T(8,128)(2,1)} %bitcast.26), calls=%async_computation | async-start | bytes 1048576 | tf_op jit(solution)/shard_map/all_to_all | solution.py:301
  111.1 1.3 slice_bitcast_fusion.2
  112.4 2.4 %collective-permute-start.14 = (bf16[768,256]{1,0:T(8,128)(2,1)S(1)}, bf16[768,256]{1,0:T(8,128)(2,1)S(1)}, u32[]{:S(2)}, u32[]{:S(2)}) collective-permute-start(bf16[768,256]{1,0:T(8,128)(2,1)S(1)} %get-tuple-element.15), channel_id=1, source_target_pairs={{0,1},{1,2},{2,3},{3,0},{4,5},{5,6},{6,7},{7,4},{8,9},{9,10},{10,1... | collective-permute-start | bytes 1179656 | tf_op jit(solution)/shard_map/ppermute | solution.py:230
  114.7 2.5 %collective-permute-start.13 = (bf16[768,256]{1,0:T(8,128)(2,1)S(1)}, bf16[768,256]{1,0:T(8,128)(2,1)S(1)}, u32[]{:S(2)}, u32[]{:S(2)}) collective-permute-start(bf16[768,256]{1,0:T(8,128)(2,1)S(1)} %get-tuple-element.16), channel_id=1, source_target_pairs={{0,2},{1,3},{2,0},{3,1},{4,6},{5,7},{6,4},{7,5},{8,10},{9,11},{10,... | collective-permute-start | bytes 1179656 | tf_op jit(solution)/shard_map/ppermute | solution.py:230
  117.2 0.3 collective-permute-start.12
  117.5 0.6 pad_maximum_fusion.1.edge
  118.2 9.2 %input_grad.1 = bf16[6144,128]{1,0:T(8,128)(2,1)} custom-call(bf16[768,256]{1,0:T(8,128)(2,1)} %g0.5, bf16[768,256]{1,0:T(8,128)(2,1)} %copy-done, bf16[768,256]{1,0:T(8,128)(2,1)} %copy-done.1, bf16[768,256]{1,0:T(8,128)(2,1)} %copy-done.2, bf16[16,1024]{1,0:T(8,128)(2,1)} %pad_maximum_fusion.1.edge, bf16[2048,1024]{1,0:T(8,128)(2,1)} %get-tuple-element.9.weights, ...), custom_call_target="tpu_custom_call" | custom-call | flops 3288334336 | bytes 13000000 | tf_op jit(solution)/shard_map/input_grad/pallas_call | solution.py:213
  127.4 7.0 %collective-permute-done.13 = bf16[768,256]{1,0:T(8,128)(2,1)S(1)} collective-permute-done((bf16[768,256]{1,0:T(8,128)(2,1)S(1)}, bf16[768,256]{1,0:T(8,128)(2,1)S(1)}, u32[]{:S(2)}, u32[]{:S(2)}) %collective-permute-start.13) | collective-permute-done | bytes 393248 | tf_op jit(solution)/shard_map/ppermute | solution.py:230
  134.4 1.9 %fusion.2 = bf16[768,256]{1,0:T(8,128)(2,1)} fusion(bf16[768,256]{1,0:T(8,128)(2,1)S(1)} %collective-permute-done.14, bf16[768,256]{1,0:T(8,128)(2,1)S(1)} %collective-permute-done.13, bf16[768,256]{1,0:T(8,128)(2,1)S(1)} %collective-permute-done.12, bf16[4,768,256]{2,1,0:T(8,128)(2,1)} %get-tuple-element.8), kind=kLoop, calls=%fused_computation.9 | loop fusion | flops 1572864 | bytes 1966080 | tf_op jit(solution)/shard_map/convert_element_type | solution.py:298
  136.3 0.1 convert_reduce_fusion
  136.4 0.6 copy.14
  (41 shorter events, 0.2 us)
Async XLA Ops:
  0.6 24.7 %collective-permute-start.15 = (bf16[768,256]{1,0:T(8,128)(2,1)}, bf16[768,256]{1,0:T(8,128)(2,1)S(1)}, u32[]{:S(2)}, u32[]{:S(2)}) collective-permute-start(bf16[768,256]{1,0:T(8,128)(2,1)} %g0.5), channel_id=1, source_target_pairs={{0,3},{1,0},{2,1},{3,2},{4,7},{5,4},{6,5},{7,6},{8,11},{9,8},{10,9... | collective-permute-start | bytes 1179656 | tf_op jit(solution)/shard_map/ppermute | solution.py:230
  3.7 21.6 %collective-permute-start.16 = (bf16[768,256]{1,0:T(8,128)(2,1)}, bf16[768,256]{1,0:T(8,128)(2,1)S(1)}, u32[]{:S(2)}, u32[]{:S(2)}) collective-permute-start(bf16[768,256]{1,0:T(8,128)(2,1)} %g0.5), channel_id=1, source_target_pairs={{0,2},{1,3},{2,0},{3,1},{4,6},{5,7},{6,4},{7,5},{8,10},{9,11},{10,... | collective-permute-start | bytes 1179656 | tf_op jit(solution)/shard_map/ppermute | solution.py:230
  4.4 21.0 %collective-permute-start.17 = (bf16[768,256]{1,0:T(8,128)(2,1)}, bf16[768,256]{1,0:T(8,128)(2,1)S(1)}, u32[]{:S(2)}, u32[]{:S(2)}) collective-permute-start(bf16[768,256]{1,0:T(8,128)(2,1)} %g0.5), channel_id=1, source_target_pairs={{0,1},{1,2},{2,3},{3,0},{4,5},{5,6},{6,7},{7,4},{8,9},{9,10},{10,1... | collective-permute-start | bytes 1179656 | tf_op jit(solution)/shard_map/ppermute | solution.py:230
  6.0 8.3 %collective-permute-start = (bf16[16,128]{1,0:T(8,128)(2,1)S(1)}, bf16[16,128]{1,0:T(8,128)(2,1)S(1)}, u32[]{:S(2)}, u32[]{:S(2)}) collective-permute-start(bf16[16,128]{1,0:T(8,128)(2,1)S(1)} %get-tuple-element.18), channel_id=1, source_target_pairs={{0,4},{4,8},{8,12},{12,16},{16,20},{20,24},{24,28},{28,32},{32,36}... | collective-permute-start | bytes 12296 | tf_op jit(solution)/shard_map/ppermute | solution.py:236
  7.9 7.6 %collective-permute-start.1 = (bf16[16,128]{1,0:T(8,128)(2,1)S(1)}, bf16[16,128]{1,0:T(8,128)(2,1)S(1)}, u32[]{:S(2)}, u32[]{:S(2)}) collective-permute-start(bf16[16,128]{1,0:T(8,128)(2,1)S(1)} %get-tuple-element.17), channel_id=1, source_target_pairs={{4,0},{8,4},{12,8},{16,12},{20,16},{24,20},{28,24},{32,28},{36,32}... | collective-permute-start | bytes 12296 | tf_op jit(solution)/shard_map/ppermute | solution.py:236
  14.3 1.3 copy-start.4
  15.6 0.6 copy-start.5
  25.3 0.7 copy-start
  25.3 0.9 copy-start.1
  25.3 1.0 copy-start.2
  32.5 33.1 %collective-permute-start.20 = (bf16[512,2048]{1,0:T(8,128)(2,1)}, bf16[512,2048]{1,0:T(8,128)(2,1)S(1)}, u32[]{:S(2)}, u32[]{:S(2)}) collective-permute-start(bf16[512,2048]{1,0:T(8,128)(2,1)} %kernel_grad_send.1), channel_id=1, source_target_pairs={{0,4},{4,0},{1,5},{5,1},{2,6},{6,2},{3,7},{7,3},{8,12},{12,8},{9,1... | collective-permute-start | bytes 6291464 | tf_op jit(solution)/shard_map/ppermute | solution.py:230
  34.8 8.9 %collective-permute-start.4 = (bf16[256,256]{1,0:T(8,128)(2,1)S(1)}, bf16[256,256]{1,0:T(8,128)(2,1)S(1)}, u32[]{:S(2)}, u32[]{:S(2)}) collective-permute-start(bf16[256,256]{1,0:T(8,128)(2,1)S(1)} %get-tuple-element.20), channel_id=1, source_target_pairs={{0,1},{1,2},{2,3},{3,0},{4,5},{5,6},{6,7},{7,4},{8,9},{9,10},{10,1... | collective-permute-start | bytes 393224 | tf_op jit(solution)/shard_map/ppermute | solution.py:230
  36.8 8.5 %collective-permute-start.3 = (bf16[256,256]{1,0:T(8,128)(2,1)S(1)}, bf16[256,256]{1,0:T(8,128)(2,1)S(1)}, u32[]{:S(2)}, u32[]{:S(2)}) collective-permute-start(bf16[256,256]{1,0:T(8,128)(2,1)S(1)} %get-tuple-element.21), channel_id=1, source_target_pairs={{0,2},{1,3},{2,0},{3,1},{4,6},{5,7},{6,4},{7,5},{8,10},{9,11},{10,... | collective-permute-start | bytes 393224 | tf_op jit(solution)/shard_map/ppermute | solution.py:230
  38.6 6.8 %collective-permute-start.2 = (bf16[256,256]{1,0:T(8,128)(2,1)S(1)}, bf16[256,256]{1,0:T(8,128)(2,1)S(1)}, u32[]{:S(2)}, u32[]{:S(2)}) collective-permute-start(bf16[256,256]{1,0:T(8,128)(2,1)S(1)} %get-tuple-element.19), channel_id=1, source_target_pairs={{0,3},{1,0},{2,1},{3,2},{4,7},{5,4},{6,5},{7,6},{8,11},{9,8},{10,9... | collective-permute-start | bytes 393224 | tf_op jit(solution)/shard_map/ppermute | solution.py:230
  45.4 18.1 %copy-start.3 = (bf16[3,256,256]{2,1,0:T(8,128)(2,1)}, bf16[3,256,256]{2,1,0:T(8,128)(2,1)S(1)}, u32[]{:S(2)}) copy-start(bf16[3,256,256]{2,1,0:T(8,128)(2,1)S(1)} %pad_maximum_fusion.refs_0_) | copy-start | bytes 1179652
  45.5 11.2 %collective-permute-start.5 = (bf16[3,256,256]{2,1,0:T(8,128)(2,1)S(1)}, bf16[3,256,256]{2,1,0:T(8,128)(2,1)S(1)}, u32[]{:S(2)}, u32[]{:S(2)}) collective-permute-start(bf16[3,256,256]{2,1,0:T(8,128)(2,1)S(1)} %pad_maximum_fusion.refs_0_), channel_id=1, source_target_pairs={{0,192},{64,0},{128,64},{192,128},{1,193},{65,1},{129,65},{193,129... | collective-permute-start | bytes 1179656 | tf_op jit(solution)/shard_map/ppermute | solution.py:230
  45.5 18.0 %collective-permute-start.6 = (bf16[3,256,256]{2,1,0:T(8,128)(2,1)S(1)}, bf16[3,256,256]{2,1,0:T(8,128)(2,1)S(1)}, u32[]{:S(2)}, u32[]{:S(2)}) collective-permute-start(bf16[3,256,256]{2,1,0:T(8,128)(2,1)S(1)} %pad_maximum_fusion.refs_0_), channel_id=1, source_target_pairs={{0,64},{64,128},{128,192},{192,0},{1,65},{65,129},{129,193},{193,1... | collective-permute-start | bytes 1179656 | tf_op jit(solution)/shard_map/ppermute | solution.py:230
  47.6 18.0 %collective-permute-start.7 = (bf16[3,256,256]{2,1,0:T(8,128)(2,1)S(1)}, bf16[3,256,256]{2,1,0:T(8,128)(2,1)S(1)}, u32[]{:S(2)}, u32[]{:S(2)}) collective-permute-start(bf16[3,256,256]{2,1,0:T(8,128)(2,1)S(1)} %pad_maximum_fusion.refs_0_), channel_id=1, source_target_pairs={{0,128},{64,192},{128,0},{192,64},{1,129},{65,193},{129,1},{193,65... | collective-permute-start | bytes 1179656 | tf_op jit(solution)/shard_map/ppermute | solution.py:230
  51.2 27.1 %collective-permute-start.8 = (bf16[3,256,256]{2,1,0:T(8,128)(2,1)S(1)}, bf16[3,256,256]{2,1,0:T(8,128)(2,1)S(1)}, u32[]{:S(2)}, u32[]{:S(2)}) collective-permute-start(bf16[3,256,256]{2,1,0:T(8,128)(2,1)S(1)} %pad_maximum_fusion.refs_0_), channel_id=1, source_target_pairs={{0,4},{4,0},{1,5},{5,1},{2,6},{6,2},{3,7},{7,3},{8,12},{12,8},{9,1... | collective-permute-start | bytes 1179656 | tf_op jit(solution)/shard_map/ppermute | solution.py:230
  56.6 6.9 %copy-start.6 = (bf16[3,256,256]{2,1,0:T(8,128)(2,1)}, bf16[3,256,256]{2,1,0:T(8,128)(2,1)S(1)}, u32[]{:S(2)}) copy-start(bf16[3,256,256]{2,1,0:T(8,128)(2,1)S(1)} %collective-permute-done.5.refs_1_) | copy-start | bytes 1179652
  56.6 21.6 %collective-permute-start.9 = (bf16[3,256,256]{2,1,0:T(8,128)(2,1)S(1)}, bf16[3,256,256]{2,1,0:T(8,128)(2,1)S(1)}, u32[]{:S(2)}, u32[]{:S(2)}) collective-permute-start(bf16[3,256,256]{2,1,0:T(8,128)(2,1)S(1)} %collective-permute-done.5.refs_1_), channel_id=1, source_target_pairs={{0,4},{4,0},{1,5},{5,1},{2,6},{6,2},{3,7},{7,3},{8,12},{12,8},{9,1... | collective-permute-start | bytes 1179656 | tf_op jit(solution)/shard_map/ppermute | solution.py:230
  63.5 4.6 %copy-start.7 = (bf16[3,256,256]{2,1,0:T(8,128)(2,1)}, bf16[3,256,256]{2,1,0:T(8,128)(2,1)S(1)}, u32[]{:S(2)}) copy-start(bf16[3,256,256]{2,1,0:T(8,128)(2,1)S(1)} %collective-permute-done.6.refs_2_) | copy-start | bytes 1179652
  63.5 16.8 %collective-permute-start.10 = (bf16[3,256,256]{2,1,0:T(8,128)(2,1)S(1)}, bf16[3,256,256]{2,1,0:T(8,128)(2,1)S(1)}, u32[]{:S(2)}, u32[]{:S(2)}) collective-permute-start(bf16[3,256,256]{2,1,0:T(8,128)(2,1)S(1)} %collective-permute-done.6.refs_2_), channel_id=1, source_target_pairs={{0,4},{4,0},{1,5},{5,1},{2,6},{6,2},{3,7},{7,3},{8,12},{12,8},{9,1... | collective-permute-start | bytes 1179656 | tf_op jit(solution)/shard_map/ppermute | solution.py:230
  65.5 2.5 %copy-start.8 = (bf16[3,256,256]{2,1,0:T(8,128)(2,1)}, bf16[3,256,256]{2,1,0:T(8,128)(2,1)S(1)}, u32[]{:S(2)}) copy-start(bf16[3,256,256]{2,1,0:T(8,128)(2,1)S(1)} %collective-permute-done.7.refs_3_) | copy-start | bytes 1179652
  65.5 19.8 %collective-permute-start.11 = (bf16[3,256,256]{2,1,0:T(8,128)(2,1)S(1)}, bf16[3,256,256]{2,1,0:T(8,128)(2,1)S(1)}, u32[]{:S(2)}, u32[]{:S(2)}) collective-permute-start(bf16[3,256,256]{2,1,0:T(8,128)(2,1)S(1)} %collective-permute-done.7.refs_3_), channel_id=1, source_target_pairs={{0,4},{4,0},{1,5},{5,1},{2,6},{6,2},{3,7},{7,3},{8,12},{12,8},{9,1... | collective-permute-start | bytes 1179656 | tf_op jit(solution)/shard_map/ppermute | solution.py:230
  68.1 28.1 %collective-permute-start.23 = (bf16[128,2048]{1,0:T(8,128)(2,1)S(1)}, bf16[128,2048]{1,0:T(8,128)(2,1)S(1)}, u32[]{:S(2)}, u32[]{:S(2)}) collective-permute-start(bf16[128,2048]{1,0:T(8,128)(2,1)S(1)} %get-tuple-element.12), channel_id=1, source_target_pairs={{0,128},{64,192},{128,0},{192,64},{1,129},{65,193},{129,1},{193,65... | collective-permute-start | bytes 1572872 | tf_op jit(solution)/shard_map/ppermute | solution.py:230
  78.2 9.1 %copy-start.9 = (bf16[3,256,256]{2,1,0:T(8,128)(2,1)}, bf16[3,256,256]{2,1,0:T(8,128)(2,1)S(1)}, u32[]{:S(2)}) copy-start(bf16[3,256,256]{2,1,0:T(8,128)(2,1)S(1)} %collective-permute-done.8.refs_4_) | copy-start | bytes 1179652
  78.2 23.7 %collective-permute-start.22 = (bf16[128,2048]{1,0:T(8,128)(2,1)S(1)}, bf16[128,2048]{1,0:T(8,128)(2,1)S(1)}, u32[]{:S(2)}, u32[]{:S(2)}) collective-permute-start(bf16[128,2048]{1,0:T(8,128)(2,1)S(1)} %get-tuple-element.13), channel_id=1, source_target_pairs={{0,192},{64,0},{128,64},{192,128},{1,193},{65,1},{129,65},{193,129... | collective-permute-start | bytes 1572872 | tf_op jit(solution)/shard_map/ppermute | solution.py:230
  78.3 9.1 %copy-start.10 = (bf16[3,256,256]{2,1,0:T(8,128)(2,1)}, bf16[3,256,256]{2,1,0:T(8,128)(2,1)S(1)}, u32[]{:S(2)}) copy-start(bf16[3,256,256]{2,1,0:T(8,128)(2,1)S(1)} %collective-permute-done.9.refs_5_) | copy-start | bytes 1179652
  78.3 23.6 %collective-permute-start.21 = (bf16[128,2048]{1,0:T(8,128)(2,1)S(1)}, bf16[128,2048]{1,0:T(8,128)(2,1)S(1)}, u32[]{:S(2)}, u32[]{:S(2)}) collective-permute-start(bf16[128,2048]{1,0:T(8,128)(2,1)S(1)} %get-tuple-element.11), channel_id=1, source_target_pairs={{0,64},{64,128},{128,192},{192,0},{1,65},{65,129},{129,193},{193,1... | collective-permute-start | bytes 1572872 | tf_op jit(solution)/shard_map/ppermute | solution.py:230
  80.3 7.0 %copy-start.11 = (bf16[3,256,256]{2,1,0:T(8,128)(2,1)}, bf16[3,256,256]{2,1,0:T(8,128)(2,1)S(1)}, u32[]{:S(2)}) copy-start(bf16[3,256,256]{2,1,0:T(8,128)(2,1)S(1)} %collective-permute-done.10.refs_6_) | copy-start | bytes 1179652
  80.3 37.2 %collective-permute-start.19 = (bf16[1,1024]{1,0:T(2,128)(2,1)S(1)}, bf16[1,1024]{1,0:T(2,128)(2,1)S(1)}, u32[]{:S(2)}, u32[]{:S(2)}) collective-permute-start(bf16[1,1024]{1,0:T(2,128)(2,1)S(1)} %pad_maximum_fusion.3), channel_id=1, source_target_pairs={{4,0},{8,4},{12,8},{16,12},{20,16},{24,20},{28,24},{32,28},{36,32}... | collective-permute-start | bytes 6152 | tf_op jit(solution)/shard_map/ppermute | solution.py:236
  85.4 2.0 %copy-start.12 = (bf16[3,256,256]{2,1,0:T(8,128)(2,1)}, bf16[3,256,256]{2,1,0:T(8,128)(2,1)S(1)}, u32[]{:S(2)}) copy-start(bf16[3,256,256]{2,1,0:T(8,128)(2,1)S(1)} %collective-permute-done.11.refs_7_) | copy-start | bytes 1179652
  85.4 32.1 %collective-permute-start.18 = (bf16[1,1024]{1,0:T(2,128)(2,1)S(1)}, bf16[1,1024]{1,0:T(2,128)(2,1)S(1)}, u32[]{:S(2)}, u32[]{:S(2)}) collective-permute-start(bf16[1,1024]{1,0:T(2,128)(2,1)S(1)} %pad_maximum_fusion.2), channel_id=1, source_target_pairs={{0,4},{4,8},{8,12},{12,16},{16,20},{20,24},{24,28},{28,32},{32,36}... | collective-permute-start | bytes 6152 | tf_op jit(solution)/shard_map/ppermute | solution.py:236
  104.3 32.0 %all-to-all-start = ((bf16[8,16,2048]{2,1,0:T(8,128)(2,1)}), bf16[8,16,2048]{2,1,0:T(8,128)(2,1)S(1)}, u32[]{:S(2)}, u32[]{:S(2)}) async-start(bf16[8,16,2048]{2,1,0:T(8,128)(2,1)} %bitcast.26), calls=%async_computation | async-start | bytes 1048576 | tf_op jit(solution)/shard_map/all_to_all | solution.py:301
  112.4 15.0 %collective-permute-start.14 = (bf16[768,256]{1,0:T(8,128)(2,1)S(1)}, bf16[768,256]{1,0:T(8,128)(2,1)S(1)}, u32[]{:S(2)}, u32[]{:S(2)}) collective-permute-start(bf16[768,256]{1,0:T(8,128)(2,1)S(1)} %get-tuple-element.15), channel_id=1, source_target_pairs={{0,1},{1,2},{2,3},{3,0},{4,5},{5,6},{6,7},{7,4},{8,9},{9,10},{10,1... | collective-permute-start | bytes 1179656 | tf_op jit(solution)/shard_map/ppermute | solution.py:230
  114.7 19.7 %collective-permute-start.13 = (bf16[768,256]{1,0:T(8,128)(2,1)S(1)}, bf16[768,256]{1,0:T(8,128)(2,1)S(1)}, u32[]{:S(2)}, u32[]{:S(2)}) collective-permute-start(bf16[768,256]{1,0:T(8,128)(2,1)S(1)} %get-tuple-element.16), channel_id=1, source_target_pairs={{0,2},{1,3},{2,0},{3,1},{4,6},{5,7},{6,4},{7,5},{8,10},{9,11},{10,... | collective-permute-start | bytes 1179656 | tf_op jit(solution)/shard_map/ppermute | solution.py:230
  117.2 17.2 %collective-permute-start.12 = (bf16[768,256]{1,0:T(8,128)(2,1)S(1)}, bf16[768,256]{1,0:T(8,128)(2,1)S(1)}, u32[]{:S(2)}, u32[]{:S(2)}) collective-permute-start(bf16[768,256]{1,0:T(8,128)(2,1)S(1)} %get-tuple-element.14), channel_id=1, source_target_pairs={{0,3},{1,0},{2,1},{3,2},{4,7},{5,4},{6,5},{7,6},{8,11},{9,8},{10,9... | collective-permute-start | bytes 1179656 | tf_op jit(solution)/shard_map/ppermute | solution.py:230

commit v2 on v0

v2 whole, which is shorter than its diff:
```python
import functools
import math

import jax
import jax.numpy as jnp
from jax import lax
from jax.experimental import pallas as pl
from jax.experimental.pallas import tpu as pltpu
from jax.sharding import Mesh
from jax.sharding import PartitionSpec as P

STRIDE = 8
TAPS = 16
BF = jnp.bfloat16
F32 = jnp.float32
TM = ("x", "z", "core")
SIN = (1.0, -1.66666666e-01, 8.33333079e-03, -1.98408371e-04, 2.75240247e-06, -2.38669497e-08)
COS = (
    1.0,
    -0.5,
    4.16666665e-02,
    -1.38888838e-03,
    2.48010074e-05,
    -2.75233926e-07,
    1.98888297e-09,
)
PI_A = 3.140625
PI_B = math.pi - PI_A
VMEM = pl.BlockSpec(memory_space=pltpu.VMEM)
SMEM = pl.BlockSpec(memory_space=pltpu.SMEM)
ANY = pl.BlockSpec(memory_space=pl.ANY)
NN = (((1,), (0,)), ((), ()))
NT = (((1,), (1,)), ((), ()))


def mul(lhs, rhs, dims=NN):
    return lax.dot_general(lhs, rhs, dims, preferred_element_type=F32)


def call(kernel, outs, specs, name, scratch=(), limit=16):
    return pl.pallas_call(
        kernel,
        out_shape=outs,
        in_specs=specs,
        out_specs=jax.tree.map(lambda _: VMEM, outs),
        scratch_shapes=scratch,
        compiler_params=pltpu.CompilerParams(vmem_limit_bytes=limit * 2**20),
        cost_estimate=pl.CostEstimate(flops=int(TIME[name] * 5.75e9), bytes_accessed=1000, transcendentals=0),
        name=name,
    )


def shape(dims, dtype=BF):
    return jax.ShapeDtypeStruct(dims, dtype)


TOKEN = shape((8, 128), F32)


TIME = dict(
    prep=7,
    weights=4,
    kernel_grad_send=3,
    kernel_grad_keep=4,
    join=1,
    encode=5,
    input_grad=6,
)


def poly(coefs, z):
    out = z * coefs[-1] + coefs[-2]
    for c in coefs[-3::-1]:
        out = out * z + c
    return out


def sincos(theta):
    n = jnp.floor(theta * (1.0 / math.pi) + 0.5)
    r = (theta - n * PI_A) - n * PI_B
    z = r * r
    return r * poly(SIN, z), poly(COS, z)


def prep_kernel(step, feat, low, high, alpha, after, taps, factor, rows):
    frames = feat.shape[0]
    a = alpha[...]
    inv = 1.0 / a

    def snake(values):
        wide = values.astype(F32)
        s, c = sincos(a * wide)
        return wide + s * s * inv, 1.0 + 2.0 * s * c

    rows[0:8, :] = snake(low[8:16, :])[0]
    rows[frames + 8 : frames + 16, :] = snake(high[0:8, :])[0]

    def body(at, carry):
        here = pl.multiple_of(at * step, step)
        act, fac = snake(feat[pl.ds(here, step), :])
        rows[pl.ds(here + 8, step), :] = act
        factor[pl.ds(here, step), :] = fac
        return carry

    lax.fori_loop(0, frames // step, body, 0)
    outs = frames // STRIDE
    for k in range(TAPS):
        taps[:, k * 128 : (k + 1) * 128] = rows[pl.ds(4 + k, outs, stride=STRIDE), :].astype(BF)


def prep(feat, low, high, alpha, after, step=256):
    frames, chans = feat.shape
    return call(
        functools.partial(prep_kernel, step),
        (shape((frames // STRIDE, TAPS * chans)), shape((frames, chans), F32)),
        [VMEM] * 5,
        "prep",
        [pltpu.VMEM((frames + 16, chans), F32)],
        limit=16,
    )(feat, low, high, alpha, after)


def weights_kernel(place, whole, own, p1, p2, p3, done, buf, rows, sem):
    y, core = place[0], place[1]
    copies = [
        pltpu.make_async_copy(
            whole.at[pl.ds(pl.multiple_of(lax.rem(y + s, 4) * 128, 128), 128)], buf.at[s], sem.at[s]
        )
        for s in range(4)
    ]
    for c in copies:
        c.start()
    for s, out in ((1, p1), (3, p3), (2, p2), (0, own)):
        copies[s].wait()
        count = TAPS if s == 0 else TAPS // 2
        for h in range(2):
            lanes = slice(h * 128, h * 128 + 128)
            rows[...] = buf[s, :, :, lanes].astype(F32).reshape(128 * TAPS, 128)
            for k in range(count):
                tap = k if s == 0 else TAPS // 2 * core + k
                out[k * 128 : (k + 1) * 128, lanes] = rows[
                    pl.ds(tap, 128, stride=TAPS), :
                ].astype(BF)
    done[...] = jnp.zeros(done.shape, F32)


def weights(place, whole):
    return call(
        weights_kernel,
        (shape((2048, 256)),) + (shape((1024, 256)),) * 3 + (TOKEN,),
        [SMEM, ANY],
        "weights",
        [
            pltpu.VMEM((4, 128, TAPS, 256), BF),
            pltpu.VMEM((128 * TAPS, 128), F32),
            pltpu.SemaphoreType.DMA((4,)),
        ],
        limit=14,
    )(place, whole)


def choose(gs, which, order, lhs):
    row = lax.broadcasted_iota(jnp.int32, (128, 256), 0)
    col = lax.broadcasted_iota(jnp.int32, (128, 256), 1)
    want = (row // 16) * 32 + which * 16 + row % 16
    pick = jnp.where(col == want, 1.0, 0.0).astype(BF)
    for d, g in enumerate(gs):
        at = pl.multiple_of(order[d] * 128, 128)
        lhs[pl.ds(at, 128), :] = mul(pick, g[...], NT).astype(BF)


def send_kernel(place, taps, g0, g1, g2, g3, out, first, last, lhs):
    choose((g0, g1, g2, g3), 1 - place[0], [place[1 + d] for d in range(4)], lhs)
    for n in range(0, 2048, 256):
        out[:, n : n + 256] = mul(lhs[...], taps[:, n : n + 256]).astype(BF)
    for d, g in enumerate((g0, g1, g2, g3)):
        first[:, d * 256 : (d + 1) * 256] = g[0:16, :]
        last[:, d * 256 : (d + 1) * 256] = g[752:768, :]


def send(place, taps, gs):
    return call(
        send_kernel,
        (shape((512, 2048)), shape((16, 1024)), shape((16, 1024))),
        [SMEM] + [VMEM] * 5,
        "kernel_grad_send",
        [pltpu.VMEM((512, 768), BF)],
        limit=12,
    )(place, taps, *gs)


def keep_kernel(place, taps, g0, g1, g2, g3, got, out, done, lhs):
    choose((g0, g1, g2, g3), place[0], [place[1 + d] for d in range(4)], lhs)
    for n in range(0, 2048, 256):
        cols = slice(n, n + 256)
        both = mul(lhs[...], taps[:, cols]) + got[:, cols].astype(F32)
        for to in range(4):
            out[to, :, cols] = both[to * 128 : (to + 1) * 128].astype(BF)
    done[...] = jnp.zeros(done.shape, F32)


def keep(place, taps, gs, got):
    return call(
        keep_kernel,
        (shape((4, 128, 2048)), TOKEN),
        [SMEM] + [VMEM] * 6,
        "kernel_grad_keep",
        [pltpu.VMEM((512, 768), BF)],
        limit=16,
    )(place, taps, *gs, got)


def join_kernel(a1, a2, a3, after, o1, o2, o3):
    for a, out in ((a1, o1), (a2, o2), (a3, o3)):
        out[...] = a[...]


def join(near, after):
    return call(join_kernel, (shape((1024, 256)),) * 3, [VMEM] * 4, "join", limit=8)(*near, after)


def encode_kernel(place, taps, own, first, last, a1, a2, a3, b1, b2, b3, out, full, o_first, o_last):
    y, core = place[0], place[1]
    here = pl.multiple_of(core * 1024, 1024)
    there = pl.multiple_of(1024 - core * 1024, 1024)
    full[:, 0:256] = own[...]
    for d, (a, b) in enumerate(((a1, b1), (a2, b2), (a3, b3))):
        cols = slice(256 * (d + 1), 256 * (d + 2))
        full[pl.ds(here, 1024), cols] = a[...]
        full[pl.ds(there, 1024), cols] = b[...]
    for d in range(4):
        out[lax.rem(y + d, 4)] = mul(taps[...], full[:, d * 256 : (d + 1) * 256]).astype(BF)
    o_first[...] = first[...]
    o_last[...] = last[...]


def encode(place, taps, own, edges, near, far):
    return call(
        encode_kernel,
        (shape((4, 768, 256)), shape((2048, 1024))) + (shape((16, 1024)),) * 2,
        [SMEM] + [VMEM] * 10,
        "encode",
        limit=20,
    )(place, taps, own, *edges, *near, *far)


def input_grad_kernel(g0, g1, g2, g3, low, high, weights, factor, after, out, full, rows):
    outs = g0.shape[0]
    frames = out.shape[0]
    for d, g in enumerate((g0, g1, g2, g3)):
        full[0:outs, d * 256 : (d + 1) * 256] = g[...]
    full[outs : outs + 16, :] = low[...]
    full[outs + 16 : outs + 32, :] = high[...]
    rows[frames : frames + 16, :] = jnp.zeros((16, 128), F32)
    for pair in range(TAPS // 2):
        res = mul(full[...], weights[pair * 256 : (pair + 1) * 256, :], NT)
        for side in range(2):
            k = 2 * pair + side
            part = res[:, side * 128 : (side + 1) * 128]
            at = pl.ds(4 + k, outs, stride=STRIDE)
            if k < STRIDE:
                rows[at, :] = part[:outs]
                if k < 4:
                    rows[frames + 4 + k : frames + 5 + k, :] = part[outs + 16 : outs + 17]
            else:
                if k >= 12:
                    rows[k - 4 : k - 3, :] = rows[k - 4 : k - 3, :] + part[outs + 15 : outs + 16]
                rows[at, :] = rows[at, :] + part[:outs]
    step = 512
    for at in range(0, frames, step):
        out[at : at + step, :] = (
            rows[at + 8 : at + 8 + step, :] * factor[at : at + step, :]
        ).astype(BF)


def input_grad(gs, low, high, weights, factor, after):
    frames, chans = factor.shape
    return call(
        input_grad_kernel,
        shape((frames, chans)),
        [VMEM] * 9,
        "input_grad",
        [pltpu.VMEM((frames // STRIDE + 32, 1024), BF), pltpu.VMEM((frames + 16, chans), F32)],
        limit=22,
    )(*gs, low, high, weights, factor, after)


def turn(value, axis, by):
    count = lax.axis_size(axis)
    return lax.ppermute(value, axis, [(i, (i + by) % count) for i in range(count)])


def beside(value, by):
    count = math.prod(lax.axis_size(a) for a in TM)
    pairs = [(i, i + by) for i in range(count) if 0 <= i + by < count]
    return lax.ppermute(value, TM, pairs)


def shards(features, snake_alpha, down_weight, grad_out):
    x, z, core, y = (lax.axis_index(a).astype(jnp.int32) for a in ("x", "z", "core", "chan"))

    gs = (
        grad_out,
        turn(grad_out, "chan", -1),
        turn(grad_out, "chan", 2),
        turn(grad_out, "chan", 1),
    )
    low, high = beside(features[-16:], 1), beside(features[:16], -1)

    at = jnp.stack([y, core])
    own, p1, p2, p3, done = weights(at, down_weight)
    near = (turn(p3, "chan", -1), turn(p2, "chan", 2), turn(p1, "chan", 1))
    taps, factor = prep(features, low, high, snake_alpha.reshape(1, -1), done)

    place = jnp.stack([core] + [(y + d) % 4 for d in range(4)])
    out, first, last = send(place, taps, gs)
    got = turn(out, "core", 1)
    kept, done = keep(place, taps, gs, got)
    summed = lax.psum_scatter(kept, "x", scatter_dimension=0)

    held = join(near, done)
    far = [turn(h, "core", 1) for h in held]
    partial, full, first, last = encode(at, taps, own, (first, last), held, far)
    edges = beside(last, 1), beside(first, -1)
    encoded = lax.psum_scatter(partial, "chan", scatter_dimension=0)
    spread = lax.all_to_all(summed.reshape(8, 16, 2048), "z", 0, 0)
    grad_features = input_grad(gs, *edges, full, factor, summed)

    scale = 1.0 / math.sqrt(features.shape[0] // STRIDE * 64)
    total = jnp.sum(spread.astype(F32), axis=0) * scale
    grad_down = total.astype(BF).reshape(16, 16, 128)
    return (encoded, grad_features, grad_down)


def solution(mesh):
    tm, chan = mesh.shape["tm"], mesh.shape["chan"]
    fine = Mesh(mesh.devices.reshape(4, tm // 8, 2, chan), (*TM, "chan"))
    placed = (P(TM, "chan"), P("chan"), P(None, None, "chan"), P(TM, "chan"))
    return jax.shard_map(
        shards,
        mesh=fine,
        in_specs=placed,
        out_specs=(P(TM, "chan"), P(TM, "chan"), P(TM, None, "chan")),
        check_vma=False,
    )
```

time: 451 us -> 120 us (0.27)
  waiting for transfers between devices: 319 us -> 30.6 us
  local copies, waits for them, and re-layouts: 45.7 us -> 13.1 us
  Pallas kernels: 0 us -> 31.4 us
  other arithmetic: 30.4 us -> 0.16 us
  matrix products: 23 us -> 0 us
  starting transfers between devices: 17.1 us -> 29.5 us
    reduce_scatter x2, waiting for transfers between devices: 258 us -> 4.31 us  [the longest x1 4.29 us: shards(): encoded = lax.psum_scatter(partial, 'chan', scatter_dimension=0)]
    all_gather x2 -> x0, waiting for transfers between devices: 60.4 us -> none  [the longest x1 60.4 us: shards(): full_cols = lax.all_gather(padded, 'chan', axis=1, tiled=True)]
    pallas_call x0 -> x7, Pallas kernels: none -> 31.4 us  [the longest x1 6.97 us: input_grad(): call(input_grad_kernel, shape((frames, chans)), [VMEM] * 9, 'input_grad',...]
    convert_element_type x2 -> x0, other arithmetic: 24 us -> none  [the longest x1 23.1 us: shards(): (grad_snaked * (1.0 + jnp.sin(2.0 * snake_alpha * wide))).astype(jnp.bflo...]
    dot_general x6 -> x0, matrix products: 23 us -> none  [the longest x1 6.72 us: shards(): jnp.einsum('up,rjp->ujr', grad_pad[1:], down_weight[:, :STRIDE], preferre...]
    ppermute x4 -> x14, waiting for transfers between devices: 1.27 us -> 21.9 us  [the longest x10 21.9 us: turn(): lax.ppermute(value, axis, [(i, (i + by) % count) for i in range(count)])]
    slice x5 -> x1, local copies, waits for them, and re-layouts: 19.4 us -> 0.7 us  [shards(): low, high = (beside(features[-16:], 1), beside(features[:16], -1))]
    add x1 -> x0, local copies, waits for them, and re-layouts: 16.4 us -> none  [shards(): jnp.einsum('up,rjp->ujr', grad_pad[1:], down_weight[:, :STRIDE], preferre...]
  transfers between devices with their start and end apart: 8 -> 17, of which waited for: 4 -> 9; matrix products, arithmetic and copies ran while one was open for 14% -> 1% of each run, Pallas kernels for 0% -> 23%
where the time goes in v2:
time: 120 us; the launch traced here: 119 us
  Pallas kernels  31.4 us (26%)
  waiting for transfers between devices  30.6 us (26%)
  starting transfers between devices  29.5 us (25%)
  between operations  14.3 us (12%)
  local copies, waits for them, and re-layouts  13.1 us (11%)
    ppermute x10, waiting for transfers between devices, turn(): lax.ppermute(value, axis, [(i, (i + by) % count) for i in range(count)])  21.9 us
    ppermute x4, starting transfers between devices, beside(): return lax.ppermute(value, TM, pairs)  15.9 us
    unnamed x43, local copies, waits for them, and re-layouts  12.3 us
    ppermute x10, starting transfers between devices, turn(): lax.ppermute(value, axis, [(i, (i + by) % count) for i in range(count)])  9.52 us
    pallas_call x1, Pallas kernels, input_grad(): call(input_grad_kernel, shape((frames, chans)), [VMEM] * 9, 'input_grad',...  6.97 us
    pallas_call x1, Pallas kernels, prep(): call(functools.partial(prep_kernel, step), (shape((frames // STRIDE, TAPS...  5.8 us
    pallas_call x1, Pallas kernels, encode(): call(encode_kernel, (shape((4, 768, 256)), shape((2048, 1024))) + (shape(...  5.68 us
    pallas_call x1, Pallas kernels, keep(): call(keep_kernel, (shape((4, 128, 2048)), TOKEN), [SMEM] + [VMEM] * 6, 'k...  5.05 us
  transfers between devices with their start and end apart: 17, of which 9 were waited for; matrix products, arithmetic and copies ran while one was open for 1% of the time, Pallas kernels for 23%

profile of v2, /device:TPU:2, one launch (start us, length us, event | category | flops | bytes accessed | tf_op | source)
XLA Modules:
  0.0 119.1 jit_solution(17253857348457517961)
XLA Ops:
  7.2 0.0 reduce-scatter.5.cloned.1.call-start
  7.2 1.7 %collective-permute-start.4 = (bf16[768,256]{1,0:T(8,128)(2,1)}, bf16[768,256]{1,0:T(8,128)(2,1)}, u32[]{:S(2)}, u32[]{:S(2)}) collective-permute-start(bf16[768,256]{1,0:T(8,128)(2,1)} %g0.5), channel_id=1, source_target_pairs={{0,1},{1,2},{2,3},{3,0},{4,5},{5,6},{6,7},{7,4},{8,9},{9,10},{10,1... | collective-permute-start | bytes 1179656 | tf_op jit(solution)/shard_map/ppermute | solution.py:290
  8.9 2.9 %collective-permute-start.3 = (bf16[768,256]{1,0:T(8,128)(2,1)}, bf16[768,256]{1,0:T(8,128)(2,1)}, u32[]{:S(2)}, u32[]{:S(2)}) collective-permute-start(bf16[768,256]{1,0:T(8,128)(2,1)} %g0.5), channel_id=1, source_target_pairs={{0,2},{1,3},{2,0},{3,1},{4,6},{5,7},{6,4},{7,5},{8,10},{9,11},{10,... | collective-permute-start | bytes 1179656 | tf_op jit(solution)/shard_map/ppermute | solution.py:290
  11.8 1.3 %collective-permute-start.2 = (bf16[768,256]{1,0:T(8,128)(2,1)}, bf16[768,256]{1,0:T(8,128)(2,1)}, u32[]{:S(2)}, u32[]{:S(2)}) collective-permute-start(bf16[768,256]{1,0:T(8,128)(2,1)} %g0.5), channel_id=1, source_target_pairs={{0,3},{1,0},{2,1},{3,2},{4,7},{5,4},{6,5},{7,6},{8,11},{9,8},{10,9... | collective-permute-start | bytes 1179656 | tf_op jit(solution)/shard_map/ppermute | solution.py:290
  13.1 0.7 fusion.1
  13.8 6.3 %collective-permute-start.1 = (bf16[16,128]{1,0:T(8,128)(2,1)S(1)}, bf16[16,128]{1,0:T(8,128)(2,1)S(1)}, u32[]{:S(2)}, u32[]{:S(2)}) collective-permute-start(bf16[16,128]{1,0:T(8,128)(2,1)S(1)} %get-tuple-element.41), channel_id=1, source_target_pairs={{4,0},{8,4},{12,8},{16,12},{20,16},{24,20},{28,24},{32,28},{36,32}... | collective-permute-start | bytes 12296 | tf_op jit(solution)/shard_map/ppermute | solution.py:296
  20.1 1.9 %collective-permute-start = (bf16[16,128]{1,0:T(8,128)(2,1)S(1)}, bf16[16,128]{1,0:T(8,128)(2,1)S(1)}, u32[]{:S(2)}, u32[]{:S(2)}) collective-permute-start(bf16[16,128]{1,0:T(8,128)(2,1)S(1)} %get-tuple-element.42), channel_id=1, source_target_pairs={{0,4},{4,8},{8,12},{12,16},{16,20},{20,24},{24,28},{28,32},{32,36}... | collective-permute-start | bytes 12296 | tf_op jit(solution)/shard_map/ppermute | solution.py:296
  22.1 0.1 pad_add_fusion.place
  22.2 2.2 %copy-done.2 = bf16[512,16,256]{2,1,0:T(8,128)(2,1)S(1)} copy-done((bf16[512,16,256]{2,1,0:T(8,128)(2,1)S(1)}, bf16[512,16,256]{2,1,0:T(8,128)(2,1)}, u32[]{:S(2)}) %copy-start.2) | copy-done | bytes 4194328
  24.4 3.3 %weights.1 = (bf16[2048,256]{1,0:T(8,128)(2,1)S(1)}, bf16[1024,256]{1,0:T(8,128)(2,1)S(1)}, bf16[1024,256]{1,0:T(8,128)(2,1)S(1)}, bf16[1024,256]{1,0:T(8,128)(2,1)S(1)}, f32[8,128]{1,0:T(8,128)S(1)}) custom-call(s32[2]{0:T(128)S(1)} %pad_add_fusion.place, bf16[512,16,256]{2,1,0:T(8,128)(2,1)S(1)} %copy-done.2), custom_call_target="tpu_custom_call" | custom-call | flops 23000000512 | bytes 1000 | tf_op jit(solution)/shard_map/weights/pallas_call | solution.py:148
  27.6 0.0 copy-done.5
  27.6 0.0 copy-start.13
  27.6 1.0 copy-done.13
  28.6 0.1 stack.32.place
  28.7 0.0 collective-permute-done.1.high
  28.7 0.0 collective-permute-done.low
  28.7 0.5 copy-done.19
  29.2 0.0 copy-done.1
  29.2 0.0 copy-done.4
  29.2 0.7 copy-done.20
  29.9 5.8 %prep.1 = (bf16[768,2048]{1,0:T(8,128)(2,1)S(1)}, f32[6144,128]{1,0:T(8,128)S(1)}) custom-call(bf16[6144,128]{1,0:T(8,128)(2,1)S(1)} %copy-done.1, bf16[16,128]{1,0:T(8,128)(2,1)S(1)} %collective-permute-done.low, bf16[16,128]{1,0:T(8,128)(2,1)S(1)} %collective-permute-done.1.high, f32[1,128]{1,0:T(1,128)S(1)} %bitcast.15, f32[8,128]{1,0:T(8,128)S(1)} %copy-done.20), custom_call_target="tpu_custom_call" | custom-call | flops 40249999360 | bytes 1000 | tf_op jit(solution)/shard_map/prep/pallas_call | solution.py:113
  35.7 0.0 copy-start.11
  35.7 0.0 collective-permute-done.4.g3
  35.7 0.0 collective-permute-done.3.g2
  35.7 0.0 collective-permute-done.2.g1
  35.8 4.5 %kernel_grad_send.1 = (bf16[512,2048]{1,0:T(8,128)(2,1)S(1)}, bf16[16,1024]{1,0:T(8,128)(2,1)S(1)}, bf16[16,1024]{1,0:T(8,128)(2,1)S(1)}) custom-call(s32[5]{0:T(128)S(1)} %stack.32.place, bf16[768,2048]{1,0:T(8,128)(2,1)S(1)} %get-tuple-element.23.taps, bf16[768,256]{1,0:T(8,128)(2,1)S(1)} %copy-done.3, bf16[768,256]{1,0:T(8,128)(2,1)} %collective-permute-done.2.g1, ...), custom_call_target="tpu_custom_call" | custom-call | flops 17250000896 | bytes 1000 | tf_op jit(solution)/shard_map/kernel_grad_send/pallas_call | solution.py:182
  40.3 0.0 copy-start.15
  40.3 0.0 copy-start.17
  40.3 0.1 collective-permute-start.8
  40.4 0.4 collective-permute-start.5
  40.8 2.5 %collective-permute-start.6 = (bf16[1024,256]{1,0:T(8,128)(2,1)S(1)}, bf16[1024,256]{1,0:T(8,128)(2,1)S(1)}, u32[]{:S(2)}, u32[]{:S(2)}) collective-permute-start(bf16[1024,256]{1,0:T(8,128)(2,1)S(1)} %get-tuple-element.28), channel_id=1, source_target_pairs={{0,2},{1,3},{2,0},{3,1},{4,6},{5,7},{6,4},{7,5},{8,10},{9,11},{10,... | collective-permute-start | bytes 1572872 | tf_op jit(solution)/shard_map/ppermute | solution.py:290
  43.3 0.0 collective-permute-start.7
  43.3 1.3 %collective-permute-done.8.got = bf16[512,2048]{1,0:T(8,128)(2,1)S(1)} collective-permute-done((bf16[512,2048]{1,0:T(8,128)(2,1)S(1)}, bf16[512,2048]{1,0:T(8,128)(2,1)S(1)}, u32[]{:S(2)}, u32[]{:S(2)}) %collective-permute-start.8) | collective-permute-done | bytes 2097184 | tf_op jit(solution)/shard_map/ppermute | solution.py:290
  44.6 5.0 %kernel_grad_keep.1 = (bf16[4,128,2048]{2,1,0:T(8,128)(2,1)}, f32[8,128]{1,0:T(8,128)S(1)}) custom-call(s32[5]{0:T(128)S(1)} %stack.32.place, bf16[768,2048]{1,0:T(8,128)(2,1)S(1)} %get-tuple-element.23.taps, bf16[768,256]{1,0:T(8,128)(2,1)S(1)} %copy-done.3, bf16[768,256]{1,0:T(8,128)(2,1)} %collective-permute-done.2.g1, ...), custom_call_target="tpu_custom_call" | custom-call | flops 23000000512 | bytes 1000 | tf_op jit(solution)/shard_map/kernel_grad_keep/pallas_call | solution.py:203
  49.6 0.0 reduce-scatter.5.cloned.1.call-update
  49.7 0.0 reduce-scatter.3.cloned.1.call-start
  49.7 5.5 %collective-permute-done.5.a1 = bf16[1024,256]{1,0:T(8,128)(2,1)S(1)} collective-permute-done((bf16[1024,256]{1,0:T(8,128)(2,1)S(1)}, bf16[1024,256]{1,0:T(8,128)(2,1)S(1)}, u32[]{:S(2)}, u32[]{:S(2)}) %collective-permute-start.5) | collective-permute-done | bytes 524320 | tf_op jit(solution)/shard_map/ppermute | solution.py:290
  55.2 1.9 %collective-permute-done.6.a2 = bf16[1024,256]{1,0:T(8,128)(2,1)S(1)} collective-permute-done((bf16[1024,256]{1,0:T(8,128)(2,1)S(1)}, bf16[1024,256]{1,0:T(8,128)(2,1)S(1)}, u32[]{:S(2)}, u32[]{:S(2)}) %collective-permute-start.6) | collective-permute-done | bytes 524320 | tf_op jit(solution)/shard_map/ppermute | solution.py:290
  57.1 10.4 %collective-permute-done.7.a3 = bf16[1024,256]{1,0:T(8,128)(2,1)S(1)} collective-permute-done((bf16[1024,256]{1,0:T(8,128)(2,1)S(1)}, bf16[1024,256]{1,0:T(8,128)(2,1)S(1)}, u32[]{:S(2)}, u32[]{:S(2)}) %collective-permute-start.7) | collective-permute-done | bytes 524320 | tf_op jit(solution)/shard_map/ppermute | solution.py:290
  67.5 0.0 copy-start.18
  67.5 0.1 join.1
  67.7 0.1 collective-permute-start.9
  67.8 0.5 collective-permute-start.10
  68.3 0.1 collective-permute-start.11
  68.4 1.3 %collective-permute-done.9.b1 = bf16[1024,256]{1,0:T(8,128)(2,1)S(1)} collective-permute-done((bf16[1024,256]{1,0:T(8,128)(2,1)S(1)}, bf16[1024,256]{1,0:T(8,128)(2,1)S(1)}, u32[]{:S(2)}, u32[]{:S(2)}) %collective-permute-start.9) | collective-permute-done | bytes 524320 | tf_op jit(solution)/shard_map/ppermute | solution.py:290
  69.7 0.7 collective-permute-done.10.b2
  70.4 0.7 collective-permute-done.11.b3
  71.2 5.7 %encode.1 = (bf16[4,768,256]{2,1,0:T(8,128)(2,1)}, bf16[2048,1024]{1,0:T(8,128)(2,1)S(1)}, bf16[16,1024]{1,0:T(8,128)(2,1)S(1)}, bf16[16,1024]{1,0:T(8,128)(2,1)S(1)}) custom-call(s32[2]{0:T(128)S(1)} %copy-done.6, bf16[768,2048]{1,0:T(8,128)(2,1)S(1)} %copy-done.8, bf16[2048,256]{1,0:T(8,128)(2,1)S(1)} %copy-done.14, bf16[16,1024]{1,0:T(8,128)(2,1)S(1)} %copy-done.16, ...), custom_call_target="tpu_custom_call" | custom-call | flops 28750000128 | bytes 1000 | tf_op jit(solution)/shard_map/encode/pallas_call | solution.py:238
  76.9 2.0 %copy-done.9 = bf16[2048,1024]{1,0:T(8,128)(2,1)} copy-done((bf16[2048,1024]{1,0:T(8,128)(2,1)}, bf16[2048,1024]{1,0:T(8,128)(2,1)S(1)}, u32[]{:S(2)}) %copy-start.9) | copy-done | bytes 4194328
  78.8 2.0 %collective-permute-start.12 = (bf16[16,1024]{1,0:T(8,128)(2,1)S(1)}, bf16[16,1024]{1,0:T(8,128)(2,1)S(1)}, u32[]{:S(2)}, u32[]{:S(2)}) collective-permute-start(bf16[16,1024]{1,0:T(8,128)(2,1)S(1)} %get-tuple-element.36), channel_id=1, source_target_pairs={{0,4},{4,8},{8,12},{12,16},{16,20},{20,24},{24,28},{28,32},{32,36}... | collective-permute-start | bytes 98312 | tf_op jit(solution)/shard_map/ppermute | solution.py:296
  80.9 5.6 %collective-permute-start.13 = (bf16[16,1024]{1,0:T(8,128)(2,1)S(1)}, bf16[16,1024]{1,0:T(8,128)(2,1)S(1)}, u32[]{:S(2)}, u32[]{:S(2)}) collective-permute-start(bf16[16,1024]{1,0:T(8,128)(2,1)S(1)} %get-tuple-element.37), channel_id=1, source_target_pairs={{4,0},{8,4},{12,8},{16,12},{20,16},{24,20},{28,24},{32,28},{36,32}... | collective-permute-start | bytes 98312 | tf_op jit(solution)/shard_map/ppermute | solution.py:296
  86.5 0.0 reduce-scatter.3.cloned.1.call-update
  86.5 0.0 reduce-scatter.5.cloned.1.call-done
  86.6 4.0 %all-to-all-start = ((bf16[8,16,2048]{2,1,0:T(8,128)(2,1)}), bf16[8,16,2048]{2,1,0:T(8,128)(2,1)S(1)}, u32[]{:S(2)}, u32[]{:S(2)}) async-start(bf16[8,16,2048]{2,1,0:T(8,128)(2,1)} %bitcast.13), calls=%async_computation.2 | async-start | bytes 1048576 | tf_op jit(solution)/shard_map/all_to_all | solution.py:326
  90.5 0.0 collective-permute-done.12.low
  90.5 0.0 collective-permute-done.13.high
  90.6 1.0 copy-done
  91.6 2.2 %copy-done.10 = bf16[2048,1024]{1,0:T(8,128)(2,1)S(1)} copy-done((bf16[2048,1024]{1,0:T(8,128)(2,1)S(1)}, bf16[2048,1024]{1,0:T(8,128)(2,1)}, u32[]{:S(2)}) %copy-start.10) | copy-done | bytes 4194328
  93.8 2.1 %copy-done.12 = f32[6144,128]{1,0:T(8,128)S(1)} copy-done((f32[6144,128]{1,0:T(8,128)S(1)}, f32[6144,128]{1,0:T(8,128)}, u32[]{:S(2)}) %copy-start.12) | copy-done | bytes 3145752
  95.9 7.0 %input_grad.1 = bf16[6144,128]{1,0:T(8,128)(2,1)} custom-call(bf16[768,256]{1,0:T(8,128)(2,1)S(1)} %copy-done.3, bf16[768,256]{1,0:T(8,128)(2,1)} %collective-permute-done.2.g1, bf16[768,256]{1,0:T(8,128)(2,1)} %collective-permute-done.3.g2, bf16[768,256]{1,0:T(8,128)(2,1)} %collective-permute-done.4.g3, bf16[16,1024]{1,0:T(8,128)(2,1)S(1)} %collective-permute-done.12.low, ...), custom_call_target="tpu_custom_call" | custom-call | flops 34500001792 | bytes 1000 | tf_op jit(solution)/shard_map/input_grad/pallas_call | solution.py:278
  102.8 4.3 %all-to-all-done = bf16[8,16,2048]{2,1,0:T(8,128)(2,1)S(1)} async-done(((bf16[8,16,2048]{2,1,0:T(8,128)(2,1)}), bf16[8,16,2048]{2,1,0:T(8,128)(2,1)S(1)}, u32[]{:S(2)}, u32[]{:S(2)}) %all-to-all-start) | async-done | bytes 524320 | tf_op jit(solution)/shard_map/all_to_all | solution.py:326
  107.2 0.1 convert_reduce_fusion
  107.3 0.6 copy.7
  107.9 4.3 %reduce-scatter.3.cloned.1.call-done = bf16[1,768,256]{2,1,0:T(8,128)(2,1)} async-done(((bf16[4,768,256]{2,1,0:T(8,128)(2,1)}), bf16[1,768,256]{2,1,0:T(8,128)(2,1)}) %reduce-scatter.3.cloned.1.call-update) | async-done | bytes 393232 | tf_op jit(solution)/shard_map/reduce_scatter | solution.py:325
  (27 shorter events, 0.1 us)
Async XLA Ops:
  7.2 79.4 %reduce-scatter.5.cloned.1.call-start = ((), (), s32[]{:S(2)}) async-start(), calls=%async_computation.4 | async-start | bytes 2621440 | tf_op jit(solution)/shard_map/reduce_scatter | solution.py:319
  7.2 28.5 %collective-permute-start.4 = (bf16[768,256]{1,0:T(8,128)(2,1)}, bf16[768,256]{1,0:T(8,128)(2,1)}, u32[]{:S(2)}, u32[]{:S(2)}) collective-permute-start(bf16[768,256]{1,0:T(8,128)(2,1)} %g0.5), channel_id=1, source_target_pairs={{0,1},{1,2},{2,3},{3,0},{4,5},{5,6},{6,7},{7,4},{8,9},{9,10},{10,1... | collective-permute-start | bytes 1179656 | tf_op jit(solution)/shard_map/ppermute | solution.py:290
  8.9 26.9 %collective-permute-start.3 = (bf16[768,256]{1,0:T(8,128)(2,1)}, bf16[768,256]{1,0:T(8,128)(2,1)}, u32[]{:S(2)}, u32[]{:S(2)}) collective-permute-start(bf16[768,256]{1,0:T(8,128)(2,1)} %g0.5), channel_id=1, source_target_pairs={{0,2},{1,3},{2,0},{3,1},{4,6},{5,7},{6,4},{7,5},{8,10},{9,11},{10,... | collective-permute-start | bytes 1179656 | tf_op jit(solution)/shard_map/ppermute | solution.py:290
  11.8 24.0 %collective-permute-start.2 = (bf16[768,256]{1,0:T(8,128)(2,1)}, bf16[768,256]{1,0:T(8,128)(2,1)}, u32[]{:S(2)}, u32[]{:S(2)}) collective-permute-start(bf16[768,256]{1,0:T(8,128)(2,1)} %g0.5), channel_id=1, source_target_pairs={{0,3},{1,0},{2,1},{3,2},{4,7},{5,4},{6,5},{7,6},{8,11},{9,8},{10,9... | collective-permute-start | bytes 1179656 | tf_op jit(solution)/shard_map/ppermute | solution.py:290
  13.8 14.9 %collective-permute-start.1 = (bf16[16,128]{1,0:T(8,128)(2,1)S(1)}, bf16[16,128]{1,0:T(8,128)(2,1)S(1)}, u32[]{:S(2)}, u32[]{:S(2)}) collective-permute-start(bf16[16,128]{1,0:T(8,128)(2,1)S(1)} %get-tuple-element.41), channel_id=1, source_target_pairs={{4,0},{8,4},{12,8},{16,12},{20,16},{24,20},{28,24},{32,28},{36,32}... | collective-permute-start | bytes 12296 | tf_op jit(solution)/shard_map/ppermute | solution.py:296
  20.1 8.5 %collective-permute-start = (bf16[16,128]{1,0:T(8,128)(2,1)S(1)}, bf16[16,128]{1,0:T(8,128)(2,1)S(1)}, u32[]{:S(2)}, u32[]{:S(2)}) collective-permute-start(bf16[16,128]{1,0:T(8,128)(2,1)S(1)} %get-tuple-element.42), channel_id=1, source_target_pairs={{0,4},{4,8},{8,12},{12,16},{16,20},{20,24},{24,28},{28,32},{32,36}... | collective-permute-start | bytes 12296 | tf_op jit(solution)/shard_map/ppermute | solution.py:296
  22.2 2.2 %copy-start.2 = (bf16[512,16,256]{2,1,0:T(8,128)(2,1)S(1)}, bf16[512,16,256]{2,1,0:T(8,128)(2,1)}, u32[]{:S(2)}) copy-start(bf16[512,16,256]{2,1,0:T(8,128)(2,1)} %whole.1) | copy-start | bytes 12582916
  24.3 3.3 %copy-start.5 = (s32[2]{0:T(128)}, s32[2]{0:T(128)S(1)}, u32[]{:S(2)}) copy-start(s32[2]{0:T(128)S(1)} %pad_add_fusion.place) | copy-start | bytes 28
  24.3 4.8 %copy-start.1 = (bf16[6144,128]{1,0:T(8,128)(2,1)S(1)}, bf16[6144,128]{1,0:T(8,128)(2,1)}, u32[]{:S(2)}) copy-start(bf16[6144,128]{1,0:T(8,128)(2,1)} %feat.1) | copy-start | bytes 4718596
  24.4 4.8 %copy-start.4 = (f32[128]{0:T(128)S(1)}, f32[128]{0:T(128)}, u32[]{:S(2)}) copy-start(f32[128]{0:T(128)} %param.5) | copy-start | bytes 1540
  27.6 1.0 copy-start.13
  28.6 0.6 copy-start.19
  29.2 0.7 copy-start.20
  29.9 5.9 %copy-start.3 = (bf16[768,256]{1,0:T(8,128)(2,1)S(1)}, bf16[768,256]{1,0:T(8,128)(2,1)}, u32[]{:S(2)}) copy-start(bf16[768,256]{1,0:T(8,128)(2,1)} %g0.5) | copy-start | bytes 1179652
  35.7 4.6 %copy-start.11 = (f32[6144,128]{1,0:T(8,128)}, f32[6144,128]{1,0:T(8,128)S(1)}, u32[]{:S(2)}) copy-start(f32[6144,128]{1,0:T(8,128)S(1)} %get-tuple-element.39.factor) | copy-start | bytes 9437188
  35.7 8.9 %copy-start.7 = (bf16[768,2048]{1,0:T(8,128)(2,1)}, bf16[768,2048]{1,0:T(8,128)(2,1)S(1)}, u32[]{:S(2)}) copy-start(bf16[768,2048]{1,0:T(8,128)(2,1)S(1)} %get-tuple-element.23.taps) | copy-start | bytes 9437188
  40.3 9.3 %copy-start.15 = (bf16[16,1024]{1,0:T(8,128)(2,1)}, bf16[16,1024]{1,0:T(8,128)(2,1)S(1)}, u32[]{:S(2)}) copy-start(bf16[16,1024]{1,0:T(8,128)(2,1)S(1)} %get-tuple-element.25.first) | copy-start | bytes 98308
  40.3 9.3 %copy-start.17 = (bf16[16,1024]{1,0:T(8,128)(2,1)}, bf16[16,1024]{1,0:T(8,128)(2,1)S(1)}, u32[]{:S(2)}) copy-start(bf16[16,1024]{1,0:T(8,128)(2,1)S(1)} %get-tuple-element.26.last) | copy-start | bytes 98308
  40.3 4.2 %collective-permute-start.8 = (bf16[512,2048]{1,0:T(8,128)(2,1)S(1)}, bf16[512,2048]{1,0:T(8,128)(2,1)S(1)}, u32[]{:S(2)}, u32[]{:S(2)}) collective-permute-start(bf16[512,2048]{1,0:T(8,128)(2,1)S(1)} %get-tuple-element.30), channel_id=1, source_target_pairs={{0,4},{4,0},{1,5},{5,1},{2,6},{6,2},{3,7},{7,3},{8,12},{12,8},{9,1... | collective-permute-start | bytes 6291464 | tf_op jit(solution)/shard_map/ppermute | solution.py:290
  40.4 14.8 %collective-permute-start.5 = (bf16[1024,256]{1,0:T(8,128)(2,1)S(1)}, bf16[1024,256]{1,0:T(8,128)(2,1)S(1)}, u32[]{:S(2)}, u32[]{:S(2)}) collective-permute-start(bf16[1024,256]{1,0:T(8,128)(2,1)S(1)} %get-tuple-element.27), channel_id=1, source_target_pairs={{0,3},{1,0},{2,1},{3,2},{4,7},{5,4},{6,5},{7,6},{8,11},{9,8},{10,9... | collective-permute-start | bytes 1572872 | tf_op jit(solution)/shard_map/ppermute | solution.py:290
  40.8 16.3 %collective-permute-start.6 = (bf16[1024,256]{1,0:T(8,128)(2,1)S(1)}, bf16[1024,256]{1,0:T(8,128)(2,1)S(1)}, u32[]{:S(2)}, u32[]{:S(2)}) collective-permute-start(bf16[1024,256]{1,0:T(8,128)(2,1)S(1)} %get-tuple-element.28), channel_id=1, source_target_pairs={{0,2},{1,3},{2,0},{3,1},{4,6},{5,7},{6,4},{7,5},{8,10},{9,11},{10,... | collective-permute-start | bytes 1572872 | tf_op jit(solution)/shard_map/ppermute | solution.py:290
  43.3 24.3 %collective-permute-start.7 = (bf16[1024,256]{1,0:T(8,128)(2,1)S(1)}, bf16[1024,256]{1,0:T(8,128)(2,1)S(1)}, u32[]{:S(2)}, u32[]{:S(2)}) collective-permute-start(bf16[1024,256]{1,0:T(8,128)(2,1)S(1)} %get-tuple-element.29), channel_id=1, source_target_pairs={{0,1},{1,2},{2,3},{3,0},{4,5},{5,6},{6,7},{7,4},{8,9},{9,10},{10,1... | collective-permute-start | bytes 1572872 | tf_op jit(solution)/shard_map/ppermute | solution.py:290
  49.7 62.6 %reduce-scatter.3.cloned.1.call-start = ((), (), s32[]{:S(2)}) async-start(), calls=%async_computation.3 | async-start | bytes 1966080 | tf_op jit(solution)/shard_map/reduce_scatter | solution.py:325
  67.5 3.6 %copy-start.6 = (s32[2]{0:T(128)S(1)}, s32[2]{0:T(128)}, u32[]{:S(2)}) copy-start(s32[2]{0:T(128)} %copy-done.5) | copy-start | bytes 28
  67.5 3.6 %copy-start.8 = (bf16[768,2048]{1,0:T(8,128)(2,1)S(1)}, bf16[768,2048]{1,0:T(8,128)(2,1)}, u32[]{:S(2)}) copy-start(bf16[768,2048]{1,0:T(8,128)(2,1)} %copy-done.7) | copy-start | bytes 9437188
  67.5 3.6 %copy-start.14 = (bf16[2048,256]{1,0:T(8,128)(2,1)S(1)}, bf16[2048,256]{1,0:T(8,128)(2,1)}, u32[]{:S(2)}) copy-start(bf16[2048,256]{1,0:T(8,128)(2,1)} %copy-done.13) | copy-start | bytes 3145732
  67.5 3.6 %copy-start.16 = (bf16[16,1024]{1,0:T(8,128)(2,1)S(1)}, bf16[16,1024]{1,0:T(8,128)(2,1)}, u32[]{:S(2)}) copy-start(bf16[16,1024]{1,0:T(8,128)(2,1)} %copy-done.15) | copy-start | bytes 98308
  67.5 3.6 %copy-start.18 = (bf16[16,1024]{1,0:T(8,128)(2,1)S(1)}, bf16[16,1024]{1,0:T(8,128)(2,1)}, u32[]{:S(2)}) copy-start(bf16[16,1024]{1,0:T(8,128)(2,1)} %copy-done.17) | copy-start | bytes 98308
  67.7 2.0 %collective-permute-start.9 = (bf16[1024,256]{1,0:T(8,128)(2,1)S(1)}, bf16[1024,256]{1,0:T(8,128)(2,1)S(1)}, u32[]{:S(2)}, u32[]{:S(2)}) collective-permute-start(bf16[1024,256]{1,0:T(8,128)(2,1)S(1)} %get-tuple-element.32.a1), channel_id=1, source_target_pairs={{0,4},{4,0},{1,5},{5,1},{2,6},{6,2},{3,7},{7,3},{8,12},{12,8},{9,1... | collective-permute-start | bytes 1572872 | tf_op jit(solution)/shard_map/ppermute | solution.py:290
  67.8 2.6 %collective-permute-start.10 = (bf16[1024,256]{1,0:T(8,128)(2,1)S(1)}, bf16[1024,256]{1,0:T(8,128)(2,1)S(1)}, u32[]{:S(2)}, u32[]{:S(2)}) collective-permute-start(bf16[1024,256]{1,0:T(8,128)(2,1)S(1)} %get-tuple-element.33.a2), channel_id=1, source_target_pairs={{0,4},{4,0},{1,5},{5,1},{2,6},{6,2},{3,7},{7,3},{8,12},{12,8},{9,1... | collective-permute-start | bytes 1572872 | tf_op jit(solution)/shard_map/ppermute | solution.py:290
  68.3 2.9 %collective-permute-start.11 = (bf16[1024,256]{1,0:T(8,128)(2,1)S(1)}, bf16[1024,256]{1,0:T(8,128)(2,1)S(1)}, u32[]{:S(2)}, u32[]{:S(2)}) collective-permute-start(bf16[1024,256]{1,0:T(8,128)(2,1)S(1)} %get-tuple-element.34.a3), channel_id=1, source_target_pairs={{0,4},{4,0},{1,5},{5,1},{2,6},{6,2},{3,7},{7,3},{8,12},{12,8},{9,1... | collective-permute-start | bytes 1572872 | tf_op jit(solution)/shard_map/ppermute | solution.py:290
  76.9 2.0 %copy-start.9 = (bf16[2048,1024]{1,0:T(8,128)(2,1)}, bf16[2048,1024]{1,0:T(8,128)(2,1)S(1)}, u32[]{:S(2)}) copy-start(bf16[2048,1024]{1,0:T(8,128)(2,1)S(1)} %get-tuple-element.38.weights) | copy-start | bytes 12582916
  78.8 11.7 %collective-permute-start.12 = (bf16[16,1024]{1,0:T(8,128)(2,1)S(1)}, bf16[16,1024]{1,0:T(8,128)(2,1)S(1)}, u32[]{:S(2)}, u32[]{:S(2)}) collective-permute-start(bf16[16,1024]{1,0:T(8,128)(2,1)S(1)} %get-tuple-element.36), channel_id=1, source_target_pairs={{0,4},{4,8},{8,12},{12,16},{16,20},{20,24},{24,28},{28,32},{32,36}... | collective-permute-start | bytes 98312 | tf_op jit(solution)/shard_map/ppermute | solution.py:296
  80.9 9.7 %collective-permute-start.13 = (bf16[16,1024]{1,0:T(8,128)(2,1)S(1)}, bf16[16,1024]{1,0:T(8,128)(2,1)S(1)}, u32[]{:S(2)}, u32[]{:S(2)}) collective-permute-start(bf16[16,1024]{1,0:T(8,128)(2,1)S(1)} %get-tuple-element.37), channel_id=1, source_target_pairs={{4,0},{8,4},{12,8},{16,12},{20,16},{24,20},{28,24},{32,28},{36,32}... | collective-permute-start | bytes 98312 | tf_op jit(solution)/shard_map/ppermute | solution.py:296
  86.6 20.6 %all-to-all-start = ((bf16[8,16,2048]{2,1,0:T(8,128)(2,1)}), bf16[8,16,2048]{2,1,0:T(8,128)(2,1)S(1)}, u32[]{:S(2)}, u32[]{:S(2)}) async-start(bf16[8,16,2048]{2,1,0:T(8,128)(2,1)} %bitcast.13), calls=%async_computation.2 | async-start | bytes 1048576 | tf_op jit(solution)/shard_map/all_to_all | solution.py:326
  90.5 1.1 copy-start
  91.6 2.2 %copy-start.10 = (bf16[2048,1024]{1,0:T(8,128)(2,1)S(1)}, bf16[2048,1024]{1,0:T(8,128)(2,1)}, u32[]{:S(2)}) copy-start(bf16[2048,1024]{1,0:T(8,128)(2,1)} %copy-done.9) | copy-start | bytes 12582916
  93.8 2.1 %copy-start.12 = (f32[6144,128]{1,0:T(8,128)S(1)}, f32[6144,128]{1,0:T(8,128)}, u32[]{:S(2)}) copy-start(f32[6144,128]{1,0:T(8,128)} %copy-done.11) | copy-start | bytes 9437188
Sparse Core Ops, SparseCore 0:
  49.8 29.8 reduce-scatter.4
  86.7 25.4 reduce-scatter.2

commit v3 on v2

--- a/solution.py
+++ b/solution.py
@@ -28,7 +28,7 @@
 PI_B = math.pi - PI_A
 VMEM = pl.BlockSpec(memory_space=pltpu.VMEM)
 SMEM = pl.BlockSpec(memory_space=pltpu.SMEM)
-ANY = pl.BlockSpec(memory_space=pl.ANY)
+HBM = pl.BlockSpec(memory_space=pltpu.HBM)
 NN = (((1,), (0,)), ((), ()))
 NT = (((1,), (1,)), ((), ()))
 
@@ -45,7 +45,7 @@
         out_specs=jax.tree.map(lambda _: VMEM, outs),
         scratch_shapes=scratch,
         compiler_params=pltpu.CompilerParams(vmem_limit_bytes=limit * 2**20),
-        cost_estimate=pl.CostEstimate(flops=int(TIME[name] * 5.75e9), bytes_accessed=1000, transcendentals=0),
+        cost_estimate=pl.CostEstimate(flops=int(TIME[name] * FACTOR * 1.15e9), bytes_accessed=1000, transcendentals=0),
         name=name,
     )
 
@@ -57,6 +57,7 @@
 TOKEN = shape((8, 128), F32)
 
 
+FACTOR = 0.1
 TIME = dict(
     prep=7,
     weights=4,
@@ -64,6 +65,7 @@
     kernel_grad_keep=4,
     join=1,
     encode=5,
+    lines=1,
     input_grad=6,
 )
 
@@ -148,7 +150,7 @@
     return call(
         weights_kernel,
         (shape((2048, 256)),) + (shape((1024, 256)),) * 3 + (TOKEN,),
-        [SMEM, ANY],
+        [SMEM, HBM],
         "weights",
         [
             pltpu.VMEM((4, 128, TAPS, 256), BF),
@@ -189,20 +191,22 @@
     )(place, taps, *gs)
 
 
-def keep_kernel(place, taps, g0, g1, g2, g3, got, out, done, lhs):
+def keep_kernel(place, taps, g0, g1, g2, g3, got, o0, o1, o2, o3, done, lhs):
     choose((g0, g1, g2, g3), place[0], [place[1 + d] for d in range(4)], lhs)
     for n in range(0, 2048, 256):
         cols = slice(n, n + 256)
         both = mul(lhs[...], taps[:, cols]) + got[:, cols].astype(F32)
-        for to in range(4):
-            out[to, :, cols] = both[to * 128 : (to + 1) * 128].astype(BF)
+        o0[:, cols] = both[0:128]
+        o1[:, cols] = both[128:256].astype(BF)
+        o2[:, cols] = both[256:384].astype(BF)
+        o3[:, cols] = both[384:512].astype(BF)
     done[...] = jnp.zeros(done.shape, F32)
 
 
 def keep(place, taps, gs, got):
     return call(
         keep_kernel,
-        (shape((4, 128, 2048)), TOKEN),
+        (shape((128, 2048), F32),) + (shape((128, 2048)),) * 3 + (TOKEN,),
         [SMEM] + [VMEM] * 6,
         "kernel_grad_keep",
         [pltpu.VMEM((512, 768), BF)],
@@ -219,29 +223,48 @@
     return call(join_kernel, (shape((1024, 256)),) * 3, [VMEM] * 4, "join", limit=8)(*near, after)
 
 
-def encode_kernel(place, taps, own, first, last, a1, a2, a3, b1, b2, b3, out, full, o_first, o_last):
-    y, core = place[0], place[1]
-    here = pl.multiple_of(core * 1024, 1024)
-    there = pl.multiple_of(1024 - core * 1024, 1024)
+def encode_kernel(
+    core, taps, own, first, last, a1, a2, a3, b1, b2, b3, o0, o1, o2, o3, full, o_first, o_last
+):
+    here = pl.multiple_of(core[0] * 1024, 1024)
+    there = pl.multiple_of(1024 - core[0] * 1024, 1024)
     full[:, 0:256] = own[...]
     for d, (a, b) in enumerate(((a1, b1), (a2, b2), (a3, b3))):
         cols = slice(256 * (d + 1), 256 * (d + 2))
         full[pl.ds(here, 1024), cols] = a[...]
         full[pl.ds(there, 1024), cols] = b[...]
-    for d in range(4):
-        out[lax.rem(y + d, 4)] = mul(taps[...], full[:, d * 256 : (d + 1) * 256]).astype(BF)
+    for d, out in enumerate((o0, o1, o2, o3)):
+        out[...] = mul(taps[...], full[:, d * 256 : (d + 1) * 256]).astype(out.dtype)
     o_first[...] = first[...]
     o_last[...] = last[...]
 
 
-def encode(place, taps, own, edges, near, far):
+def encode(core, taps, own, edges, near, far):
     return call(
         encode_kernel,
-        (shape((4, 768, 256)), shape((2048, 1024))) + (shape((16, 1024)),) * 2,
+        (shape((768, 256), F32),)
+        + (shape((768, 256)),) * 3
+        + (shape((2048, 1024)),)
+        + (shape((16, 1024)),) * 2,
         [SMEM] + [VMEM] * 10,
         "encode",
         limit=20,
-    )(place, taps, own, *edges, *near, *far)
+    )(core, taps, own, *edges, *near, *far)
+
+
+def lines_kernel(own, a1, a2, a3, out, done):
+    for m in range(8):
+        here = slice(m * 16, m * 16 + 16)
+        out[m] = (
+            own[here, :] + a1[here, :].astype(F32) + a2[here, :].astype(F32) + a3[here, :].astype(F32)
+        ).astype(BF)
+    done[...] = jnp.zeros(done.shape, F32)
+
+
+def lines(own, arrived):
+    return call(lines_kernel, (shape((8, 16, 2048)), TOKEN), [VMEM] * 4, "lines", limit=8)(
+        own, *arrived
+    )
 
 
 def input_grad_kernel(g0, g1, g2, g3, low, high, weights, factor, after, out, full, rows):
@@ -312,19 +335,24 @@
     near = (turn(p3, "chan", -1), turn(p2, "chan", 2), turn(p1, "chan", 1))
     taps, factor = prep(features, low, high, snake_alpha.reshape(1, -1), done)
 
-    place = jnp.stack([core] + [(y + d) % 4 for d in range(4)])
+    place = jnp.stack([core] + [(y + d + 4 - x) % 4 for d in range(4)])
     out, first, last = send(place, taps, gs)
     got = turn(out, "core", 1)
-    kept, done = keep(place, taps, gs, got)
-    summed = lax.psum_scatter(kept, "x", scatter_dimension=0)
+    keep0, keep1, keep2, keep3, done = keep(place, taps, gs, got)
+    arrived = (turn(keep1, "x", 1), turn(keep3, "x", -1), turn(keep2, "x", 2))
 
     held = join(near, done)
     far = [turn(h, "core", 1) for h in held]
-    partial, full, first, last = encode(at, taps, own, (first, last), held, far)
+    mine, part1, part2, part3, full, first, last = encode(
+        core.reshape(1), taps, own, (first, last), held, far
+    )
+    others = (turn(part1, "chan", 1), turn(part3, "chan", -1), turn(part2, "chan", 2))
     edges = beside(last, 1), beside(first, -1)
-    encoded = lax.psum_scatter(partial, "chan", scatter_dimension=0)
-    spread = lax.all_to_all(summed.reshape(8, 16, 2048), "z", 0, 0)
-    grad_features = input_grad(gs, *edges, full, factor, summed)
+    summed, done = lines(keep0, arrived)
+    spread = lax.all_to_all(summed, "z", 0, 0)
+    grad_features = input_grad(gs, *edges, full, factor, done)
+
+    encoded = (mine + sum(o.astype(F32) for o in others)).astype(BF)
 
     scale = 1.0 / math.sqrt(features.shape[0] // STRIDE * 64)
     total = jnp.sum(spread.astype(F32), axis=0) * scale

time: 120 us -> 122 us (1.017); the launches traced: 119 us -> 119 us
  starting transfers between devices: 29.5 us -> 46.4 us
  between operations: 14.3 us -> 0.86 us
  waiting for transfers between devices: 30.6 us -> 23.5 us
  local copies, waits for them, and re-layouts: 13.1 us -> 15.5 us
  other arithmetic: 0.16 us -> 2.17 us
    ppermute x10 -> x16, starting transfers between devices: 9.52 us -> 23.3 us  [turn(): lax.ppermute(value, axis, [(i, (i + by) % count) for i in range(count)])]
    all_to_all x1, waiting for transfers between devices: 4.34 us -> 0.01 us  [shards(): spread = lax.all_to_all(summed, 'z', 0, 0)]
    reduce_scatter x2 -> x0, waiting for transfers between devices: 4.31 us -> none  [the longest x1 4.29 us: shards(): encoded = lax.psum_scatter(partial, 'chan', scatter_dimension=0)]
    all_to_all x1, starting transfers between devices: 3.95 us -> 6.99 us  [shards(): spread = lax.all_to_all(summed, 'z', 0, 0)]
    unnamed x43 -> x39, local copies, waits for them, and re-layouts: 12.3 us -> 14.7 us
    ppermute x4, waiting for transfers between devices: 0.01 us -> 1.35 us  [beside(): return lax.ppermute(value, TM, pairs)]
    pallas_call x2 -> x3, Pallas kernels: 10.7 us -> 9.85 us  [the longest x1 5.98 us: encode(): call(encode_kernel, (shape((768, 256), F32),) + (shape((768, 256)),) * 3...]
    ppermute x10 -> x16, waiting for transfers between devices: 21.9 us -> 22.1 us  [turn(): lax.ppermute(value, axis, [(i, (i + by) % count) for i in range(count)])]
  transfers between devices with their start and end apart: 17 -> 21, of which waited for: 9 -> 5; matrix products, arithmetic and copies ran while one was open for 1% -> 2% of each run, Pallas kernels for 23% -> 23%
where the time goes in v3:
time: 122 us; the launch traced here: 119 us
  starting transfers between devices  46.4 us (38%)
  Pallas kernels  30.9 us (25%)
  waiting for transfers between devices  23.5 us (19%)
  local copies, waits for them, and re-layouts  15.5 us (13%)
  other arithmetic  2.17 us (2%)
    ppermute x16, starting transfers between devices, turn(): lax.ppermute(value, axis, [(i, (i + by) % count) for i in range(count)])  23.3 us
    ppermute x16, waiting for transfers between devices, turn(): lax.ppermute(value, axis, [(i, (i + by) % count) for i in range(count)])  22.1 us
    ppermute x4, starting transfers between devices, beside(): return lax.ppermute(value, TM, pairs)  16.1 us
    unnamed x39, local copies, waits for them, and re-layouts  14.7 us
    all_to_all x1, starting transfers between devices, shards(): spread = lax.all_to_all(summed, 'z', 0, 0)  6.99 us
    pallas_call x1, Pallas kernels, input_grad(): call(input_grad_kernel, shape((frames, chans)), [VMEM] * 9, 'input_grad',...  6.95 us
    pallas_call x1, Pallas kernels, encode(): call(encode_kernel, (shape((768, 256), F32),) + (shape((768, 256)),) * 3...  5.98 us
    pallas_call x1, Pallas kernels, prep(): call(functools.partial(prep_kernel, step), (shape((frames // STRIDE, TAPS...  5.8 us
  transfers between devices with their start and end apart: 21, of which 5 were waited for; matrix products, arithmetic and copies ran while one was open for 2% of the time, Pallas kernels for 23%

profile of v3, /device:TPU:2, one launch (start us, length us, event | category | flops | bytes accessed | tf_op | source)
XLA Modules:
  0.0 119.3 jit_solution(17229711718826246995)
XLA Ops:
  0.6 3.1 %collective-permute-start.2 = (bf16[768,256]{1,0:T(8,128)(2,1)}, bf16[768,256]{1,0:T(8,128)(2,1)}, u32[]{:S(2)}, u32[]{:S(2)}) collective-permute-start(bf16[768,256]{1,0:T(8,128)(2,1)} %g0.5), channel_id=1, source_target_pairs={{0,3},{1,0},{2,1},{3,2},{4,7},{5,4},{6,5},{7,6},{8,11},{9,8},{10,9... | collective-permute-start | bytes 1179656 | tf_op jit(solution)/shard_map/ppermute | solution.py:313
  3.7 0.6 collective-permute-start.3
  4.4 1.0 collective-permute-start.4
  5.3 0.7 fusion.1
  6.0 1.9 %collective-permute-start = (bf16[16,128]{1,0:T(8,128)(2,1)S(1)}, bf16[16,128]{1,0:T(8,128)(2,1)S(1)}, u32[]{:S(2)}, u32[]{:S(2)}) collective-permute-start(bf16[16,128]{1,0:T(8,128)(2,1)S(1)} %get-tuple-element.58), channel_id=1, source_target_pairs={{0,4},{4,8},{8,12},{12,16},{16,20},{20,24},{24,28},{28,32},{32,36}... | collective-permute-start | bytes 12296 | tf_op jit(solution)/shard_map/ppermute | solution.py:319
  7.9 6.3 %collective-permute-start.1 = (bf16[16,128]{1,0:T(8,128)(2,1)S(1)}, bf16[16,128]{1,0:T(8,128)(2,1)S(1)}, u32[]{:S(2)}, u32[]{:S(2)}) collective-permute-start(bf16[16,128]{1,0:T(8,128)(2,1)S(1)} %get-tuple-element.57), channel_id=1, source_target_pairs={{4,0},{8,4},{12,8},{16,12},{20,16},{24,20},{28,24},{32,28},{36,32}... | collective-permute-start | bytes 12296 | tf_op jit(solution)/shard_map/ppermute | solution.py:319
  14.3 0.1 pad_add_fusion.place
  14.4 2.2 %copy-done = bf16[512,16,256]{2,1,0:T(8,128)(2,1)S(1)} copy-done((bf16[512,16,256]{2,1,0:T(8,128)(2,1)S(1)}, bf16[512,16,256]{2,1,0:T(8,128)(2,1)}, u32[]{:S(2)}) %copy-start) | copy-done | bytes 4194328
  16.6 3.3 %weights.1 = (bf16[2048,256]{1,0:T(8,128)(2,1)S(1)}, bf16[1024,256]{1,0:T(8,128)(2,1)S(1)}, bf16[1024,256]{1,0:T(8,128)(2,1)S(1)}, bf16[1024,256]{1,0:T(8,128)(2,1)S(1)}, f32[8,128]{1,0:T(8,128)S(1)}) custom-call(s32[2]{0:T(128)S(1)} %pad_add_fusion.place, bf16[512,16,256]{2,1,0:T(8,128)(2,1)S(1)} %copy-done), custom_call_target="tpu_custom_call" | custom-call | flops 460000000 | bytes 1000 | tf_op jit(solution)/shard_map/weights/pallas_call | solution.py:150
  19.8 0.0 copy-start.4
  19.8 1.0 copy-done.4
  20.8 0.8 copy-done.12
  21.6 0.8 copy-done.14
  22.4 0.8 copy-done.16
  23.2 0.1 stack.29.place
  23.3 0.0 collective-permute-done.low
  23.3 0.0 collective-permute-done.1.high
  23.3 1.4 %copy-done.11 = bf16[6144,128]{1,0:T(8,128)(2,1)S(1)} copy-done((bf16[6144,128]{1,0:T(8,128)(2,1)S(1)}, bf16[6144,128]{1,0:T(8,128)(2,1)}, u32[]{:S(2)}) %copy-start.11) | copy-done | bytes 1572888
  24.7 0.7 copy-done.18
  25.4 5.8 %prep.1 = (bf16[768,2048]{1,0:T(8,128)(2,1)S(1)}, f32[6144,128]{1,0:T(8,128)S(1)}) custom-call(bf16[6144,128]{1,0:T(8,128)(2,1)S(1)} %copy-done.11, bf16[16,128]{1,0:T(8,128)(2,1)S(1)} %collective-permute-done.low, bf16[16,128]{1,0:T(8,128)(2,1)S(1)} %collective-permute-done.1.high, f32[1,128]{1,0:T(1,128)S(1)} %bitcast.10, f32[8,128]{1,0:T(8,128)S(1)} %get-tuple-element.30.after), custom_call_target="tpu_custom_call" | custom-call | flops 805000000 | bytes 1000 | tf_op jit(solution)/shard_map/prep/pallas_call | solution.py:115
  31.2 1.6 %copy-done.2 = f32[6144,128]{1,0:T(8,128)} copy-done((f32[6144,128]{1,0:T(8,128)}, f32[6144,128]{1,0:T(8,128)S(1)}, u32[]{:S(2)}) %copy-start.2) | copy-done | bytes 3145752
  32.9 3.8 %kernel_grad_send.1 = (bf16[512,2048]{1,0:T(8,128)(2,1)S(1)}, bf16[16,1024]{1,0:T(8,128)(2,1)S(1)}, bf16[16,1024]{1,0:T(8,128)(2,1)S(1)}) custom-call(s32[5]{0:T(128)S(1)} %stack.29.place, bf16[768,2048]{1,0:T(8,128)(2,1)S(1)} %get-tuple-element.31.taps, bf16[768,256]{1,0:T(8,128)(2,1)S(1)} %copy-done.1, bf16[768,256]{1,0:T(8,128)(2,1)} %collective-permute-done.2.g1, ...), custom_call_target="tpu_custom_call" | custom-call | flops 345000000 | bytes 1000 | tf_op jit(solution)/shard_map/kernel_grad_send/pallas_call | solution.py:184
  36.6 0.0 copy-start.7
  36.7 0.6 copy-done.7
  37.3 0.6 copy-done.9
  37.9 0.0 collective-permute-start.8
  37.9 2.3 %collective-permute-start.5 = (bf16[1024,256]{1,0:T(8,128)(2,1)S(1)}, bf16[1024,256]{1,0:T(8,128)(2,1)S(1)}, u32[]{:S(2)}, u32[]{:S(2)}) collective-permute-start(bf16[1024,256]{1,0:T(8,128)(2,1)S(1)} %copy-done.17), channel_id=1, source_target_pairs={{0,3},{1,0},{2,1},{3,2},{4,7},{5,4},{6,5},{7,6},{8,11},{9,8},{10,9... | collective-permute-start | bytes 1572872 | tf_op jit(solution)/shard_map/ppermute | solution.py:313
  40.1 1.7 %collective-permute-start.6 = (bf16[1024,256]{1,0:T(8,128)(2,1)S(1)}, bf16[1024,256]{1,0:T(8,128)(2,1)S(1)}, u32[]{:S(2)}, u32[]{:S(2)}) collective-permute-start(bf16[1024,256]{1,0:T(8,128)(2,1)S(1)} %copy-done.15), channel_id=1, source_target_pairs={{0,2},{1,3},{2,0},{3,1},{4,6},{5,7},{6,4},{7,5},{8,10},{9,11},{10,... | collective-permute-start | bytes 1572872 | tf_op jit(solution)/shard_map/ppermute | solution.py:313
  41.8 0.0 collective-permute-start.7
  41.8 0.2 collective-permute-done.8.got
  42.0 3.6 %kernel_grad_keep.1 = (f32[128,2048]{1,0:T(8,128)S(1)}, bf16[128,2048]{1,0:T(8,128)(2,1)S(1)}, bf16[128,2048]{1,0:T(8,128)(2,1)S(1)}, bf16[128,2048]{1,0:T(8,128)(2,1)S(1)}, f32[8,128]{1,0:T(8,128)S(1)}) custom-call(s32[5]{0:T(128)S(1)} %stack.29.place, bf16[768,2048]{1,0:T(8,128)(2,1)S(1)} %get-tuple-element.31.taps, bf16[768,256]{1,0:T(8,128)(2,1)S(1)} %copy-done.1, ...), custom_call_target="tpu_custom_call" | custom-call | flops 460000000 | bytes 1000 | tf_op jit(solution)/shard_map/kernel_grad_keep/pallas_call | solution.py:207
  45.7 1.6 %collective-permute-start.17 = (bf16[128,2048]{1,0:T(8,128)(2,1)S(1)}, bf16[128,2048]{1,0:T(8,128)(2,1)S(1)}, u32[]{:S(2)}, u32[]{:S(2)}) collective-permute-start(bf16[128,2048]{1,0:T(8,128)(2,1)S(1)} %get-tuple-element.52), channel_id=1, source_target_pairs={{0,64},{64,128},{128,192},{192,0},{1,65},{65,129},{129,193},{193,1... | collective-permute-start | bytes 1572872 | tf_op jit(solution)/shard_map/ppermute | solution.py:313
  47.3 0.5 collective-permute-start.18
  47.8 15.5 %collective-permute-done.5.a1 = bf16[1024,256]{1,0:T(8,128)(2,1)S(1)} collective-permute-done((bf16[1024,256]{1,0:T(8,128)(2,1)S(1)}, bf16[1024,256]{1,0:T(8,128)(2,1)S(1)}, u32[]{:S(2)}, u32[]{:S(2)}) %collective-permute-start.5) | collective-permute-done | bytes 524320 | tf_op jit(solution)/shard_map/ppermute | solution.py:313
  63.3 2.4 %collective-permute-start.19 = (bf16[128,2048]{1,0:T(8,128)(2,1)S(1)}, bf16[128,2048]{1,0:T(8,128)(2,1)S(1)}, u32[]{:S(2)}, u32[]{:S(2)}) collective-permute-start(bf16[128,2048]{1,0:T(8,128)(2,1)S(1)} %get-tuple-element.54), channel_id=1, source_target_pairs={{0,128},{64,192},{128,0},{192,64},{1,129},{65,193},{129,1},{193,65... | collective-permute-start | bytes 1572872 | tf_op jit(solution)/shard_map/ppermute | solution.py:313
  65.7 1.2 %collective-permute-done.7.a3 = bf16[1024,256]{1,0:T(8,128)(2,1)S(1)} collective-permute-done((bf16[1024,256]{1,0:T(8,128)(2,1)S(1)}, bf16[1024,256]{1,0:T(8,128)(2,1)S(1)}, u32[]{:S(2)}, u32[]{:S(2)}) %collective-permute-start.7) | collective-permute-done | bytes 524320 | tf_op jit(solution)/shard_map/ppermute | solution.py:313
  66.9 1.3 %join.1 = (bf16[1024,256]{1,0:T(8,128)(2,1)}, bf16[1024,256]{1,0:T(8,128)(2,1)}, bf16[1024,256]{1,0:T(8,128)(2,1)}) custom-call(bf16[1024,256]{1,0:T(8,128)(2,1)S(1)} %collective-permute-done.5.a1, bf16[1024,256]{1,0:T(8,128)(2,1)S(1)} %collective-permute-done.6.a2, bf16[1024,256]{1,0:T(8,128)(2,1)S(1)} %collective-permute-done.7.a3, ...), custom_call_target="tpu_custom_call" | custom-call | flops 115000000 | bytes 1000 | tf_op jit(solution)/shard_map/join/pallas_call | solution.py:223
  68.2 0.0 collective-permute-start.10
  68.3 0.5 collective-permute-start.11
  68.8 0.0 collective-permute-done.17.a1
  68.8 0.0 collective-permute-start.9
  68.8 5.2 %collective-permute-done.19.a3 = bf16[128,2048]{1,0:T(8,128)(2,1)S(1)} collective-permute-done((bf16[128,2048]{1,0:T(8,128)(2,1)S(1)}, bf16[128,2048]{1,0:T(8,128)(2,1)S(1)}, u32[]{:S(2)}, u32[]{:S(2)}) %collective-permute-start.19) | collective-permute-done | bytes 524320 | tf_op jit(solution)/shard_map/ppermute | solution.py:313
  74.0 0.2 lines.1
  74.2 0.8 copy-done.6
  75.0 7.0 %all-to-all-start = ((bf16[8,16,2048]{2,1,0:T(8,128)(2,1)}), bf16[8,16,2048]{2,1,0:T(8,128)(2,1)}, u32[]{:S(2)}, u32[]{:S(2)}) async-start(bf16[8,16,2048]{2,1,0:T(8,128)(2,1)} %copy-done.6), calls=%async_computation | async-start | bytes 1048576 | tf_op jit(solution)/shard_map/all_to_all | solution.py:352
  82.0 0.0 collective-permute-done.10.b2
  82.0 0.0 collective-permute-done.11.b3
  82.0 0.0 copy-start.5
  82.0 1.2 %copy-done.5 = bf16[2048,256]{1,0:T(8,128)(2,1)S(1)} copy-done((bf16[2048,256]{1,0:T(8,128)(2,1)S(1)}, bf16[2048,256]{1,0:T(8,128)(2,1)}, u32[]{:S(2)}) %copy-start.5) | copy-done | bytes 1048600
  83.2 0.8 copy-done.8
  84.0 0.8 copy-done.10
  84.7 6.0 %encode.1 = (f32[768,256]{1,0:T(8,128)S(1)}, bf16[768,256]{1,0:T(8,128)(2,1)S(1)}, bf16[768,256]{1,0:T(8,128)(2,1)S(1)}, bf16[768,256]{1,0:T(8,128)(2,1)S(1)}, b...) custom-call(s32[1]{0:T(128)} %bitcast.core, ...), custom_call_target="tpu_custom_call" | custom-call | flops 575000000 | bytes 1000 | tf_op jit(solution)/shard_map/encode/pallas_call | solution.py:243
  90.7 6.5 %collective-permute-start.12 = (bf16[768,256]{1,0:T(8,128)(2,1)S(1)}, bf16[768,256]{1,0:T(8,128)(2,1)S(1)}, u32[]{:S(2)}, u32[]{:S(2)}) collective-permute-start(bf16[768,256]{1,0:T(8,128)(2,1)S(1)} %get-tuple-element.44), channel_id=1, source_target_pairs={{0,1},{1,2},{2,3},{3,0},{4,5},{5,6},{6,7},{7,4},{8,9},{9,10},{10,1... | collective-permute-start | bytes 1179656 | tf_op jit(solution)/shard_map/ppermute | solution.py:313
  97.3 1.7 %collective-permute-start.13 = (bf16[768,256]{1,0:T(8,128)(2,1)S(1)}, bf16[768,256]{1,0:T(8,128)(2,1)S(1)}, u32[]{:S(2)}, u32[]{:S(2)}) collective-permute-start(bf16[768,256]{1,0:T(8,128)(2,1)S(1)} %get-tuple-element.45), channel_id=1, source_target_pairs={{0,3},{1,0},{2,1},{3,2},{4,7},{5,4},{6,5},{7,6},{8,11},{9,8},{10,9... | collective-permute-start | bytes 1179656 | tf_op jit(solution)/shard_map/ppermute | solution.py:313
  99.0 1.4 %collective-permute-start.14 = (bf16[768,256]{1,0:T(8,128)(2,1)S(1)}, bf16[768,256]{1,0:T(8,128)(2,1)S(1)}, u32[]{:S(2)}, u32[]{:S(2)}) collective-permute-start(bf16[768,256]{1,0:T(8,128)(2,1)S(1)} %get-tuple-element.46), channel_id=1, source_target_pairs={{0,2},{1,3},{2,0},{3,1},{4,6},{5,7},{6,4},{7,5},{8,10},{9,11},{10,... | collective-permute-start | bytes 1179656 | tf_op jit(solution)/shard_map/ppermute | solution.py:313
  100.3 1.9 %collective-permute-start.15 = (bf16[16,1024]{1,0:T(8,128)(2,1)S(1)}, bf16[16,1024]{1,0:T(8,128)(2,1)S(1)}, u32[]{:S(2)}, u32[]{:S(2)}) collective-permute-start(bf16[16,1024]{1,0:T(8,128)(2,1)S(1)} %get-tuple-element.47), channel_id=1, source_target_pairs={{0,4},{4,8},{8,12},{12,16},{16,20},{20,24},{24,28},{28,32},{32,36}... | collective-permute-start | bytes 98312 | tf_op jit(solution)/shard_map/ppermute | solution.py:319
  102.2 6.0 %collective-permute-start.16 = (bf16[16,1024]{1,0:T(8,128)(2,1)S(1)}, bf16[16,1024]{1,0:T(8,128)(2,1)S(1)}, u32[]{:S(2)}, u32[]{:S(2)}) collective-permute-start(bf16[16,1024]{1,0:T(8,128)(2,1)S(1)} %get-tuple-element.48), channel_id=1, source_target_pairs={{4,0},{8,4},{12,8},{16,12},{20,16},{24,20},{28,24},{32,28},{36,32}... | collective-permute-start | bytes 98312 | tf_op jit(solution)/shard_map/ppermute | solution.py:319
  108.2 1.3 %collective-permute-done.16.high = bf16[16,1024]{1,0:T(8,128)(2,1)S(1)} collective-permute-done((bf16[16,1024]{1,0:T(8,128)(2,1)S(1)}, bf16[16,1024]{1,0:T(8,128)(2,1)S(1)}, u32[]{:S(2)}, u32[]{:S(2)}) %collective-permute-start.16) | collective-permute-done | bytes 32800 | tf_op jit(solution)/shard_map/ppermute | solution.py:319
  109.6 7.0 %input_grad.1 = bf16[6144,128]{1,0:T(8,128)(2,1)} custom-call(bf16[768,256]{1,0:T(8,128)(2,1)S(1)} %copy-done.1, bf16[768,256]{1,0:T(8,128)(2,1)} %collective-permute-done.2.g1, bf16[768,256]{1,0:T(8,128)(2,1)} %collective-permute-done.3.g2, bf16[768,256]{1,0:T(8,128)(2,1)} %collective-permute-done.4.g3, bf16[16,1024]{1,0:T(8,128)(2,1)S(1)} %collective-permute-done.15.low, ...), custom_call_target="tpu_custom_call" | custom-call | flops 690000000 | bytes 1000 | tf_op jit(solution)/shard_map/input_grad/pallas_call | solution.py:301
  116.5 0.0 collective-permute-done.12
  116.5 0.0 collective-permute-done.13
  116.6 1.0 add_convert_fusion
  117.5 1.1 convert_reduce_fusion
  118.7 0.6 copy.7
  (31 shorter events, 0.1 us)
Async XLA Ops:
  0.6 32.2 %collective-permute-start.2 = (bf16[768,256]{1,0:T(8,128)(2,1)}, bf16[768,256]{1,0:T(8,128)(2,1)}, u32[]{:S(2)}, u32[]{:S(2)}) collective-permute-start(bf16[768,256]{1,0:T(8,128)(2,1)} %g0.5), channel_id=1, source_target_pairs={{0,3},{1,0},{2,1},{3,2},{4,7},{5,4},{6,5},{7,6},{8,11},{9,8},{10,9... | collective-permute-start | bytes 1179656 | tf_op jit(solution)/shard_map/ppermute | solution.py:313
  3.7 29.1 %collective-permute-start.3 = (bf16[768,256]{1,0:T(8,128)(2,1)}, bf16[768,256]{1,0:T(8,128)(2,1)}, u32[]{:S(2)}, u32[]{:S(2)}) collective-permute-start(bf16[768,256]{1,0:T(8,128)(2,1)} %g0.5), channel_id=1, source_target_pairs={{0,2},{1,3},{2,0},{3,1},{4,6},{5,7},{6,4},{7,5},{8,10},{9,11},{10,... | collective-permute-start | bytes 1179656 | tf_op jit(solution)/shard_map/ppermute | solution.py:313
  4.4 28.5 %collective-permute-start.4 = (bf16[768,256]{1,0:T(8,128)(2,1)}, bf16[768,256]{1,0:T(8,128)(2,1)}, u32[]{:S(2)}, u32[]{:S(2)}) collective-permute-start(bf16[768,256]{1,0:T(8,128)(2,1)} %g0.5), channel_id=1, source_target_pairs={{0,1},{1,2},{2,3},{3,0},{4,5},{5,6},{6,7},{7,4},{8,9},{9,10},{10,1... | collective-permute-start | bytes 1179656 | tf_op jit(solution)/shard_map/ppermute | solution.py:313
  6.0 17.2 %collective-permute-start = (bf16[16,128]{1,0:T(8,128)(2,1)S(1)}, bf16[16,128]{1,0:T(8,128)(2,1)S(1)}, u32[]{:S(2)}, u32[]{:S(2)}) collective-permute-start(bf16[16,128]{1,0:T(8,128)(2,1)S(1)} %get-tuple-element.58), channel_id=1, source_target_pairs={{0,4},{4,8},{8,12},{12,16},{16,20},{20,24},{24,28},{28,32},{32,36}... | collective-permute-start | bytes 12296 | tf_op jit(solution)/shard_map/ppermute | solution.py:319
  7.9 15.3 %collective-permute-start.1 = (bf16[16,128]{1,0:T(8,128)(2,1)S(1)}, bf16[16,128]{1,0:T(8,128)(2,1)S(1)}, u32[]{:S(2)}, u32[]{:S(2)}) collective-permute-start(bf16[16,128]{1,0:T(8,128)(2,1)S(1)} %get-tuple-element.57), channel_id=1, source_target_pairs={{4,0},{8,4},{12,8},{16,12},{20,16},{24,20},{28,24},{32,28},{36,32}... | collective-permute-start | bytes 12296 | tf_op jit(solution)/shard_map/ppermute | solution.py:319
  14.4 2.2 %copy-start = (bf16[512,16,256]{2,1,0:T(8,128)(2,1)S(1)}, bf16[512,16,256]{2,1,0:T(8,128)(2,1)}, u32[]{:S(2)}) copy-start(bf16[512,16,256]{2,1,0:T(8,128)(2,1)} %whole.1) | copy-start | bytes 12582916
  19.8 1.0 copy-start.4
  20.8 0.8 copy-start.12
  21.6 0.8 copy-start.14
  22.4 0.8 copy-start.16
  23.2 9.7 %copy-start.1 = (bf16[768,256]{1,0:T(8,128)(2,1)S(1)}, bf16[768,256]{1,0:T(8,128)(2,1)}, u32[]{:S(2)}) copy-start(bf16[768,256]{1,0:T(8,128)(2,1)} %g0.5) | copy-start | bytes 1179652
  23.3 1.4 %copy-start.11 = (bf16[6144,128]{1,0:T(8,128)(2,1)S(1)}, bf16[6144,128]{1,0:T(8,128)(2,1)}, u32[]{:S(2)}) copy-start(bf16[6144,128]{1,0:T(8,128)(2,1)} %feat.1) | copy-start | bytes 4718596
  24.7 0.7 copy-start.18
  31.2 1.6 %copy-start.2 = (f32[6144,128]{1,0:T(8,128)}, f32[6144,128]{1,0:T(8,128)S(1)}, u32[]{:S(2)}) copy-start(f32[6144,128]{1,0:T(8,128)S(1)} %get-tuple-element.50.factor) | copy-start | bytes 9437188
  32.8 5.0 %copy-start.17 = (bf16[1024,256]{1,0:T(8,128)(2,1)S(1)}, bf16[1024,256]{1,0:T(8,128)(2,1)}, u32[]{:S(2)}) copy-start(bf16[1024,256]{1,0:T(8,128)(2,1)} %copy-done.16) | copy-start | bytes 1572868
  32.9 7.3 %copy-start.15 = (bf16[1024,256]{1,0:T(8,128)(2,1)S(1)}, bf16[1024,256]{1,0:T(8,128)(2,1)}, u32[]{:S(2)}) copy-start(bf16[1024,256]{1,0:T(8,128)(2,1)} %copy-done.14) | copy-start | bytes 1572868
  32.9 9.0 %copy-start.13 = (bf16[1024,256]{1,0:T(8,128)(2,1)S(1)}, bf16[1024,256]{1,0:T(8,128)(2,1)}, u32[]{:S(2)}) copy-start(bf16[1024,256]{1,0:T(8,128)(2,1)} %copy-done.12) | copy-start | bytes 1572868
  36.6 0.6 copy-start.7
  37.3 0.6 copy-start.9
  37.9 4.2 %collective-permute-start.8 = (bf16[512,2048]{1,0:T(8,128)(2,1)S(1)}, bf16[512,2048]{1,0:T(8,128)(2,1)S(1)}, u32[]{:S(2)}, u32[]{:S(2)}) collective-permute-start(bf16[512,2048]{1,0:T(8,128)(2,1)S(1)} %get-tuple-element.38), channel_id=1, source_target_pairs={{0,4},{4,0},{1,5},{5,1},{2,6},{6,2},{3,7},{7,3},{8,12},{12,8},{9,1... | collective-permute-start | bytes 6291464 | tf_op jit(solution)/shard_map/ppermute | solution.py:313
  37.9 25.4 %collective-permute-start.5 = (bf16[1024,256]{1,0:T(8,128)(2,1)S(1)}, bf16[1024,256]{1,0:T(8,128)(2,1)S(1)}, u32[]{:S(2)}, u32[]{:S(2)}) collective-permute-start(bf16[1024,256]{1,0:T(8,128)(2,1)S(1)} %copy-done.17), channel_id=1, source_target_pairs={{0,3},{1,0},{2,1},{3,2},{4,7},{5,4},{6,5},{7,6},{8,11},{9,8},{10,9... | collective-permute-start | bytes 1572872 | tf_op jit(solution)/shard_map/ppermute | solution.py:313
  40.1 25.5 %collective-permute-start.6 = (bf16[1024,256]{1,0:T(8,128)(2,1)S(1)}, bf16[1024,256]{1,0:T(8,128)(2,1)S(1)}, u32[]{:S(2)}, u32[]{:S(2)}) collective-permute-start(bf16[1024,256]{1,0:T(8,128)(2,1)S(1)} %copy-done.15), channel_id=1, source_target_pairs={{0,2},{1,3},{2,0},{3,1},{4,6},{5,7},{6,4},{7,5},{8,10},{9,11},{10,... | collective-permute-start | bytes 1572872 | tf_op jit(solution)/shard_map/ppermute | solution.py:313
  41.8 25.1 %collective-permute-start.7 = (bf16[1024,256]{1,0:T(8,128)(2,1)S(1)}, bf16[1024,256]{1,0:T(8,128)(2,1)S(1)}, u32[]{:S(2)}, u32[]{:S(2)}) collective-permute-start(bf16[1024,256]{1,0:T(8,128)(2,1)S(1)} %copy-done.13), channel_id=1, source_target_pairs={{0,1},{1,2},{2,3},{3,0},{4,5},{5,6},{6,7},{7,4},{8,9},{9,10},{10,1... | collective-permute-start | bytes 1572872 | tf_op jit(solution)/shard_map/ppermute | solution.py:313
  45.7 23.1 %collective-permute-start.17 = (bf16[128,2048]{1,0:T(8,128)(2,1)S(1)}, bf16[128,2048]{1,0:T(8,128)(2,1)S(1)}, u32[]{:S(2)}, u32[]{:S(2)}) collective-permute-start(bf16[128,2048]{1,0:T(8,128)(2,1)S(1)} %get-tuple-element.52), channel_id=1, source_target_pairs={{0,64},{64,128},{128,192},{192,0},{1,65},{65,129},{129,193},{193,1... | collective-permute-start | bytes 1572872 | tf_op jit(solution)/shard_map/ppermute | solution.py:313
  47.3 21.5 %collective-permute-start.18 = (bf16[128,2048]{1,0:T(8,128)(2,1)S(1)}, bf16[128,2048]{1,0:T(8,128)(2,1)S(1)}, u32[]{:S(2)}, u32[]{:S(2)}) collective-permute-start(bf16[128,2048]{1,0:T(8,128)(2,1)S(1)} %get-tuple-element.53), channel_id=1, source_target_pairs={{0,192},{64,0},{128,64},{192,128},{1,193},{65,1},{129,65},{193,129... | collective-permute-start | bytes 1572872 | tf_op jit(solution)/shard_map/ppermute | solution.py:313
  63.3 10.7 %collective-permute-start.19 = (bf16[128,2048]{1,0:T(8,128)(2,1)S(1)}, bf16[128,2048]{1,0:T(8,128)(2,1)S(1)}, u32[]{:S(2)}, u32[]{:S(2)}) collective-permute-start(bf16[128,2048]{1,0:T(8,128)(2,1)S(1)} %get-tuple-element.54), channel_id=1, source_target_pairs={{0,128},{64,192},{128,0},{192,64},{1,129},{65,193},{129,1},{193,65... | collective-permute-start | bytes 1572872 | tf_op jit(solution)/shard_map/ppermute | solution.py:313
  68.2 13.7 %collective-permute-start.10 = (bf16[1024,256]{1,0:T(8,128)(2,1)}, bf16[1024,256]{1,0:T(8,128)(2,1)}, u32[]{:S(2)}, u32[]{:S(2)}) collective-permute-start(bf16[1024,256]{1,0:T(8,128)(2,1)} %get-tuple-element.41.a2), channel_id=1, source_target_pairs={{0,4},{4,0},{1,5},{5,1},{2,6},{6,2},{3,7},{7,3},{8,12},{12,8},{9,1... | collective-permute-start | bytes 1572872 | tf_op jit(solution)/shard_map/ppermute | solution.py:313
  68.3 13.7 %collective-permute-start.11 = (bf16[1024,256]{1,0:T(8,128)(2,1)}, bf16[1024,256]{1,0:T(8,128)(2,1)}, u32[]{:S(2)}, u32[]{:S(2)}) collective-permute-start(bf16[1024,256]{1,0:T(8,128)(2,1)} %get-tuple-element.42.a3), channel_id=1, source_target_pairs={{0,4},{4,0},{1,5},{5,1},{2,6},{6,2},{3,7},{7,3},{8,12},{12,8},{9,1... | collective-permute-start | bytes 1572872 | tf_op jit(solution)/shard_map/ppermute | solution.py:313
  68.8 13.2 %collective-permute-start.9 = (bf16[1024,256]{1,0:T(8,128)(2,1)}, bf16[1024,256]{1,0:T(8,128)(2,1)}, u32[]{:S(2)}, u32[]{:S(2)}) collective-permute-start(bf16[1024,256]{1,0:T(8,128)(2,1)} %get-tuple-element.40.a1), channel_id=1, source_target_pairs={{0,4},{4,0},{1,5},{5,1},{2,6},{6,2},{3,7},{7,3},{8,12},{12,8},{9,1... | collective-permute-start | bytes 1572872 | tf_op jit(solution)/shard_map/ppermute | solution.py:313
  74.2 0.8 copy-start.6
  75.0 42.5 %all-to-all-start = ((bf16[8,16,2048]{2,1,0:T(8,128)(2,1)}), bf16[8,16,2048]{2,1,0:T(8,128)(2,1)}, u32[]{:S(2)}, u32[]{:S(2)}) async-start(bf16[8,16,2048]{2,1,0:T(8,128)(2,1)} %copy-done.6), calls=%async_computation | async-start | bytes 1048576 | tf_op jit(solution)/shard_map/all_to_all | solution.py:352
  82.0 1.2 %copy-start.5 = (bf16[2048,256]{1,0:T(8,128)(2,1)S(1)}, bf16[2048,256]{1,0:T(8,128)(2,1)}, u32[]{:S(2)}) copy-start(bf16[2048,256]{1,0:T(8,128)(2,1)} %copy-done.4) | copy-start | bytes 3145732
  83.2 0.8 copy-start.8
  84.0 0.8 copy-start.10
  84.7 24.8 %copy-start.3 = (f32[6144,128]{1,0:T(8,128)S(1)}, f32[6144,128]{1,0:T(8,128)}, u32[]{:S(2)}) copy-start(f32[6144,128]{1,0:T(8,128)} %copy-done.2) | copy-start | bytes 9437188
  90.7 25.8 %collective-permute-start.12 = (bf16[768,256]{1,0:T(8,128)(2,1)S(1)}, bf16[768,256]{1,0:T(8,128)(2,1)S(1)}, u32[]{:S(2)}, u32[]{:S(2)}) collective-permute-start(bf16[768,256]{1,0:T(8,128)(2,1)S(1)} %get-tuple-element.44), channel_id=1, source_target_pairs={{0,1},{1,2},{2,3},{3,0},{4,5},{5,6},{6,7},{7,4},{8,9},{9,10},{10,1... | collective-permute-start | bytes 1179656 | tf_op jit(solution)/shard_map/ppermute | solution.py:313
  97.3 19.3 %collective-permute-start.13 = (bf16[768,256]{1,0:T(8,128)(2,1)S(1)}, bf16[768,256]{1,0:T(8,128)(2,1)S(1)}, u32[]{:S(2)}, u32[]{:S(2)}) collective-permute-start(bf16[768,256]{1,0:T(8,128)(2,1)S(1)} %get-tuple-element.45), channel_id=1, source_target_pairs={{0,3},{1,0},{2,1},{3,2},{4,7},{5,4},{6,5},{7,6},{8,11},{9,8},{10,9... | collective-permute-start | bytes 1179656 | tf_op jit(solution)/shard_map/ppermute | solution.py:313
  99.0 17.6 %collective-permute-start.14 = (bf16[768,256]{1,0:T(8,128)(2,1)S(1)}, bf16[768,256]{1,0:T(8,128)(2,1)S(1)}, u32[]{:S(2)}, u32[]{:S(2)}) collective-permute-start(bf16[768,256]{1,0:T(8,128)(2,1)S(1)} %get-tuple-element.46), channel_id=1, source_target_pairs={{0,2},{1,3},{2,0},{3,1},{4,6},{5,7},{6,4},{7,5},{8,10},{9,11},{10,... | collective-permute-start | bytes 1179656 | tf_op jit(solution)/shard_map/ppermute | solution.py:313
  100.3 7.9 %collective-permute-start.15 = (bf16[16,1024]{1,0:T(8,128)(2,1)S(1)}, bf16[16,1024]{1,0:T(8,128)(2,1)S(1)}, u32[]{:S(2)}, u32[]{:S(2)}) collective-permute-start(bf16[16,1024]{1,0:T(8,128)(2,1)S(1)} %get-tuple-element.47), channel_id=1, source_target_pairs={{0,4},{4,8},{8,12},{12,16},{16,20},{20,24},{24,28},{28,32},{32,36}... | collective-permute-start | bytes 98312 | tf_op jit(solution)/shard_map/ppermute | solution.py:319
  102.2 7.3 %collective-permute-start.16 = (bf16[16,1024]{1,0:T(8,128)(2,1)S(1)}, bf16[16,1024]{1,0:T(8,128)(2,1)S(1)}, u32[]{:S(2)}, u32[]{:S(2)}) collective-permute-start(bf16[16,1024]{1,0:T(8,128)(2,1)S(1)} %get-tuple-element.48), channel_id=1, source_target_pairs={{4,0},{8,4},{12,8},{16,12},{20,16},{24,20},{28,24},{32,28},{36,32}... | collective-permute-start | bytes 98312 | tf_op jit(solution)/shard_map/ppermute | solution.py:319

commit v4 on v3

--- a/solution.py
+++ b/solution.py
@@ -37,7 +37,7 @@
     return lax.dot_general(lhs, rhs, dims, preferred_element_type=F32)
 
 
-def call(kernel, outs, specs, name, scratch=(), limit=16):
+def call(kernel, outs, specs, name, scratch=(), limit=24):
     return pl.pallas_call(
         kernel,
         out_shape=outs,
@@ -118,11 +118,11 @@
         [VMEM] * 5,
         "prep",
         [pltpu.VMEM((frames + 16, chans), F32)],
-        limit=16,
+        limit=24,
     )(feat, low, high, alpha, after)
 
 
-def weights_kernel(place, whole, own, p1, p2, p3, done, buf, rows, sem):
+def weights_kernel(place, whole, own, parts, done, buf, rows, sem):
     y, core = place[0], place[1]
     copies = [
         pltpu.make_async_copy(
@@ -132,24 +132,29 @@
     ]
     for c in copies:
         c.start()
-    for s, out in ((1, p1), (3, p3), (2, p2), (0, own)):
+    half = TAPS // 2
+    for s in (1, 3, 2, 0):
         copies[s].wait()
-        count = TAPS if s == 0 else TAPS // 2
+        to = lax.rem(y + s, 4)
         for h in range(2):
             lanes = slice(h * 128, h * 128 + 128)
             rows[...] = buf[s, :, :, lanes].astype(F32).reshape(128 * TAPS, 128)
-            for k in range(count):
-                tap = k if s == 0 else TAPS // 2 * core + k
-                out[k * 128 : (k + 1) * 128, lanes] = rows[
-                    pl.ds(tap, 128, stride=TAPS), :
+            for k in range(half):
+                parts[to, k * 128 : (k + 1) * 128, lanes] = rows[
+                    pl.ds(half * core + k, 128, stride=TAPS), :
                 ].astype(BF)
+            if s == 0:
+                for k in range(TAPS):
+                    own[k * 128 : (k + 1) * 128, lanes] = rows[
+                        pl.ds(k, 128, stride=TAPS), :
+                    ].astype(BF)
     done[...] = jnp.zeros(done.shape, F32)
 
 
 def weights(place, whole):
     return call(
         weights_kernel,
-        (shape((2048, 256)),) + (shape((1024, 256)),) * 3 + (TOKEN,),
+        (shape((2048, 256)), shape((4, 1024, 256)), TOKEN),
         [SMEM, HBM],
         "weights",
         [
@@ -157,7 +162,7 @@
             pltpu.VMEM((128 * TAPS, 128), F32),
             pltpu.SemaphoreType.DMA((4,)),
         ],
-        limit=14,
+        limit=24,
     )(place, whole)
 
 
@@ -187,7 +192,7 @@
         [SMEM] + [VMEM] * 5,
         "kernel_grad_send",
         [pltpu.VMEM((512, 768), BF)],
-        limit=12,
+        limit=24,
     )(place, taps, *gs)
 
 
@@ -210,17 +215,19 @@
         [SMEM] + [VMEM] * 6,
         "kernel_grad_keep",
         [pltpu.VMEM((512, 768), BF)],
-        limit=16,
+        limit=24,
     )(place, taps, *gs, got)
 
 
-def join_kernel(a1, a2, a3, after, o1, o2, o3):
-    for a, out in ((a1, o1), (a2, o2), (a3, o3)):
-        out[...] = a[...]
-
-
-def join(near, after):
-    return call(join_kernel, (shape((1024, 256)),) * 3, [VMEM] * 4, "join", limit=8)(*near, after)
+def join_kernel(y, parts, after, o1, o2, o3):
+    for d, out in ((1, o1), (2, o2), (3, o3)):
+        out[...] = parts[lax.rem(y[0] + d, 4)]
+
+
+def join(y, parts, after):
+    return call(join_kernel, (shape((1024, 256)),) * 3, [SMEM, VMEM, VMEM], "join", limit=24)(
+        y, parts, after
+    )
 
 
 def encode_kernel(
@@ -248,7 +255,7 @@
         + (shape((16, 1024)),) * 2,
         [SMEM] + [VMEM] * 10,
         "encode",
-        limit=20,
+        limit=24,
     )(core, taps, own, *edges, *near, *far)
 
 
@@ -262,7 +269,7 @@
 
 
 def lines(own, arrived):
-    return call(lines_kernel, (shape((8, 16, 2048)), TOKEN), [VMEM] * 4, "lines", limit=8)(
+    return call(lines_kernel, (shape((8, 16, 2048)), TOKEN), [VMEM] * 4, "lines", limit=24)(
         own, *arrived
     )
 
@@ -304,7 +311,7 @@
         [VMEM] * 9,
         "input_grad",
         [pltpu.VMEM((frames // STRIDE + 32, 1024), BF), pltpu.VMEM((frames + 16, chans), F32)],
-        limit=22,
+        limit=24,
     )(*gs, low, high, weights, factor, after)
 
 
@@ -331,8 +338,8 @@
     low, high = beside(features[-16:], 1), beside(features[:16], -1)
 
     at = jnp.stack([y, core])
-    own, p1, p2, p3, done = weights(at, down_weight)
-    near = (turn(p3, "chan", -1), turn(p2, "chan", 2), turn(p1, "chan", 1))
+    own, parts, done = weights(at, down_weight)
+    near = lax.all_to_all(parts, "chan", 0, 0)
     taps, factor = prep(features, low, high, snake_alpha.reshape(1, -1), done)
 
     place = jnp.stack([core] + [(y + d + 4 - x) % 4 for d in range(4)])
@@ -341,7 +348,7 @@
     keep0, keep1, keep2, keep3, done = keep(place, taps, gs, got)
     arrived = (turn(keep1, "x", 1), turn(keep3, "x", -1), turn(keep2, "x", 2))
 
-    held = join(near, done)
+    held = join(y.reshape(1), near, done)
     far = [turn(h, "core", 1) for h in held]
     mine, part1, part2, part3, full, first, last = encode(
         core.reshape(1), taps, own, (first, last), held, far

time: 122 us -> 123 us (level)
  Pallas kernels: 30.9 us -> 37.4 us
  starting transfers between devices: 46.4 us -> 41.4 us
    ppermute x16 -> x13, waiting for transfers between devices: 22.1 us -> 5.33 us  [turn(): lax.ppermute(value, axis, [(i, (i + by) % count) for i in range(count)])]
    all_to_all x0 -> x1, waiting for transfers between devices: none -> 16.4 us  [shards(): near = lax.all_to_all(parts, 'chan', 0, 0)]
    ppermute x16 -> x13, starting transfers between devices: 23.3 us -> 14.3 us  [turn(): lax.ppermute(value, axis, [(i, (i + by) % count) for i in range(count)])]
    all_to_all x0 -> x1, starting transfers between devices: none -> 4.44 us  [shards(): near = lax.all_to_all(parts, 'chan', 0, 0)]
    pallas_call x2, Pallas kernels: 4.55 us -> 6.58 us  [the longest x1 3.63 us: weights(): call(weights_kernel, (shape((2048, 256)), shape((4, 1024, 256)), TOKEN),...]
    pallas_call x1, Pallas kernels: 3.65 us -> 5.45 us  [keep(): call(keep_kernel, (shape((128, 2048), F32),) + (shape((128, 2048)),) * 3...]
    pallas_call x1, Pallas kernels: 0.22 us -> 1.58 us  [lines(): call(lines_kernel, (shape((8, 16, 2048)), TOKEN), [VMEM] * 4, 'lines', li...]
    pallas_call x1, Pallas kernels: 3.76 us -> 5.05 us  [send(): call(send_kernel, (shape((512, 2048)), shape((16, 1024)), shape((16, 1024...]
  transfers between devices with their start and end apart: 21 -> 19, of which waited for: 5 -> 4; matrix products, arithmetic and copies ran while one was open for 2% -> 1% of each run, Pallas kernels for 23% -> 27%
where the time goes in v4:
time: 123 us; the launch traced here: 121 us
  starting transfers between devices  41.4 us (34%)
  Pallas kernels  37.4 us (30%)
  waiting for transfers between devices  23.3 us (19%)
  local copies, waits for them, and re-layouts  15.5 us (13%)
  other arithmetic  2.16 us (2%)
    all_to_all x1, waiting for transfers between devices, shards(): near = lax.all_to_all(parts, 'chan', 0, 0)  16.4 us
    ppermute x4, starting transfers between devices, beside(): return lax.ppermute(value, TM, pairs)  15.9 us
    unnamed x33, local copies, waits for them, and re-layouts  14.7 us
    ppermute x13, starting transfers between devices, turn(): lax.ppermute(value, axis, [(i, (i + by) % count) for i in range(count)])  14.3 us
    pallas_call x1, Pallas kernels, input_grad(): call(input_grad_kernel, shape((frames, chans)), [VMEM] * 9, 'input_grad',...  6.96 us
    all_to_all x1, starting transfers between devices, shards(): spread = lax.all_to_all(summed, 'z', 0, 0)  6.69 us
    pallas_call x1, Pallas kernels, encode(): call(encode_kernel, (shape((768, 256), F32),) + (shape((768, 256)),) * 3...  5.99 us
    pallas_call x1, Pallas kernels, prep(): call(functools.partial(prep_kernel, step), (shape((frames // STRIDE, TAPS...  5.8 us
  transfers between devices with their start and end apart: 19, of which 4 were waited for; matrix products, arithmetic and copies ran while one was open for 1% of the time, Pallas kernels for 27%

profile of v4, /device:TPU:2, one launch (start us, length us, event | category | flops | bytes accessed | tf_op | source)
XLA Modules:
  0.0 120.5 jit_solution(11729537314362613756)
XLA Ops:
  0.6 3.1 %collective-permute-start.2 = (bf16[768,256]{1,0:T(8,128)(2,1)}, bf16[768,256]{1,0:T(8,128)(2,1)}, u32[]{:S(2)}, u32[]{:S(2)}) collective-permute-start(bf16[768,256]{1,0:T(8,128)(2,1)} %g0.5), channel_id=1, source_target_pairs={{0,3},{1,0},{2,1},{3,2},{4,7},{5,4},{6,5},{7,6},{8,11},{9,8},{10,9... | collective-permute-start | bytes 1179656 | tf_op jit(solution)/shard_map/ppermute | solution.py:320
  3.7 0.6 collective-permute-start.3
  4.4 1.0 collective-permute-start.4
  5.3 0.7 fusion.1
  6.0 1.9 %collective-permute-start = (bf16[16,128]{1,0:T(8,128)(2,1)S(1)}, bf16[16,128]{1,0:T(8,128)(2,1)S(1)}, u32[]{:S(2)}, u32[]{:S(2)}) collective-permute-start(bf16[16,128]{1,0:T(8,128)(2,1)S(1)} %get-tuple-element.54), channel_id=1, source_target_pairs={{0,4},{4,8},{8,12},{12,16},{16,20},{20,24},{24,28},{28,32},{32,36}... | collective-permute-start | bytes 12296 | tf_op jit(solution)/shard_map/ppermute | solution.py:326
  7.9 6.3 %collective-permute-start.1 = (bf16[16,128]{1,0:T(8,128)(2,1)S(1)}, bf16[16,128]{1,0:T(8,128)(2,1)S(1)}, u32[]{:S(2)}, u32[]{:S(2)}) collective-permute-start(bf16[16,128]{1,0:T(8,128)(2,1)S(1)} %get-tuple-element.53), channel_id=1, source_target_pairs={{4,0},{8,4},{12,8},{16,12},{20,16},{24,20},{28,24},{32,28},{36,32}... | collective-permute-start | bytes 12296 | tf_op jit(solution)/shard_map/ppermute | solution.py:326
  14.3 0.1 pad_add_fusion.place
  14.4 2.2 %copy-done = bf16[512,16,256]{2,1,0:T(8,128)(2,1)S(1)} copy-done((bf16[512,16,256]{2,1,0:T(8,128)(2,1)S(1)}, bf16[512,16,256]{2,1,0:T(8,128)(2,1)}, u32[]{:S(2)}) %copy-start) | copy-done | bytes 4194328
  16.6 3.6 %weights.1 = (bf16[2048,256]{1,0:T(8,128)(2,1)S(1)}, bf16[4,1024,256]{2,1,0:T(8,128)(2,1)S(1)}, f32[8,128]{1,0:T(8,128)S(1)}) custom-call(s32[2]{0:T(128)S(1)} %pad_add_fusion.place, bf16[512,16,256]{2,1,0:T(8,128)(2,1)S(1)} %copy-done), custom_call_target="tpu_custom_call" | custom-call | flops 460000000 | bytes 1000 | tf_op jit(solution)/shard_map/weights/pallas_call | solution.py:155
  20.2 1.4 %copy-done.4 = bf16[4,1024,256]{2,1,0:T(8,128)(2,1)} copy-done((bf16[4,1024,256]{2,1,0:T(8,128)(2,1)}, bf16[4,1024,256]{2,1,0:T(8,128)(2,1)S(1)}, u32[]{:S(2)}) %copy-start.4) | copy-done | bytes 2097176
  21.6 1.0 copy-done.7
  22.5 0.1 stack.29.place
  22.6 0.0 collective-permute-done.low
  22.6 0.0 collective-permute-done.1.high
  22.6 1.4 %copy-done.14 = bf16[6144,128]{1,0:T(8,128)(2,1)S(1)} copy-done((bf16[6144,128]{1,0:T(8,128)(2,1)S(1)}, bf16[6144,128]{1,0:T(8,128)(2,1)}, u32[]{:S(2)}) %copy-start.14) | copy-done | bytes 1572888
  24.1 0.7 copy-done.15
  24.7 5.8 %prep.1 = (bf16[768,2048]{1,0:T(8,128)(2,1)S(1)}, f32[6144,128]{1,0:T(8,128)S(1)}) custom-call(bf16[6144,128]{1,0:T(8,128)(2,1)S(1)} %copy-done.14, bf16[16,128]{1,0:T(8,128)(2,1)S(1)} %collective-permute-done.low, bf16[16,128]{1,0:T(8,128)(2,1)S(1)} %collective-permute-done.1.high, f32[1,128]{1,0:T(1,128)S(1)} %bitcast.10, f32[8,128]{1,0:T(8,128)S(1)} %get-tuple-element.28.after), custom_call_target="tpu_custom_call" | custom-call | flops 805000000 | bytes 1000 | tf_op jit(solution)/shard_map/prep/pallas_call | solution.py:115
  30.5 1.6 %copy-done.2 = f32[6144,128]{1,0:T(8,128)} copy-done((f32[6144,128]{1,0:T(8,128)}, f32[6144,128]{1,0:T(8,128)S(1)}, u32[]{:S(2)}) %copy-start.2) | copy-done | bytes 3145752
  32.2 0.0 collective-permute-done.2.g1
  32.2 0.0 collective-permute-done.3.g2
  32.2 0.0 collective-permute-done.4.g3
  32.2 5.1 %kernel_grad_send.1 = (bf16[512,2048]{1,0:T(8,128)(2,1)}, bf16[16,1024]{1,0:T(8,128)(2,1)S(1)}, bf16[16,1024]{1,0:T(8,128)(2,1)S(1)}) custom-call(s32[5]{0:T(128)S(1)} %stack.29.place, bf16[768,2048]{1,0:T(8,128)(2,1)S(1)} %get-tuple-element.29.taps, bf16[768,256]{1,0:T(8,128)(2,1)S(1)} %copy-done.1, bf16[768,256]{1,0:T(8,128)(2,1)} %collective-permute-done.2.g1, ...), custom_call_target="tpu_custom_call" | custom-call | flops 345000000 | bytes 1000 | tf_op jit(solution)/shard_map/kernel_grad_send/pallas_call | solution.py:189
  37.2 0.6 copy-done.10
  37.9 0.6 copy-done.12
  38.5 0.0 collective-permute-start.5
  38.5 4.4 %all-to-all-start = ((bf16[4,1024,256]{2,1,0:T(8,128)(2,1)}), bf16[4,1024,256]{2,1,0:T(8,128)(2,1)}, u32[]{:S(2)}, u32[]{:S(2)}) async-start(bf16[4,1024,256]{2,1,0:T(8,128)(2,1)} %copy-done.4), calls=%async_computation | async-start | bytes 4194304 | tf_op jit(solution)/shard_map/all_to_all | solution.py:342
  42.9 0.1 collective-permute-done.5.got
  43.0 5.5 %kernel_grad_keep.1 = (f32[128,2048]{1,0:T(8,128)S(1)}, bf16[128,2048]{1,0:T(8,128)(2,1)}, bf16[128,2048]{1,0:T(8,128)(2,1)}, bf16[128,2048]{1,0:T(8,128)(2,1)}, f32[8,128]{1,0:T(8,128)S(1)}) custom-call(s32[5]{0:T(128)S(1)} %stack.29.place, bf16[768,2048]{1,0:T(8,128)(2,1)S(1)} %get-tuple-element.29.taps, bf16[768,256]{1,0:T(8,128)(2,1)S(1)} %copy-done.1, ...), custom_call_target="tpu_custom_call" | custom-call | flops 460000000 | bytes 1000 | tf_op jit(solution)/shard_map/kernel_grad_keep/pallas_call | solution.py:212
  48.4 1.0 copy-done.5
  49.5 1.5 %collective-permute-start.14 = (bf16[128,2048]{1,0:T(8,128)(2,1)}, bf16[128,2048]{1,0:T(8,128)(2,1)}, u32[]{:S(2)}, u32[]{:S(2)}) collective-permute-start(bf16[128,2048]{1,0:T(8,128)(2,1)} %get-tuple-element.48), channel_id=1, source_target_pairs={{0,64},{64,128},{128,192},{192,0},{1,65},{65,129},{129,193},{193,1... | collective-permute-start | bytes 1572872 | tf_op jit(solution)/shard_map/ppermute | solution.py:320
  51.0 0.5 collective-permute-start.15
  51.5 2.4 %collective-permute-start.16 = (bf16[128,2048]{1,0:T(8,128)(2,1)}, bf16[128,2048]{1,0:T(8,128)(2,1)}, u32[]{:S(2)}, u32[]{:S(2)}) collective-permute-start(bf16[128,2048]{1,0:T(8,128)(2,1)} %get-tuple-element.50), channel_id=1, source_target_pairs={{0,128},{64,192},{128,0},{192,64},{1,129},{65,193},{129,1},{193,65... | collective-permute-start | bytes 1572872 | tf_op jit(solution)/shard_map/ppermute | solution.py:320
  53.9 16.4 %all-to-all-done.parts = bf16[4,1024,256]{2,1,0:T(8,128)(2,1)} async-done(((bf16[4,1024,256]{2,1,0:T(8,128)(2,1)}), bf16[4,1024,256]{2,1,0:T(8,128)(2,1)}, u32[]{:S(2)}, u32[]{:S(2)}) %all-to-all-start) | async-done | bytes 2097184 | tf_op jit(solution)/shard_map/all_to_all | solution.py:342
  70.3 2.9 %join.1 = (bf16[1024,256]{1,0:T(8,128)(2,1)}, bf16[1024,256]{1,0:T(8,128)(2,1)}, bf16[1024,256]{1,0:T(8,128)(2,1)}) custom-call(s32[1]{0:T(128)} %bitcast.2.y, bf16[4,1024,256]{2,1,0:T(8,128)(2,1)} %all-to-all-done.parts, f32[8,128]{1,0:T(8,128)S(1)} %get-tuple-element.35.after), custom_call_target="tpu_custom_call" | custom-call | flops 115000000 | bytes 1000 | tf_op jit(solution)/shard_map/join/pallas_call | solution.py:228
  73.2 0.0 collective-permute-start.6
  73.2 0.5 collective-permute-start.7
  73.7 0.0 collective-permute-done.14.a1
  73.7 0.0 collective-permute-start.8
  73.7 0.0 collective-permute-done.15.a2
  73.7 3.7 %collective-permute-done.16.a3 = bf16[128,2048]{1,0:T(8,128)(2,1)} collective-permute-done((bf16[128,2048]{1,0:T(8,128)(2,1)}, bf16[128,2048]{1,0:T(8,128)(2,1)}, u32[]{:S(2)}, u32[]{:S(2)}) %collective-permute-start.16) | collective-permute-done | bytes 524320 | tf_op jit(solution)/shard_map/ppermute | solution.py:320
  77.5 1.6 %lines.1 = (bf16[8,16,2048]{2,1,0:T(8,128)(2,1)S(1)}, f32[8,128]{1,0:T(8,128)S(1)}) custom-call(f32[128,2048]{1,0:T(8,128)S(1)} %copy-done.6, bf16[128,2048]{1,0:T(8,128)(2,1)} %collective-permute-done.14.a1, bf16[128,2048]{1,0:T(8,128)(2,1)} %collective-permute-done.15.a2, bf16[128,2048]{1,0:T(8,128)(2,1)} %collective-permute-done.16.a3), custom_call_target="tpu_custom_call" | custom-call | flops 115000000 | bytes 1000 | tf_op jit(solution)/shard_map/lines/pallas_call | solution.py:272
  79.1 0.8 copy-done.9
  79.9 6.7 %all-to-all-start.1 = ((bf16[8,16,2048]{2,1,0:T(8,128)(2,1)}), bf16[8,16,2048]{2,1,0:T(8,128)(2,1)}, u32[]{:S(2)}, u32[]{:S(2)}) async-start(bf16[8,16,2048]{2,1,0:T(8,128)(2,1)} %copy-done.9), calls=%async_computation.1 | async-start | bytes 1048576 | tf_op jit(solution)/shard_map/all_to_all | solution.py:359
  86.6 0.0 collective-permute-done.6.b1
  86.6 0.0 collective-permute-done.7.b2
  86.6 0.0 collective-permute-done.8.b3
  86.6 0.0 copy-start.8
  86.6 1.2 %copy-done.8 = bf16[2048,256]{1,0:T(8,128)(2,1)S(1)} copy-done((bf16[2048,256]{1,0:T(8,128)(2,1)S(1)}, bf16[2048,256]{1,0:T(8,128)(2,1)}, u32[]{:S(2)}) %copy-start.8) | copy-done | bytes 1048600
  87.8 0.8 copy-done.11
  88.6 0.8 copy-done.13
  89.3 6.0 %encode.1 = (f32[768,256]{1,0:T(8,128)S(1)}, bf16[768,256]{1,0:T(8,128)(2,1)S(1)}, bf16[768,256]{1,0:T(8,128)(2,1)S(1)}, bf16[768,256]{1,0:T(8,128)(2,1)S(1)}, b...) custom-call(s32[1]{0:T(128)} %bitcast.core, ...), custom_call_target="tpu_custom_call" | custom-call | flops 575000000 | bytes 1000 | tf_op jit(solution)/shard_map/encode/pallas_call | solution.py:250
  95.3 3.0 %collective-permute-start.10 = (bf16[768,256]{1,0:T(8,128)(2,1)S(1)}, bf16[768,256]{1,0:T(8,128)(2,1)S(1)}, u32[]{:S(2)}, u32[]{:S(2)}) collective-permute-start(bf16[768,256]{1,0:T(8,128)(2,1)S(1)} %get-tuple-element.41), channel_id=1, source_target_pairs={{0,3},{1,0},{2,1},{3,2},{4,7},{5,4},{6,5},{7,6},{8,11},{9,8},{10,9... | collective-permute-start | bytes 1179656 | tf_op jit(solution)/shard_map/ppermute | solution.py:320
  98.3 1.1 collective-permute-start.11
  99.4 0.6 collective-permute-start.9
  100.0 1.9 %collective-permute-start.12 = (bf16[16,1024]{1,0:T(8,128)(2,1)S(1)}, bf16[16,1024]{1,0:T(8,128)(2,1)S(1)}, u32[]{:S(2)}, u32[]{:S(2)}) collective-permute-start(bf16[16,1024]{1,0:T(8,128)(2,1)S(1)} %get-tuple-element.43), channel_id=1, source_target_pairs={{0,4},{4,8},{8,12},{12,16},{16,20},{20,24},{24,28},{28,32},{32,36}... | collective-permute-start | bytes 98312 | tf_op jit(solution)/shard_map/ppermute | solution.py:326
  101.9 5.8 %collective-permute-start.13 = (bf16[16,1024]{1,0:T(8,128)(2,1)S(1)}, bf16[16,1024]{1,0:T(8,128)(2,1)S(1)}, u32[]{:S(2)}, u32[]{:S(2)}) collective-permute-start(bf16[16,1024]{1,0:T(8,128)(2,1)S(1)} %get-tuple-element.44), channel_id=1, source_target_pairs={{4,0},{8,4},{12,8},{16,12},{20,16},{24,20},{28,24},{32,28},{36,32}... | collective-permute-start | bytes 98312 | tf_op jit(solution)/shard_map/ppermute | solution.py:326
  107.7 1.6 %collective-permute-done.13.high = bf16[16,1024]{1,0:T(8,128)(2,1)S(1)} collective-permute-done((bf16[16,1024]{1,0:T(8,128)(2,1)S(1)}, bf16[16,1024]{1,0:T(8,128)(2,1)S(1)}, u32[]{:S(2)}, u32[]{:S(2)}) %collective-permute-start.13) | collective-permute-done | bytes 32800 | tf_op jit(solution)/shard_map/ppermute | solution.py:326
  109.3 7.0 %input_grad.1 = bf16[6144,128]{1,0:T(8,128)(2,1)} custom-call(bf16[768,256]{1,0:T(8,128)(2,1)S(1)} %copy-done.1, bf16[768,256]{1,0:T(8,128)(2,1)} %collective-permute-done.2.g1, bf16[768,256]{1,0:T(8,128)(2,1)} %collective-permute-done.3.g2, bf16[768,256]{1,0:T(8,128)(2,1)} %collective-permute-done.4.g3, bf16[16,1024]{1,0:T(8,128)(2,1)S(1)} %collective-permute-done.12.low, ...), custom_call_target="tpu_custom_call" | custom-call | flops 690000000 | bytes 1000 | tf_op jit(solution)/shard_map/input_grad/pallas_call | solution.py:308
  116.2 0.0 collective-permute-done.10
  116.2 1.5 %collective-permute-done.9 = bf16[768,256]{1,0:T(8,128)(2,1)S(1)} collective-permute-done((bf16[768,256]{1,0:T(8,128)(2,1)S(1)}, bf16[768,256]{1,0:T(8,128)(2,1)S(1)}, u32[]{:S(2)}, u32[]{:S(2)}) %collective-permute-start.9) | collective-permute-done | bytes 393248 | tf_op jit(solution)/shard_map/ppermute | solution.py:320
  117.8 0.9 add_convert_fusion
  118.7 0.0 all-to-all-done.1
  118.7 1.1 convert_reduce_fusion
  119.9 0.6 copy.7
  (21 shorter events, 0.1 us)
Async XLA Ops:
  0.6 31.5 %collective-permute-start.2 = (bf16[768,256]{1,0:T(8,128)(2,1)}, bf16[768,256]{1,0:T(8,128)(2,1)}, u32[]{:S(2)}, u32[]{:S(2)}) collective-permute-start(bf16[768,256]{1,0:T(8,128)(2,1)} %g0.5), channel_id=1, source_target_pairs={{0,3},{1,0},{2,1},{3,2},{4,7},{5,4},{6,5},{7,6},{8,11},{9,8},{10,9... | collective-permute-start | bytes 1179656 | tf_op jit(solution)/shard_map/ppermute | solution.py:320
  3.7 28.5 %collective-permute-start.3 = (bf16[768,256]{1,0:T(8,128)(2,1)}, bf16[768,256]{1,0:T(8,128)(2,1)}, u32[]{:S(2)}, u32[]{:S(2)}) collective-permute-start(bf16[768,256]{1,0:T(8,128)(2,1)} %g0.5), channel_id=1, source_target_pairs={{0,2},{1,3},{2,0},{3,1},{4,6},{5,7},{6,4},{7,5},{8,10},{9,11},{10,... | collective-permute-start | bytes 1179656 | tf_op jit(solution)/shard_map/ppermute | solution.py:320
  4.4 27.8 %collective-permute-start.4 = (bf16[768,256]{1,0:T(8,128)(2,1)}, bf16[768,256]{1,0:T(8,128)(2,1)}, u32[]{:S(2)}, u32[]{:S(2)}) collective-permute-start(bf16[768,256]{1,0:T(8,128)(2,1)} %g0.5), channel_id=1, source_target_pairs={{0,1},{1,2},{2,3},{3,0},{4,5},{5,6},{6,7},{7,4},{8,9},{9,10},{10,1... | collective-permute-start | bytes 1179656 | tf_op jit(solution)/shard_map/ppermute | solution.py:320
  6.0 16.6 %collective-permute-start = (bf16[16,128]{1,0:T(8,128)(2,1)S(1)}, bf16[16,128]{1,0:T(8,128)(2,1)S(1)}, u32[]{:S(2)}, u32[]{:S(2)}) collective-permute-start(bf16[16,128]{1,0:T(8,128)(2,1)S(1)} %get-tuple-element.54), channel_id=1, source_target_pairs={{0,4},{4,8},{8,12},{12,16},{16,20},{20,24},{24,28},{28,32},{32,36}... | collective-permute-start | bytes 12296 | tf_op jit(solution)/shard_map/ppermute | solution.py:326
  7.9 14.7 %collective-permute-start.1 = (bf16[16,128]{1,0:T(8,128)(2,1)S(1)}, bf16[16,128]{1,0:T(8,128)(2,1)S(1)}, u32[]{:S(2)}, u32[]{:S(2)}) collective-permute-start(bf16[16,128]{1,0:T(8,128)(2,1)S(1)} %get-tuple-element.53), channel_id=1, source_target_pairs={{4,0},{8,4},{12,8},{16,12},{20,16},{24,20},{28,24},{32,28},{36,32}... | collective-permute-start | bytes 12296 | tf_op jit(solution)/shard_map/ppermute | solution.py:326
  14.4 2.2 %copy-start = (bf16[512,16,256]{2,1,0:T(8,128)(2,1)S(1)}, bf16[512,16,256]{2,1,0:T(8,128)(2,1)}, u32[]{:S(2)}) copy-start(bf16[512,16,256]{2,1,0:T(8,128)(2,1)} %whole.1) | copy-start | bytes 12582916
  20.2 1.4 %copy-start.4 = (bf16[4,1024,256]{2,1,0:T(8,128)(2,1)}, bf16[4,1024,256]{2,1,0:T(8,128)(2,1)S(1)}, u32[]{:S(2)}) copy-start(bf16[4,1024,256]{2,1,0:T(8,128)(2,1)S(1)} %get-tuple-element.33) | copy-start | bytes 6291460
  21.6 1.0 copy-start.7
  22.5 9.7 %copy-start.1 = (bf16[768,256]{1,0:T(8,128)(2,1)S(1)}, bf16[768,256]{1,0:T(8,128)(2,1)}, u32[]{:S(2)}) copy-start(bf16[768,256]{1,0:T(8,128)(2,1)} %g0.5) | copy-start | bytes 1179652
  22.6 1.4 %copy-start.14 = (bf16[6144,128]{1,0:T(8,128)(2,1)S(1)}, bf16[6144,128]{1,0:T(8,128)(2,1)}, u32[]{:S(2)}) copy-start(bf16[6144,128]{1,0:T(8,128)(2,1)} %feat.1) | copy-start | bytes 4718596
  24.1 0.7 copy-start.15
  30.5 1.6 %copy-start.2 = (f32[6144,128]{1,0:T(8,128)}, f32[6144,128]{1,0:T(8,128)S(1)}, u32[]{:S(2)}) copy-start(f32[6144,128]{1,0:T(8,128)S(1)} %get-tuple-element.46.factor) | copy-start | bytes 9437188
  37.2 0.6 copy-start.10
  37.9 0.6 copy-start.12
  38.5 4.5 %collective-permute-start.5 = (bf16[512,2048]{1,0:T(8,128)(2,1)}, bf16[512,2048]{1,0:T(8,128)(2,1)}, u32[]{:S(2)}, u32[]{:S(2)}) collective-permute-start(bf16[512,2048]{1,0:T(8,128)(2,1)} %get-tuple-element.34), channel_id=1, source_target_pairs={{0,4},{4,0},{1,5},{5,1},{2,6},{6,2},{3,7},{7,3},{8,12},{12,8},{9,1... | collective-permute-start | bytes 6291464 | tf_op jit(solution)/shard_map/ppermute | solution.py:320
  38.5 31.8 %all-to-all-start = ((bf16[4,1024,256]{2,1,0:T(8,128)(2,1)}), bf16[4,1024,256]{2,1,0:T(8,128)(2,1)}, u32[]{:S(2)}, u32[]{:S(2)}) async-start(bf16[4,1024,256]{2,1,0:T(8,128)(2,1)} %copy-done.4), calls=%async_computation | async-start | bytes 4194304 | tf_op jit(solution)/shard_map/all_to_all | solution.py:342
  48.4 1.0 copy-start.5
  49.5 24.3 %collective-permute-start.14 = (bf16[128,2048]{1,0:T(8,128)(2,1)}, bf16[128,2048]{1,0:T(8,128)(2,1)}, u32[]{:S(2)}, u32[]{:S(2)}) collective-permute-start(bf16[128,2048]{1,0:T(8,128)(2,1)} %get-tuple-element.48), channel_id=1, source_target_pairs={{0,64},{64,128},{128,192},{192,0},{1,65},{65,129},{129,193},{193,1... | collective-permute-start | bytes 1572872 | tf_op jit(solution)/shard_map/ppermute | solution.py:320
  51.0 22.8 %collective-permute-start.15 = (bf16[128,2048]{1,0:T(8,128)(2,1)}, bf16[128,2048]{1,0:T(8,128)(2,1)}, u32[]{:S(2)}, u32[]{:S(2)}) collective-permute-start(bf16[128,2048]{1,0:T(8,128)(2,1)} %get-tuple-element.49), channel_id=1, source_target_pairs={{0,192},{64,0},{128,64},{192,128},{1,193},{65,1},{129,65},{193,129... | collective-permute-start | bytes 1572872 | tf_op jit(solution)/shard_map/ppermute | solution.py:320
  51.5 26.0 %collective-permute-start.16 = (bf16[128,2048]{1,0:T(8,128)(2,1)}, bf16[128,2048]{1,0:T(8,128)(2,1)}, u32[]{:S(2)}, u32[]{:S(2)}) collective-permute-start(bf16[128,2048]{1,0:T(8,128)(2,1)} %get-tuple-element.50), channel_id=1, source_target_pairs={{0,128},{64,192},{128,0},{192,64},{1,129},{65,193},{129,1},{193,65... | collective-permute-start | bytes 1572872 | tf_op jit(solution)/shard_map/ppermute | solution.py:320
  70.3 7.2 %copy-start.6 = (f32[128,2048]{1,0:T(8,128)S(1)}, f32[128,2048]{1,0:T(8,128)}, u32[]{:S(2)}) copy-start(f32[128,2048]{1,0:T(8,128)} %copy-done.5) | copy-start | bytes 3145732
  73.2 13.3 %collective-permute-start.6 = (bf16[1024,256]{1,0:T(8,128)(2,1)}, bf16[1024,256]{1,0:T(8,128)(2,1)}, u32[]{:S(2)}, u32[]{:S(2)}) collective-permute-start(bf16[1024,256]{1,0:T(8,128)(2,1)} %get-tuple-element.36.a1), channel_id=1, source_target_pairs={{0,4},{4,0},{1,5},{5,1},{2,6},{6,2},{3,7},{7,3},{8,12},{12,8},{9,1... | collective-permute-start | bytes 1572872 | tf_op jit(solution)/shard_map/ppermute | solution.py:320
  73.2 13.3 %collective-permute-start.7 = (bf16[1024,256]{1,0:T(8,128)(2,1)}, bf16[1024,256]{1,0:T(8,128)(2,1)}, u32[]{:S(2)}, u32[]{:S(2)}) collective-permute-start(bf16[1024,256]{1,0:T(8,128)(2,1)} %get-tuple-element.37.a2), channel_id=1, source_target_pairs={{0,4},{4,0},{1,5},{5,1},{2,6},{6,2},{3,7},{7,3},{8,12},{12,8},{9,1... | collective-permute-start | bytes 1572872 | tf_op jit(solution)/shard_map/ppermute | solution.py:320
  73.7 12.8 %collective-permute-start.8 = (bf16[1024,256]{1,0:T(8,128)(2,1)}, bf16[1024,256]{1,0:T(8,128)(2,1)}, u32[]{:S(2)}, u32[]{:S(2)}) collective-permute-start(bf16[1024,256]{1,0:T(8,128)(2,1)} %get-tuple-element.38.a3), channel_id=1, source_target_pairs={{0,4},{4,0},{1,5},{5,1},{2,6},{6,2},{3,7},{7,3},{8,12},{12,8},{9,1... | collective-permute-start | bytes 1572872 | tf_op jit(solution)/shard_map/ppermute | solution.py:320
  79.0 0.8 copy-start.9
  79.9 38.9 %all-to-all-start.1 = ((bf16[8,16,2048]{2,1,0:T(8,128)(2,1)}), bf16[8,16,2048]{2,1,0:T(8,128)(2,1)}, u32[]{:S(2)}, u32[]{:S(2)}) async-start(bf16[8,16,2048]{2,1,0:T(8,128)(2,1)} %copy-done.9), calls=%async_computation.1 | async-start | bytes 1048576 | tf_op jit(solution)/shard_map/all_to_all | solution.py:359
  86.6 1.2 %copy-start.8 = (bf16[2048,256]{1,0:T(8,128)(2,1)S(1)}, bf16[2048,256]{1,0:T(8,128)(2,1)}, u32[]{:S(2)}) copy-start(bf16[2048,256]{1,0:T(8,128)(2,1)} %copy-done.7) | copy-start | bytes 3145732
  87.8 0.8 copy-start.11
  88.6 0.8 copy-start.13
  89.3 20.0 %copy-start.3 = (f32[6144,128]{1,0:T(8,128)S(1)}, f32[6144,128]{1,0:T(8,128)}, u32[]{:S(2)}) copy-start(f32[6144,128]{1,0:T(8,128)} %copy-done.2) | copy-start | bytes 9437188
  95.3 20.9 %collective-permute-start.10 = (bf16[768,256]{1,0:T(8,128)(2,1)S(1)}, bf16[768,256]{1,0:T(8,128)(2,1)S(1)}, u32[]{:S(2)}, u32[]{:S(2)}) collective-permute-start(bf16[768,256]{1,0:T(8,128)(2,1)S(1)} %get-tuple-element.41), channel_id=1, source_target_pairs={{0,3},{1,0},{2,1},{3,2},{4,7},{5,4},{6,5},{7,6},{8,11},{9,8},{10,9... | collective-permute-start | bytes 1179656 | tf_op jit(solution)/shard_map/ppermute | solution.py:320
  98.3 17.9 %collective-permute-start.11 = (bf16[768,256]{1,0:T(8,128)(2,1)S(1)}, bf16[768,256]{1,0:T(8,128)(2,1)S(1)}, u32[]{:S(2)}, u32[]{:S(2)}) collective-permute-start(bf16[768,256]{1,0:T(8,128)(2,1)S(1)} %get-tuple-element.42), channel_id=1, source_target_pairs={{0,2},{1,3},{2,0},{3,1},{4,6},{5,7},{6,4},{7,5},{8,10},{9,11},{10,... | collective-permute-start | bytes 1179656 | tf_op jit(solution)/shard_map/ppermute | solution.py:320
  99.4 18.4 %collective-permute-start.9 = (bf16[768,256]{1,0:T(8,128)(2,1)S(1)}, bf16[768,256]{1,0:T(8,128)(2,1)S(1)}, u32[]{:S(2)}, u32[]{:S(2)}) collective-permute-start(bf16[768,256]{1,0:T(8,128)(2,1)S(1)} %get-tuple-element.40), channel_id=1, source_target_pairs={{0,1},{1,2},{2,3},{3,0},{4,5},{5,6},{6,7},{7,4},{8,9},{9,10},{10,1... | collective-permute-start | bytes 1179656 | tf_op jit(solution)/shard_map/ppermute | solution.py:320
  100.0 7.7 %collective-permute-start.12 = (bf16[16,1024]{1,0:T(8,128)(2,1)S(1)}, bf16[16,1024]{1,0:T(8,128)(2,1)S(1)}, u32[]{:S(2)}, u32[]{:S(2)}) collective-permute-start(bf16[16,1024]{1,0:T(8,128)(2,1)S(1)} %get-tuple-element.43), channel_id=1, source_target_pairs={{0,4},{4,8},{8,12},{12,16},{16,20},{20,24},{24,28},{28,32},{32,36}... | collective-permute-start | bytes 98312 | tf_op jit(solution)/shard_map/ppermute | solution.py:326
  101.9 7.3 %collective-permute-start.13 = (bf16[16,1024]{1,0:T(8,128)(2,1)S(1)}, bf16[16,1024]{1,0:T(8,128)(2,1)S(1)}, u32[]{:S(2)}, u32[]{:S(2)}) collective-permute-start(bf16[16,1024]{1,0:T(8,128)(2,1)S(1)} %get-tuple-element.44), channel_id=1, source_target_pairs={{4,0},{8,4},{12,8},{16,12},{20,16},{24,20},{28,24},{32,28},{36,32}... | collective-permute-start | bytes 98312 | tf_op jit(solution)/shard_map/ppermute | solution.py:326

commit v5 on v3

--- a/solution.py
+++ b/solution.py
@@ -37,7 +37,7 @@
     return lax.dot_general(lhs, rhs, dims, preferred_element_type=F32)
 
 
-def call(kernel, outs, specs, name, scratch=(), limit=16):
+def call(kernel, outs, specs, name, scratch=(), limit=24):
     return pl.pallas_call(
         kernel,
         out_shape=outs,
@@ -57,13 +57,14 @@
 TOKEN = shape((8, 128), F32)
 
 
-FACTOR = 0.1
+FACTOR = 1.3
 TIME = dict(
     prep=7,
     weights=4,
     kernel_grad_send=3,
     kernel_grad_keep=4,
     join=1,
+    total=1,
     encode=5,
     lines=1,
     input_grad=6,
@@ -118,7 +119,7 @@
         [VMEM] * 5,
         "prep",
         [pltpu.VMEM((frames + 16, chans), F32)],
-        limit=16,
+        limit=24,
     )(feat, low, high, alpha, after)
 
 
@@ -157,7 +158,7 @@
             pltpu.VMEM((128 * TAPS, 128), F32),
             pltpu.SemaphoreType.DMA((4,)),
         ],
-        limit=14,
+        limit=24,
     )(place, whole)
 
 
@@ -171,46 +172,41 @@
         lhs[pl.ds(at, 128), :] = mul(pick, g[...], NT).astype(BF)
 
 
-def send_kernel(place, taps, g0, g1, g2, g3, out, first, last, lhs):
+def send_kernel(place, taps, g0, g1, g2, g3, out, lhs):
     choose((g0, g1, g2, g3), 1 - place[0], [place[1 + d] for d in range(4)], lhs)
     for n in range(0, 2048, 256):
         out[:, n : n + 256] = mul(lhs[...], taps[:, n : n + 256]).astype(BF)
-    for d, g in enumerate((g0, g1, g2, g3)):
-        first[:, d * 256 : (d + 1) * 256] = g[0:16, :]
-        last[:, d * 256 : (d + 1) * 256] = g[752:768, :]
 
 
 def send(place, taps, gs):
     return call(
         send_kernel,
-        (shape((512, 2048)), shape((16, 1024)), shape((16, 1024))),
+        shape((512, 2048)),
         [SMEM] + [VMEM] * 5,
         "kernel_grad_send",
         [pltpu.VMEM((512, 768), BF)],
-        limit=12,
+        limit=24,
     )(place, taps, *gs)
 
 
-def keep_kernel(place, taps, g0, g1, g2, g3, got, o0, o1, o2, o3, done, lhs):
+def keep_kernel(place, taps, g0, g1, g2, g3, got, out, done, lhs):
     choose((g0, g1, g2, g3), place[0], [place[1 + d] for d in range(4)], lhs)
     for n in range(0, 2048, 256):
         cols = slice(n, n + 256)
         both = mul(lhs[...], taps[:, cols]) + got[:, cols].astype(F32)
-        o0[:, cols] = both[0:128]
-        o1[:, cols] = both[128:256].astype(BF)
-        o2[:, cols] = both[256:384].astype(BF)
-        o3[:, cols] = both[384:512].astype(BF)
+        for to in range(4):
+            out[to, :, cols] = both[to * 128 : (to + 1) * 128].astype(BF)
     done[...] = jnp.zeros(done.shape, F32)
 
 
 def keep(place, taps, gs, got):
     return call(
         keep_kernel,
-        (shape((128, 2048), F32),) + (shape((128, 2048)),) * 3 + (TOKEN,),
+        (shape((4, 128, 2048)), TOKEN),
         [SMEM] + [VMEM] * 6,
         "kernel_grad_keep",
         [pltpu.VMEM((512, 768), BF)],
-        limit=16,
+        limit=24,
     )(place, taps, *gs, got)
 
 
@@ -220,11 +216,11 @@
 
 
 def join(near, after):
-    return call(join_kernel, (shape((1024, 256)),) * 3, [VMEM] * 4, "join", limit=8)(*near, after)
+    return call(join_kernel, (shape((1024, 256)),) * 3, [VMEM] * 4, "join", limit=24)(*near, after)
 
 
 def encode_kernel(
-    core, taps, own, first, last, a1, a2, a3, b1, b2, b3, o0, o1, o2, o3, full, o_first, o_last
+    core, taps, own, g0, g1, g2, g3, a1, a2, a3, b1, b2, b3, o0, o1, o2, o3, full, o_first, o_last, done
 ):
     here = pl.multiple_of(core[0] * 1024, 1024)
     there = pl.multiple_of(1024 - core[0] * 1024, 1024)
@@ -235,39 +231,40 @@
         full[pl.ds(there, 1024), cols] = b[...]
     for d, out in enumerate((o0, o1, o2, o3)):
         out[...] = mul(taps[...], full[:, d * 256 : (d + 1) * 256]).astype(out.dtype)
-    o_first[...] = first[...]
-    o_last[...] = last[...]
-
-
-def encode(core, taps, own, edges, near, far):
+    for d, g in enumerate((g0, g1, g2, g3)):
+        o_first[:, d * 256 : (d + 1) * 256] = g[0:16, :]
+        o_last[:, d * 256 : (d + 1) * 256] = g[752:768, :]
+    done[...] = jnp.zeros(done.shape, F32)
+
+
+def encode(core, taps, own, gs, near, far):
     return call(
         encode_kernel,
         (shape((768, 256), F32),)
         + (shape((768, 256)),) * 3
         + (shape((2048, 1024)),)
-        + (shape((16, 1024)),) * 2,
-        [SMEM] + [VMEM] * 10,
+        + (shape((16, 1024)),) * 2
+        + (TOKEN,),
+        [SMEM] + [VMEM] * 12,
         "encode",
-        limit=20,
-    )(core, taps, own, *edges, *near, *far)
-
-
-def lines_kernel(own, a1, a2, a3, out, done):
+        limit=24,
+    )(core, taps, own, *gs, *near, *far)
+
+
+def lines_kernel(parts, after, out, done):
     for m in range(8):
         here = slice(m * 16, m * 16 + 16)
-        out[m] = (
-            own[here, :] + a1[here, :].astype(F32) + a2[here, :].astype(F32) + a3[here, :].astype(F32)
-        ).astype(BF)
-    done[...] = jnp.zeros(done.shape, F32)
-
-
-def lines(own, arrived):
-    return call(lines_kernel, (shape((8, 16, 2048)), TOKEN), [VMEM] * 4, "lines", limit=8)(
-        own, *arrived
-    )
-
-
-def input_grad_kernel(g0, g1, g2, g3, low, high, weights, factor, after, out, full, rows):
+        out[m] = sum(parts[n, here, :].astype(F32) for n in range(4)).astype(BF)
+    done[...] = jnp.zeros(done.shape, F32)
+
+
+def lines(parts, after):
+    return call(lines_kernel, (shape((8, 16, 2048)), TOKEN), [VMEM] * 2, "lines", limit=24)(
+        parts, after
+    )
+
+
+def input_grad_kernel(g0, g1, g2, g3, low, high, weights, factor, after, out, done, full, rows):
     outs = g0.shape[0]
     frames = out.shape[0]
     for d, g in enumerate((g0, g1, g2, g3)):
@@ -294,18 +291,31 @@
         out[at : at + step, :] = (
             rows[at + 8 : at + 8 + step, :] * factor[at : at + step, :]
         ).astype(BF)
+    done[...] = jnp.zeros(done.shape, F32)
 
 
 def input_grad(gs, low, high, weights, factor, after):
     frames, chans = factor.shape
     return call(
         input_grad_kernel,
-        shape((frames, chans)),
+        (shape((frames, chans)), TOKEN),
         [VMEM] * 9,
         "input_grad",
         [pltpu.VMEM((frames // STRIDE + 32, 1024), BF), pltpu.VMEM((frames + 16, chans), F32)],
-        limit=22,
+        limit=24,
     )(*gs, low, high, weights, factor, after)
+
+
+def total_kernel(own, a1, a2, a3, after, out):
+    out[...] = (
+        own[...] + a1[...].astype(F32) + a2[...].astype(F32) + a3[...].astype(F32)
+    ).astype(BF)
+
+
+def total(own, others, after):
+    return call(total_kernel, shape((768, 256)), [VMEM] * 5, "total", limit=24)(
+        own, *others, after
+    )
 
 
 def turn(value, axis, by):
@@ -335,28 +345,28 @@
     near = (turn(p3, "chan", -1), turn(p2, "chan", 2), turn(p1, "chan", 1))
     taps, factor = prep(features, low, high, snake_alpha.reshape(1, -1), done)
 
-    place = jnp.stack([core] + [(y + d + 4 - x) % 4 for d in range(4)])
-    out, first, last = send(place, taps, gs)
+    place = jnp.stack([core] + [(y + d) % 4 for d in range(4)])
+    out = send(place, taps, gs)
     got = turn(out, "core", 1)
-    keep0, keep1, keep2, keep3, done = keep(place, taps, gs, got)
-    arrived = (turn(keep1, "x", 1), turn(keep3, "x", -1), turn(keep2, "x", 2))
+    kept, done = keep(place, taps, gs, got)
+    arrived = lax.all_to_all(kept, "x", 0, 0)
 
     held = join(near, done)
     far = [turn(h, "core", 1) for h in held]
-    mine, part1, part2, part3, full, first, last = encode(
-        core.reshape(1), taps, own, (first, last), held, far
+    mine, part1, part2, part3, full, first, last, done = encode(
+        core.reshape(1), taps, own, gs, held, far
     )
     others = (turn(part1, "chan", 1), turn(part3, "chan", -1), turn(part2, "chan", 2))
     edges = beside(last, 1), beside(first, -1)
-    summed, done = lines(keep0, arrived)
+    summed, done = lines(arrived, done)
     spread = lax.all_to_all(summed, "z", 0, 0)
-    grad_features = input_grad(gs, *edges, full, factor, done)
-
-    encoded = (mine + sum(o.astype(F32) for o in others)).astype(BF)
+    grad_features, done = input_grad(gs, *edges, full, factor, done)
+
+    encoded = total(mine, others, done)
 
     scale = 1.0 / math.sqrt(features.shape[0] // STRIDE * 64)
-    total = jnp.sum(spread.astype(F32), axis=0) * scale
-    grad_down = total.astype(BF).reshape(16, 16, 128)
+    down = jnp.sum(spread.astype(F32), axis=0) * scale
+    grad_down = down.astype(BF).reshape(16, 16, 128)
     return (encoded, grad_features, grad_down)
 
 

time: 122 us -> 109 us (0.89); the launches traced: 119 us -> 108 us
  starting transfers between devices: 46.4 us -> 38.1 us
  Pallas kernels: 30.9 us -> 34.3 us
  waiting for transfers between devices: 23.5 us -> 20.1 us
  other arithmetic: 2.17 us -> 0.16 us
    ppermute x16 -> x13, starting transfers between devices: 23.3 us -> 13.4 us  [turn(): lax.ppermute(value, axis, [(i, (i + by) % count) for i in range(count)])]
    all_to_all x0 -> x1, starting transfers between devices: none -> 4.86 us  [shards(): arrived = lax.all_to_all(kept, 'x', 0, 0)]
    ppermute x16 -> x13, waiting for transfers between devices: 22.1 us -> 17.4 us  [turn(): lax.ppermute(value, axis, [(i, (i + by) % count) for i in range(count)])]
    pallas_call x5 -> x6, Pallas kernels: 15.9 us -> 19.4 us  [the longest x1 6.9 us: input_grad(): call(input_grad_kernel, (shape((frames, chans)), TOKEN), [VMEM] * 9, 'inp...]
    all_to_all x1, starting transfers between devices: 6.99 us -> 3.94 us  [shards(): spread = lax.all_to_all(summed, 'z', 0, 0)]
    all_to_all x1, waiting for transfers between devices: 0.01 us -> 2.64 us  [shards(): spread = lax.all_to_all(summed, 'z', 0, 0)]
    ppermute x4, waiting for transfers between devices: 1.35 us -> 0.01 us  [beside(): return lax.ppermute(value, TM, pairs)]
    unnamed x39 -> x35, local copies, waits for them, and re-layouts: 14.7 us -> 13.8 us
  transfers between devices with their start and end apart: 21 -> 19, of which waited for: 5 -> 8; matrix products, arithmetic and copies ran while one was open for 2% -> 1% of each run, Pallas kernels for 23% -> 28%
where the time goes in v5:
time: 109 us; the launch traced here: 108 us
  starting transfers between devices  38.1 us (35%)
  Pallas kernels  34.3 us (31%)
  waiting for transfers between devices  20.1 us (18%)
  local copies, waits for them, and re-layouts  14.6 us (13%)
    ppermute x13, waiting for transfers between devices, turn(): lax.ppermute(value, axis, [(i, (i + by) % count) for i in range(count)])  17.4 us
    ppermute x4, starting transfers between devices, beside(): return lax.ppermute(value, TM, pairs)  15.9 us
    unnamed x35, local copies, waits for them, and re-layouts  13.8 us
    ppermute x13, starting transfers between devices, turn(): lax.ppermute(value, axis, [(i, (i + by) % count) for i in range(count)])  13.4 us
    pallas_call x1, Pallas kernels, input_grad(): call(input_grad_kernel, (shape((frames, chans)), TOKEN), [VMEM] * 9, 'inp...  6.9 us
    pallas_call x1, Pallas kernels, encode(): call(encode_kernel, (shape((768, 256), F32),) + (shape((768, 256)),) * 3...  5.88 us
    pallas_call x1, Pallas kernels, prep(): call(functools.partial(prep_kernel, step), (shape((frames // STRIDE, TAPS...  5.8 us
    all_to_all x1, starting transfers between devices, shards(): arrived = lax.all_to_all(kept, 'x', 0, 0)  4.86 us
  transfers between devices with their start and end apart: 19, of which 8 were waited for; matrix products, arithmetic and copies ran while one was open for 1% of the time, Pallas kernels for 28%

profile of v5, /device:TPU:2, one launch (start us, length us, event | category | flops | bytes accessed | tf_op | source)
XLA Modules:
  0.0 108.0 jit_solution(9928537762621411836)
XLA Ops:
  0.6 1.7 %collective-permute-start.4 = (bf16[768,256]{1,0:T(8,128)(2,1)}, bf16[768,256]{1,0:T(8,128)(2,1)S(1)}, u32[]{:S(2)}, u32[]{:S(2)}) collective-permute-start(bf16[768,256]{1,0:T(8,128)(2,1)} %g0.7), channel_id=1, source_target_pairs={{0,1},{1,2},{2,3},{3,0},{4,5},{5,6},{6,7},{7,4},{8,9},{9,10},{10,1... | collective-permute-start | bytes 1179656 | tf_op jit(solution)/shard_map/ppermute | solution.py:323
  2.3 2.9 %collective-permute-start.3 = (bf16[768,256]{1,0:T(8,128)(2,1)}, bf16[768,256]{1,0:T(8,128)(2,1)}, u32[]{:S(2)}, u32[]{:S(2)}) collective-permute-start(bf16[768,256]{1,0:T(8,128)(2,1)} %g0.7), channel_id=1, source_target_pairs={{0,2},{1,3},{2,0},{3,1},{4,6},{5,7},{6,4},{7,5},{8,10},{9,11},{10,... | collective-permute-start | bytes 1179656 | tf_op jit(solution)/shard_map/ppermute | solution.py:323
  5.2 1.3 %collective-permute-start.2 = (bf16[768,256]{1,0:T(8,128)(2,1)}, bf16[768,256]{1,0:T(8,128)(2,1)}, u32[]{:S(2)}, u32[]{:S(2)}) collective-permute-start(bf16[768,256]{1,0:T(8,128)(2,1)} %g0.7), channel_id=1, source_target_pairs={{0,3},{1,0},{2,1},{3,2},{4,7},{5,4},{6,5},{7,6},{8,11},{9,8},{10,9... | collective-permute-start | bytes 1179656 | tf_op jit(solution)/shard_map/ppermute | solution.py:323
  6.5 0.7 fusion.1
  7.2 6.3 %collective-permute-start.1 = (bf16[16,128]{1,0:T(8,128)(2,1)S(1)}, bf16[16,128]{1,0:T(8,128)(2,1)S(1)}, u32[]{:S(2)}, u32[]{:S(2)}) collective-permute-start(bf16[16,128]{1,0:T(8,128)(2,1)S(1)} %get-tuple-element.51), channel_id=1, source_target_pairs={{4,0},{8,4},{12,8},{16,12},{20,16},{24,20},{28,24},{32,28},{36,32}... | collective-permute-start | bytes 12296 | tf_op jit(solution)/shard_map/ppermute | solution.py:329
  13.6 1.9 %collective-permute-start = (bf16[16,128]{1,0:T(8,128)(2,1)S(1)}, bf16[16,128]{1,0:T(8,128)(2,1)S(1)}, u32[]{:S(2)}, u32[]{:S(2)}) collective-permute-start(bf16[16,128]{1,0:T(8,128)(2,1)S(1)} %get-tuple-element.52), channel_id=1, source_target_pairs={{0,4},{4,8},{8,12},{12,16},{16,20},{20,24},{24,28},{28,32},{32,36}... | collective-permute-start | bytes 12296 | tf_op jit(solution)/shard_map/ppermute | solution.py:329
  15.5 0.1 pad_add_fusion.place
  15.6 2.2 %copy-done.2 = bf16[512,16,256]{2,1,0:T(8,128)(2,1)S(1)} copy-done((bf16[512,16,256]{2,1,0:T(8,128)(2,1)S(1)}, bf16[512,16,256]{2,1,0:T(8,128)(2,1)}, u32[]{:S(2)}) %copy-start.2) | copy-done | bytes 4194328
  17.8 3.3 %weights.1 = (bf16[2048,256]{1,0:T(8,128)(2,1)S(1)}, bf16[1024,256]{1,0:T(8,128)(2,1)S(1)}, bf16[1024,256]{1,0:T(8,128)(2,1)S(1)}, bf16[1024,256]{1,0:T(8,128)(2,1)}, f32[8,128]{1,0:T(8,128)S(1)}) custom-call(s32[2]{0:T(128)S(1)} %pad_add_fusion.place, bf16[512,16,256]{2,1,0:T(8,128)(2,1)S(1)} %copy-done.2), custom_call_target="tpu_custom_call" | custom-call | flops 5980000256 | bytes 1000 | tf_op jit(solution)/shard_map/weights/pallas_call | solution.py:151
  21.0 0.0 copy-start.15
  21.1 1.0 copy-done.15
  22.0 0.1 stack.29.place
  22.1 0.0 collective-permute-done.1.high
  22.1 0.0 collective-permute-done.low
  22.1 0.0 copy-done.6
  22.1 0.0 copy-start.3
  22.1 5.8 %prep.1 = (bf16[768,2048]{1,0:T(8,128)(2,1)S(1)}, f32[6144,128]{1,0:T(8,128)S(1)}) custom-call(bf16[6144,128]{1,0:T(8,128)(2,1)S(1)} %copy-done.1, bf16[16,128]{1,0:T(8,128)(2,1)S(1)} %collective-permute-done.low, bf16[16,128]{1,0:T(8,128)(2,1)S(1)} %collective-permute-done.1.high, f32[1,128]{1,0:T(1,128)S(1)} %bitcast.10, f32[8,128]{1,0:T(8,128)S(1)} %get-tuple-element.27.after), custom_call_target="tpu_custom_call" | custom-call | flops 10465000448 | bytes 1000 | tf_op jit(solution)/shard_map/prep/pallas_call | solution.py:116
  28.0 1.6 %copy-done.13 = f32[6144,128]{1,0:T(8,128)} copy-done((f32[6144,128]{1,0:T(8,128)}, f32[6144,128]{1,0:T(8,128)S(1)}, u32[]{:S(2)}) %copy-start.13) | copy-done | bytes 3145752
  29.6 0.0 collective-permute-done.4.g3
  29.6 0.0 collective-permute-done.3.g2
  29.6 0.0 collective-permute-done.2.g1
  29.6 0.0 copy-done.3
  29.6 4.1 %kernel_grad_send.1 = bf16[512,2048]{1,0:T(8,128)(2,1)S(1)} custom-call(s32[5]{0:T(128)S(1)} %stack.29.place, bf16[768,2048]{1,0:T(8,128)(2,1)S(1)} %get-tuple-element.28.taps, bf16[768,256]{1,0:T(8,128)(2,1)S(1)} %copy-done.3, bf16[768,256]{1,0:T(8,128)(2,1)} %collective-permute-done.2.g1, bf16[768,256]{1,0:T(8,128)(2,1)} %collective-permute-done.3.g2, ...), custom_call_target="tpu_custom_call" | custom-call | flops 4485000192 | bytes 1000 | tf_op jit(solution)/shard_map/kernel_grad_send/pallas_call | solution.py:182
  33.7 0.1 collective-permute-start.8
  33.8 0.4 collective-permute-start.5
  34.2 2.5 %collective-permute-start.6 = (bf16[1024,256]{1,0:T(8,128)(2,1)S(1)}, bf16[1024,256]{1,0:T(8,128)(2,1)}, u32[]{:S(2)}, u32[]{:S(2)}) collective-permute-start(bf16[1024,256]{1,0:T(8,128)(2,1)S(1)} %get-tuple-element.31), channel_id=1, source_target_pairs={{0,2},{1,3},{2,0},{3,1},{4,6},{5,7},{6,4},{7,5},{8,10},{9,11},{10,... | collective-permute-start | bytes 1572872 | tf_op jit(solution)/shard_map/ppermute | solution.py:323
  36.6 0.0 collective-permute-start.7
  36.6 1.3 %collective-permute-done.8.got = bf16[512,2048]{1,0:T(8,128)(2,1)S(1)} collective-permute-done((bf16[512,2048]{1,0:T(8,128)(2,1)S(1)}, bf16[512,2048]{1,0:T(8,128)(2,1)S(1)}, u32[]{:S(2)}, u32[]{:S(2)}) %collective-permute-start.8) | collective-permute-done | bytes 2097184 | tf_op jit(solution)/shard_map/ppermute | solution.py:323
  38.0 3.5 %kernel_grad_keep.1 = (bf16[4,128,2048]{2,1,0:T(8,128)(2,1)S(1)}, f32[8,128]{1,0:T(8,128)S(1)}) custom-call(s32[5]{0:T(128)S(1)} %stack.29.place, bf16[768,2048]{1,0:T(8,128)(2,1)S(1)} %get-tuple-element.28.taps, bf16[768,256]{1,0:T(8,128)(2,1)S(1)} %copy-done.3, bf16[768,256]{1,0:T(8,128)(2,1)} %collective-permute-done.2.g1, ...), custom_call_target="tpu_custom_call" | custom-call | flops 5980000256 | bytes 1000 | tf_op jit(solution)/shard_map/kernel_grad_keep/pallas_call | solution.py:203
  41.5 1.3 %copy-done = bf16[4,128,2048]{2,1,0:T(8,128)(2,1)} copy-done((bf16[4,128,2048]{2,1,0:T(8,128)(2,1)}, bf16[4,128,2048]{2,1,0:T(8,128)(2,1)S(1)}, u32[]{:S(2)}) %copy-start) | copy-done | bytes 2097176
  42.9 4.9 %all-to-all-start = ((bf16[4,128,2048]{2,1,0:T(8,128)(2,1)}), bf16[4,128,2048]{2,1,0:T(8,128)(2,1)S(1)}, u32[]{:S(2)}, u32[]{:S(2)}) async-start(bf16[4,128,2048]{2,1,0:T(8,128)(2,1)} %copy-done), calls=%async_computation | async-start | bytes 4194304 | tf_op jit(solution)/shard_map/all_to_all | solution.py:352
  47.7 1.2 %collective-permute-done.5.a1 = bf16[1024,256]{1,0:T(8,128)(2,1)} collective-permute-done((bf16[1024,256]{1,0:T(8,128)(2,1)}, bf16[1024,256]{1,0:T(8,128)(2,1)}, u32[]{:S(2)}, u32[]{:S(2)}) %collective-permute-start.5) | collective-permute-done | bytes 524320 | tf_op jit(solution)/shard_map/ppermute | solution.py:323
  48.9 1.7 %collective-permute-done.6.a2 = bf16[1024,256]{1,0:T(8,128)(2,1)} collective-permute-done((bf16[1024,256]{1,0:T(8,128)(2,1)S(1)}, bf16[1024,256]{1,0:T(8,128)(2,1)}, u32[]{:S(2)}, u32[]{:S(2)}) %collective-permute-start.6) | collective-permute-done | bytes 524320 | tf_op jit(solution)/shard_map/ppermute | solution.py:323
  50.6 10.4 %collective-permute-done.7.a3 = bf16[1024,256]{1,0:T(8,128)(2,1)} collective-permute-done((bf16[1024,256]{1,0:T(8,128)(2,1)S(1)}, bf16[1024,256]{1,0:T(8,128)(2,1)}, u32[]{:S(2)}, u32[]{:S(2)}) %collective-permute-start.7) | collective-permute-done | bytes 524320 | tf_op jit(solution)/shard_map/ppermute | solution.py:323
  61.0 1.6 %join.1 = (bf16[1024,256]{1,0:T(8,128)(2,1)S(1)}, bf16[1024,256]{1,0:T(8,128)(2,1)S(1)}, bf16[1024,256]{1,0:T(8,128)(2,1)S(1)}) custom-call(bf16[1024,256]{1,0:T(8,128)(2,1)} %collective-permute-done.5.a1, bf16[1024,256]{1,0:T(8,128)(2,1)} %collective-permute-done.6.a2, bf16[1024,256]{1,0:T(8,128)(2,1)} %collective-permute-done.7.a3, ...), custom_call_target="tpu_custom_call" | custom-call | flops 1495000064 | bytes 1000 | tf_op jit(solution)/shard_map/join/pallas_call | solution.py:219
  62.6 0.1 collective-permute-start.9
  62.7 0.5 collective-permute-start.10
  63.2 0.1 collective-permute-start.11
  63.3 1.3 %collective-permute-done.9.b1 = bf16[1024,256]{1,0:T(8,128)(2,1)S(1)} collective-permute-done((bf16[1024,256]{1,0:T(8,128)(2,1)S(1)}, bf16[1024,256]{1,0:T(8,128)(2,1)S(1)}, u32[]{:S(2)}, u32[]{:S(2)}) %collective-permute-start.9) | collective-permute-done | bytes 524320 | tf_op jit(solution)/shard_map/ppermute | solution.py:323
  64.6 0.7 collective-permute-done.10.b2
  65.4 0.7 collective-permute-done.11.b3
  66.1 5.9 %encode.1 = (f32[768,256]{1,0:T(8,128)S(1)}, bf16[768,256]{1,0:T(8,128)(2,1)}, bf16[768,256]{1,0:T(8,128)(2,1)S(1)}, bf16[768,256]{1,0:T(8,128)(2,1)}, bf16[2048...) custom-call(s32[1]{0:T(128)} %bitcast.core, ...), custom_call_target="tpu_custom_call" | custom-call | flops 7474999808 | bytes 1000 | tf_op jit(solution)/shard_map/encode/pallas_call | solution.py:241
  72.0 0.9 copy-done.7
  72.9 2.1 %copy-done.11 = bf16[2048,1024]{1,0:T(8,128)(2,1)} copy-done((bf16[2048,1024]{1,0:T(8,128)(2,1)}, bf16[2048,1024]{1,0:T(8,128)(2,1)S(1)}, u32[]{:S(2)}) %copy-start.11) | copy-done | bytes 4194328
  74.9 2.0 %collective-permute-start.15 = (bf16[16,1024]{1,0:T(8,128)(2,1)S(1)}, bf16[16,1024]{1,0:T(8,128)(2,1)S(1)}, u32[]{:S(2)}, u32[]{:S(2)}) collective-permute-start(bf16[16,1024]{1,0:T(8,128)(2,1)S(1)} %get-tuple-element.41), channel_id=1, source_target_pairs={{0,4},{4,8},{8,12},{12,16},{16,20},{20,24},{24,28},{28,32},{32,36}... | collective-permute-start | bytes 98312 | tf_op jit(solution)/shard_map/ppermute | solution.py:329
  77.0 5.6 %collective-permute-start.16 = (bf16[16,1024]{1,0:T(8,128)(2,1)S(1)}, bf16[16,1024]{1,0:T(8,128)(2,1)S(1)}, u32[]{:S(2)}, u32[]{:S(2)}) collective-permute-start(bf16[16,1024]{1,0:T(8,128)(2,1)S(1)} %get-tuple-element.42), channel_id=1, source_target_pairs={{4,0},{8,4},{12,8},{16,12},{20,16},{24,20},{28,24},{32,28},{36,32}... | collective-permute-start | bytes 98312 | tf_op jit(solution)/shard_map/ppermute | solution.py:329
  82.6 1.1 %collective-permute-start.12 = (bf16[768,256]{1,0:T(8,128)(2,1)}, bf16[768,256]{1,0:T(8,128)(2,1)}, u32[]{:S(2)}, u32[]{:S(2)}) collective-permute-start(bf16[768,256]{1,0:T(8,128)(2,1)} %get-tuple-element.38), channel_id=1, source_target_pairs={{0,1},{1,2},{2,3},{3,0},{4,5},{5,6},{6,7},{7,4},{8,9},{9,10},{10,1... | collective-permute-start | bytes 1179656 | tf_op jit(solution)/shard_map/ppermute | solution.py:323
  83.7 2.2 %collective-permute-start.13 = (bf16[768,256]{1,0:T(8,128)(2,1)}, bf16[768,256]{1,0:T(8,128)(2,1)}, u32[]{:S(2)}, u32[]{:S(2)}) collective-permute-start(bf16[768,256]{1,0:T(8,128)(2,1)} %get-tuple-element.39), channel_id=1, source_target_pairs={{0,3},{1,0},{2,1},{3,2},{4,7},{5,4},{6,5},{7,6},{8,11},{9,8},{10,9... | collective-permute-start | bytes 1179656 | tf_op jit(solution)/shard_map/ppermute | solution.py:323
  85.9 0.5 collective-permute-start.14
  86.5 0.0 all-to-all-done.parts
  86.5 1.1 lines.1
  87.5 3.9 %all-to-all-start.1 = ((bf16[8,16,2048]{2,1,0:T(8,128)(2,1)}), bf16[8,16,2048]{2,1,0:T(8,128)(2,1)S(1)}, u32[]{:S(2)}, u32[]{:S(2)}) async-start(bf16[8,16,2048]{2,1,0:T(8,128)(2,1)} %get-tuple-element.50), calls=%async_computation.1 | async-start | bytes 1048576 | tf_op jit(solution)/shard_map/all_to_all | solution.py:362
  91.5 0.0 collective-permute-done.15.low
  91.5 0.0 collective-permute-done.16.high
  91.5 2.2 %copy-done.12 = bf16[2048,1024]{1,0:T(8,128)(2,1)S(1)} copy-done((bf16[2048,1024]{1,0:T(8,128)(2,1)S(1)}, bf16[2048,1024]{1,0:T(8,128)(2,1)}, u32[]{:S(2)}) %copy-start.12) | copy-done | bytes 4194328
  93.7 1.9 %copy-done.14 = f32[6144,128]{1,0:T(8,128)S(1)} copy-done((f32[6144,128]{1,0:T(8,128)S(1)}, f32[6144,128]{1,0:T(8,128)}, u32[]{:S(2)}) %copy-start.14) | copy-done | bytes 3145752
  95.6 6.9 %input_grad.1 = (bf16[6144,128]{1,0:T(8,128)(2,1)}, f32[8,128]{1,0:T(8,128)S(1)}) custom-call(bf16[768,256]{1,0:T(8,128)(2,1)S(1)} %copy-done.3, bf16[768,256]{1,0:T(8,128)(2,1)} %collective-permute-done.2.g1, bf16[768,256]{1,0:T(8,128)(2,1)} %collective-permute-done.3.g2, bf16[768,256]{1,0:T(8,128)(2,1)S(1)} %copy-done.5, ...), custom_call_target="tpu_custom_call" | custom-call | flops 8970000384 | bytes 1000 | tf_op jit(solution)/shard_map/input_grad/pallas_call | solution.py:299
  102.5 0.0 collective-permute-done.12.a1
  102.5 0.0 collective-permute-done.13.a2
  102.5 0.0 collective-permute-done.14.a3
  102.5 2.2 %total.1 = bf16[768,256]{1,0:T(8,128)(2,1)} custom-call(f32[768,256]{1,0:T(8,128)S(1)} %copy-done.8, bf16[768,256]{1,0:T(8,128)(2,1)} %collective-permute-done.12.a1, bf16[768,256]{1,0:T(8,128)(2,1)} %collective-permute-done.13.a2, bf16[768,256]{1,0:T(8,128)(2,1)} %collective-permute-done.14.a3, f32[8,128]{1,0:T(8,128)S(1)} %get-tuple-element.48.after), custom_call_target="tpu_custom_call" | custom-call | flops 1495000064 | bytes 1000 | tf_op jit(solution)/shard_map/total/pallas_call | solution.py:316
  104.7 2.6 %all-to-all-done.1 = bf16[8,16,2048]{2,1,0:T(8,128)(2,1)S(1)} async-done(((bf16[8,16,2048]{2,1,0:T(8,128)(2,1)}), bf16[8,16,2048]{2,1,0:T(8,128)(2,1)S(1)}, u32[]{:S(2)}, u32[]{:S(2)}) %all-to-all-start.1) | async-done | bytes 524320 | tf_op jit(solution)/shard_map/all_to_all | solution.py:362
  107.3 0.1 convert_reduce_fusion
  107.4 0.6 copy.7
  (23 shorter events, 0.1 us)
Async XLA Ops:
  0.6 28.9 %collective-permute-start.4 = (bf16[768,256]{1,0:T(8,128)(2,1)}, bf16[768,256]{1,0:T(8,128)(2,1)S(1)}, u32[]{:S(2)}, u32[]{:S(2)}) collective-permute-start(bf16[768,256]{1,0:T(8,128)(2,1)} %g0.7), channel_id=1, source_target_pairs={{0,1},{1,2},{2,3},{3,0},{4,5},{5,6},{6,7},{7,4},{8,9},{9,10},{10,1... | collective-permute-start | bytes 1179656 | tf_op jit(solution)/shard_map/ppermute | solution.py:323
  2.3 27.3 %collective-permute-start.3 = (bf16[768,256]{1,0:T(8,128)(2,1)}, bf16[768,256]{1,0:T(8,128)(2,1)}, u32[]{:S(2)}, u32[]{:S(2)}) collective-permute-start(bf16[768,256]{1,0:T(8,128)(2,1)} %g0.7), channel_id=1, source_target_pairs={{0,2},{1,3},{2,0},{3,1},{4,6},{5,7},{6,4},{7,5},{8,10},{9,11},{10,... | collective-permute-start | bytes 1179656 | tf_op jit(solution)/shard_map/ppermute | solution.py:323
  5.2 24.4 %collective-permute-start.2 = (bf16[768,256]{1,0:T(8,128)(2,1)}, bf16[768,256]{1,0:T(8,128)(2,1)}, u32[]{:S(2)}, u32[]{:S(2)}) collective-permute-start(bf16[768,256]{1,0:T(8,128)(2,1)} %g0.7), channel_id=1, source_target_pairs={{0,3},{1,0},{2,1},{3,2},{4,7},{5,4},{6,5},{7,6},{8,11},{9,8},{10,9... | collective-permute-start | bytes 1179656 | tf_op jit(solution)/shard_map/ppermute | solution.py:323
  7.2 14.9 %collective-permute-start.1 = (bf16[16,128]{1,0:T(8,128)(2,1)S(1)}, bf16[16,128]{1,0:T(8,128)(2,1)S(1)}, u32[]{:S(2)}, u32[]{:S(2)}) collective-permute-start(bf16[16,128]{1,0:T(8,128)(2,1)S(1)} %get-tuple-element.51), channel_id=1, source_target_pairs={{4,0},{8,4},{12,8},{16,12},{20,16},{24,20},{28,24},{32,28},{36,32}... | collective-permute-start | bytes 12296 | tf_op jit(solution)/shard_map/ppermute | solution.py:329
  13.6 8.5 %collective-permute-start = (bf16[16,128]{1,0:T(8,128)(2,1)S(1)}, bf16[16,128]{1,0:T(8,128)(2,1)S(1)}, u32[]{:S(2)}, u32[]{:S(2)}) collective-permute-start(bf16[16,128]{1,0:T(8,128)(2,1)S(1)} %get-tuple-element.52), channel_id=1, source_target_pairs={{0,4},{4,8},{8,12},{12,16},{16,20},{20,24},{24,28},{28,32},{32,36}... | collective-permute-start | bytes 12296 | tf_op jit(solution)/shard_map/ppermute | solution.py:329
  15.6 2.2 %copy-start.2 = (bf16[512,16,256]{2,1,0:T(8,128)(2,1)S(1)}, bf16[512,16,256]{2,1,0:T(8,128)(2,1)}, u32[]{:S(2)}) copy-start(bf16[512,16,256]{2,1,0:T(8,128)(2,1)} %whole.1) | copy-start | bytes 12582916
  17.8 4.3 %copy-start.1 = (bf16[6144,128]{1,0:T(8,128)(2,1)S(1)}, bf16[6144,128]{1,0:T(8,128)(2,1)}, u32[]{:S(2)}) copy-start(bf16[6144,128]{1,0:T(8,128)(2,1)} %feat.1) | copy-start | bytes 4718596
  17.8 4.3 %copy-start.6 = (f32[128]{0:T(128)S(1)}, f32[128]{0:T(128)}, u32[]{:S(2)}) copy-start(f32[128]{0:T(128)} %param.5) | copy-start | bytes 1540
  21.0 1.0 copy-start.15
  22.1 7.5 %copy-start.3 = (bf16[768,256]{1,0:T(8,128)(2,1)S(1)}, bf16[768,256]{1,0:T(8,128)(2,1)}, u32[]{:S(2)}) copy-start(bf16[768,256]{1,0:T(8,128)(2,1)} %g0.7) | copy-start | bytes 1179652
  27.9 1.6 %copy-start.13 = (f32[6144,128]{1,0:T(8,128)}, f32[6144,128]{1,0:T(8,128)S(1)}, u32[]{:S(2)}) copy-start(f32[6144,128]{1,0:T(8,128)S(1)} %get-tuple-element.44.factor) | copy-start | bytes 9437188
  29.6 8.4 %copy-start.9 = (bf16[768,2048]{1,0:T(8,128)(2,1)}, bf16[768,2048]{1,0:T(8,128)(2,1)S(1)}, u32[]{:S(2)}) copy-start(bf16[768,2048]{1,0:T(8,128)(2,1)S(1)} %get-tuple-element.28.taps) | copy-start | bytes 9437188
  29.6 8.4 %copy-start.4 = (bf16[768,256]{1,0:T(8,128)(2,1)}, bf16[768,256]{1,0:T(8,128)(2,1)S(1)}, u32[]{:S(2)}) copy-start(bf16[768,256]{1,0:T(8,128)(2,1)S(1)} %collective-permute-done.4.g3) | copy-start | bytes 1179652
  33.7 4.2 %collective-permute-start.8 = (bf16[512,2048]{1,0:T(8,128)(2,1)S(1)}, bf16[512,2048]{1,0:T(8,128)(2,1)S(1)}, u32[]{:S(2)}, u32[]{:S(2)}) collective-permute-start(bf16[512,2048]{1,0:T(8,128)(2,1)S(1)} %kernel_grad_send.1), channel_id=1, source_target_pairs={{0,4},{4,0},{1,5},{5,1},{2,6},{6,2},{3,7},{7,3},{8,12},{12,8},{9,1... | collective-permute-start | bytes 6291464 | tf_op jit(solution)/shard_map/ppermute | solution.py:323
  33.8 15.1 %collective-permute-start.5 = (bf16[1024,256]{1,0:T(8,128)(2,1)}, bf16[1024,256]{1,0:T(8,128)(2,1)}, u32[]{:S(2)}, u32[]{:S(2)}) collective-permute-start(bf16[1024,256]{1,0:T(8,128)(2,1)} %get-tuple-element.30), channel_id=1, source_target_pairs={{0,3},{1,0},{2,1},{3,2},{4,7},{5,4},{6,5},{7,6},{8,11},{9,8},{10,9... | collective-permute-start | bytes 1572872 | tf_op jit(solution)/shard_map/ppermute | solution.py:323
  34.2 16.4 %collective-permute-start.6 = (bf16[1024,256]{1,0:T(8,128)(2,1)S(1)}, bf16[1024,256]{1,0:T(8,128)(2,1)}, u32[]{:S(2)}, u32[]{:S(2)}) collective-permute-start(bf16[1024,256]{1,0:T(8,128)(2,1)S(1)} %get-tuple-element.31), channel_id=1, source_target_pairs={{0,2},{1,3},{2,0},{3,1},{4,6},{5,7},{6,4},{7,5},{8,10},{9,11},{10,... | collective-permute-start | bytes 1572872 | tf_op jit(solution)/shard_map/ppermute | solution.py:323
  36.6 24.4 %collective-permute-start.7 = (bf16[1024,256]{1,0:T(8,128)(2,1)S(1)}, bf16[1024,256]{1,0:T(8,128)(2,1)}, u32[]{:S(2)}, u32[]{:S(2)}) collective-permute-start(bf16[1024,256]{1,0:T(8,128)(2,1)S(1)} %get-tuple-element.32), channel_id=1, source_target_pairs={{0,1},{1,2},{2,3},{3,0},{4,5},{5,6},{6,7},{7,4},{8,9},{9,10},{10,1... | collective-permute-start | bytes 1572872 | tf_op jit(solution)/shard_map/ppermute | solution.py:323
  41.5 1.3 %copy-start = (bf16[4,128,2048]{2,1,0:T(8,128)(2,1)}, bf16[4,128,2048]{2,1,0:T(8,128)(2,1)S(1)}, u32[]{:S(2)}) copy-start(bf16[4,128,2048]{2,1,0:T(8,128)(2,1)S(1)} %get-tuple-element.45) | copy-start | bytes 6291460
  42.9 43.6 %all-to-all-start = ((bf16[4,128,2048]{2,1,0:T(8,128)(2,1)}), bf16[4,128,2048]{2,1,0:T(8,128)(2,1)S(1)}, u32[]{:S(2)}, u32[]{:S(2)}) async-start(bf16[4,128,2048]{2,1,0:T(8,128)(2,1)} %copy-done), calls=%async_computation | async-start | bytes 4194304 | tf_op jit(solution)/shard_map/all_to_all | solution.py:352
  61.0 5.1 %copy-start.5 = (bf16[768,256]{1,0:T(8,128)(2,1)S(1)}, bf16[768,256]{1,0:T(8,128)(2,1)}, u32[]{:S(2)}) copy-start(bf16[768,256]{1,0:T(8,128)(2,1)} %copy-done.4) | copy-start | bytes 1179652
  61.0 5.1 %copy-start.10 = (bf16[768,2048]{1,0:T(8,128)(2,1)S(1)}, bf16[768,2048]{1,0:T(8,128)(2,1)}, u32[]{:S(2)}) copy-start(bf16[768,2048]{1,0:T(8,128)(2,1)} %copy-done.9) | copy-start | bytes 9437188
  61.0 5.1 %copy-start.16 = (bf16[2048,256]{1,0:T(8,128)(2,1)S(1)}, bf16[2048,256]{1,0:T(8,128)(2,1)}, u32[]{:S(2)}) copy-start(bf16[2048,256]{1,0:T(8,128)(2,1)} %copy-done.15) | copy-start | bytes 3145732
  62.6 2.0 %collective-permute-start.9 = (bf16[1024,256]{1,0:T(8,128)(2,1)S(1)}, bf16[1024,256]{1,0:T(8,128)(2,1)S(1)}, u32[]{:S(2)}, u32[]{:S(2)}) collective-permute-start(bf16[1024,256]{1,0:T(8,128)(2,1)S(1)} %get-tuple-element.34.a1), channel_id=1, source_target_pairs={{0,4},{4,0},{1,5},{5,1},{2,6},{6,2},{3,7},{7,3},{8,12},{12,8},{9,1... | collective-permute-start | bytes 1572872 | tf_op jit(solution)/shard_map/ppermute | solution.py:323
  62.7 2.6 %collective-permute-start.10 = (bf16[1024,256]{1,0:T(8,128)(2,1)S(1)}, bf16[1024,256]{1,0:T(8,128)(2,1)S(1)}, u32[]{:S(2)}, u32[]{:S(2)}) collective-permute-start(bf16[1024,256]{1,0:T(8,128)(2,1)S(1)} %get-tuple-element.35.a2), channel_id=1, source_target_pairs={{0,4},{4,0},{1,5},{5,1},{2,6},{6,2},{3,7},{7,3},{8,12},{12,8},{9,1... | collective-permute-start | bytes 1572872 | tf_op jit(solution)/shard_map/ppermute | solution.py:323
  63.2 2.9 %collective-permute-start.11 = (bf16[1024,256]{1,0:T(8,128)(2,1)S(1)}, bf16[1024,256]{1,0:T(8,128)(2,1)S(1)}, u32[]{:S(2)}, u32[]{:S(2)}) collective-permute-start(bf16[1024,256]{1,0:T(8,128)(2,1)S(1)} %get-tuple-element.36.a3), channel_id=1, source_target_pairs={{0,4},{4,0},{1,5},{5,1},{2,6},{6,2},{3,7},{7,3},{8,12},{12,8},{9,1... | collective-permute-start | bytes 1572872 | tf_op jit(solution)/shard_map/ppermute | solution.py:323
  72.0 0.9 copy-start.7
  72.9 2.1 %copy-start.11 = (bf16[2048,1024]{1,0:T(8,128)(2,1)}, bf16[2048,1024]{1,0:T(8,128)(2,1)S(1)}, u32[]{:S(2)}) copy-start(bf16[2048,1024]{1,0:T(8,128)(2,1)S(1)} %get-tuple-element.43.weights) | copy-start | bytes 12582916
  74.9 16.5 %collective-permute-start.15 = (bf16[16,1024]{1,0:T(8,128)(2,1)S(1)}, bf16[16,1024]{1,0:T(8,128)(2,1)S(1)}, u32[]{:S(2)}, u32[]{:S(2)}) collective-permute-start(bf16[16,1024]{1,0:T(8,128)(2,1)S(1)} %get-tuple-element.41), channel_id=1, source_target_pairs={{0,4},{4,8},{8,12},{12,16},{16,20},{20,24},{24,28},{28,32},{32,36}... | collective-permute-start | bytes 98312 | tf_op jit(solution)/shard_map/ppermute | solution.py:329
  77.0 14.5 %collective-permute-start.16 = (bf16[16,1024]{1,0:T(8,128)(2,1)S(1)}, bf16[16,1024]{1,0:T(8,128)(2,1)S(1)}, u32[]{:S(2)}, u32[]{:S(2)}) collective-permute-start(bf16[16,1024]{1,0:T(8,128)(2,1)S(1)} %get-tuple-element.42), channel_id=1, source_target_pairs={{4,0},{8,4},{12,8},{16,12},{20,16},{24,20},{28,24},{32,28},{36,32}... | collective-permute-start | bytes 98312 | tf_op jit(solution)/shard_map/ppermute | solution.py:329
  82.6 19.9 %collective-permute-start.12 = (bf16[768,256]{1,0:T(8,128)(2,1)}, bf16[768,256]{1,0:T(8,128)(2,1)}, u32[]{:S(2)}, u32[]{:S(2)}) collective-permute-start(bf16[768,256]{1,0:T(8,128)(2,1)} %get-tuple-element.38), channel_id=1, source_target_pairs={{0,1},{1,2},{2,3},{3,0},{4,5},{5,6},{6,7},{7,4},{8,9},{9,10},{10,1... | collective-permute-start | bytes 1179656 | tf_op jit(solution)/shard_map/ppermute | solution.py:323
  83.7 18.8 %collective-permute-start.13 = (bf16[768,256]{1,0:T(8,128)(2,1)}, bf16[768,256]{1,0:T(8,128)(2,1)}, u32[]{:S(2)}, u32[]{:S(2)}) collective-permute-start(bf16[768,256]{1,0:T(8,128)(2,1)} %get-tuple-element.39), channel_id=1, source_target_pairs={{0,3},{1,0},{2,1},{3,2},{4,7},{5,4},{6,5},{7,6},{8,11},{9,8},{10,9... | collective-permute-start | bytes 1179656 | tf_op jit(solution)/shard_map/ppermute | solution.py:323
  85.9 16.6 %collective-permute-start.14 = (bf16[768,256]{1,0:T(8,128)(2,1)S(1)}, bf16[768,256]{1,0:T(8,128)(2,1)}, u32[]{:S(2)}, u32[]{:S(2)}) collective-permute-start(bf16[768,256]{1,0:T(8,128)(2,1)S(1)} %get-tuple-element.40), channel_id=1, source_target_pairs={{0,2},{1,3},{2,0},{3,1},{4,6},{5,7},{6,4},{7,5},{8,10},{9,11},{10,... | collective-permute-start | bytes 1179656 | tf_op jit(solution)/shard_map/ppermute | solution.py:323
  87.5 19.8 %all-to-all-start.1 = ((bf16[8,16,2048]{2,1,0:T(8,128)(2,1)}), bf16[8,16,2048]{2,1,0:T(8,128)(2,1)S(1)}, u32[]{:S(2)}, u32[]{:S(2)}) async-start(bf16[8,16,2048]{2,1,0:T(8,128)(2,1)} %get-tuple-element.50), calls=%async_computation.1 | async-start | bytes 1048576 | tf_op jit(solution)/shard_map/all_to_all | solution.py:362
  91.5 2.2 %copy-start.12 = (bf16[2048,1024]{1,0:T(8,128)(2,1)S(1)}, bf16[2048,1024]{1,0:T(8,128)(2,1)}, u32[]{:S(2)}) copy-start(bf16[2048,1024]{1,0:T(8,128)(2,1)} %copy-done.11) | copy-start | bytes 12582916
  93.7 1.9 %copy-start.14 = (f32[6144,128]{1,0:T(8,128)S(1)}, f32[6144,128]{1,0:T(8,128)}, u32[]{:S(2)}) copy-start(f32[6144,128]{1,0:T(8,128)} %copy-done.13) | copy-start | bytes 9437188
  95.6 6.9 %copy-start.8 = (f32[768,256]{1,0:T(8,128)S(1)}, f32[768,256]{1,0:T(8,128)}, u32[]{:S(2)}) copy-start(f32[768,256]{1,0:T(8,128)} %copy-done.7) | copy-start | bytes 2359300

commit v6 on v5

--- a/solution.py
+++ b/solution.py
@@ -37,12 +37,12 @@
     return lax.dot_general(lhs, rhs, dims, preferred_element_type=F32)
 
 
-def call(kernel, outs, specs, name, scratch=(), limit=24):
+def call(kernel, outs, specs, name, scratch=(), limit=24, out_specs=None):
     return pl.pallas_call(
         kernel,
         out_shape=outs,
         in_specs=specs,
-        out_specs=jax.tree.map(lambda _: VMEM, outs),
+        out_specs=out_specs or jax.tree.map(lambda _: VMEM, outs),
         scratch_shapes=scratch,
         compiler_params=pltpu.CompilerParams(vmem_limit_bytes=limit * 2**20),
         cost_estimate=pl.CostEstimate(flops=int(TIME[name] * FACTOR * 1.15e9), bytes_accessed=1000, transcendentals=0),
@@ -57,7 +57,7 @@
 TOKEN = shape((8, 128), F32)
 
 
-FACTOR = 1.3
+FACTOR = 1.1
 TIME = dict(
     prep=7,
     weights=4,
@@ -71,6 +71,10 @@
 )
 
 
+def far_shape(dims, dtype=BF):
+    return pltpu.HBM(dims, dtype)
+
+
 def poly(coefs, z):
     out = z * coefs[-1] + coefs[-2]
     for c in coefs[-3::-1]:
@@ -85,7 +89,7 @@
     return r * poly(SIN, z), poly(COS, z)
 
 
-def prep_kernel(step, feat, low, high, alpha, after, taps, factor, rows):
+def prep_kernel(feat, low, high, alpha, taps, factor, done, rows, held, sem):
     frames = feat.shape[0]
     a = alpha[...]
     inv = 1.0 / a
@@ -97,33 +101,49 @@
 
     rows[0:8, :] = snake(low[8:16, :])[0]
     rows[frames + 8 : frames + 16, :] = snake(high[0:8, :])[0]
-
-    def body(at, carry):
-        here = pl.multiple_of(at * step, step)
-        act, fac = snake(feat[pl.ds(here, step), :])
-        rows[pl.ds(here + 8, step), :] = act
-        factor[pl.ds(here, step), :] = fac
-        return carry
-
-    lax.fori_loop(0, frames // step, body, 0)
+    step, parts = 256, 4
+    size = frames // parts
+    copies = []
+    for part in range(parts):
+
+        def body(at, carry, part=part):
+            here = pl.multiple_of(part * size + at * step, step)
+            act, fac = snake(feat[pl.ds(here, step), :])
+            rows[pl.ds(here + 8, step), :] = act
+            held[pl.ds(here, step), :] = fac
+            return carry
+
+        lax.fori_loop(0, size // step, body, 0)
+        lines = pl.ds(part * size, size)
+        copies.append(pltpu.make_async_copy(held.at[lines], factor.at[lines], sem.at[part]))
+        copies[-1].start()
     outs = frames // STRIDE
     for k in range(TAPS):
         taps[:, k * 128 : (k + 1) * 128] = rows[pl.ds(4 + k, outs, stride=STRIDE), :].astype(BF)
-
-
-def prep(feat, low, high, alpha, after, step=256):
+    done[...] = jnp.zeros(done.shape, F32)
+    for c in copies:
+        c.wait()
+
+
+def prep(feat, low, high, alpha):
     frames, chans = feat.shape
     return call(
-        functools.partial(prep_kernel, step),
-        (shape((frames // STRIDE, TAPS * chans)), shape((frames, chans), F32)),
-        [VMEM] * 5,
+        prep_kernel,
+        (shape((frames // STRIDE, TAPS * chans)), far_shape((frames, chans), F32), TOKEN),
+        [VMEM] * 4,
         "prep",
-        [pltpu.VMEM((frames + 16, chans), F32)],
-        limit=24,
-    )(feat, low, high, alpha, after)
-
-
-def weights_kernel(place, whole, own, p1, p2, p3, done, buf, rows, sem):
+        [
+            pltpu.VMEM((frames + 16, chans), F32),
+            pltpu.VMEM((frames, chans), F32),
+            pltpu.SemaphoreType.DMA((4,)),
+        ],
+        out_specs=(VMEM, HBM, VMEM),
+    )(feat, low, high, alpha)
+
+
+def weights_kernel(
+    place, whole, after, own, p1, p2, p3, done, buf, rows, held, sem, out_sem
+):
     y, core = place[0], place[1]
     copies = [
         pltpu.make_async_copy(
@@ -133,7 +153,7 @@
     ]
     for c in copies:
         c.start()
-    for s, out in ((1, p1), (3, p3), (2, p2), (0, own)):
+    for s, out in ((0, held), (1, p1), (3, p3), (2, p2)):
         copies[s].wait()
         count = TAPS if s == 0 else TAPS // 2
         for h in range(2):
@@ -144,22 +164,28 @@
                 out[k * 128 : (k + 1) * 128, lanes] = rows[
                     pl.ds(tap, 128, stride=TAPS), :
                 ].astype(BF)
-    done[...] = jnp.zeros(done.shape, F32)
-
-
-def weights(place, whole):
+        if s == 0:
+            sent = pltpu.make_async_copy(held, own, out_sem)
+            sent.start()
+    sent.wait()
+    done[...] = jnp.zeros(done.shape, F32)
+
+
+def weights(place, whole, after):
     return call(
         weights_kernel,
-        (shape((2048, 256)),) + (shape((1024, 256)),) * 3 + (TOKEN,),
-        [SMEM, HBM],
+        (far_shape((2048, 256)),) + (shape((1024, 256)),) * 3 + (TOKEN,),
+        [SMEM, HBM, VMEM],
         "weights",
         [
             pltpu.VMEM((4, 128, TAPS, 256), BF),
             pltpu.VMEM((128 * TAPS, 128), F32),
+            pltpu.VMEM((2048, 256), BF),
             pltpu.SemaphoreType.DMA((4,)),
+            pltpu.SemaphoreType.DMA,
         ],
-        limit=24,
-    )(place, whole)
+        out_specs=(HBM,) + (VMEM,) * 4,
+    )(place, whole, after)
 
 
 def choose(gs, which, order, lhs):
@@ -172,83 +198,118 @@
         lhs[pl.ds(at, 128), :] = mul(pick, g[...], NT).astype(BF)
 
 
-def send_kernel(place, taps, g0, g1, g2, g3, out, lhs):
+def send_kernel(place, taps, g0, g1, g2, g3, after, out, lhs):
     choose((g0, g1, g2, g3), 1 - place[0], [place[1 + d] for d in range(4)], lhs)
     for n in range(0, 2048, 256):
         out[:, n : n + 256] = mul(lhs[...], taps[:, n : n + 256]).astype(BF)
 
 
-def send(place, taps, gs):
+def send(place, taps, gs, after):
     return call(
         send_kernel,
         shape((512, 2048)),
-        [SMEM] + [VMEM] * 5,
+        [SMEM] + [VMEM] * 6,
         "kernel_grad_send",
         [pltpu.VMEM((512, 768), BF)],
         limit=24,
-    )(place, taps, *gs)
-
-
-def keep_kernel(place, taps, g0, g1, g2, g3, got, out, done, lhs):
+    )(place, taps, *gs, after)
+
+
+def keep_kernel(place, taps, g0, g1, g2, g3, got, out, first, last, done, lhs, held, ends, sem):
     choose((g0, g1, g2, g3), place[0], [place[1 + d] for d in range(4)], lhs)
-    for n in range(0, 2048, 256):
-        cols = slice(n, n + 256)
+    for d, g in enumerate((g0, g1, g2, g3)):
+        ends[0, :, d * 256 : (d + 1) * 256] = g[0:16, :]
+        ends[1, :, d * 256 : (d + 1) * 256] = g[752:768, :]
+    copies = [
+        pltpu.make_async_copy(ends.at[0], first, sem.at[4]),
+        pltpu.make_async_copy(ends.at[1], last, sem.at[5]),
+    ]
+    for c in copies:
+        c.start()
+    for n in range(0, 2048, 512):
+        cols = slice(n, n + 512)
         both = mul(lhs[...], taps[:, cols]) + got[:, cols].astype(F32)
         for to in range(4):
-            out[to, :, cols] = both[to * 128 : (to + 1) * 128].astype(BF)
-    done[...] = jnp.zeros(done.shape, F32)
+            held[to, :, cols] = both[to * 128 : (to + 1) * 128].astype(BF)
+        copies.append(
+            pltpu.make_async_copy(held.at[:, :, cols], out.at[:, :, cols], sem.at[n // 512])
+        )
+        copies[-1].start()
+    done[...] = jnp.zeros(done.shape, F32)
+    for c in copies:
+        c.wait()
 
 
 def keep(place, taps, gs, got):
     return call(
         keep_kernel,
-        (shape((4, 128, 2048)), TOKEN),
+        (far_shape((4, 128, 2048)),) + (far_shape((16, 1024)),) * 2 + (TOKEN,),
         [SMEM] + [VMEM] * 6,
         "kernel_grad_keep",
-        [pltpu.VMEM((512, 768), BF)],
+        [
+            pltpu.VMEM((512, 768), BF),
+            pltpu.VMEM((4, 128, 2048), BF),
+            pltpu.VMEM((2, 16, 1024), BF),
+            pltpu.SemaphoreType.DMA((6,)),
+        ],
+        out_specs=(HBM,) * 3 + (VMEM,),
         limit=24,
     )(place, taps, *gs, got)
 
 
-def join_kernel(a1, a2, a3, after, o1, o2, o3):
+def join_kernel(a1, a2, a3, low, high, after, o1, o2, o3):
     for a, out in ((a1, o1), (a2, o2), (a3, o3)):
         out[...] = a[...]
 
 
-def join(near, after):
-    return call(join_kernel, (shape((1024, 256)),) * 3, [VMEM] * 4, "join", limit=24)(*near, after)
+def join(near, edges, after):
+    return call(join_kernel, (shape((1024, 256)),) * 3, [VMEM] * 6, "join", limit=24)(*near, *edges, after)
 
 
 def encode_kernel(
-    core, taps, own, g0, g1, g2, g3, a1, a2, a3, b1, b2, b3, o0, o1, o2, o3, full, o_first, o_last, done
+    core, taps, own, a1, a2, a3, b1, b2, b3, o0, o1, o2, o3, full, done, held, mine, theirs, sem
 ):
     here = pl.multiple_of(core[0] * 1024, 1024)
     there = pl.multiple_of(1024 - core[0] * 1024, 1024)
-    full[:, 0:256] = own[...]
+    first = pltpu.make_async_copy(own, held.at[:, 0:256], sem.at[0])
+    first.start()
     for d, (a, b) in enumerate(((a1, b1), (a2, b2), (a3, b3))):
         cols = slice(256 * (d + 1), 256 * (d + 2))
-        full[pl.ds(here, 1024), cols] = a[...]
-        full[pl.ds(there, 1024), cols] = b[...]
-    for d, out in enumerate((o0, o1, o2, o3)):
-        out[...] = mul(taps[...], full[:, d * 256 : (d + 1) * 256]).astype(out.dtype)
-    for d, g in enumerate((g0, g1, g2, g3)):
-        o_first[:, d * 256 : (d + 1) * 256] = g[0:16, :]
-        o_last[:, d * 256 : (d + 1) * 256] = g[752:768, :]
-    done[...] = jnp.zeros(done.shape, F32)
-
-
-def encode(core, taps, own, gs, near, far):
+        held[pl.ds(here, 1024), cols] = a[...]
+        held[pl.ds(there, 1024), cols] = b[...]
+    first.wait()
+    copies = [pltpu.make_async_copy(held, full, sem.at[1])]
+    copies[0].start()
+    for d, out in ((0, o0), (1, o1), (3, o3), (2, o2)):
+        value = mul(taps[...], held[:, d * 256 : (d + 1) * 256])
+        if d == 0:
+            mine[...] = value
+            copies.append(pltpu.make_async_copy(mine, out, sem.at[2]))
+        else:
+            theirs[d - 1] = value.astype(BF)
+            copies.append(pltpu.make_async_copy(theirs.at[d - 1], out, sem.at[2 + d]))
+        copies[-1].start()
+    done[...] = jnp.zeros(done.shape, F32)
+    for c in copies:
+        c.wait()
+
+
+def encode(core, taps, own, near, far):
     return call(
         encode_kernel,
-        (shape((768, 256), F32),)
-        + (shape((768, 256)),) * 3
-        + (shape((2048, 1024)),)
-        + (shape((16, 1024)),) * 2
-        + (TOKEN,),
-        [SMEM] + [VMEM] * 12,
+        (far_shape((768, 256), F32),)
+        + (far_shape((768, 256)),) * 3
+        + (far_shape((2048, 1024)), TOKEN),
+        [SMEM, VMEM, HBM] + [VMEM] * 6,
         "encode",
-        limit=24,
-    )(core, taps, own, *gs, *near, *far)
+        [
+            pltpu.VMEM((2048, 1024), BF),
+            pltpu.VMEM((768, 256), F32),
+            pltpu.VMEM((3, 768, 256), BF),
+            pltpu.SemaphoreType.DMA((6,)),
+        ],
+        out_specs=(HBM,) * 5 + (VMEM,),
+    )(core, taps, own, *near, *far)
 
 
 def lines_kernel(parts, after, out, done):
@@ -341,23 +402,23 @@
     low, high = beside(features[-16:], 1), beside(features[:16], -1)
 
     at = jnp.stack([y, core])
-    own, p1, p2, p3, done = weights(at, down_weight)
+    taps, factor, done = prep(features, low, high, snake_alpha.reshape(1, -1))
+    own, p1, p2, p3, done = weights(at, down_weight, done)
     near = (turn(p3, "chan", -1), turn(p2, "chan", 2), turn(p1, "chan", 1))
-    taps, factor = prep(features, low, high, snake_alpha.reshape(1, -1), done)
 
     place = jnp.stack([core] + [(y + d) % 4 for d in range(4)])
-    out = send(place, taps, gs)
+    out = send(place, taps, gs, done)
     got = turn(out, "core", 1)
-    kept, done = keep(place, taps, gs, got)
+    kept, first, last, done = keep(place, taps, gs, got)
+    edges = beside(last, 1), beside(first, -1)
     arrived = lax.all_to_all(kept, "x", 0, 0)
 
-    held = join(near, done)
+    held = join(near, edges, done)
     far = [turn(h, "core", 1) for h in held]
-    mine, part1, part2, part3, full, first, last, done = encode(
-        core.reshape(1), taps, own, gs, held, far
+    mine, part1, part2, part3, full, done = encode(
+        core.reshape(1), taps, own, held, far
     )
     others = (turn(part1, "chan", 1), turn(part3, "chan", -1), turn(part2, "chan", 2))
-    edges = beside(last, 1), beside(first, -1)
     summed, done = lines(arrived, done)
     spread = lax.all_to_all(summed, "z", 0, 0)
     grad_features, done = input_grad(gs, *edges, full, factor, done)

time: 109 us -> 102 us (0.936)
  local copies, waits for them, and re-layouts: 14.6 us -> 8.62 us
  Pallas kernels: 34.3 us -> 31.1 us
  waiting for transfers between devices: 20.1 us -> 22.3 us
    unnamed x35 -> x41, local copies, waits for them, and re-layouts: 13.8 us -> 7.83 us
    ppermute x4, waiting for transfers between devices: 0.01 us -> 4.95 us  [beside(): return lax.ppermute(value, TM, pairs)]
    all_to_all x1, waiting for transfers between devices: 2.64 us -> 0.01 us  [shards(): spread = lax.all_to_all(summed, 'z', 0, 0)]
    pallas_call x1, Pallas kernels: 2.15 us -> 0.93 us  [total(): call(total_kernel, shape((768, 256)), [VMEM] * 5, 'total', limit=24)]
    pallas_call x1, Pallas kernels: 6.9 us -> 5.71 us  [input_grad(): call(input_grad_kernel, (shape((frames, chans)), TOKEN), [VMEM] * 9, 'inp...]
  transfers between devices with their start and end apart: 19 -> 19, of which waited for: 8 -> 8; matrix products, arithmetic and copies ran while one was open for 1% -> 1% of each run, Pallas kernels for 28% -> 27%
where the time goes in v6:
time: 102 us; the launch traced here: 101 us
  starting transfers between devices  37.4 us (37%)
  Pallas kernels  31.1 us (30%)
  waiting for transfers between devices  22.3 us (22%)
  local copies, waits for them, and re-layouts  8.62 us (8%)
    ppermute x13, waiting for transfers between devices, turn(): lax.ppermute(value, axis, [(i, (i + by) % count) for i in range(count)])  16.6 us
    ppermute x4, starting transfers between devices, beside(): return lax.ppermute(value, TM, pairs)  15.9 us
    ppermute x13, starting transfers between devices, turn(): lax.ppermute(value, axis, [(i, (i + by) % count) for i in range(count)])  13.2 us
    unnamed x41, local copies, waits for them, and re-layouts  7.83 us
    pallas_call x1, Pallas kernels, prep(): call(prep_kernel, (shape((frames // STRIDE, TAPS * chans)), far_shape((fr...  5.88 us
    pallas_call x1, Pallas kernels, input_grad(): call(input_grad_kernel, (shape((frames, chans)), TOKEN), [VMEM] * 9, 'inp...  5.71 us
    pallas_call x1, Pallas kernels, encode(): call(encode_kernel, (far_shape((768, 256), F32),) + (far_shape((768, 256)...  5.01 us
    ppermute x4, waiting for transfers between devices, beside(): return lax.ppermute(value, TM, pairs)  4.95 us
  transfers between devices with their start and end apart: 19, of which 8 were waited for; matrix products, arithmetic and copies ran while one was open for 1% of the time, Pallas kernels for 27%

profile of v6, /device:TPU:2, one launch (start us, length us, event | category | flops | bytes accessed | tf_op | source)
XLA Modules:
  0.0 100.6 jit_solution(2585746340048597364)
XLA Ops:
  0.6 1.7 %collective-permute-start.7 = (bf16[768,256]{1,0:T(8,128)(2,1)}, bf16[768,256]{1,0:T(8,128)(2,1)S(1)}, u32[]{:S(2)}, u32[]{:S(2)}) collective-permute-start(bf16[768,256]{1,0:T(8,128)(2,1)} %g0.5), channel_id=1, source_target_pairs={{0,1},{1,2},{2,3},{3,0},{4,5},{5,6},{6,7},{7,4},{8,9},{9,10},{10,1... | collective-permute-start | bytes 1179656 | tf_op jit(solution)/shard_map/ppermute | solution.py:384
  2.3 2.9 %collective-permute-start.6 = (bf16[768,256]{1,0:T(8,128)(2,1)}, bf16[768,256]{1,0:T(8,128)(2,1)S(1)}, u32[]{:S(2)}, u32[]{:S(2)}) collective-permute-start(bf16[768,256]{1,0:T(8,128)(2,1)} %g0.5), channel_id=1, source_target_pairs={{0,2},{1,3},{2,0},{3,1},{4,6},{5,7},{6,4},{7,5},{8,10},{9,11},{10,... | collective-permute-start | bytes 1179656 | tf_op jit(solution)/shard_map/ppermute | solution.py:384
  5.2 1.3 %collective-permute-start.5 = (bf16[768,256]{1,0:T(8,128)(2,1)}, bf16[768,256]{1,0:T(8,128)(2,1)S(1)}, u32[]{:S(2)}, u32[]{:S(2)}) collective-permute-start(bf16[768,256]{1,0:T(8,128)(2,1)} %g0.5), channel_id=1, source_target_pairs={{0,3},{1,0},{2,1},{3,2},{4,7},{5,4},{6,5},{7,6},{8,11},{9,8},{10,9... | collective-permute-start | bytes 1179656 | tf_op jit(solution)/shard_map/ppermute | solution.py:384
  6.5 0.7 fusion.1
  7.2 6.3 %collective-permute-start.1 = (bf16[16,128]{1,0:T(8,128)(2,1)S(1)}, bf16[16,128]{1,0:T(8,128)(2,1)S(1)}, u32[]{:S(2)}, u32[]{:S(2)}) collective-permute-start(bf16[16,128]{1,0:T(8,128)(2,1)S(1)} %get-tuple-element.53), channel_id=1, source_target_pairs={{4,0},{8,4},{12,8},{16,12},{20,16},{24,20},{28,24},{32,28},{36,32}... | collective-permute-start | bytes 12296 | tf_op jit(solution)/shard_map/ppermute | solution.py:390
  13.6 1.9 %collective-permute-start = (bf16[16,128]{1,0:T(8,128)(2,1)S(1)}, bf16[16,128]{1,0:T(8,128)(2,1)S(1)}, u32[]{:S(2)}, u32[]{:S(2)}) collective-permute-start(bf16[16,128]{1,0:T(8,128)(2,1)S(1)} %get-tuple-element.54), channel_id=1, source_target_pairs={{0,4},{4,8},{8,12},{12,16},{16,20},{20,24},{24,28},{28,32},{32,36}... | collective-permute-start | bytes 12296 | tf_op jit(solution)/shard_map/ppermute | solution.py:390
  15.5 0.1 pad_add_fusion.place
  15.6 0.1 stack.29.place
  15.7 0.0 collective-permute-done.1.high
  15.7 4.9 %collective-permute-done.low = bf16[16,128]{1,0:T(8,128)(2,1)S(1)} collective-permute-done((bf16[16,128]{1,0:T(8,128)(2,1)S(1)}, bf16[16,128]{1,0:T(8,128)(2,1)S(1)}, u32[]{:S(2)}, u32[]{:S(2)}) %collective-permute-start) | collective-permute-done | bytes 4128 | tf_op jit(solution)/shard_map/ppermute | solution.py:390
  20.6 1.4 %copy-done = bf16[6144,128]{1,0:T(8,128)(2,1)S(1)} copy-done((bf16[6144,128]{1,0:T(8,128)(2,1)S(1)}, bf16[6144,128]{1,0:T(8,128)(2,1)}, u32[]{:S(2)}) %copy-start) | copy-done | bytes 1572888
  22.0 0.7 copy-done.13
  22.7 5.9 %prep.1 = (bf16[768,2048]{1,0:T(8,128)(2,1)S(1)}, f32[6144,128]{1,0:T(8,128)}, f32[8,128]{1,0:T(8,128)S(1)}) custom-call(bf16[6144,128]{1,0:T(8,128)(2,1)S(1)} %copy-done, bf16[16,128]{1,0:T(8,128)(2,1)S(1)} %collective-permute-done.low, bf16[16,128]{1,0:T(8,128)(2,1)S(1)} %collective-permute-done.1.high, f32[1,128]{1,0:T(1,128)S(1)} %bitcast.10), custom_call_target="tpu_custom_call" | custom-call | flops 8855000064 | bytes 1000 | tf_op jit(solution)/shard_map/prep/pallas_call | solution.py:130
  28.6 0.0 copy-start.2
  28.6 4.1 %weights.1 = (bf16[2048,256]{1,0:T(8,128)(2,1)}, bf16[1024,256]{1,0:T(8,128)(2,1)S(1)}, bf16[1024,256]{1,0:T(8,128)(2,1)S(1)}, bf16[1024,256]{1,0:T(8,128)(2,1)}, f32[8,128]{1,0:T(8,128)S(1)}) custom-call(s32[2]{0:T(128)S(1)} %pad_add_fusion.place, bf16[512,16,256]{2,1,0:T(8,128)(2,1)S(1)} %copy-done.1, f32[8,128]{1,0:T(8,128)S(1)} %get-tuple-element.29.after), custom_call_target="tpu_custom_call" | custom-call | flops 5059999744 | bytes 1000 | tf_op jit(solution)/shard_map/weights/pallas_call | solution.py:175
  32.7 0.0 collective-permute-done.7.g3
  32.7 0.0 copy-start.3
  32.7 0.0 collective-permute-done.6.g2
  32.7 0.0 collective-permute-done.5.g1
  32.7 3.0 %kernel_grad_send.1 = bf16[512,2048]{1,0:T(8,128)(2,1)S(1)} custom-call(s32[5]{0:T(128)S(1)} %stack.29.place, bf16[768,2048]{1,0:T(8,128)(2,1)S(1)} %get-tuple-element.28.taps, bf16[768,256]{1,0:T(8,128)(2,1)S(1)} %copy-done.2, bf16[768,256]{1,0:T(8,128)(2,1)S(1)} %collective-permute-done.5.g1, bf16[768,256]{1,0:T(8,128)(2,1)S(1)} %collective-permute-done.6.g2, ...), custom_call_target="tpu_custom_call" | custom-call | flops 3795000064 | bytes 1000 | tf_op jit(solution)/shard_map/kernel_grad_send/pallas_call | solution.py:208
  35.7 0.1 collective-permute-start.8
  35.8 0.4 collective-permute-start.2
  36.1 2.5 %collective-permute-start.3 = (bf16[1024,256]{1,0:T(8,128)(2,1)S(1)}, bf16[1024,256]{1,0:T(8,128)(2,1)}, u32[]{:S(2)}, u32[]{:S(2)}) collective-permute-start(bf16[1024,256]{1,0:T(8,128)(2,1)S(1)} %get-tuple-element.32), channel_id=1, source_target_pairs={{0,2},{1,3},{2,0},{3,1},{4,6},{5,7},{6,4},{7,5},{8,10},{9,11},{10,... | collective-permute-start | bytes 1572872 | tf_op jit(solution)/shard_map/ppermute | solution.py:384
  38.6 0.0 collective-permute-start.4
  38.6 1.3 %collective-permute-done.8.got = bf16[512,2048]{1,0:T(8,128)(2,1)S(1)} collective-permute-done((bf16[512,2048]{1,0:T(8,128)(2,1)S(1)}, bf16[512,2048]{1,0:T(8,128)(2,1)S(1)}, u32[]{:S(2)}, u32[]{:S(2)}) %collective-permute-start.8) | collective-permute-done | bytes 2097184 | tf_op jit(solution)/shard_map/ppermute | solution.py:384
  40.0 3.9 %kernel_grad_keep.1 = (bf16[4,128,2048]{2,1,0:T(8,128)(2,1)}, bf16[16,1024]{1,0:T(8,128)(2,1)}, bf16[16,1024]{1,0:T(8,128)(2,1)}, f32[8,128]{1,0:T(8,128)S(1)}) custom-call(s32[5]{0:T(128)S(1)} %stack.29.place, bf16[768,2048]{1,0:T(8,128)(2,1)S(1)} %get-tuple-element.28.taps, bf16[768,256]{1,0:T(8,128)(2,1)S(1)} %copy-done.2, ...), custom_call_target="tpu_custom_call" | custom-call | flops 5059999744 | bytes 1000 | tf_op jit(solution)/shard_map/kernel_grad_keep/pallas_call | solution.py:244
  43.9 4.9 %all-to-all-start = ((bf16[4,128,2048]{2,1,0:T(8,128)(2,1)}), bf16[4,128,2048]{2,1,0:T(8,128)(2,1)S(1)}, u32[]{:S(2)}, u32[]{:S(2)}) async-start(bf16[4,128,2048]{2,1,0:T(8,128)(2,1)} %get-tuple-element.47), calls=%async_computation | async-start | bytes 4194304 | tf_op jit(solution)/shard_map/all_to_all | solution.py:414
  48.7 1.9 %collective-permute-start.9 = (bf16[16,1024]{1,0:T(8,128)(2,1)}, bf16[16,1024]{1,0:T(8,128)(2,1)S(1)}, u32[]{:S(2)}, u32[]{:S(2)}) collective-permute-start(bf16[16,1024]{1,0:T(8,128)(2,1)} %get-tuple-element.35), channel_id=1, source_target_pairs={{0,4},{4,8},{8,12},{12,16},{16,20},{20,24},{24,28},{28,32},{32,36}... | collective-permute-start | bytes 98312 | tf_op jit(solution)/shard_map/ppermute | solution.py:390
  50.6 5.8 %collective-permute-start.10 = (bf16[16,1024]{1,0:T(8,128)(2,1)}, bf16[16,1024]{1,0:T(8,128)(2,1)S(1)}, u32[]{:S(2)}, u32[]{:S(2)}) collective-permute-start(bf16[16,1024]{1,0:T(8,128)(2,1)} %get-tuple-element.36), channel_id=1, source_target_pairs={{4,0},{8,4},{12,8},{16,12},{20,16},{24,20},{28,24},{32,28},{36,32}... | collective-permute-start | bytes 98312 | tf_op jit(solution)/shard_map/ppermute | solution.py:390
  56.4 0.0 collective-permute-done.2.a1
  56.4 0.0 collective-permute-done.3.a2
  56.4 6.6 %collective-permute-done.4.a3 = bf16[1024,256]{1,0:T(8,128)(2,1)} collective-permute-done((bf16[1024,256]{1,0:T(8,128)(2,1)S(1)}, bf16[1024,256]{1,0:T(8,128)(2,1)}, u32[]{:S(2)}, u32[]{:S(2)}) %collective-permute-start.4) | collective-permute-done | bytes 524320 | tf_op jit(solution)/shard_map/ppermute | solution.py:384
  63.0 0.0 collective-permute-done.9.low
  63.0 0.0 collective-permute-done.10.high
  63.0 0.0 copy-start.11
  63.0 0.0 copy-start.16
  63.0 0.0 copy-start.19
  63.0 1.6 %join.1 = (bf16[1024,256]{1,0:T(8,128)(2,1)S(1)}, bf16[1024,256]{1,0:T(8,128)(2,1)S(1)}, bf16[1024,256]{1,0:T(8,128)(2,1)S(1)}) custom-call(bf16[1024,256]{1,0:T(8,128)(2,1)} %collective-permute-done.2.a1, bf16[1024,256]{1,0:T(8,128)(2,1)} %collective-permute-done.3.a2, bf16[1024,256]{1,0:T(8,128)(2,1)} %collective-permute-done.4.a3, ...), custom_call_target="tpu_custom_call" | custom-call | flops 1264999936 | bytes 1000 | tf_op jit(solution)/shard_map/join/pallas_call | solution.py:266
  64.7 0.1 collective-permute-start.11
  64.8 0.5 collective-permute-start.12
  65.3 0.1 collective-permute-start.13
  65.4 1.3 %collective-permute-done.11.b1 = bf16[1024,256]{1,0:T(8,128)(2,1)S(1)} collective-permute-done((bf16[1024,256]{1,0:T(8,128)(2,1)S(1)}, bf16[1024,256]{1,0:T(8,128)(2,1)S(1)}, u32[]{:S(2)}, u32[]{:S(2)}) %collective-permute-start.11) | collective-permute-done | bytes 524320 | tf_op jit(solution)/shard_map/ppermute | solution.py:384
  66.7 0.7 collective-permute-done.12.b2
  67.4 0.7 collective-permute-done.13.b3
  68.2 0.0 copy-done.19
  68.2 5.0 %encode.1 = (f32[768,256]{1,0:T(8,128)}, bf16[768,256]{1,0:T(8,128)(2,1)}, bf16[768,256]{1,0:T(8,128)(2,1)}, bf16[768,256]{1,0:T(8,128)(2,1)}, bf16[2048,1024]{1,0:T(8,128)(2,1)}, /*index=5*/f32[8,128]{1,0:T(8,128)S(1)}) custom-call(s32[1]{0:T(128)} %bitcast.core, bf16[768,2048]{1,0:T(8,128)(2,1)S(1)} %copy-done.16, bf16[2048,256]{1,0:T(8,128)(2,1)S(1)} %copy-done.19, ...), custom_call_target="tpu_custom_call" | custom-call | flops 6325000192 | bytes 1000 | tf_op jit(solution)/shard_map/encode/pallas_call | solution.py:298
  73.2 0.7 all-to-all-done.parts
  73.9 1.1 %lines.1 = (bf16[8,16,2048]{2,1,0:T(8,128)(2,1)}, f32[8,128]{1,0:T(8,128)S(1)}) custom-call(bf16[4,128,2048]{2,1,0:T(8,128)(2,1)S(1)} %all-to-all-done.parts, f32[8,128]{1,0:T(8,128)S(1)} %get-tuple-element.48.after), custom_call_target="tpu_custom_call" | custom-call | flops 1264999936 | bytes 1000 | tf_op jit(solution)/shard_map/lines/pallas_call | solution.py:323
  75.0 3.5 %all-to-all-start.1 = ((bf16[8,16,2048]{2,1,0:T(8,128)(2,1)}), bf16[8,16,2048]{2,1,0:T(8,128)(2,1)S(1)}, u32[]{:S(2)}, u32[]{:S(2)}) async-start(bf16[8,16,2048]{2,1,0:T(8,128)(2,1)} %get-tuple-element.52), calls=%async_computation.1 | async-start | bytes 1048576 | tf_op jit(solution)/shard_map/all_to_all | solution.py:423
  78.5 0.8 collective-permute-start.14
  79.2 2.6 %collective-permute-start.15 = (bf16[768,256]{1,0:T(8,128)(2,1)}, bf16[768,256]{1,0:T(8,128)(2,1)S(1)}, u32[]{:S(2)}, u32[]{:S(2)}) collective-permute-start(bf16[768,256]{1,0:T(8,128)(2,1)} %get-tuple-element.43), channel_id=1, source_target_pairs={{0,3},{1,0},{2,1},{3,2},{4,7},{5,4},{6,5},{7,6},{8,11},{9,8},{10,9... | collective-permute-start | bytes 1179656 | tf_op jit(solution)/shard_map/ppermute | solution.py:384
  81.8 0.4 collective-permute-start.16
  82.2 0.0 copy-done.6
  82.2 1.0 copy-done.8
  83.2 2.2 %copy-done.17 = bf16[2048,1024]{1,0:T(8,128)(2,1)S(1)} copy-done((bf16[2048,1024]{1,0:T(8,128)(2,1)S(1)}, bf16[2048,1024]{1,0:T(8,128)(2,1)}, u32[]{:S(2)}) %copy-start.17) | copy-done | bytes 4194328
  85.4 1.9 %copy-done.18 = f32[6144,128]{1,0:T(8,128)S(1)} copy-done((f32[6144,128]{1,0:T(8,128)S(1)}, f32[6144,128]{1,0:T(8,128)}, u32[]{:S(2)}) %copy-start.18) | copy-done | bytes 3145752
  87.2 5.7 %input_grad.1 = (bf16[6144,128]{1,0:T(8,128)(2,1)}, f32[8,128]{1,0:T(8,128)S(1)}) custom-call(bf16[768,256]{1,0:T(8,128)(2,1)S(1)} %copy-done.2, bf16[768,256]{1,0:T(8,128)(2,1)S(1)} %copy-done.8, bf16[768,256]{1,0:T(8,128)(2,1)S(1)} %copy-done.6, bf16[768,256]{1,0:T(8,128)(2,1)S(1)} %copy-done.4, bf16[16,1024]{1,0:T(8,128)(2,1)S(1)} %copy-done.10, ...), custom_call_target="tpu_custom_call" | custom-call | flops 7590000128 | bytes 1000 | tf_op jit(solution)/shard_map/input_grad/pallas_call | solution.py:360
  93.0 5.9 %collective-permute-done.14.a1 = bf16[768,256]{1,0:T(8,128)(2,1)S(1)} collective-permute-done((bf16[768,256]{1,0:T(8,128)(2,1)}, bf16[768,256]{1,0:T(8,128)(2,1)S(1)}, u32[]{:S(2)}, u32[]{:S(2)}) %collective-permute-start.14) | collective-permute-done | bytes 393248 | tf_op jit(solution)/shard_map/ppermute | solution.py:384
  98.9 0.0 collective-permute-done.15.a2
  98.9 0.0 collective-permute-done.16.a3
  98.9 0.9 total.1
  99.8 0.0 all-to-all-done.1
  99.8 0.1 convert_reduce_fusion
  99.9 0.6 copy.7
  (29 shorter events, 0.1 us)
Async XLA Ops:
  0.6 32.0 %collective-permute-start.7 = (bf16[768,256]{1,0:T(8,128)(2,1)}, bf16[768,256]{1,0:T(8,128)(2,1)S(1)}, u32[]{:S(2)}, u32[]{:S(2)}) collective-permute-start(bf16[768,256]{1,0:T(8,128)(2,1)} %g0.5), channel_id=1, source_target_pairs={{0,1},{1,2},{2,3},{3,0},{4,5},{5,6},{6,7},{7,4},{8,9},{9,10},{10,1... | collective-permute-start | bytes 1179656 | tf_op jit(solution)/shard_map/ppermute | solution.py:384
  2.3 30.4 %collective-permute-start.6 = (bf16[768,256]{1,0:T(8,128)(2,1)}, bf16[768,256]{1,0:T(8,128)(2,1)S(1)}, u32[]{:S(2)}, u32[]{:S(2)}) collective-permute-start(bf16[768,256]{1,0:T(8,128)(2,1)} %g0.5), channel_id=1, source_target_pairs={{0,2},{1,3},{2,0},{3,1},{4,6},{5,7},{6,4},{7,5},{8,10},{9,11},{10,... | collective-permute-start | bytes 1179656 | tf_op jit(solution)/shard_map/ppermute | solution.py:384
  5.2 27.5 %collective-permute-start.5 = (bf16[768,256]{1,0:T(8,128)(2,1)}, bf16[768,256]{1,0:T(8,128)(2,1)S(1)}, u32[]{:S(2)}, u32[]{:S(2)}) collective-permute-start(bf16[768,256]{1,0:T(8,128)(2,1)} %g0.5), channel_id=1, source_target_pairs={{0,3},{1,0},{2,1},{3,2},{4,7},{5,4},{6,5},{7,6},{8,11},{9,8},{10,9... | collective-permute-start | bytes 1179656 | tf_op jit(solution)/shard_map/ppermute | solution.py:384
  7.2 8.4 %collective-permute-start.1 = (bf16[16,128]{1,0:T(8,128)(2,1)S(1)}, bf16[16,128]{1,0:T(8,128)(2,1)S(1)}, u32[]{:S(2)}, u32[]{:S(2)}) collective-permute-start(bf16[16,128]{1,0:T(8,128)(2,1)S(1)} %get-tuple-element.53), channel_id=1, source_target_pairs={{4,0},{8,4},{12,8},{16,12},{20,16},{24,20},{28,24},{32,28},{36,32}... | collective-permute-start | bytes 12296 | tf_op jit(solution)/shard_map/ppermute | solution.py:390
  13.6 7.0 %collective-permute-start = (bf16[16,128]{1,0:T(8,128)(2,1)S(1)}, bf16[16,128]{1,0:T(8,128)(2,1)S(1)}, u32[]{:S(2)}, u32[]{:S(2)}) collective-permute-start(bf16[16,128]{1,0:T(8,128)(2,1)S(1)} %get-tuple-element.54), channel_id=1, source_target_pairs={{0,4},{4,8},{8,12},{12,16},{16,20},{20,24},{24,28},{28,32},{32,36}... | collective-permute-start | bytes 12296 | tf_op jit(solution)/shard_map/ppermute | solution.py:390
  20.6 1.4 %copy-start = (bf16[6144,128]{1,0:T(8,128)(2,1)S(1)}, bf16[6144,128]{1,0:T(8,128)(2,1)}, u32[]{:S(2)}) copy-start(bf16[6144,128]{1,0:T(8,128)(2,1)} %feat.1) | copy-start | bytes 4718596
  22.0 0.7 copy-start.13
  22.7 5.9 %copy-start.1 = (bf16[512,16,256]{2,1,0:T(8,128)(2,1)S(1)}, bf16[512,16,256]{2,1,0:T(8,128)(2,1)}, u32[]{:S(2)}) copy-start(bf16[512,16,256]{2,1,0:T(8,128)(2,1)} %whole.1) | copy-start | bytes 12582916
  28.6 11.4 %copy-start.15 = (bf16[768,2048]{1,0:T(8,128)(2,1)}, bf16[768,2048]{1,0:T(8,128)(2,1)S(1)}, u32[]{:S(2)}) copy-start(bf16[768,2048]{1,0:T(8,128)(2,1)S(1)} %get-tuple-element.28.taps) | copy-start | bytes 9437188
  28.6 4.1 %copy-start.2 = (bf16[768,256]{1,0:T(8,128)(2,1)S(1)}, bf16[768,256]{1,0:T(8,128)(2,1)}, u32[]{:S(2)}) copy-start(bf16[768,256]{1,0:T(8,128)(2,1)} %g0.5) | copy-start | bytes 1179652
  32.7 7.3 %copy-start.3 = (bf16[768,256]{1,0:T(8,128)(2,1)}, bf16[768,256]{1,0:T(8,128)(2,1)S(1)}, u32[]{:S(2)}) copy-start(bf16[768,256]{1,0:T(8,128)(2,1)S(1)} %collective-permute-done.7.g3) | copy-start | bytes 1179652
  32.7 7.3 %copy-start.5 = (bf16[768,256]{1,0:T(8,128)(2,1)}, bf16[768,256]{1,0:T(8,128)(2,1)S(1)}, u32[]{:S(2)}) copy-start(bf16[768,256]{1,0:T(8,128)(2,1)S(1)} %collective-permute-done.6.g2) | copy-start | bytes 1179652
  32.7 7.2 %copy-start.7 = (bf16[768,256]{1,0:T(8,128)(2,1)}, bf16[768,256]{1,0:T(8,128)(2,1)S(1)}, u32[]{:S(2)}) copy-start(bf16[768,256]{1,0:T(8,128)(2,1)S(1)} %collective-permute-done.5.g1) | copy-start | bytes 1179652
  35.7 4.2 %collective-permute-start.8 = (bf16[512,2048]{1,0:T(8,128)(2,1)S(1)}, bf16[512,2048]{1,0:T(8,128)(2,1)S(1)}, u32[]{:S(2)}, u32[]{:S(2)}) collective-permute-start(bf16[512,2048]{1,0:T(8,128)(2,1)S(1)} %kernel_grad_send.1), channel_id=1, source_target_pairs={{0,4},{4,0},{1,5},{5,1},{2,6},{6,2},{3,7},{7,3},{8,12},{12,8},{9,1... | collective-permute-start | bytes 6291464 | tf_op jit(solution)/shard_map/ppermute | solution.py:384
  35.8 20.6 %collective-permute-start.2 = (bf16[1024,256]{1,0:T(8,128)(2,1)}, bf16[1024,256]{1,0:T(8,128)(2,1)}, u32[]{:S(2)}, u32[]{:S(2)}) collective-permute-start(bf16[1024,256]{1,0:T(8,128)(2,1)} %get-tuple-element.31), channel_id=1, source_target_pairs={{0,3},{1,0},{2,1},{3,2},{4,7},{5,4},{6,5},{7,6},{8,11},{9,8},{10,9... | collective-permute-start | bytes 1572872 | tf_op jit(solution)/shard_map/ppermute | solution.py:384
  36.1 20.3 %collective-permute-start.3 = (bf16[1024,256]{1,0:T(8,128)(2,1)S(1)}, bf16[1024,256]{1,0:T(8,128)(2,1)}, u32[]{:S(2)}, u32[]{:S(2)}) collective-permute-start(bf16[1024,256]{1,0:T(8,128)(2,1)S(1)} %get-tuple-element.32), channel_id=1, source_target_pairs={{0,2},{1,3},{2,0},{3,1},{4,6},{5,7},{6,4},{7,5},{8,10},{9,11},{10,... | collective-permute-start | bytes 1572872 | tf_op jit(solution)/shard_map/ppermute | solution.py:384
  38.6 24.4 %collective-permute-start.4 = (bf16[1024,256]{1,0:T(8,128)(2,1)S(1)}, bf16[1024,256]{1,0:T(8,128)(2,1)}, u32[]{:S(2)}, u32[]{:S(2)}) collective-permute-start(bf16[1024,256]{1,0:T(8,128)(2,1)S(1)} %get-tuple-element.33), channel_id=1, source_target_pairs={{0,1},{1,2},{2,3},{3,0},{4,5},{5,6},{6,7},{7,4},{8,9},{9,10},{10,1... | collective-permute-start | bytes 1572872 | tf_op jit(solution)/shard_map/ppermute | solution.py:384
  43.9 30.0 %all-to-all-start = ((bf16[4,128,2048]{2,1,0:T(8,128)(2,1)}), bf16[4,128,2048]{2,1,0:T(8,128)(2,1)S(1)}, u32[]{:S(2)}, u32[]{:S(2)}) async-start(bf16[4,128,2048]{2,1,0:T(8,128)(2,1)} %get-tuple-element.47), calls=%async_computation | async-start | bytes 4194304 | tf_op jit(solution)/shard_map/all_to_all | solution.py:414
  48.7 14.3 %collective-permute-start.9 = (bf16[16,1024]{1,0:T(8,128)(2,1)}, bf16[16,1024]{1,0:T(8,128)(2,1)S(1)}, u32[]{:S(2)}, u32[]{:S(2)}) collective-permute-start(bf16[16,1024]{1,0:T(8,128)(2,1)} %get-tuple-element.35), channel_id=1, source_target_pairs={{0,4},{4,8},{8,12},{12,16},{16,20},{20,24},{24,28},{28,32},{32,36}... | collective-permute-start | bytes 98312 | tf_op jit(solution)/shard_map/ppermute | solution.py:390
  50.6 12.4 %collective-permute-start.10 = (bf16[16,1024]{1,0:T(8,128)(2,1)}, bf16[16,1024]{1,0:T(8,128)(2,1)S(1)}, u32[]{:S(2)}, u32[]{:S(2)}) collective-permute-start(bf16[16,1024]{1,0:T(8,128)(2,1)} %get-tuple-element.36), channel_id=1, source_target_pairs={{4,0},{8,4},{12,8},{16,12},{20,16},{24,20},{28,24},{32,28},{36,32}... | collective-permute-start | bytes 98312 | tf_op jit(solution)/shard_map/ppermute | solution.py:390
  63.0 1.7 %copy-start.9 = (bf16[16,1024]{1,0:T(8,128)(2,1)}, bf16[16,1024]{1,0:T(8,128)(2,1)S(1)}, u32[]{:S(2)}) copy-start(bf16[16,1024]{1,0:T(8,128)(2,1)S(1)} %collective-permute-done.9.low) | copy-start | bytes 98308
  63.0 1.7 %copy-start.11 = (bf16[16,1024]{1,0:T(8,128)(2,1)}, bf16[16,1024]{1,0:T(8,128)(2,1)S(1)}, u32[]{:S(2)}) copy-start(bf16[16,1024]{1,0:T(8,128)(2,1)S(1)} %collective-permute-done.10.high) | copy-start | bytes 98308
  63.0 5.2 %copy-start.16 = (bf16[768,2048]{1,0:T(8,128)(2,1)S(1)}, bf16[768,2048]{1,0:T(8,128)(2,1)}, u32[]{:S(2)}) copy-start(bf16[768,2048]{1,0:T(8,128)(2,1)} %copy-done.15) | copy-start | bytes 9437188
  63.0 5.2 %copy-start.19 = (bf16[2048,256]{1,0:T(8,128)(2,1)S(1)}, bf16[2048,256]{1,0:T(8,128)(2,1)}, u32[]{:S(2)}) copy-start(bf16[2048,256]{1,0:T(8,128)(2,1)} %get-tuple-element.30.own) | copy-start | bytes 3145732
  64.7 2.0 %collective-permute-start.11 = (bf16[1024,256]{1,0:T(8,128)(2,1)S(1)}, bf16[1024,256]{1,0:T(8,128)(2,1)S(1)}, u32[]{:S(2)}, u32[]{:S(2)}) collective-permute-start(bf16[1024,256]{1,0:T(8,128)(2,1)S(1)} %get-tuple-element.38.a1), channel_id=1, source_target_pairs={{0,4},{4,0},{1,5},{5,1},{2,6},{6,2},{3,7},{7,3},{8,12},{12,8},{9,1... | collective-permute-start | bytes 1572872 | tf_op jit(solution)/shard_map/ppermute | solution.py:384
  64.8 2.6 %collective-permute-start.12 = (bf16[1024,256]{1,0:T(8,128)(2,1)S(1)}, bf16[1024,256]{1,0:T(8,128)(2,1)S(1)}, u32[]{:S(2)}, u32[]{:S(2)}) collective-permute-start(bf16[1024,256]{1,0:T(8,128)(2,1)S(1)} %get-tuple-element.39.a2), channel_id=1, source_target_pairs={{0,4},{4,0},{1,5},{5,1},{2,6},{6,2},{3,7},{7,3},{8,12},{12,8},{9,1... | collective-permute-start | bytes 1572872 | tf_op jit(solution)/shard_map/ppermute | solution.py:384
  65.3 2.9 %collective-permute-start.13 = (bf16[1024,256]{1,0:T(8,128)(2,1)S(1)}, bf16[1024,256]{1,0:T(8,128)(2,1)S(1)}, u32[]{:S(2)}, u32[]{:S(2)}) collective-permute-start(bf16[1024,256]{1,0:T(8,128)(2,1)S(1)} %get-tuple-element.40.a3), channel_id=1, source_target_pairs={{0,4},{4,0},{1,5},{5,1},{2,6},{6,2},{3,7},{7,3},{8,12},{12,8},{9,1... | collective-permute-start | bytes 1572872 | tf_op jit(solution)/shard_map/ppermute | solution.py:384
  73.9 8.3 %copy-start.4 = (bf16[768,256]{1,0:T(8,128)(2,1)S(1)}, bf16[768,256]{1,0:T(8,128)(2,1)}, u32[]{:S(2)}) copy-start(bf16[768,256]{1,0:T(8,128)(2,1)} %copy-done.3) | copy-start | bytes 1179652
  73.9 8.3 %copy-start.6 = (bf16[768,256]{1,0:T(8,128)(2,1)S(1)}, bf16[768,256]{1,0:T(8,128)(2,1)}, u32[]{:S(2)}) copy-start(bf16[768,256]{1,0:T(8,128)(2,1)} %copy-done.5) | copy-start | bytes 1179652
  73.9 8.3 %copy-start.10 = (bf16[16,1024]{1,0:T(8,128)(2,1)S(1)}, bf16[16,1024]{1,0:T(8,128)(2,1)}, u32[]{:S(2)}) copy-start(bf16[16,1024]{1,0:T(8,128)(2,1)} %copy-done.9) | copy-start | bytes 98308
  73.9 8.3 %copy-start.12 = (bf16[16,1024]{1,0:T(8,128)(2,1)S(1)}, bf16[16,1024]{1,0:T(8,128)(2,1)}, u32[]{:S(2)}) copy-start(bf16[16,1024]{1,0:T(8,128)(2,1)} %copy-done.11) | copy-start | bytes 98308
  75.0 24.9 %all-to-all-start.1 = ((bf16[8,16,2048]{2,1,0:T(8,128)(2,1)}), bf16[8,16,2048]{2,1,0:T(8,128)(2,1)S(1)}, u32[]{:S(2)}, u32[]{:S(2)}) async-start(bf16[8,16,2048]{2,1,0:T(8,128)(2,1)} %get-tuple-element.52), calls=%async_computation.1 | async-start | bytes 1048576 | tf_op jit(solution)/shard_map/all_to_all | solution.py:423
  78.5 20.4 %collective-permute-start.14 = (bf16[768,256]{1,0:T(8,128)(2,1)}, bf16[768,256]{1,0:T(8,128)(2,1)S(1)}, u32[]{:S(2)}, u32[]{:S(2)}) collective-permute-start(bf16[768,256]{1,0:T(8,128)(2,1)} %get-tuple-element.42), channel_id=1, source_target_pairs={{0,1},{1,2},{2,3},{3,0},{4,5},{5,6},{6,7},{7,4},{8,9},{9,10},{10,1... | collective-permute-start | bytes 1179656 | tf_op jit(solution)/shard_map/ppermute | solution.py:384
  79.2 19.7 %collective-permute-start.15 = (bf16[768,256]{1,0:T(8,128)(2,1)}, bf16[768,256]{1,0:T(8,128)(2,1)S(1)}, u32[]{:S(2)}, u32[]{:S(2)}) collective-permute-start(bf16[768,256]{1,0:T(8,128)(2,1)} %get-tuple-element.43), channel_id=1, source_target_pairs={{0,3},{1,0},{2,1},{3,2},{4,7},{5,4},{6,5},{7,6},{8,11},{9,8},{10,9... | collective-permute-start | bytes 1179656 | tf_op jit(solution)/shard_map/ppermute | solution.py:384
  81.8 17.1 %collective-permute-start.16 = (bf16[768,256]{1,0:T(8,128)(2,1)}, bf16[768,256]{1,0:T(8,128)(2,1)S(1)}, u32[]{:S(2)}, u32[]{:S(2)}) collective-permute-start(bf16[768,256]{1,0:T(8,128)(2,1)} %get-tuple-element.44), channel_id=1, source_target_pairs={{0,2},{1,3},{2,0},{3,1},{4,6},{5,7},{6,4},{7,5},{8,10},{9,11},{10,... | collective-permute-start | bytes 1179656 | tf_op jit(solution)/shard_map/ppermute | solution.py:384
  82.2 1.0 copy-start.8
  83.2 2.2 %copy-start.17 = (bf16[2048,1024]{1,0:T(8,128)(2,1)S(1)}, bf16[2048,1024]{1,0:T(8,128)(2,1)}, u32[]{:S(2)}) copy-start(bf16[2048,1024]{1,0:T(8,128)(2,1)} %get-tuple-element.45.weights) | copy-start | bytes 12582916
  85.4 1.9 %copy-start.18 = (f32[6144,128]{1,0:T(8,128)S(1)}, f32[6144,128]{1,0:T(8,128)}, u32[]{:S(2)}) copy-start(f32[6144,128]{1,0:T(8,128)} %get-tuple-element.46.factor) | copy-start | bytes 9437188
  87.2 11.7 %copy-start.14 = (f32[768,256]{1,0:T(8,128)S(1)}, f32[768,256]{1,0:T(8,128)}, u32[]{:S(2)}) copy-start(f32[768,256]{1,0:T(8,128)} %get-tuple-element.41.own) | copy-start | bytes 2359300

commit v7 on v6

--- a/solution.py
+++ b/solution.py
@@ -28,6 +28,7 @@
 PI_B = math.pi - PI_A
 VMEM = pl.BlockSpec(memory_space=pltpu.VMEM)
 SMEM = pl.BlockSpec(memory_space=pltpu.SMEM)
+ANY = pl.BlockSpec(memory_space=pl.ANY)
 HBM = pl.BlockSpec(memory_space=pltpu.HBM)
 NN = (((1,), (0,)), ((), ()))
 NT = (((1,), (1,)), ((), ()))
@@ -37,7 +38,7 @@
     return lax.dot_general(lhs, rhs, dims, preferred_element_type=F32)
 
 
-def call(kernel, outs, specs, name, scratch=(), limit=24, out_specs=None):
+def call(kernel, outs, specs, name, scratch=(), limit=24, out_specs=None, aliases=None):
     return pl.pallas_call(
         kernel,
         out_shape=outs,
@@ -47,6 +48,7 @@
         compiler_params=pltpu.CompilerParams(vmem_limit_bytes=limit * 2**20),
         cost_estimate=pl.CostEstimate(flops=int(TIME[name] * FACTOR * 1.15e9), bytes_accessed=1000, transcendentals=0),
         name=name,
+        input_output_aliases=aliases or {},
     )
 
 
@@ -89,7 +91,7 @@
     return r * poly(SIN, z), poly(COS, z)
 
 
-def prep_kernel(feat, low, high, alpha, taps, factor, done, rows, held, sem):
+def prep_kernel(feat, low, high, alpha, after, taps, factor, rows, held, sem):
     frames = feat.shape[0]
     a = alpha[...]
     inv = 1.0 / a
@@ -120,29 +122,28 @@
     outs = frames // STRIDE
     for k in range(TAPS):
         taps[:, k * 128 : (k + 1) * 128] = rows[pl.ds(4 + k, outs, stride=STRIDE), :].astype(BF)
-    done[...] = jnp.zeros(done.shape, F32)
     for c in copies:
         c.wait()
 
 
-def prep(feat, low, high, alpha):
+def prep(feat, low, high, alpha, after):
     frames, chans = feat.shape
     return call(
         prep_kernel,
-        (shape((frames // STRIDE, TAPS * chans)), far_shape((frames, chans), F32), TOKEN),
-        [VMEM] * 4,
+        (shape((frames // STRIDE, TAPS * chans)), far_shape((frames, chans), F32)),
+        [VMEM] * 5,
         "prep",
         [
             pltpu.VMEM((frames + 16, chans), F32),
             pltpu.VMEM((frames, chans), F32),
             pltpu.SemaphoreType.DMA((4,)),
         ],
-        out_specs=(VMEM, HBM, VMEM),
-    )(feat, low, high, alpha)
+        out_specs=(VMEM, HBM),
+    )(feat, low, high, alpha, after)
 
 
 def weights_kernel(
-    place, whole, after, own, p1, p2, p3, done, buf, rows, held, sem, out_sem
+    place, whole, own, p1, p2, p3, done, buf, rows, held, sem, out_sem
 ):
     y, core = place[0], place[1]
     copies = [
@@ -171,11 +172,11 @@
     done[...] = jnp.zeros(done.shape, F32)
 
 
-def weights(place, whole, after):
+def weights(place, whole):
     return call(
         weights_kernel,
         (far_shape((2048, 256)),) + (shape((1024, 256)),) * 3 + (TOKEN,),
-        [SMEM, HBM, VMEM],
+        [SMEM, HBM],
         "weights",
         [
             pltpu.VMEM((4, 128, TAPS, 256), BF),
@@ -185,7 +186,7 @@
             pltpu.SemaphoreType.DMA,
         ],
         out_specs=(HBM,) + (VMEM,) * 4,
-    )(place, whole, after)
+    )(place, whole)
 
 
 def choose(gs, which, order, lhs):
@@ -198,21 +199,21 @@
         lhs[pl.ds(at, 128), :] = mul(pick, g[...], NT).astype(BF)
 
 
-def send_kernel(place, taps, g0, g1, g2, g3, after, out, lhs):
+def send_kernel(place, taps, g0, g1, g2, g3, out, lhs):
     choose((g0, g1, g2, g3), 1 - place[0], [place[1 + d] for d in range(4)], lhs)
     for n in range(0, 2048, 256):
         out[:, n : n + 256] = mul(lhs[...], taps[:, n : n + 256]).astype(BF)
 
 
-def send(place, taps, gs, after):
+def send(place, taps, gs):
     return call(
         send_kernel,
         shape((512, 2048)),
-        [SMEM] + [VMEM] * 6,
+        [SMEM] + [VMEM] * 5,
         "kernel_grad_send",
         [pltpu.VMEM((512, 768), BF)],
         limit=24,
-    )(place, taps, *gs, after)
+    )(place, taps, *gs)
 
 
 def keep_kernel(place, taps, g0, g1, g2, g3, got, out, first, last, done, lhs, held, ends, sem):
@@ -257,13 +258,19 @@
     )(place, taps, *gs, got)
 
 
-def join_kernel(a1, a2, a3, low, high, after, o1, o2, o3):
-    for a, out in ((a1, o1), (a2, o2), (a3, o3)):
-        out[...] = a[...]
+def join_kernel(*refs):
+    del refs
 
 
 def join(near, edges, after):
-    return call(join_kernel, (shape((1024, 256)),) * 3, [VMEM] * 6, "join", limit=24)(*near, *edges, after)
+    return call(
+        join_kernel,
+        (shape((1024, 256)),) * 3,
+        [ANY] * 6,
+        "join",
+        out_specs=(ANY,) * 3,
+        aliases={0: 0, 1: 1, 2: 2},
+    )(*near, *edges, after)
 
 
 def encode_kernel(
@@ -402,12 +409,12 @@
     low, high = beside(features[-16:], 1), beside(features[:16], -1)
 
     at = jnp.stack([y, core])
-    taps, factor, done = prep(features, low, high, snake_alpha.reshape(1, -1))
-    own, p1, p2, p3, done = weights(at, down_weight, done)
+    own, p1, p2, p3, done = weights(at, down_weight)
+    taps, factor = prep(features, low, high, snake_alpha.reshape(1, -1), done)
     near = (turn(p3, "chan", -1), turn(p2, "chan", 2), turn(p1, "chan", 1))
 
     place = jnp.stack([core] + [(y + d) % 4 for d in range(4)])
-    out = send(place, taps, gs, done)
+    out = send(place, taps, gs)
     got = turn(out, "core", 1)
     kept, first, last, done = keep(place, taps, gs, got)
     edges = beside(last, 1), beside(first, -1)

time: 102 us -> 100 us (0.980)
  waiting for transfers between devices: 22.3 us -> 16.9 us
  Pallas kernels: 31.1 us -> 33.8 us
  starting transfers between devices: 37.4 us -> 39.1 us
    ppermute x4, waiting for transfers between devices: 4.95 us -> 0.01 us  [beside(): return lax.ppermute(value, TM, pairs)]
    all_to_all x1, starting transfers between devices: 3.49 us -> 5.74 us  [shards(): spread = lax.all_to_all(summed, 'z', 0, 0)]
    pallas_call x1, Pallas kernels: 5.01 us -> 6.34 us  [encode(): call(encode_kernel, (far_shape((768, 256), F32),) + (far_shape((768, 256)...]
    pallas_call x1, Pallas kernels: 5.71 us -> 6.91 us  [input_grad(): call(input_grad_kernel, (shape((frames, chans)), TOKEN), [VMEM] * 9, 'inp...]
    unnamed x41 -> x33, local copies, waits for them, and re-layouts: 7.83 us -> 7.53 us
  transfers between devices with their start and end apart: 19 -> 19, of which waited for: 8 -> 7; matrix products, arithmetic and copies ran while one was open for 1% -> 1% of each run, Pallas kernels for 27% -> 29%
where the time goes in v7:
time: 100 us; the launch traced here: 99.2 us
  starting transfers between devices  39.1 us (39%)
  Pallas kernels  33.8 us (34%)
  waiting for transfers between devices  16.9 us (17%)
  local copies, waits for them, and re-layouts  8.32 us (8%)
    ppermute x13, waiting for transfers between devices, turn(): lax.ppermute(value, axis, [(i, (i + by) % count) for i in range(count)])  16 us
    ppermute x4, starting transfers between devices, beside(): return lax.ppermute(value, TM, pairs)  15.9 us
    ppermute x13, starting transfers between devices, turn(): lax.ppermute(value, axis, [(i, (i + by) % count) for i in range(count)])  12.6 us
    unnamed x33, local copies, waits for them, and re-layouts  7.53 us
    pallas_call x1, Pallas kernels, input_grad(): call(input_grad_kernel, (shape((frames, chans)), TOKEN), [VMEM] * 9, 'inp...  6.91 us
    pallas_call x1, Pallas kernels, encode(): call(encode_kernel, (far_shape((768, 256), F32),) + (far_shape((768, 256)...  6.34 us
    pallas_call x1, Pallas kernels, prep(): call(prep_kernel, (shape((frames // STRIDE, TAPS * chans)), far_shape((fr...  5.88 us
    all_to_all x1, starting transfers between devices, shards(): spread = lax.all_to_all(summed, 'z', 0, 0)  5.74 us
  transfers between devices with their start and end apart: 19, of which 7 were waited for; matrix products, arithmetic and copies ran while one was open for 1% of the time, Pallas kernels for 29%

profile of v7, /device:TPU:2, one launch (start us, length us, event | category | flops | bytes accessed | tf_op | source)
XLA Modules:
  0.0 99.2 jit_solution(10699319074397999457)
XLA Ops:
  0.6 1.7 %collective-permute-start.7 = (bf16[768,256]{1,0:T(8,128)(2,1)}, bf16[768,256]{1,0:T(8,128)(2,1)S(1)}, u32[]{:S(2)}, u32[]{:S(2)}) collective-permute-start(bf16[768,256]{1,0:T(8,128)(2,1)} %g0.5), channel_id=1, source_target_pairs={{0,1},{1,2},{2,3},{3,0},{4,5},{5,6},{6,7},{7,4},{8,9},{9,10},{10,1... | collective-permute-start | bytes 1179656 | tf_op jit(solution)/shard_map/ppermute | solution.py:391
  2.3 2.9 %collective-permute-start.6 = (bf16[768,256]{1,0:T(8,128)(2,1)}, bf16[768,256]{1,0:T(8,128)(2,1)}, u32[]{:S(2)}, u32[]{:S(2)}) collective-permute-start(bf16[768,256]{1,0:T(8,128)(2,1)} %g0.5), channel_id=1, source_target_pairs={{0,2},{1,3},{2,0},{3,1},{4,6},{5,7},{6,4},{7,5},{8,10},{9,11},{10,... | collective-permute-start | bytes 1179656 | tf_op jit(solution)/shard_map/ppermute | solution.py:391
  5.2 1.3 %collective-permute-start.5 = (bf16[768,256]{1,0:T(8,128)(2,1)}, bf16[768,256]{1,0:T(8,128)(2,1)}, u32[]{:S(2)}, u32[]{:S(2)}) collective-permute-start(bf16[768,256]{1,0:T(8,128)(2,1)} %g0.5), channel_id=1, source_target_pairs={{0,3},{1,0},{2,1},{3,2},{4,7},{5,4},{6,5},{7,6},{8,11},{9,8},{10,9... | collective-permute-start | bytes 1179656 | tf_op jit(solution)/shard_map/ppermute | solution.py:391
  6.5 0.7 fusion.1
  7.2 6.3 %collective-permute-start.1 = (bf16[16,128]{1,0:T(8,128)(2,1)S(1)}, bf16[16,128]{1,0:T(8,128)(2,1)S(1)}, u32[]{:S(2)}, u32[]{:S(2)}) collective-permute-start(bf16[16,128]{1,0:T(8,128)(2,1)S(1)} %get-tuple-element.51), channel_id=1, source_target_pairs={{4,0},{8,4},{12,8},{16,12},{20,16},{24,20},{28,24},{32,28},{36,32}... | collective-permute-start | bytes 12296 | tf_op jit(solution)/shard_map/ppermute | solution.py:397
  13.6 1.9 %collective-permute-start = (bf16[16,128]{1,0:T(8,128)(2,1)S(1)}, bf16[16,128]{1,0:T(8,128)(2,1)S(1)}, u32[]{:S(2)}, u32[]{:S(2)}) collective-permute-start(bf16[16,128]{1,0:T(8,128)(2,1)S(1)} %get-tuple-element.52), channel_id=1, source_target_pairs={{0,4},{4,8},{8,12},{12,16},{16,20},{20,24},{24,28},{28,32},{32,36}... | collective-permute-start | bytes 12296 | tf_op jit(solution)/shard_map/ppermute | solution.py:397
  15.5 0.1 pad_add_fusion.place
  15.6 2.2 %copy-done.1 = bf16[512,16,256]{2,1,0:T(8,128)(2,1)S(1)} copy-done((bf16[512,16,256]{2,1,0:T(8,128)(2,1)S(1)}, bf16[512,16,256]{2,1,0:T(8,128)(2,1)}, u32[]{:S(2)}) %copy-start.1) | copy-done | bytes 4194328
  17.8 4.1 %weights.1 = (bf16[2048,256]{1,0:T(8,128)(2,1)}, bf16[1024,256]{1,0:T(8,128)(2,1)S(1)}, bf16[1024,256]{1,0:T(8,128)(2,1)S(1)}, bf16[1024,256]{1,0:T(8,128)(2,1)}, f32[8,128]{1,0:T(8,128)S(1)}) custom-call(s32[2]{0:T(128)S(1)} %pad_add_fusion.place, bf16[512,16,256]{2,1,0:T(8,128)(2,1)S(1)} %copy-done.1), custom_call_target="tpu_custom_call" | custom-call | flops 5059999744 | bytes 1000 | tf_op jit(solution)/shard_map/weights/pallas_call | solution.py:176
  21.9 0.1 stack.29.place
  22.0 0.0 collective-permute-done.1.high
  22.0 0.0 collective-permute-done.low
  22.0 0.0 copy-start.2
  22.0 5.9 %prep.1 = (bf16[768,2048]{1,0:T(8,128)(2,1)S(1)}, f32[6144,128]{1,0:T(8,128)}) custom-call(bf16[6144,128]{1,0:T(8,128)(2,1)S(1)} %copy-done, bf16[16,128]{1,0:T(8,128)(2,1)S(1)} %collective-permute-done.low, bf16[16,128]{1,0:T(8,128)(2,1)S(1)} %collective-permute-done.1.high, f32[1,128]{1,0:T(1,128)S(1)} %bitcast.10, f32[8,128]{1,0:T(8,128)S(1)} %get-tuple-element.27.after), custom_call_target="tpu_custom_call" | custom-call | flops 8855000064 | bytes 1000 | tf_op jit(solution)/shard_map/prep/pallas_call | solution.py:131
  27.9 0.0 collective-permute-done.7.g3
  27.9 0.0 copy-start.3
  27.9 0.0 collective-permute-done.6.g2
  27.9 0.0 collective-permute-done.5.g1
  27.9 4.1 %kernel_grad_send.1 = bf16[512,2048]{1,0:T(8,128)(2,1)S(1)} custom-call(s32[5]{0:T(128)S(1)} %stack.29.place, bf16[768,2048]{1,0:T(8,128)(2,1)S(1)} %get-tuple-element.28.taps, bf16[768,256]{1,0:T(8,128)(2,1)S(1)} %copy-done.2, bf16[768,256]{1,0:T(8,128)(2,1)} %collective-permute-done.5.g1, bf16[768,256]{1,0:T(8,128)(2,1)} %collective-permute-done.6.g2, ...), custom_call_target="tpu_custom_call" | custom-call | flops 3795000064 | bytes 1000 | tf_op jit(solution)/shard_map/kernel_grad_send/pallas_call | solution.py:209
  32.1 0.1 collective-permute-start.8
  32.2 0.4 collective-permute-start.2
  32.6 2.5 %collective-permute-start.3 = (bf16[1024,256]{1,0:T(8,128)(2,1)S(1)}, bf16[1024,256]{1,0:T(8,128)(2,1)}, u32[]{:S(2)}, u32[]{:S(2)}) collective-permute-start(bf16[1024,256]{1,0:T(8,128)(2,1)S(1)} %get-tuple-element.31), channel_id=1, source_target_pairs={{0,2},{1,3},{2,0},{3,1},{4,6},{5,7},{6,4},{7,5},{8,10},{9,11},{10,... | collective-permute-start | bytes 1572872 | tf_op jit(solution)/shard_map/ppermute | solution.py:391
  35.0 0.0 collective-permute-start.4
  35.0 1.3 %collective-permute-done.8.got = bf16[512,2048]{1,0:T(8,128)(2,1)S(1)} collective-permute-done((bf16[512,2048]{1,0:T(8,128)(2,1)S(1)}, bf16[512,2048]{1,0:T(8,128)(2,1)S(1)}, u32[]{:S(2)}, u32[]{:S(2)}) %collective-permute-start.8) | collective-permute-done | bytes 2097184 | tf_op jit(solution)/shard_map/ppermute | solution.py:391
  36.3 0.0 copy-done.11
  36.3 4.5 %kernel_grad_keep.1 = (bf16[4,128,2048]{2,1,0:T(8,128)(2,1)}, bf16[16,1024]{1,0:T(8,128)(2,1)}, bf16[16,1024]{1,0:T(8,128)(2,1)}, f32[8,128]{1,0:T(8,128)S(1)}) custom-call(s32[5]{0:T(128)S(1)} %stack.29.place, bf16[768,2048]{1,0:T(8,128)(2,1)S(1)} %get-tuple-element.28.taps, bf16[768,256]{1,0:T(8,128)(2,1)S(1)} %copy-done.2, ...), custom_call_target="tpu_custom_call" | custom-call | flops 5059999744 | bytes 1000 | tf_op jit(solution)/shard_map/kernel_grad_keep/pallas_call | solution.py:245
  40.8 4.9 %all-to-all-start = ((bf16[4,128,2048]{2,1,0:T(8,128)(2,1)}), bf16[4,128,2048]{2,1,0:T(8,128)(2,1)S(1)}, u32[]{:S(2)}, u32[]{:S(2)}) async-start(bf16[4,128,2048]{2,1,0:T(8,128)(2,1)} %get-tuple-element.45), calls=%async_computation | async-start | bytes 4194304 | tf_op jit(solution)/shard_map/all_to_all | solution.py:421
  45.7 1.9 %collective-permute-start.9 = (bf16[16,1024]{1,0:T(8,128)(2,1)}, bf16[16,1024]{1,0:T(8,128)(2,1)S(1)}, u32[]{:S(2)}, u32[]{:S(2)}) collective-permute-start(bf16[16,1024]{1,0:T(8,128)(2,1)} %get-tuple-element.33), channel_id=1, source_target_pairs={{0,4},{4,8},{8,12},{12,16},{16,20},{20,24},{24,28},{28,32},{32,36}... | collective-permute-start | bytes 98312 | tf_op jit(solution)/shard_map/ppermute | solution.py:397
  47.6 5.8 %collective-permute-start.10 = (bf16[16,1024]{1,0:T(8,128)(2,1)}, bf16[16,1024]{1,0:T(8,128)(2,1)S(1)}, u32[]{:S(2)}, u32[]{:S(2)}) collective-permute-start(bf16[16,1024]{1,0:T(8,128)(2,1)} %get-tuple-element.34), channel_id=1, source_target_pairs={{4,0},{8,4},{12,8},{16,12},{20,16},{24,20},{28,24},{32,28},{36,32}... | collective-permute-start | bytes 98312 | tf_op jit(solution)/shard_map/ppermute | solution.py:397
  53.4 0.0 collective-permute-done.2.refs_0_
  53.4 0.0 collective-permute-done.3.refs_1_
  53.4 6.0 %collective-permute-done.4.refs_2_ = bf16[1024,256]{1,0:T(8,128)(2,1)} collective-permute-done((bf16[1024,256]{1,0:T(8,128)(2,1)S(1)}, bf16[1024,256]{1,0:T(8,128)(2,1)}, u32[]{:S(2)}, u32[]{:S(2)}) %collective-permute-start.4) | collective-permute-done | bytes 524320 | tf_op jit(solution)/shard_map/ppermute | solution.py:391
  59.4 0.0 collective-permute-done.9.refs_3_.low
  59.4 0.0 collective-permute-done.10.refs_4_.high
  59.4 0.0 copy-start.7
  59.4 0.0 copy-start.12
  59.4 0.0 copy-start.15
  59.4 0.6 copy-done.5
  60.0 0.0 copy-done.7
  60.0 0.0 collective-permute-start.11
  60.0 0.5 collective-permute-start.12
  60.5 0.0 collective-permute-start.13
  60.5 1.6 %collective-permute-done.11.b1 = bf16[1024,256]{1,0:T(8,128)(2,1)S(1)} collective-permute-done((bf16[1024,256]{1,0:T(8,128)(2,1)}, bf16[1024,256]{1,0:T(8,128)(2,1)S(1)}, u32[]{:S(2)}, u32[]{:S(2)}) %collective-permute-start.11) | collective-permute-done | bytes 524320 | tf_op jit(solution)/shard_map/ppermute | solution.py:391
  62.1 0.7 collective-permute-done.12.b2
  62.9 0.7 collective-permute-done.13.b3
  63.6 0.0 copy-done.12
  63.6 6.3 %encode.1 = (f32[768,256]{1,0:T(8,128)}, bf16[768,256]{1,0:T(8,128)(2,1)}, bf16[768,256]{1,0:T(8,128)(2,1)}, bf16[768,256]{1,0:T(8,128)(2,1)}, bf16[2048,1024]{1,0:T(8,128)(2,1)}, /*index=5*/f32[8,128]{1,0:T(8,128)S(1)}) custom-call(s32[1]{0:T(128)} %bitcast.core, bf16[768,2048]{1,0:T(8,128)(2,1)S(1)} %copy-done.12, bf16[2048,256]{1,0:T(8,128)(2,1)S(1)} %copy-done.15, ...), custom_call_target="tpu_custom_call" | custom-call | flops 6325000192 | bytes 1000 | tf_op jit(solution)/shard_map/encode/pallas_call | solution.py:305
  70.0 0.9 all-to-all-done.parts
  70.9 1.1 %lines.1 = (bf16[8,16,2048]{2,1,0:T(8,128)(2,1)}, f32[8,128]{1,0:T(8,128)S(1)}) custom-call(bf16[4,128,2048]{2,1,0:T(8,128)(2,1)S(1)} %all-to-all-done.parts, f32[8,128]{1,0:T(8,128)S(1)} %get-tuple-element.46.after), custom_call_target="tpu_custom_call" | custom-call | flops 1264999936 | bytes 1000 | tf_op jit(solution)/shard_map/lines/pallas_call | solution.py:330
  72.0 5.7 %all-to-all-start.1 = ((bf16[8,16,2048]{2,1,0:T(8,128)(2,1)}), bf16[8,16,2048]{2,1,0:T(8,128)(2,1)S(1)}, u32[]{:S(2)}, u32[]{:S(2)}) async-start(bf16[8,16,2048]{2,1,0:T(8,128)(2,1)} %get-tuple-element.50), calls=%async_computation.1 | async-start | bytes 1048576 | tf_op jit(solution)/shard_map/all_to_all | solution.py:430
  77.7 0.7 collective-permute-start.14
  78.4 2.6 %collective-permute-start.15 = (bf16[768,256]{1,0:T(8,128)(2,1)}, bf16[768,256]{1,0:T(8,128)(2,1)S(1)}, u32[]{:S(2)}, u32[]{:S(2)}) collective-permute-start(bf16[768,256]{1,0:T(8,128)(2,1)} %get-tuple-element.41), channel_id=1, source_target_pairs={{0,3},{1,0},{2,1},{3,2},{4,7},{5,4},{6,5},{7,6},{8,11},{9,8},{10,9... | collective-permute-start | bytes 1179656 | tf_op jit(solution)/shard_map/ppermute | solution.py:391
  81.0 0.0 collective-permute-start.16
  81.0 0.0 copy-done.6
  81.0 2.2 %copy-done.13 = bf16[2048,1024]{1,0:T(8,128)(2,1)S(1)} copy-done((bf16[2048,1024]{1,0:T(8,128)(2,1)S(1)}, bf16[2048,1024]{1,0:T(8,128)(2,1)}, u32[]{:S(2)}) %copy-start.13) | copy-done | bytes 4194328
  83.2 1.9 %copy-done.14 = f32[6144,128]{1,0:T(8,128)S(1)} copy-done((f32[6144,128]{1,0:T(8,128)S(1)}, f32[6144,128]{1,0:T(8,128)}, u32[]{:S(2)}) %copy-start.14) | copy-done | bytes 3145752
  85.1 6.9 %input_grad.1 = (bf16[6144,128]{1,0:T(8,128)(2,1)}, f32[8,128]{1,0:T(8,128)S(1)}) custom-call(bf16[768,256]{1,0:T(8,128)(2,1)S(1)} %copy-done.2, bf16[768,256]{1,0:T(8,128)(2,1)} %collective-permute-done.5.g1, bf16[768,256]{1,0:T(8,128)(2,1)} %collective-permute-done.6.g2, bf16[768,256]{1,0:T(8,128)(2,1)S(1)} %copy-done.4, bf16[16,1024]{1,0:T(8,128)(2,1)S(1)} %copy-done.6, ...), custom_call_target="tpu_custom_call" | custom-call | flops 7590000128 | bytes 1000 | tf_op jit(solution)/shard_map/input_grad/pallas_call | solution.py:367
  92.0 5.5 %collective-permute-done.14.a1 = bf16[768,256]{1,0:T(8,128)(2,1)S(1)} collective-permute-done((bf16[768,256]{1,0:T(8,128)(2,1)}, bf16[768,256]{1,0:T(8,128)(2,1)S(1)}, u32[]{:S(2)}, u32[]{:S(2)}) %collective-permute-start.14) | collective-permute-done | bytes 393248 | tf_op jit(solution)/shard_map/ppermute | solution.py:391
  97.5 0.0 collective-permute-done.15.a2
  97.5 0.0 collective-permute-done.16.a3
  97.6 0.9 total.1
  98.5 0.0 all-to-all-done.1
  98.5 0.1 convert_reduce_fusion
  98.6 0.6 copy.10
  (21 shorter events, 0.1 us)
Async XLA Ops:
  0.6 27.3 %collective-permute-start.7 = (bf16[768,256]{1,0:T(8,128)(2,1)}, bf16[768,256]{1,0:T(8,128)(2,1)S(1)}, u32[]{:S(2)}, u32[]{:S(2)}) collective-permute-start(bf16[768,256]{1,0:T(8,128)(2,1)} %g0.5), channel_id=1, source_target_pairs={{0,1},{1,2},{2,3},{3,0},{4,5},{5,6},{6,7},{7,4},{8,9},{9,10},{10,1... | collective-permute-start | bytes 1179656 | tf_op jit(solution)/shard_map/ppermute | solution.py:391
  2.3 25.6 %collective-permute-start.6 = (bf16[768,256]{1,0:T(8,128)(2,1)}, bf16[768,256]{1,0:T(8,128)(2,1)}, u32[]{:S(2)}, u32[]{:S(2)}) collective-permute-start(bf16[768,256]{1,0:T(8,128)(2,1)} %g0.5), channel_id=1, source_target_pairs={{0,2},{1,3},{2,0},{3,1},{4,6},{5,7},{6,4},{7,5},{8,10},{9,11},{10,... | collective-permute-start | bytes 1179656 | tf_op jit(solution)/shard_map/ppermute | solution.py:391
  5.2 22.7 %collective-permute-start.5 = (bf16[768,256]{1,0:T(8,128)(2,1)}, bf16[768,256]{1,0:T(8,128)(2,1)}, u32[]{:S(2)}, u32[]{:S(2)}) collective-permute-start(bf16[768,256]{1,0:T(8,128)(2,1)} %g0.5), channel_id=1, source_target_pairs={{0,3},{1,0},{2,1},{3,2},{4,7},{5,4},{6,5},{7,6},{8,11},{9,8},{10,9... | collective-permute-start | bytes 1179656 | tf_op jit(solution)/shard_map/ppermute | solution.py:391
  7.2 14.7 %collective-permute-start.1 = (bf16[16,128]{1,0:T(8,128)(2,1)S(1)}, bf16[16,128]{1,0:T(8,128)(2,1)S(1)}, u32[]{:S(2)}, u32[]{:S(2)}) collective-permute-start(bf16[16,128]{1,0:T(8,128)(2,1)S(1)} %get-tuple-element.51), channel_id=1, source_target_pairs={{4,0},{8,4},{12,8},{16,12},{20,16},{24,20},{28,24},{32,28},{36,32}... | collective-permute-start | bytes 12296 | tf_op jit(solution)/shard_map/ppermute | solution.py:397
  13.6 8.4 %collective-permute-start = (bf16[16,128]{1,0:T(8,128)(2,1)S(1)}, bf16[16,128]{1,0:T(8,128)(2,1)S(1)}, u32[]{:S(2)}, u32[]{:S(2)}) collective-permute-start(bf16[16,128]{1,0:T(8,128)(2,1)S(1)} %get-tuple-element.52), channel_id=1, source_target_pairs={{0,4},{4,8},{8,12},{12,16},{16,20},{20,24},{24,28},{28,32},{32,36}... | collective-permute-start | bytes 12296 | tf_op jit(solution)/shard_map/ppermute | solution.py:397
  15.6 2.2 %copy-start.1 = (bf16[512,16,256]{2,1,0:T(8,128)(2,1)S(1)}, bf16[512,16,256]{2,1,0:T(8,128)(2,1)}, u32[]{:S(2)}) copy-start(bf16[512,16,256]{2,1,0:T(8,128)(2,1)} %whole.1) | copy-start | bytes 12582916
  17.8 4.2 %copy-start = (bf16[6144,128]{1,0:T(8,128)(2,1)S(1)}, bf16[6144,128]{1,0:T(8,128)(2,1)}, u32[]{:S(2)}) copy-start(bf16[6144,128]{1,0:T(8,128)(2,1)} %feat.1) | copy-start | bytes 4718596
  17.8 4.2 %copy-start.9 = (f32[128]{0:T(128)S(1)}, f32[128]{0:T(128)}, u32[]{:S(2)}) copy-start(f32[128]{0:T(128)} %param.5) | copy-start | bytes 1540
  22.0 6.0 %copy-start.2 = (bf16[768,256]{1,0:T(8,128)(2,1)S(1)}, bf16[768,256]{1,0:T(8,128)(2,1)}, u32[]{:S(2)}) copy-start(bf16[768,256]{1,0:T(8,128)(2,1)} %g0.5) | copy-start | bytes 1179652
  27.9 8.5 %copy-start.11 = (bf16[768,2048]{1,0:T(8,128)(2,1)}, bf16[768,2048]{1,0:T(8,128)(2,1)S(1)}, u32[]{:S(2)}) copy-start(bf16[768,2048]{1,0:T(8,128)(2,1)S(1)} %get-tuple-element.28.taps) | copy-start | bytes 9437188
  27.9 8.4 %copy-start.3 = (bf16[768,256]{1,0:T(8,128)(2,1)}, bf16[768,256]{1,0:T(8,128)(2,1)S(1)}, u32[]{:S(2)}) copy-start(bf16[768,256]{1,0:T(8,128)(2,1)S(1)} %collective-permute-done.7.g3) | copy-start | bytes 1179652
  32.1 4.2 %collective-permute-start.8 = (bf16[512,2048]{1,0:T(8,128)(2,1)S(1)}, bf16[512,2048]{1,0:T(8,128)(2,1)S(1)}, u32[]{:S(2)}, u32[]{:S(2)}) collective-permute-start(bf16[512,2048]{1,0:T(8,128)(2,1)S(1)} %kernel_grad_send.1), channel_id=1, source_target_pairs={{0,4},{4,0},{1,5},{5,1},{2,6},{6,2},{3,7},{7,3},{8,12},{12,8},{9,1... | collective-permute-start | bytes 6291464 | tf_op jit(solution)/shard_map/ppermute | solution.py:391
  32.2 21.2 %collective-permute-start.2 = (bf16[1024,256]{1,0:T(8,128)(2,1)}, bf16[1024,256]{1,0:T(8,128)(2,1)}, u32[]{:S(2)}, u32[]{:S(2)}) collective-permute-start(bf16[1024,256]{1,0:T(8,128)(2,1)} %get-tuple-element.30), channel_id=1, source_target_pairs={{0,3},{1,0},{2,1},{3,2},{4,7},{5,4},{6,5},{7,6},{8,11},{9,8},{10,9... | collective-permute-start | bytes 1572872 | tf_op jit(solution)/shard_map/ppermute | solution.py:391
  32.6 20.8 %collective-permute-start.3 = (bf16[1024,256]{1,0:T(8,128)(2,1)S(1)}, bf16[1024,256]{1,0:T(8,128)(2,1)}, u32[]{:S(2)}, u32[]{:S(2)}) collective-permute-start(bf16[1024,256]{1,0:T(8,128)(2,1)S(1)} %get-tuple-element.31), channel_id=1, source_target_pairs={{0,2},{1,3},{2,0},{3,1},{4,6},{5,7},{6,4},{7,5},{8,10},{9,11},{10,... | collective-permute-start | bytes 1572872 | tf_op jit(solution)/shard_map/ppermute | solution.py:391
  35.0 24.4 %collective-permute-start.4 = (bf16[1024,256]{1,0:T(8,128)(2,1)S(1)}, bf16[1024,256]{1,0:T(8,128)(2,1)}, u32[]{:S(2)}, u32[]{:S(2)}) collective-permute-start(bf16[1024,256]{1,0:T(8,128)(2,1)S(1)} %get-tuple-element.32), channel_id=1, source_target_pairs={{0,1},{1,2},{2,3},{3,0},{4,5},{5,6},{6,7},{7,4},{8,9},{9,10},{10,1... | collective-permute-start | bytes 1572872 | tf_op jit(solution)/shard_map/ppermute | solution.py:391
  40.8 30.0 %all-to-all-start = ((bf16[4,128,2048]{2,1,0:T(8,128)(2,1)}), bf16[4,128,2048]{2,1,0:T(8,128)(2,1)S(1)}, u32[]{:S(2)}, u32[]{:S(2)}) async-start(bf16[4,128,2048]{2,1,0:T(8,128)(2,1)} %get-tuple-element.45), calls=%async_computation | async-start | bytes 4194304 | tf_op jit(solution)/shard_map/all_to_all | solution.py:421
  45.7 13.7 %collective-permute-start.9 = (bf16[16,1024]{1,0:T(8,128)(2,1)}, bf16[16,1024]{1,0:T(8,128)(2,1)S(1)}, u32[]{:S(2)}, u32[]{:S(2)}) collective-permute-start(bf16[16,1024]{1,0:T(8,128)(2,1)} %get-tuple-element.33), channel_id=1, source_target_pairs={{0,4},{4,8},{8,12},{12,16},{16,20},{20,24},{24,28},{28,32},{32,36}... | collective-permute-start | bytes 98312 | tf_op jit(solution)/shard_map/ppermute | solution.py:397
  47.6 11.8 %collective-permute-start.10 = (bf16[16,1024]{1,0:T(8,128)(2,1)}, bf16[16,1024]{1,0:T(8,128)(2,1)S(1)}, u32[]{:S(2)}, u32[]{:S(2)}) collective-permute-start(bf16[16,1024]{1,0:T(8,128)(2,1)} %get-tuple-element.34), channel_id=1, source_target_pairs={{4,0},{8,4},{12,8},{16,12},{20,16},{24,20},{28,24},{32,28},{36,32}... | collective-permute-start | bytes 98312 | tf_op jit(solution)/shard_map/ppermute | solution.py:397
  59.4 0.6 copy-start.5
  59.4 0.6 copy-start.7
  59.4 4.2 %copy-start.12 = (bf16[768,2048]{1,0:T(8,128)(2,1)S(1)}, bf16[768,2048]{1,0:T(8,128)(2,1)}, u32[]{:S(2)}) copy-start(bf16[768,2048]{1,0:T(8,128)(2,1)} %copy-done.11) | copy-start | bytes 9437188
  59.4 4.2 %copy-start.15 = (bf16[2048,256]{1,0:T(8,128)(2,1)S(1)}, bf16[2048,256]{1,0:T(8,128)(2,1)}, u32[]{:S(2)}) copy-start(bf16[2048,256]{1,0:T(8,128)(2,1)} %get-tuple-element.29.own) | copy-start | bytes 3145732
  60.0 2.1 %collective-permute-start.11 = (bf16[1024,256]{1,0:T(8,128)(2,1)}, bf16[1024,256]{1,0:T(8,128)(2,1)S(1)}, u32[]{:S(2)}, u32[]{:S(2)}) collective-permute-start(bf16[1024,256]{1,0:T(8,128)(2,1)} %get-tuple-element.36.a1), channel_id=1, source_target_pairs={{0,4},{4,0},{1,5},{5,1},{2,6},{6,2},{3,7},{7,3},{8,12},{12,8},{9,1... | collective-permute-start | bytes 1572872 | tf_op jit(solution)/shard_map/ppermute | solution.py:391
  60.0 2.9 %collective-permute-start.12 = (bf16[1024,256]{1,0:T(8,128)(2,1)}, bf16[1024,256]{1,0:T(8,128)(2,1)S(1)}, u32[]{:S(2)}, u32[]{:S(2)}) collective-permute-start(bf16[1024,256]{1,0:T(8,128)(2,1)} %get-tuple-element.37.a2), channel_id=1, source_target_pairs={{0,4},{4,0},{1,5},{5,1},{2,6},{6,2},{3,7},{7,3},{8,12},{12,8},{9,1... | collective-permute-start | bytes 1572872 | tf_op jit(solution)/shard_map/ppermute | solution.py:391
  60.5 3.1 %collective-permute-start.13 = (bf16[1024,256]{1,0:T(8,128)(2,1)}, bf16[1024,256]{1,0:T(8,128)(2,1)S(1)}, u32[]{:S(2)}, u32[]{:S(2)}) collective-permute-start(bf16[1024,256]{1,0:T(8,128)(2,1)} %get-tuple-element.38.a3), channel_id=1, source_target_pairs={{0,4},{4,0},{1,5},{5,1},{2,6},{6,2},{3,7},{7,3},{8,12},{12,8},{9,1... | collective-permute-start | bytes 1572872 | tf_op jit(solution)/shard_map/ppermute | solution.py:391
  70.9 10.1 %copy-start.4 = (bf16[768,256]{1,0:T(8,128)(2,1)S(1)}, bf16[768,256]{1,0:T(8,128)(2,1)}, u32[]{:S(2)}) copy-start(bf16[768,256]{1,0:T(8,128)(2,1)} %copy-done.3) | copy-start | bytes 1179652
  70.9 10.1 %copy-start.6 = (bf16[16,1024]{1,0:T(8,128)(2,1)S(1)}, bf16[16,1024]{1,0:T(8,128)(2,1)}, u32[]{:S(2)}) copy-start(bf16[16,1024]{1,0:T(8,128)(2,1)} %copy-done.5) | copy-start | bytes 98308
  70.9 10.1 %copy-start.8 = (bf16[16,1024]{1,0:T(8,128)(2,1)S(1)}, bf16[16,1024]{1,0:T(8,128)(2,1)}, u32[]{:S(2)}) copy-start(bf16[16,1024]{1,0:T(8,128)(2,1)} %copy-done.7) | copy-start | bytes 98308
  72.0 26.5 %all-to-all-start.1 = ((bf16[8,16,2048]{2,1,0:T(8,128)(2,1)}), bf16[8,16,2048]{2,1,0:T(8,128)(2,1)S(1)}, u32[]{:S(2)}, u32[]{:S(2)}) async-start(bf16[8,16,2048]{2,1,0:T(8,128)(2,1)} %get-tuple-element.50), calls=%async_computation.1 | async-start | bytes 1048576 | tf_op jit(solution)/shard_map/all_to_all | solution.py:430
  77.7 19.8 %collective-permute-start.14 = (bf16[768,256]{1,0:T(8,128)(2,1)}, bf16[768,256]{1,0:T(8,128)(2,1)S(1)}, u32[]{:S(2)}, u32[]{:S(2)}) collective-permute-start(bf16[768,256]{1,0:T(8,128)(2,1)} %get-tuple-element.40), channel_id=1, source_target_pairs={{0,1},{1,2},{2,3},{3,0},{4,5},{5,6},{6,7},{7,4},{8,9},{9,10},{10,1... | collective-permute-start | bytes 1179656 | tf_op jit(solution)/shard_map/ppermute | solution.py:391
  78.4 19.2 %collective-permute-start.15 = (bf16[768,256]{1,0:T(8,128)(2,1)}, bf16[768,256]{1,0:T(8,128)(2,1)S(1)}, u32[]{:S(2)}, u32[]{:S(2)}) collective-permute-start(bf16[768,256]{1,0:T(8,128)(2,1)} %get-tuple-element.41), channel_id=1, source_target_pairs={{0,3},{1,0},{2,1},{3,2},{4,7},{5,4},{6,5},{7,6},{8,11},{9,8},{10,9... | collective-permute-start | bytes 1179656 | tf_op jit(solution)/shard_map/ppermute | solution.py:391
  81.0 16.6 %collective-permute-start.16 = (bf16[768,256]{1,0:T(8,128)(2,1)}, bf16[768,256]{1,0:T(8,128)(2,1)S(1)}, u32[]{:S(2)}, u32[]{:S(2)}) collective-permute-start(bf16[768,256]{1,0:T(8,128)(2,1)} %get-tuple-element.42), channel_id=1, source_target_pairs={{0,2},{1,3},{2,0},{3,1},{4,6},{5,7},{6,4},{7,5},{8,10},{9,11},{10,... | collective-permute-start | bytes 1179656 | tf_op jit(solution)/shard_map/ppermute | solution.py:391
  81.0 2.2 %copy-start.13 = (bf16[2048,1024]{1,0:T(8,128)(2,1)S(1)}, bf16[2048,1024]{1,0:T(8,128)(2,1)}, u32[]{:S(2)}) copy-start(bf16[2048,1024]{1,0:T(8,128)(2,1)} %get-tuple-element.43.weights) | copy-start | bytes 12582916
  83.2 1.9 %copy-start.14 = (f32[6144,128]{1,0:T(8,128)S(1)}, f32[6144,128]{1,0:T(8,128)}, u32[]{:S(2)}) copy-start(f32[6144,128]{1,0:T(8,128)} %get-tuple-element.44.factor) | copy-start | bytes 9437188
  85.1 12.5 %copy-start.10 = (f32[768,256]{1,0:T(8,128)S(1)}, f32[768,256]{1,0:T(8,128)}, u32[]{:S(2)}) copy-start(f32[768,256]{1,0:T(8,128)} %get-tuple-element.39.own) | copy-start | bytes 2359300

commit v8 on v7

--- a/solution.py
+++ b/solution.py
@@ -61,8 +61,8 @@
 
 FACTOR = 1.1
 TIME = dict(
-    prep=7,
-    weights=4,
+    prep=2,
+    weights=1,
     kernel_grad_send=3,
     kernel_grad_keep=4,
     join=1,
@@ -143,7 +143,7 @@
 
 
 def weights_kernel(
-    place, whole, own, p1, p2, p3, done, buf, rows, held, sem, out_sem
+    place, whole, head, tail, own, p1, p2, p3, o_head, o_tail, done, buf, rows, held, sem, out_sem
 ):
     y, core = place[0], place[1]
     copies = [
@@ -168,15 +168,17 @@
         if s == 0:
             sent = pltpu.make_async_copy(held, own, out_sem)
             sent.start()
+    o_head[...] = head[...]
+    o_tail[...] = tail[...]
     sent.wait()
     done[...] = jnp.zeros(done.shape, F32)
 
 
-def weights(place, whole):
+def weights(place, whole, head, tail):
     return call(
         weights_kernel,
-        (far_shape((2048, 256)),) + (shape((1024, 256)),) * 3 + (TOKEN,),
-        [SMEM, HBM],
+        (far_shape((2048, 256)),) + (shape((1024, 256)),) * 3 + (shape((16, 128)),) * 2 + (TOKEN,),
+        [SMEM, HBM, VMEM, VMEM],
         "weights",
         [
             pltpu.VMEM((4, 128, TAPS, 256), BF),
@@ -185,8 +187,8 @@
             pltpu.SemaphoreType.DMA((4,)),
             pltpu.SemaphoreType.DMA,
         ],
-        out_specs=(HBM,) + (VMEM,) * 4,
-    )(place, whole)
+        out_specs=(HBM,) + (VMEM,) * 6,
+    )(place, whole, head, tail)
 
 
 def choose(gs, which, order, lhs):
@@ -406,10 +408,10 @@
         turn(grad_out, "chan", 2),
         turn(grad_out, "chan", 1),
     )
-    low, high = beside(features[-16:], 1), beside(features[:16], -1)
 
     at = jnp.stack([y, core])
-    own, p1, p2, p3, done = weights(at, down_weight)
+    own, p1, p2, p3, head, tail, done = weights(at, down_weight, features[:16], features[-16:])
+    low, high = beside(tail, 1), beside(head, -1)
     taps, factor = prep(features, low, high, snake_alpha.reshape(1, -1), done)
     near = (turn(p3, "chan", -1), turn(p2, "chan", 2), turn(p1, "chan", 1))
 

time: 100 us -> 104 us (1.040); the launches traced: 99.2 us -> 102 us
  starting transfers between devices: 39.1 us -> 40.9 us
  waiting for transfers between devices: 16.9 us -> 18 us
    all_to_all x1, starting transfers between devices: 5.74 us -> 7.47 us  [shards(): spread = lax.all_to_all(summed, 'z', 0, 0)]
    ppermute x4, waiting for transfers between devices: 0.01 us -> 1.19 us  [beside(): return lax.ppermute(value, TM, pairs)]
  transfers between devices with their start and end apart: 19 -> 19, of which waited for: 7 -> 8; matrix products, arithmetic and copies ran while one was open for 1% -> 1% of each run, Pallas kernels for 29% -> 28%
where the time goes in v8:
time: 104 us; the launch traced here: 102 us
  starting transfers between devices  40.9 us (39%)
  Pallas kernels  33.8 us (32%)
  waiting for transfers between devices  18 us (17%)
  local copies, waits for them, and re-layouts  8.32 us (8%)
    ppermute x13, waiting for transfers between devices, turn(): lax.ppermute(value, axis, [(i, (i + by) % count) for i in range(count)])  16 us
    ppermute x4, starting transfers between devices, beside(): return lax.ppermute(value, TM, pairs)  15.9 us
    ppermute x13, starting transfers between devices, turn(): lax.ppermute(value, axis, [(i, (i + by) % count) for i in range(count)])  12.6 us
    unnamed x33, local copies, waits for them, and re-layouts  7.52 us
    all_to_all x1, starting transfers between devices, shards(): spread = lax.all_to_all(summed, 'z', 0, 0)  7.47 us
    pallas_call x1, Pallas kernels, input_grad(): call(input_grad_kernel, (shape((frames, chans)), TOKEN), [VMEM] * 9, 'inp...  6.9 us
    pallas_call x1, Pallas kernels, encode(): call(encode_kernel, (far_shape((768, 256), F32),) + (far_shape((768, 256)...  6.34 us
    pallas_call x1, Pallas kernels, prep(): call(prep_kernel, (shape((frames // STRIDE, TAPS * chans)), far_shape((fr...  5.88 us
  transfers between devices with their start and end apart: 19, of which 8 were waited for; matrix products, arithmetic and copies ran while one was open for 1% of the time, Pallas kernels for 28%

profile of v8, /device:TPU:2, one launch (start us, length us, event | category | flops | bytes accessed | tf_op | source)
XLA Modules:
  0.0 102.1 jit_solution(4423618326528379388)
XLA Ops:
  0.6 1.7 %collective-permute-start.7 = (bf16[768,256]{1,0:T(8,128)(2,1)}, bf16[768,256]{1,0:T(8,128)(2,1)S(1)}, u32[]{:S(2)}, u32[]{:S(2)}) collective-permute-start(bf16[768,256]{1,0:T(8,128)(2,1)} %g0.5), channel_id=1, source_target_pairs={{0,1},{1,2},{2,3},{3,0},{4,5},{5,6},{6,7},{7,4},{8,9},{9,10},{10,1... | collective-permute-start | bytes 1179656 | tf_op jit(solution)/shard_map/ppermute | solution.py:393
  2.3 2.9 %collective-permute-start.6 = (bf16[768,256]{1,0:T(8,128)(2,1)}, bf16[768,256]{1,0:T(8,128)(2,1)}, u32[]{:S(2)}, u32[]{:S(2)}) collective-permute-start(bf16[768,256]{1,0:T(8,128)(2,1)} %g0.5), channel_id=1, source_target_pairs={{0,2},{1,3},{2,0},{3,1},{4,6},{5,7},{6,4},{7,5},{8,10},{9,11},{10,... | collective-permute-start | bytes 1179656 | tf_op jit(solution)/shard_map/ppermute | solution.py:393
  5.2 1.3 %collective-permute-start.5 = (bf16[768,256]{1,0:T(8,128)(2,1)}, bf16[768,256]{1,0:T(8,128)(2,1)}, u32[]{:S(2)}, u32[]{:S(2)}) collective-permute-start(bf16[768,256]{1,0:T(8,128)(2,1)} %g0.5), channel_id=1, source_target_pairs={{0,3},{1,0},{2,1},{3,2},{4,7},{5,4},{6,5},{7,6},{8,11},{9,8},{10,9... | collective-permute-start | bytes 1179656 | tf_op jit(solution)/shard_map/ppermute | solution.py:393
  6.5 0.7 fusion.1
  7.2 0.1 pad_add_fusion.place
  7.3 2.2 %copy-done.1 = bf16[512,16,256]{2,1,0:T(8,128)(2,1)S(1)} copy-done((bf16[512,16,256]{2,1,0:T(8,128)(2,1)S(1)}, bf16[512,16,256]{2,1,0:T(8,128)(2,1)}, u32[]{:S(2)}) %copy-start.1) | copy-done | bytes 4194328
  9.5 4.1 %weights.1 = (bf16[2048,256]{1,0:T(8,128)(2,1)}, bf16[1024,256]{1,0:T(8,128)(2,1)S(1)}, bf16[1024,256]{1,0:T(8,128)(2,1)S(1)}, bf16[1024,256]{1,0:T(8,128)(2,1)}...) custom-call(s32[2]{0:T(128)S(1)} %pad_add_fusion.place, ...), custom_call_target="tpu_custom_call" | custom-call | flops 1264999936 | bytes 1000 | tf_op jit(solution)/shard_map/weights/pallas_call | solution.py:178
  13.6 1.9 %collective-permute-start = (bf16[16,128]{1,0:T(8,128)(2,1)S(1)}, bf16[16,128]{1,0:T(8,128)(2,1)S(1)}, u32[]{:S(2)}, u32[]{:S(2)}) collective-permute-start(bf16[16,128]{1,0:T(8,128)(2,1)S(1)} %get-tuple-element.29), channel_id=1, source_target_pairs={{0,4},{4,8},{8,12},{12,16},{16,20},{20,24},{24,28},{28,32},{32,36}... | collective-permute-start | bytes 12296 | tf_op jit(solution)/shard_map/ppermute | solution.py:399
  15.5 6.3 %collective-permute-start.1 = (bf16[16,128]{1,0:T(8,128)(2,1)S(1)}, bf16[16,128]{1,0:T(8,128)(2,1)S(1)}, u32[]{:S(2)}, u32[]{:S(2)}) collective-permute-start(bf16[16,128]{1,0:T(8,128)(2,1)S(1)} %get-tuple-element.30), channel_id=1, source_target_pairs={{4,0},{8,4},{12,8},{16,12},{20,16},{24,20},{28,24},{32,28},{36,32}... | collective-permute-start | bytes 12296 | tf_op jit(solution)/shard_map/ppermute | solution.py:399
  21.9 0.1 stack.29.place
  22.0 0.0 collective-permute-done.low
  22.0 1.2 %collective-permute-done.1.high = bf16[16,128]{1,0:T(8,128)(2,1)S(1)} collective-permute-done((bf16[16,128]{1,0:T(8,128)(2,1)S(1)}, bf16[16,128]{1,0:T(8,128)(2,1)S(1)}, u32[]{:S(2)}, u32[]{:S(2)}) %collective-permute-start.1) | collective-permute-done | bytes 4128 | tf_op jit(solution)/shard_map/ppermute | solution.py:399
  23.1 0.0 copy-done
  23.2 0.0 copy-done.9
  23.2 5.9 %prep.1 = (bf16[768,2048]{1,0:T(8,128)(2,1)S(1)}, f32[6144,128]{1,0:T(8,128)}) custom-call(bf16[6144,128]{1,0:T(8,128)(2,1)S(1)} %copy-done, bf16[16,128]{1,0:T(8,128)(2,1)S(1)} %collective-permute-done.low, bf16[16,128]{1,0:T(8,128)(2,1)S(1)} %collective-permute-done.1.high, f32[1,128]{1,0:T(1,128)S(1)} %bitcast.10, f32[8,128]{1,0:T(8,128)S(1)} %get-tuple-element.31.after), custom_call_target="tpu_custom_call" | custom-call | flops 2529999872 | bytes 1000 | tf_op jit(solution)/shard_map/prep/pallas_call | solution.py:131
  29.0 0.0 copy-start.12
  29.1 0.0 collective-permute-done.7.g3
  29.1 0.0 collective-permute-done.6.g2
  29.1 0.0 collective-permute-done.5.g1
  29.1 0.0 copy-done.2
  29.1 4.1 %kernel_grad_send.1 = bf16[512,2048]{1,0:T(8,128)(2,1)S(1)} custom-call(s32[5]{0:T(128)S(1)} %stack.29.place, bf16[768,2048]{1,0:T(8,128)(2,1)S(1)} %get-tuple-element.32.taps, bf16[768,256]{1,0:T(8,128)(2,1)S(1)} %copy-done.2, bf16[768,256]{1,0:T(8,128)(2,1)} %collective-permute-done.5.g1, bf16[768,256]{1,0:T(8,128)(2,1)} %collective-permute-done.6.g2, ...), custom_call_target="tpu_custom_call" | custom-call | flops 3795000064 | bytes 1000 | tf_op jit(solution)/shard_map/kernel_grad_send/pallas_call | solution.py:211
  33.2 0.1 collective-permute-start.8
  33.3 0.4 collective-permute-start.2
  33.7 2.5 %collective-permute-start.3 = (bf16[1024,256]{1,0:T(8,128)(2,1)S(1)}, bf16[1024,256]{1,0:T(8,128)(2,1)}, u32[]{:S(2)}, u32[]{:S(2)}) collective-permute-start(bf16[1024,256]{1,0:T(8,128)(2,1)S(1)} %get-tuple-element.35), channel_id=1, source_target_pairs={{0,2},{1,3},{2,0},{3,1},{4,6},{5,7},{6,4},{7,5},{8,10},{9,11},{10,... | collective-permute-start | bytes 1572872 | tf_op jit(solution)/shard_map/ppermute | solution.py:393
  36.2 0.0 collective-permute-start.4
  36.2 1.3 %collective-permute-done.8.got = bf16[512,2048]{1,0:T(8,128)(2,1)S(1)} collective-permute-done((bf16[512,2048]{1,0:T(8,128)(2,1)S(1)}, bf16[512,2048]{1,0:T(8,128)(2,1)S(1)}, u32[]{:S(2)}, u32[]{:S(2)}) %collective-permute-start.8) | collective-permute-done | bytes 2097184 | tf_op jit(solution)/shard_map/ppermute | solution.py:393
  37.5 0.0 copy-done.3
  37.5 4.5 %kernel_grad_keep.1 = (bf16[4,128,2048]{2,1,0:T(8,128)(2,1)}, bf16[16,1024]{1,0:T(8,128)(2,1)}, bf16[16,1024]{1,0:T(8,128)(2,1)}, f32[8,128]{1,0:T(8,128)S(1)}) custom-call(s32[5]{0:T(128)S(1)} %stack.29.place, bf16[768,2048]{1,0:T(8,128)(2,1)S(1)} %get-tuple-element.32.taps, bf16[768,256]{1,0:T(8,128)(2,1)S(1)} %copy-done.2, ...), custom_call_target="tpu_custom_call" | custom-call | flops 5059999744 | bytes 1000 | tf_op jit(solution)/shard_map/kernel_grad_keep/pallas_call | solution.py:247
  42.0 4.9 %all-to-all-start = ((bf16[4,128,2048]{2,1,0:T(8,128)(2,1)}), bf16[4,128,2048]{2,1,0:T(8,128)(2,1)S(1)}, u32[]{:S(2)}, u32[]{:S(2)}) async-start(bf16[4,128,2048]{2,1,0:T(8,128)(2,1)} %get-tuple-element.49), calls=%async_computation | async-start | bytes 4194304 | tf_op jit(solution)/shard_map/all_to_all | solution.py:423
  46.9 1.9 %collective-permute-start.9 = (bf16[16,1024]{1,0:T(8,128)(2,1)}, bf16[16,1024]{1,0:T(8,128)(2,1)S(1)}, u32[]{:S(2)}, u32[]{:S(2)}) collective-permute-start(bf16[16,1024]{1,0:T(8,128)(2,1)} %get-tuple-element.37), channel_id=1, source_target_pairs={{0,4},{4,8},{8,12},{12,16},{16,20},{20,24},{24,28},{28,32},{32,36}... | collective-permute-start | bytes 98312 | tf_op jit(solution)/shard_map/ppermute | solution.py:399
  48.8 5.8 %collective-permute-start.10 = (bf16[16,1024]{1,0:T(8,128)(2,1)}, bf16[16,1024]{1,0:T(8,128)(2,1)S(1)}, u32[]{:S(2)}, u32[]{:S(2)}) collective-permute-start(bf16[16,1024]{1,0:T(8,128)(2,1)} %get-tuple-element.38), channel_id=1, source_target_pairs={{4,0},{8,4},{12,8},{16,12},{20,16},{24,20},{28,24},{32,28},{36,32}... | collective-permute-start | bytes 98312 | tf_op jit(solution)/shard_map/ppermute | solution.py:399
  54.5 0.0 collective-permute-done.2.refs_0_
  54.5 0.0 collective-permute-done.3.refs_1_
  54.5 6.0 %collective-permute-done.4.refs_2_ = bf16[1024,256]{1,0:T(8,128)(2,1)} collective-permute-done((bf16[1024,256]{1,0:T(8,128)(2,1)S(1)}, bf16[1024,256]{1,0:T(8,128)(2,1)}, u32[]{:S(2)}, u32[]{:S(2)}) %collective-permute-start.4) | collective-permute-done | bytes 524320 | tf_op jit(solution)/shard_map/ppermute | solution.py:393
  60.5 0.0 collective-permute-done.9.refs_3_.low
  60.5 0.0 collective-permute-done.10.refs_4_.high
  60.5 0.0 copy-start.7
  60.6 0.0 copy-start.10
  60.6 0.6 copy-done.5
  61.1 0.0 copy-done.7
  61.2 0.0 collective-permute-start.11
  61.2 0.5 collective-permute-start.12
  61.7 0.0 collective-permute-start.13
  61.7 1.6 %collective-permute-done.11.b1 = bf16[1024,256]{1,0:T(8,128)(2,1)S(1)} collective-permute-done((bf16[1024,256]{1,0:T(8,128)(2,1)}, bf16[1024,256]{1,0:T(8,128)(2,1)S(1)}, u32[]{:S(2)}, u32[]{:S(2)}) %collective-permute-start.11) | collective-permute-done | bytes 524320 | tf_op jit(solution)/shard_map/ppermute | solution.py:393
  63.3 0.7 collective-permute-done.12.b2
  64.0 0.7 collective-permute-done.13.b3
  64.8 0.0 copy-done.13
  64.8 6.3 %encode.1 = (f32[768,256]{1,0:T(8,128)}, bf16[768,256]{1,0:T(8,128)(2,1)}, bf16[768,256]{1,0:T(8,128)(2,1)}, bf16[768,256]{1,0:T(8,128)(2,1)}, bf16[2048,1024]{1,0:T(8,128)(2,1)}, /*index=5*/f32[8,128]{1,0:T(8,128)S(1)}) custom-call(s32[1]{0:T(128)} %bitcast.core, bf16[768,2048]{1,0:T(8,128)(2,1)S(1)} %copy-done.13, bf16[2048,256]{1,0:T(8,128)(2,1)S(1)} %copy-done.10, ...), custom_call_target="tpu_custom_call" | custom-call | flops 6325000192 | bytes 1000 | tf_op jit(solution)/shard_map/encode/pallas_call | solution.py:307
  71.1 0.9 all-to-all-done.parts
  72.0 1.1 %lines.1 = (bf16[8,16,2048]{2,1,0:T(8,128)(2,1)}, f32[8,128]{1,0:T(8,128)S(1)}) custom-call(bf16[4,128,2048]{2,1,0:T(8,128)(2,1)S(1)} %all-to-all-done.parts, f32[8,128]{1,0:T(8,128)S(1)} %get-tuple-element.50.after), custom_call_target="tpu_custom_call" | custom-call | flops 1264999936 | bytes 1000 | tf_op jit(solution)/shard_map/lines/pallas_call | solution.py:332
  73.1 7.5 %all-to-all-start.1 = ((bf16[8,16,2048]{2,1,0:T(8,128)(2,1)}), bf16[8,16,2048]{2,1,0:T(8,128)(2,1)S(1)}, u32[]{:S(2)}, u32[]{:S(2)}) async-start(bf16[8,16,2048]{2,1,0:T(8,128)(2,1)} %get-tuple-element.54), calls=%async_computation.1 | async-start | bytes 1048576 | tf_op jit(solution)/shard_map/all_to_all | solution.py:432
  80.6 0.7 collective-permute-start.14
  81.3 2.6 %collective-permute-start.15 = (bf16[768,256]{1,0:T(8,128)(2,1)}, bf16[768,256]{1,0:T(8,128)(2,1)S(1)}, u32[]{:S(2)}, u32[]{:S(2)}) collective-permute-start(bf16[768,256]{1,0:T(8,128)(2,1)} %get-tuple-element.45), channel_id=1, source_target_pairs={{0,3},{1,0},{2,1},{3,2},{4,7},{5,4},{6,5},{7,6},{8,11},{9,8},{10,9... | collective-permute-start | bytes 1179656 | tf_op jit(solution)/shard_map/ppermute | solution.py:393
  83.8 0.0 collective-permute-start.16
  83.9 1.9 %copy-done.14 = f32[6144,128]{1,0:T(8,128)S(1)} copy-done((f32[6144,128]{1,0:T(8,128)S(1)}, f32[6144,128]{1,0:T(8,128)}, u32[]{:S(2)}) %copy-start.14) | copy-done | bytes 3145752
  85.8 2.2 %copy-done.15 = bf16[2048,1024]{1,0:T(8,128)(2,1)S(1)} copy-done((bf16[2048,1024]{1,0:T(8,128)(2,1)S(1)}, bf16[2048,1024]{1,0:T(8,128)(2,1)}, u32[]{:S(2)}) %copy-start.15) | copy-done | bytes 4194328
  88.0 6.9 %input_grad.1 = (bf16[6144,128]{1,0:T(8,128)(2,1)}, f32[8,128]{1,0:T(8,128)S(1)}) custom-call(bf16[768,256]{1,0:T(8,128)(2,1)S(1)} %copy-done.2, bf16[768,256]{1,0:T(8,128)(2,1)} %collective-permute-done.5.g1, bf16[768,256]{1,0:T(8,128)(2,1)} %collective-permute-done.6.g2, bf16[768,256]{1,0:T(8,128)(2,1)S(1)} %copy-done.4, bf16[16,1024]{1,0:T(8,128)(2,1)S(1)} %copy-done.6, ...), custom_call_target="tpu_custom_call" | custom-call | flops 7590000128 | bytes 1000 | tf_op jit(solution)/shard_map/input_grad/pallas_call | solution.py:369
  94.9 5.5 %collective-permute-done.14.a1 = bf16[768,256]{1,0:T(8,128)(2,1)S(1)} collective-permute-done((bf16[768,256]{1,0:T(8,128)(2,1)}, bf16[768,256]{1,0:T(8,128)(2,1)S(1)}, u32[]{:S(2)}, u32[]{:S(2)}) %collective-permute-start.14) | collective-permute-done | bytes 393248 | tf_op jit(solution)/shard_map/ppermute | solution.py:393
  100.4 0.0 collective-permute-done.15.a2
  100.4 0.0 collective-permute-done.16.a3
  100.4 0.9 total.1
  101.4 0.0 all-to-all-done.1
  101.4 0.1 convert_reduce_fusion
  101.5 0.6 copy.10
  (21 shorter events, 0.1 us)
Async XLA Ops:
  0.6 28.4 %collective-permute-start.7 = (bf16[768,256]{1,0:T(8,128)(2,1)}, bf16[768,256]{1,0:T(8,128)(2,1)S(1)}, u32[]{:S(2)}, u32[]{:S(2)}) collective-permute-start(bf16[768,256]{1,0:T(8,128)(2,1)} %g0.5), channel_id=1, source_target_pairs={{0,1},{1,2},{2,3},{3,0},{4,5},{5,6},{6,7},{7,4},{8,9},{9,10},{10,1... | collective-permute-start | bytes 1179656 | tf_op jit(solution)/shard_map/ppermute | solution.py:393
  2.3 26.8 %collective-permute-start.6 = (bf16[768,256]{1,0:T(8,128)(2,1)}, bf16[768,256]{1,0:T(8,128)(2,1)}, u32[]{:S(2)}, u32[]{:S(2)}) collective-permute-start(bf16[768,256]{1,0:T(8,128)(2,1)} %g0.5), channel_id=1, source_target_pairs={{0,2},{1,3},{2,0},{3,1},{4,6},{5,7},{6,4},{7,5},{8,10},{9,11},{10,... | collective-permute-start | bytes 1179656 | tf_op jit(solution)/shard_map/ppermute | solution.py:393
  5.2 23.9 %collective-permute-start.5 = (bf16[768,256]{1,0:T(8,128)(2,1)}, bf16[768,256]{1,0:T(8,128)(2,1)}, u32[]{:S(2)}, u32[]{:S(2)}) collective-permute-start(bf16[768,256]{1,0:T(8,128)(2,1)} %g0.5), channel_id=1, source_target_pairs={{0,3},{1,0},{2,1},{3,2},{4,7},{5,4},{6,5},{7,6},{8,11},{9,8},{10,9... | collective-permute-start | bytes 1179656 | tf_op jit(solution)/shard_map/ppermute | solution.py:393
  7.3 2.2 %copy-start.1 = (bf16[512,16,256]{2,1,0:T(8,128)(2,1)S(1)}, bf16[512,16,256]{2,1,0:T(8,128)(2,1)}, u32[]{:S(2)}) copy-start(bf16[512,16,256]{2,1,0:T(8,128)(2,1)} %whole.1) | copy-start | bytes 12582916
  9.5 13.6 %copy-start = (bf16[6144,128]{1,0:T(8,128)(2,1)S(1)}, bf16[6144,128]{1,0:T(8,128)(2,1)}, u32[]{:S(2)}) copy-start(bf16[6144,128]{1,0:T(8,128)(2,1)} %feat.1) | copy-start | bytes 4718596
  9.5 13.6 %copy-start.9 = (f32[128]{0:T(128)S(1)}, f32[128]{0:T(128)}, u32[]{:S(2)}) copy-start(f32[128]{0:T(128)} %param.5) | copy-start | bytes 1540
  13.6 8.4 %collective-permute-start = (bf16[16,128]{1,0:T(8,128)(2,1)S(1)}, bf16[16,128]{1,0:T(8,128)(2,1)S(1)}, u32[]{:S(2)}, u32[]{:S(2)}) collective-permute-start(bf16[16,128]{1,0:T(8,128)(2,1)S(1)} %get-tuple-element.29), channel_id=1, source_target_pairs={{0,4},{4,8},{8,12},{12,16},{16,20},{20,24},{24,28},{28,32},{32,36}... | collective-permute-start | bytes 12296 | tf_op jit(solution)/shard_map/ppermute | solution.py:399
  15.5 7.6 %collective-permute-start.1 = (bf16[16,128]{1,0:T(8,128)(2,1)S(1)}, bf16[16,128]{1,0:T(8,128)(2,1)S(1)}, u32[]{:S(2)}, u32[]{:S(2)}) collective-permute-start(bf16[16,128]{1,0:T(8,128)(2,1)S(1)} %get-tuple-element.30), channel_id=1, source_target_pairs={{4,0},{8,4},{12,8},{16,12},{20,16},{24,20},{28,24},{32,28},{36,32}... | collective-permute-start | bytes 12296 | tf_op jit(solution)/shard_map/ppermute | solution.py:399
  23.2 5.9 %copy-start.2 = (bf16[768,256]{1,0:T(8,128)(2,1)S(1)}, bf16[768,256]{1,0:T(8,128)(2,1)}, u32[]{:S(2)}) copy-start(bf16[768,256]{1,0:T(8,128)(2,1)} %g0.5) | copy-start | bytes 1179652
  29.0 8.5 %copy-start.12 = (bf16[768,2048]{1,0:T(8,128)(2,1)}, bf16[768,2048]{1,0:T(8,128)(2,1)S(1)}, u32[]{:S(2)}) copy-start(bf16[768,2048]{1,0:T(8,128)(2,1)S(1)} %get-tuple-element.32.taps) | copy-start | bytes 9437188
  29.1 8.4 %copy-start.3 = (bf16[768,256]{1,0:T(8,128)(2,1)}, bf16[768,256]{1,0:T(8,128)(2,1)S(1)}, u32[]{:S(2)}) copy-start(bf16[768,256]{1,0:T(8,128)(2,1)S(1)} %collective-permute-done.7.g3) | copy-start | bytes 1179652
  33.2 4.2 %collective-permute-start.8 = (bf16[512,2048]{1,0:T(8,128)(2,1)S(1)}, bf16[512,2048]{1,0:T(8,128)(2,1)S(1)}, u32[]{:S(2)}, u32[]{:S(2)}) collective-permute-start(bf16[512,2048]{1,0:T(8,128)(2,1)S(1)} %kernel_grad_send.1), channel_id=1, source_target_pairs={{0,4},{4,0},{1,5},{5,1},{2,6},{6,2},{3,7},{7,3},{8,12},{12,8},{9,1... | collective-permute-start | bytes 6291464 | tf_op jit(solution)/shard_map/ppermute | solution.py:393
  33.3 21.2 %collective-permute-start.2 = (bf16[1024,256]{1,0:T(8,128)(2,1)}, bf16[1024,256]{1,0:T(8,128)(2,1)}, u32[]{:S(2)}, u32[]{:S(2)}) collective-permute-start(bf16[1024,256]{1,0:T(8,128)(2,1)} %get-tuple-element.34), channel_id=1, source_target_pairs={{0,3},{1,0},{2,1},{3,2},{4,7},{5,4},{6,5},{7,6},{8,11},{9,8},{10,9... | collective-permute-start | bytes 1572872 | tf_op jit(solution)/shard_map/ppermute | solution.py:393
  33.7 20.8 %collective-permute-start.3 = (bf16[1024,256]{1,0:T(8,128)(2,1)S(1)}, bf16[1024,256]{1,0:T(8,128)(2,1)}, u32[]{:S(2)}, u32[]{:S(2)}) collective-permute-start(bf16[1024,256]{1,0:T(8,128)(2,1)S(1)} %get-tuple-element.35), channel_id=1, source_target_pairs={{0,2},{1,3},{2,0},{3,1},{4,6},{5,7},{6,4},{7,5},{8,10},{9,11},{10,... | collective-permute-start | bytes 1572872 | tf_op jit(solution)/shard_map/ppermute | solution.py:393
  36.2 24.4 %collective-permute-start.4 = (bf16[1024,256]{1,0:T(8,128)(2,1)S(1)}, bf16[1024,256]{1,0:T(8,128)(2,1)}, u32[]{:S(2)}, u32[]{:S(2)}) collective-permute-start(bf16[1024,256]{1,0:T(8,128)(2,1)S(1)} %get-tuple-element.36), channel_id=1, source_target_pairs={{0,1},{1,2},{2,3},{3,0},{4,5},{5,6},{6,7},{7,4},{8,9},{9,10},{10,1... | collective-permute-start | bytes 1572872 | tf_op jit(solution)/shard_map/ppermute | solution.py:393
  42.0 30.0 %all-to-all-start = ((bf16[4,128,2048]{2,1,0:T(8,128)(2,1)}), bf16[4,128,2048]{2,1,0:T(8,128)(2,1)S(1)}, u32[]{:S(2)}, u32[]{:S(2)}) async-start(bf16[4,128,2048]{2,1,0:T(8,128)(2,1)} %get-tuple-element.49), calls=%async_computation | async-start | bytes 4194304 | tf_op jit(solution)/shard_map/all_to_all | solution.py:423
  46.9 13.7 %collective-permute-start.9 = (bf16[16,1024]{1,0:T(8,128)(2,1)}, bf16[16,1024]{1,0:T(8,128)(2,1)S(1)}, u32[]{:S(2)}, u32[]{:S(2)}) collective-permute-start(bf16[16,1024]{1,0:T(8,128)(2,1)} %get-tuple-element.37), channel_id=1, source_target_pairs={{0,4},{4,8},{8,12},{12,16},{16,20},{20,24},{24,28},{28,32},{32,36}... | collective-permute-start | bytes 98312 | tf_op jit(solution)/shard_map/ppermute | solution.py:399
  48.8 11.8 %collective-permute-start.10 = (bf16[16,1024]{1,0:T(8,128)(2,1)}, bf16[16,1024]{1,0:T(8,128)(2,1)S(1)}, u32[]{:S(2)}, u32[]{:S(2)}) collective-permute-start(bf16[16,1024]{1,0:T(8,128)(2,1)} %get-tuple-element.38), channel_id=1, source_target_pairs={{4,0},{8,4},{12,8},{16,12},{20,16},{24,20},{28,24},{32,28},{36,32}... | collective-permute-start | bytes 98312 | tf_op jit(solution)/shard_map/ppermute | solution.py:399
  60.5 0.6 copy-start.5
  60.5 0.6 copy-start.7
  60.6 4.2 %copy-start.10 = (bf16[2048,256]{1,0:T(8,128)(2,1)S(1)}, bf16[2048,256]{1,0:T(8,128)(2,1)}, u32[]{:S(2)}) copy-start(bf16[2048,256]{1,0:T(8,128)(2,1)} %get-tuple-element.33.own) | copy-start | bytes 3145732
  60.6 4.2 %copy-start.13 = (bf16[768,2048]{1,0:T(8,128)(2,1)S(1)}, bf16[768,2048]{1,0:T(8,128)(2,1)}, u32[]{:S(2)}) copy-start(bf16[768,2048]{1,0:T(8,128)(2,1)} %copy-done.12) | copy-start | bytes 9437188
  61.2 2.1 %collective-permute-start.11 = (bf16[1024,256]{1,0:T(8,128)(2,1)}, bf16[1024,256]{1,0:T(8,128)(2,1)S(1)}, u32[]{:S(2)}, u32[]{:S(2)}) collective-permute-start(bf16[1024,256]{1,0:T(8,128)(2,1)} %get-tuple-element.40.a1), channel_id=1, source_target_pairs={{0,4},{4,0},{1,5},{5,1},{2,6},{6,2},{3,7},{7,3},{8,12},{12,8},{9,1... | collective-permute-start | bytes 1572872 | tf_op jit(solution)/shard_map/ppermute | solution.py:393
  61.2 2.9 %collective-permute-start.12 = (bf16[1024,256]{1,0:T(8,128)(2,1)}, bf16[1024,256]{1,0:T(8,128)(2,1)S(1)}, u32[]{:S(2)}, u32[]{:S(2)}) collective-permute-start(bf16[1024,256]{1,0:T(8,128)(2,1)} %get-tuple-element.41.a2), channel_id=1, source_target_pairs={{0,4},{4,0},{1,5},{5,1},{2,6},{6,2},{3,7},{7,3},{8,12},{12,8},{9,1... | collective-permute-start | bytes 1572872 | tf_op jit(solution)/shard_map/ppermute | solution.py:393
  61.7 3.1 %collective-permute-start.13 = (bf16[1024,256]{1,0:T(8,128)(2,1)}, bf16[1024,256]{1,0:T(8,128)(2,1)S(1)}, u32[]{:S(2)}, u32[]{:S(2)}) collective-permute-start(bf16[1024,256]{1,0:T(8,128)(2,1)} %get-tuple-element.42.a3), channel_id=1, source_target_pairs={{0,4},{4,0},{1,5},{5,1},{2,6},{6,2},{3,7},{7,3},{8,12},{12,8},{9,1... | collective-permute-start | bytes 1572872 | tf_op jit(solution)/shard_map/ppermute | solution.py:393
  72.0 11.9 %copy-start.4 = (bf16[768,256]{1,0:T(8,128)(2,1)S(1)}, bf16[768,256]{1,0:T(8,128)(2,1)}, u32[]{:S(2)}) copy-start(bf16[768,256]{1,0:T(8,128)(2,1)} %copy-done.3) | copy-start | bytes 1179652
  72.0 11.9 %copy-start.6 = (bf16[16,1024]{1,0:T(8,128)(2,1)S(1)}, bf16[16,1024]{1,0:T(8,128)(2,1)}, u32[]{:S(2)}) copy-start(bf16[16,1024]{1,0:T(8,128)(2,1)} %copy-done.5) | copy-start | bytes 98308
  72.0 11.9 %copy-start.8 = (bf16[16,1024]{1,0:T(8,128)(2,1)S(1)}, bf16[16,1024]{1,0:T(8,128)(2,1)}, u32[]{:S(2)}) copy-start(bf16[16,1024]{1,0:T(8,128)(2,1)} %copy-done.7) | copy-start | bytes 98308
  73.1 28.2 %all-to-all-start.1 = ((bf16[8,16,2048]{2,1,0:T(8,128)(2,1)}), bf16[8,16,2048]{2,1,0:T(8,128)(2,1)S(1)}, u32[]{:S(2)}, u32[]{:S(2)}) async-start(bf16[8,16,2048]{2,1,0:T(8,128)(2,1)} %get-tuple-element.54), calls=%async_computation.1 | async-start | bytes 1048576 | tf_op jit(solution)/shard_map/all_to_all | solution.py:432
  80.6 19.8 %collective-permute-start.14 = (bf16[768,256]{1,0:T(8,128)(2,1)}, bf16[768,256]{1,0:T(8,128)(2,1)S(1)}, u32[]{:S(2)}, u32[]{:S(2)}) collective-permute-start(bf16[768,256]{1,0:T(8,128)(2,1)} %get-tuple-element.44), channel_id=1, source_target_pairs={{0,1},{1,2},{2,3},{3,0},{4,5},{5,6},{6,7},{7,4},{8,9},{9,10},{10,1... | collective-permute-start | bytes 1179656 | tf_op jit(solution)/shard_map/ppermute | solution.py:393
  81.3 19.2 %collective-permute-start.15 = (bf16[768,256]{1,0:T(8,128)(2,1)}, bf16[768,256]{1,0:T(8,128)(2,1)S(1)}, u32[]{:S(2)}, u32[]{:S(2)}) collective-permute-start(bf16[768,256]{1,0:T(8,128)(2,1)} %get-tuple-element.45), channel_id=1, source_target_pairs={{0,3},{1,0},{2,1},{3,2},{4,7},{5,4},{6,5},{7,6},{8,11},{9,8},{10,9... | collective-permute-start | bytes 1179656 | tf_op jit(solution)/shard_map/ppermute | solution.py:393
  83.8 16.6 %collective-permute-start.16 = (bf16[768,256]{1,0:T(8,128)(2,1)}, bf16[768,256]{1,0:T(8,128)(2,1)S(1)}, u32[]{:S(2)}, u32[]{:S(2)}) collective-permute-start(bf16[768,256]{1,0:T(8,128)(2,1)} %get-tuple-element.46), channel_id=1, source_target_pairs={{0,2},{1,3},{2,0},{3,1},{4,6},{5,7},{6,4},{7,5},{8,10},{9,11},{10,... | collective-permute-start | bytes 1179656 | tf_op jit(solution)/shard_map/ppermute | solution.py:393
  83.9 1.9 %copy-start.14 = (f32[6144,128]{1,0:T(8,128)S(1)}, f32[6144,128]{1,0:T(8,128)}, u32[]{:S(2)}) copy-start(f32[6144,128]{1,0:T(8,128)} %get-tuple-element.48.factor) | copy-start | bytes 9437188
  85.8 2.2 %copy-start.15 = (bf16[2048,1024]{1,0:T(8,128)(2,1)S(1)}, bf16[2048,1024]{1,0:T(8,128)(2,1)}, u32[]{:S(2)}) copy-start(bf16[2048,1024]{1,0:T(8,128)(2,1)} %get-tuple-element.47.weights) | copy-start | bytes 12582916
  88.0 12.5 %copy-start.11 = (f32[768,256]{1,0:T(8,128)S(1)}, f32[768,256]{1,0:T(8,128)}, u32[]{:S(2)}) copy-start(f32[768,256]{1,0:T(8,128)} %get-tuple-element.43.own) | copy-start | bytes 2359300

commit v9 on v7

--- a/solution.py
+++ b/solution.py
@@ -59,7 +59,7 @@
 TOKEN = shape((8, 128), F32)
 
 
-FACTOR = 1.1
+FACTOR = 1.3
 TIME = dict(
     prep=7,
     weights=4,

time: 100 us -> 98.5 us (0.985)
  waiting for transfers between devices: 16.9 us -> 14.3 us
  Pallas kernels: 33.8 us -> 35 us
    ppermute x13, waiting for transfers between devices: 16 us -> 10.4 us  [turn(): lax.ppermute(value, axis, [(i, (i + by) % count) for i in range(count)])]
    all_to_all x1, waiting for transfers between devices: 0.01 us -> 3.89 us  [shards(): spread = lax.all_to_all(summed, 'z', 0, 0)]
    pallas_call x1, Pallas kernels: 0.93 us -> 2.03 us  [total(): call(total_kernel, shape((768, 256)), [VMEM] * 5, 'total', limit=24)]
  transfers between devices with their start and end apart: 19 -> 19, of which waited for: 7 -> 6; matrix products, arithmetic and copies ran while one was open for 1% -> 1% of each run, Pallas kernels for 29% -> 31%
where the time goes in v9:
time: 98.5 us; the launch traced here: 97.9 us
  starting transfers between devices  39.2 us (40%)
  Pallas kernels  35 us (36%)
  waiting for transfers between devices  14.3 us (15%)
  local copies, waits for them, and re-layouts  8.31 us (8%)
    ppermute x4, starting transfers between devices, beside(): return lax.ppermute(value, TM, pairs)  15.9 us
    ppermute x13, starting transfers between devices, turn(): lax.ppermute(value, axis, [(i, (i + by) % count) for i in range(count)])  13.2 us
    ppermute x13, waiting for transfers between devices, turn(): lax.ppermute(value, axis, [(i, (i + by) % count) for i in range(count)])  10.4 us
    unnamed x33, local copies, waits for them, and re-layouts  7.52 us
    pallas_call x1, Pallas kernels, input_grad(): call(input_grad_kernel, (shape((frames, chans)), TOKEN), [VMEM] * 9, 'inp...  6.91 us
    pallas_call x1, Pallas kernels, encode(): call(encode_kernel, (far_shape((768, 256), F32),) + (far_shape((768, 256)...  6.34 us
    pallas_call x1, Pallas kernels, prep(): call(prep_kernel, (shape((frames // STRIDE, TAPS * chans)), far_shape((fr...  5.88 us
    all_to_all x1, starting transfers between devices, shards(): spread = lax.all_to_all(summed, 'z', 0, 0)  5.21 us
  transfers between devices with their start and end apart: 19, of which 6 were waited for; matrix products, arithmetic and copies ran while one was open for 1% of the time, Pallas kernels for 31%

profile of v9, /device:TPU:2, one launch (start us, length us, event | category | flops | bytes accessed | tf_op | source)
XLA Modules:
  0.0 97.9 jit_solution(15310737226280511800)
XLA Ops:
  0.6 1.7 %collective-permute-start.7 = (bf16[768,256]{1,0:T(8,128)(2,1)}, bf16[768,256]{1,0:T(8,128)(2,1)S(1)}, u32[]{:S(2)}, u32[]{:S(2)}) collective-permute-start(bf16[768,256]{1,0:T(8,128)(2,1)} %g0.5), channel_id=1, source_target_pairs={{0,1},{1,2},{2,3},{3,0},{4,5},{5,6},{6,7},{7,4},{8,9},{9,10},{10,1... | collective-permute-start | bytes 1179656 | tf_op jit(solution)/shard_map/ppermute | solution.py:391
  2.3 2.9 %collective-permute-start.6 = (bf16[768,256]{1,0:T(8,128)(2,1)}, bf16[768,256]{1,0:T(8,128)(2,1)}, u32[]{:S(2)}, u32[]{:S(2)}) collective-permute-start(bf16[768,256]{1,0:T(8,128)(2,1)} %g0.5), channel_id=1, source_target_pairs={{0,2},{1,3},{2,0},{3,1},{4,6},{5,7},{6,4},{7,5},{8,10},{9,11},{10,... | collective-permute-start | bytes 1179656 | tf_op jit(solution)/shard_map/ppermute | solution.py:391
  5.2 1.3 %collective-permute-start.5 = (bf16[768,256]{1,0:T(8,128)(2,1)}, bf16[768,256]{1,0:T(8,128)(2,1)}, u32[]{:S(2)}, u32[]{:S(2)}) collective-permute-start(bf16[768,256]{1,0:T(8,128)(2,1)} %g0.5), channel_id=1, source_target_pairs={{0,3},{1,0},{2,1},{3,2},{4,7},{5,4},{6,5},{7,6},{8,11},{9,8},{10,9... | collective-permute-start | bytes 1179656 | tf_op jit(solution)/shard_map/ppermute | solution.py:391
  6.5 0.7 fusion.1
  7.2 6.3 %collective-permute-start.1 = (bf16[16,128]{1,0:T(8,128)(2,1)S(1)}, bf16[16,128]{1,0:T(8,128)(2,1)S(1)}, u32[]{:S(2)}, u32[]{:S(2)}) collective-permute-start(bf16[16,128]{1,0:T(8,128)(2,1)S(1)} %get-tuple-element.51), channel_id=1, source_target_pairs={{4,0},{8,4},{12,8},{16,12},{20,16},{24,20},{28,24},{32,28},{36,32}... | collective-permute-start | bytes 12296 | tf_op jit(solution)/shard_map/ppermute | solution.py:397
  13.6 1.9 %collective-permute-start = (bf16[16,128]{1,0:T(8,128)(2,1)S(1)}, bf16[16,128]{1,0:T(8,128)(2,1)S(1)}, u32[]{:S(2)}, u32[]{:S(2)}) collective-permute-start(bf16[16,128]{1,0:T(8,128)(2,1)S(1)} %get-tuple-element.52), channel_id=1, source_target_pairs={{0,4},{4,8},{8,12},{12,16},{16,20},{20,24},{24,28},{28,32},{32,36}... | collective-permute-start | bytes 12296 | tf_op jit(solution)/shard_map/ppermute | solution.py:397
  15.5 0.1 pad_add_fusion.place
  15.6 2.2 %copy-done.1 = bf16[512,16,256]{2,1,0:T(8,128)(2,1)S(1)} copy-done((bf16[512,16,256]{2,1,0:T(8,128)(2,1)S(1)}, bf16[512,16,256]{2,1,0:T(8,128)(2,1)}, u32[]{:S(2)}) %copy-start.1) | copy-done | bytes 4194328
  17.8 4.1 %weights.1 = (bf16[2048,256]{1,0:T(8,128)(2,1)}, bf16[1024,256]{1,0:T(8,128)(2,1)S(1)}, bf16[1024,256]{1,0:T(8,128)(2,1)S(1)}, bf16[1024,256]{1,0:T(8,128)(2,1)}, f32[8,128]{1,0:T(8,128)S(1)}) custom-call(s32[2]{0:T(128)S(1)} %pad_add_fusion.place, bf16[512,16,256]{2,1,0:T(8,128)(2,1)S(1)} %copy-done.1), custom_call_target="tpu_custom_call" | custom-call | flops 5980000256 | bytes 1000 | tf_op jit(solution)/shard_map/weights/pallas_call | solution.py:176
  21.9 0.1 stack.29.place
  22.0 0.0 collective-permute-done.1.high
  22.0 0.0 collective-permute-done.low
  22.0 0.0 copy-start.2
  22.0 5.9 %prep.1 = (bf16[768,2048]{1,0:T(8,128)(2,1)S(1)}, f32[6144,128]{1,0:T(8,128)}) custom-call(bf16[6144,128]{1,0:T(8,128)(2,1)S(1)} %copy-done, bf16[16,128]{1,0:T(8,128)(2,1)S(1)} %collective-permute-done.low, bf16[16,128]{1,0:T(8,128)(2,1)S(1)} %collective-permute-done.1.high, f32[1,128]{1,0:T(1,128)S(1)} %bitcast.10, f32[8,128]{1,0:T(8,128)S(1)} %get-tuple-element.27.after), custom_call_target="tpu_custom_call" | custom-call | flops 10465000448 | bytes 1000 | tf_op jit(solution)/shard_map/prep/pallas_call | solution.py:131
  27.9 0.0 collective-permute-done.7.g3
  27.9 0.0 copy-start.3
  27.9 0.0 collective-permute-done.6.g2
  27.9 0.0 collective-permute-done.5.g1
  27.9 4.1 %kernel_grad_send.1 = bf16[512,2048]{1,0:T(8,128)(2,1)S(1)} custom-call(s32[5]{0:T(128)S(1)} %stack.29.place, bf16[768,2048]{1,0:T(8,128)(2,1)S(1)} %get-tuple-element.28.taps, bf16[768,256]{1,0:T(8,128)(2,1)S(1)} %copy-done.2, bf16[768,256]{1,0:T(8,128)(2,1)} %collective-permute-done.5.g1, bf16[768,256]{1,0:T(8,128)(2,1)} %collective-permute-done.6.g2, ...), custom_call_target="tpu_custom_call" | custom-call | flops 4485000192 | bytes 1000 | tf_op jit(solution)/shard_map/kernel_grad_send/pallas_call | solution.py:209
  32.1 0.1 collective-permute-start.8
  32.2 0.4 collective-permute-start.2
  32.6 2.5 %collective-permute-start.3 = (bf16[1024,256]{1,0:T(8,128)(2,1)S(1)}, bf16[1024,256]{1,0:T(8,128)(2,1)}, u32[]{:S(2)}, u32[]{:S(2)}) collective-permute-start(bf16[1024,256]{1,0:T(8,128)(2,1)S(1)} %get-tuple-element.31), channel_id=1, source_target_pairs={{0,2},{1,3},{2,0},{3,1},{4,6},{5,7},{6,4},{7,5},{8,10},{9,11},{10,... | collective-permute-start | bytes 1572872 | tf_op jit(solution)/shard_map/ppermute | solution.py:391
  35.0 0.0 collective-permute-start.4
  35.0 1.3 %collective-permute-done.8.got = bf16[512,2048]{1,0:T(8,128)(2,1)S(1)} collective-permute-done((bf16[512,2048]{1,0:T(8,128)(2,1)S(1)}, bf16[512,2048]{1,0:T(8,128)(2,1)S(1)}, u32[]{:S(2)}, u32[]{:S(2)}) %collective-permute-start.8) | collective-permute-done | bytes 2097184 | tf_op jit(solution)/shard_map/ppermute | solution.py:391
  36.3 0.0 copy-done.11
  36.3 4.5 %kernel_grad_keep.1 = (bf16[4,128,2048]{2,1,0:T(8,128)(2,1)}, bf16[16,1024]{1,0:T(8,128)(2,1)}, bf16[16,1024]{1,0:T(8,128)(2,1)}, f32[8,128]{1,0:T(8,128)S(1)}) custom-call(s32[5]{0:T(128)S(1)} %stack.29.place, bf16[768,2048]{1,0:T(8,128)(2,1)S(1)} %get-tuple-element.28.taps, bf16[768,256]{1,0:T(8,128)(2,1)S(1)} %copy-done.2, ...), custom_call_target="tpu_custom_call" | custom-call | flops 5980000256 | bytes 1000 | tf_op jit(solution)/shard_map/kernel_grad_keep/pallas_call | solution.py:245
  40.8 4.9 %all-to-all-start = ((bf16[4,128,2048]{2,1,0:T(8,128)(2,1)}), bf16[4,128,2048]{2,1,0:T(8,128)(2,1)S(1)}, u32[]{:S(2)}, u32[]{:S(2)}) async-start(bf16[4,128,2048]{2,1,0:T(8,128)(2,1)} %get-tuple-element.45), calls=%async_computation | async-start | bytes 4194304 | tf_op jit(solution)/shard_map/all_to_all | solution.py:421
  45.7 1.9 %collective-permute-start.9 = (bf16[16,1024]{1,0:T(8,128)(2,1)}, bf16[16,1024]{1,0:T(8,128)(2,1)S(1)}, u32[]{:S(2)}, u32[]{:S(2)}) collective-permute-start(bf16[16,1024]{1,0:T(8,128)(2,1)} %get-tuple-element.33), channel_id=1, source_target_pairs={{0,4},{4,8},{8,12},{12,16},{16,20},{20,24},{24,28},{28,32},{32,36}... | collective-permute-start | bytes 98312 | tf_op jit(solution)/shard_map/ppermute | solution.py:397
  47.6 5.8 %collective-permute-start.10 = (bf16[16,1024]{1,0:T(8,128)(2,1)}, bf16[16,1024]{1,0:T(8,128)(2,1)S(1)}, u32[]{:S(2)}, u32[]{:S(2)}) collective-permute-start(bf16[16,1024]{1,0:T(8,128)(2,1)} %get-tuple-element.34), channel_id=1, source_target_pairs={{4,0},{8,4},{12,8},{16,12},{20,16},{24,20},{28,24},{32,28},{36,32}... | collective-permute-start | bytes 98312 | tf_op jit(solution)/shard_map/ppermute | solution.py:397
  53.4 0.0 collective-permute-done.2.refs_0_
  53.4 0.0 collective-permute-done.3.refs_1_
  53.4 6.0 %collective-permute-done.4.refs_2_ = bf16[1024,256]{1,0:T(8,128)(2,1)} collective-permute-done((bf16[1024,256]{1,0:T(8,128)(2,1)S(1)}, bf16[1024,256]{1,0:T(8,128)(2,1)}, u32[]{:S(2)}, u32[]{:S(2)}) %collective-permute-start.4) | collective-permute-done | bytes 524320 | tf_op jit(solution)/shard_map/ppermute | solution.py:391
  59.4 0.0 collective-permute-done.9.refs_3_.low
  59.4 0.0 collective-permute-done.10.refs_4_.high
  59.4 0.0 copy-start.7
  59.4 0.0 copy-start.12
  59.4 0.0 copy-start.15
  59.4 0.6 copy-done.5
  60.0 0.0 copy-done.7
  60.0 0.0 collective-permute-start.11
  60.0 0.5 collective-permute-start.12
  60.5 0.0 collective-permute-start.13
  60.5 1.6 %collective-permute-done.11.b1 = bf16[1024,256]{1,0:T(8,128)(2,1)S(1)} collective-permute-done((bf16[1024,256]{1,0:T(8,128)(2,1)}, bf16[1024,256]{1,0:T(8,128)(2,1)S(1)}, u32[]{:S(2)}, u32[]{:S(2)}) %collective-permute-start.11) | collective-permute-done | bytes 524320 | tf_op jit(solution)/shard_map/ppermute | solution.py:391
  62.1 0.7 collective-permute-done.12.b2
  62.9 0.7 collective-permute-done.13.b3
  63.6 0.0 copy-done.12
  63.6 6.3 %encode.1 = (f32[768,256]{1,0:T(8,128)}, bf16[768,256]{1,0:T(8,128)(2,1)}, bf16[768,256]{1,0:T(8,128)(2,1)}, bf16[768,256]{1,0:T(8,128)(2,1)}, bf16[2048,1024]{1,0:T(8,128)(2,1)}, /*index=5*/f32[8,128]{1,0:T(8,128)S(1)}) custom-call(s32[1]{0:T(128)} %bitcast.core, bf16[768,2048]{1,0:T(8,128)(2,1)S(1)} %copy-done.12, bf16[2048,256]{1,0:T(8,128)(2,1)S(1)} %copy-done.15, ...), custom_call_target="tpu_custom_call" | custom-call | flops 7474999808 | bytes 1000 | tf_op jit(solution)/shard_map/encode/pallas_call | solution.py:305
  70.0 1.1 %collective-permute-start.14 = (bf16[768,256]{1,0:T(8,128)(2,1)}, bf16[768,256]{1,0:T(8,128)(2,1)S(1)}, u32[]{:S(2)}, u32[]{:S(2)}) collective-permute-start(bf16[768,256]{1,0:T(8,128)(2,1)} %get-tuple-element.40), channel_id=1, source_target_pairs={{0,1},{1,2},{2,3},{3,0},{4,5},{5,6},{6,7},{7,4},{8,9},{9,10},{10,1... | collective-permute-start | bytes 1179656 | tf_op jit(solution)/shard_map/ppermute | solution.py:391
  71.1 2.2 %collective-permute-start.15 = (bf16[768,256]{1,0:T(8,128)(2,1)}, bf16[768,256]{1,0:T(8,128)(2,1)}, u32[]{:S(2)}, u32[]{:S(2)}) collective-permute-start(bf16[768,256]{1,0:T(8,128)(2,1)} %get-tuple-element.41), channel_id=1, source_target_pairs={{0,3},{1,0},{2,1},{3,2},{4,7},{5,4},{6,5},{7,6},{8,11},{9,8},{10,9... | collective-permute-start | bytes 1179656 | tf_op jit(solution)/shard_map/ppermute | solution.py:391
  73.3 0.5 collective-permute-start.16
  73.8 0.0 all-to-all-done.parts
  73.8 1.1 %lines.1 = (bf16[8,16,2048]{2,1,0:T(8,128)(2,1)}, f32[8,128]{1,0:T(8,128)S(1)}) custom-call(bf16[4,128,2048]{2,1,0:T(8,128)(2,1)S(1)} %all-to-all-done.parts, f32[8,128]{1,0:T(8,128)S(1)} %get-tuple-element.46.after), custom_call_target="tpu_custom_call" | custom-call | flops 1495000064 | bytes 1000 | tf_op jit(solution)/shard_map/lines/pallas_call | solution.py:330
  75.0 5.2 %all-to-all-start.1 = ((bf16[8,16,2048]{2,1,0:T(8,128)(2,1)}), bf16[8,16,2048]{2,1,0:T(8,128)(2,1)S(1)}, u32[]{:S(2)}, u32[]{:S(2)}) async-start(bf16[8,16,2048]{2,1,0:T(8,128)(2,1)} %get-tuple-element.50), calls=%async_computation.1 | async-start | bytes 1048576 | tf_op jit(solution)/shard_map/all_to_all | solution.py:430
  80.2 0.0 copy-done.4
  80.2 2.2 %copy-done.13 = bf16[2048,1024]{1,0:T(8,128)(2,1)S(1)} copy-done((bf16[2048,1024]{1,0:T(8,128)(2,1)S(1)}, bf16[2048,1024]{1,0:T(8,128)(2,1)}, u32[]{:S(2)}) %copy-start.13) | copy-done | bytes 4194328
  82.4 1.9 %copy-done.14 = f32[6144,128]{1,0:T(8,128)S(1)} copy-done((f32[6144,128]{1,0:T(8,128)S(1)}, f32[6144,128]{1,0:T(8,128)}, u32[]{:S(2)}) %copy-start.14) | copy-done | bytes 3145752
  84.3 6.9 %input_grad.1 = (bf16[6144,128]{1,0:T(8,128)(2,1)}, f32[8,128]{1,0:T(8,128)S(1)}) custom-call(bf16[768,256]{1,0:T(8,128)(2,1)S(1)} %copy-done.2, bf16[768,256]{1,0:T(8,128)(2,1)} %collective-permute-done.5.g1, bf16[768,256]{1,0:T(8,128)(2,1)} %collective-permute-done.6.g2, bf16[768,256]{1,0:T(8,128)(2,1)S(1)} %copy-done.4, bf16[16,1024]{1,0:T(8,128)(2,1)S(1)} %copy-done.6, ...), custom_call_target="tpu_custom_call" | custom-call | flops 8970000384 | bytes 1000 | tf_op jit(solution)/shard_map/input_grad/pallas_call | solution.py:367
  91.2 0.0 collective-permute-done.14.a1
  91.2 0.0 collective-permute-done.15.a2
  91.2 0.0 collective-permute-done.16.a3
  91.2 2.0 %total.1 = bf16[768,256]{1,0:T(8,128)(2,1)} custom-call(f32[768,256]{1,0:T(8,128)S(1)} %copy-done.10, bf16[768,256]{1,0:T(8,128)(2,1)S(1)} %collective-permute-done.14.a1, bf16[768,256]{1,0:T(8,128)(2,1)} %collective-permute-done.15.a2, bf16[768,256]{1,0:T(8,128)(2,1)} %collective-permute-done.16.a3, f32[8,128]{1,0:T(8,128)S(1)} %get-tuple-element.48.after), custom_call_target="tpu_custom_call" | custom-call | flops 1495000064 | bytes 1000 | tf_op jit(solution)/shard_map/total/pallas_call | solution.py:384
  93.2 3.9 %all-to-all-done.1 = bf16[8,16,2048]{2,1,0:T(8,128)(2,1)S(1)} async-done(((bf16[8,16,2048]{2,1,0:T(8,128)(2,1)}), bf16[8,16,2048]{2,1,0:T(8,128)(2,1)S(1)}, u32[]{:S(2)}, u32[]{:S(2)}) %all-to-all-start.1) | async-done | bytes 524320 | tf_op jit(solution)/shard_map/all_to_all | solution.py:430
  97.1 0.1 convert_reduce_fusion
  97.2 0.6 copy.10
  (21 shorter events, 0.1 us)
Async XLA Ops:
  0.6 27.3 %collective-permute-start.7 = (bf16[768,256]{1,0:T(8,128)(2,1)}, bf16[768,256]{1,0:T(8,128)(2,1)S(1)}, u32[]{:S(2)}, u32[]{:S(2)}) collective-permute-start(bf16[768,256]{1,0:T(8,128)(2,1)} %g0.5), channel_id=1, source_target_pairs={{0,1},{1,2},{2,3},{3,0},{4,5},{5,6},{6,7},{7,4},{8,9},{9,10},{10,1... | collective-permute-start | bytes 1179656 | tf_op jit(solution)/shard_map/ppermute | solution.py:391
  2.3 25.6 %collective-permute-start.6 = (bf16[768,256]{1,0:T(8,128)(2,1)}, bf16[768,256]{1,0:T(8,128)(2,1)}, u32[]{:S(2)}, u32[]{:S(2)}) collective-permute-start(bf16[768,256]{1,0:T(8,128)(2,1)} %g0.5), channel_id=1, source_target_pairs={{0,2},{1,3},{2,0},{3,1},{4,6},{5,7},{6,4},{7,5},{8,10},{9,11},{10,... | collective-permute-start | bytes 1179656 | tf_op jit(solution)/shard_map/ppermute | solution.py:391
  5.2 22.7 %collective-permute-start.5 = (bf16[768,256]{1,0:T(8,128)(2,1)}, bf16[768,256]{1,0:T(8,128)(2,1)}, u32[]{:S(2)}, u32[]{:S(2)}) collective-permute-start(bf16[768,256]{1,0:T(8,128)(2,1)} %g0.5), channel_id=1, source_target_pairs={{0,3},{1,0},{2,1},{3,2},{4,7},{5,4},{6,5},{7,6},{8,11},{9,8},{10,9... | collective-permute-start | bytes 1179656 | tf_op jit(solution)/shard_map/ppermute | solution.py:391
  7.2 14.7 %collective-permute-start.1 = (bf16[16,128]{1,0:T(8,128)(2,1)S(1)}, bf16[16,128]{1,0:T(8,128)(2,1)S(1)}, u32[]{:S(2)}, u32[]{:S(2)}) collective-permute-start(bf16[16,128]{1,0:T(8,128)(2,1)S(1)} %get-tuple-element.51), channel_id=1, source_target_pairs={{4,0},{8,4},{12,8},{16,12},{20,16},{24,20},{28,24},{32,28},{36,32}... | collective-permute-start | bytes 12296 | tf_op jit(solution)/shard_map/ppermute | solution.py:397
  13.6 8.4 %collective-permute-start = (bf16[16,128]{1,0:T(8,128)(2,1)S(1)}, bf16[16,128]{1,0:T(8,128)(2,1)S(1)}, u32[]{:S(2)}, u32[]{:S(2)}) collective-permute-start(bf16[16,128]{1,0:T(8,128)(2,1)S(1)} %get-tuple-element.52), channel_id=1, source_target_pairs={{0,4},{4,8},{8,12},{12,16},{16,20},{20,24},{24,28},{28,32},{32,36}... | collective-permute-start | bytes 12296 | tf_op jit(solution)/shard_map/ppermute | solution.py:397
  15.6 2.2 %copy-start.1 = (bf16[512,16,256]{2,1,0:T(8,128)(2,1)S(1)}, bf16[512,16,256]{2,1,0:T(8,128)(2,1)}, u32[]{:S(2)}) copy-start(bf16[512,16,256]{2,1,0:T(8,128)(2,1)} %whole.1) | copy-start | bytes 12582916
  17.8 4.2 %copy-start = (bf16[6144,128]{1,0:T(8,128)(2,1)S(1)}, bf16[6144,128]{1,0:T(8,128)(2,1)}, u32[]{:S(2)}) copy-start(bf16[6144,128]{1,0:T(8,128)(2,1)} %feat.1) | copy-start | bytes 4718596
  17.8 4.2 %copy-start.9 = (f32[128]{0:T(128)S(1)}, f32[128]{0:T(128)}, u32[]{:S(2)}) copy-start(f32[128]{0:T(128)} %param.5) | copy-start | bytes 1540
  22.0 6.0 %copy-start.2 = (bf16[768,256]{1,0:T(8,128)(2,1)S(1)}, bf16[768,256]{1,0:T(8,128)(2,1)}, u32[]{:S(2)}) copy-start(bf16[768,256]{1,0:T(8,128)(2,1)} %g0.5) | copy-start | bytes 1179652
  27.9 8.5 %copy-start.11 = (bf16[768,2048]{1,0:T(8,128)(2,1)}, bf16[768,2048]{1,0:T(8,128)(2,1)S(1)}, u32[]{:S(2)}) copy-start(bf16[768,2048]{1,0:T(8,128)(2,1)S(1)} %get-tuple-element.28.taps) | copy-start | bytes 9437188
  27.9 8.4 %copy-start.3 = (bf16[768,256]{1,0:T(8,128)(2,1)}, bf16[768,256]{1,0:T(8,128)(2,1)S(1)}, u32[]{:S(2)}) copy-start(bf16[768,256]{1,0:T(8,128)(2,1)S(1)} %collective-permute-done.7.g3) | copy-start | bytes 1179652
  32.1 4.2 %collective-permute-start.8 = (bf16[512,2048]{1,0:T(8,128)(2,1)S(1)}, bf16[512,2048]{1,0:T(8,128)(2,1)S(1)}, u32[]{:S(2)}, u32[]{:S(2)}) collective-permute-start(bf16[512,2048]{1,0:T(8,128)(2,1)S(1)} %kernel_grad_send.1), channel_id=1, source_target_pairs={{0,4},{4,0},{1,5},{5,1},{2,6},{6,2},{3,7},{7,3},{8,12},{12,8},{9,1... | collective-permute-start | bytes 6291464 | tf_op jit(solution)/shard_map/ppermute | solution.py:391
  32.2 21.2 %collective-permute-start.2 = (bf16[1024,256]{1,0:T(8,128)(2,1)}, bf16[1024,256]{1,0:T(8,128)(2,1)}, u32[]{:S(2)}, u32[]{:S(2)}) collective-permute-start(bf16[1024,256]{1,0:T(8,128)(2,1)} %get-tuple-element.30), channel_id=1, source_target_pairs={{0,3},{1,0},{2,1},{3,2},{4,7},{5,4},{6,5},{7,6},{8,11},{9,8},{10,9... | collective-permute-start | bytes 1572872 | tf_op jit(solution)/shard_map/ppermute | solution.py:391
  32.6 20.8 %collective-permute-start.3 = (bf16[1024,256]{1,0:T(8,128)(2,1)S(1)}, bf16[1024,256]{1,0:T(8,128)(2,1)}, u32[]{:S(2)}, u32[]{:S(2)}) collective-permute-start(bf16[1024,256]{1,0:T(8,128)(2,1)S(1)} %get-tuple-element.31), channel_id=1, source_target_pairs={{0,2},{1,3},{2,0},{3,1},{4,6},{5,7},{6,4},{7,5},{8,10},{9,11},{10,... | collective-permute-start | bytes 1572872 | tf_op jit(solution)/shard_map/ppermute | solution.py:391
  35.0 24.4 %collective-permute-start.4 = (bf16[1024,256]{1,0:T(8,128)(2,1)S(1)}, bf16[1024,256]{1,0:T(8,128)(2,1)}, u32[]{:S(2)}, u32[]{:S(2)}) collective-permute-start(bf16[1024,256]{1,0:T(8,128)(2,1)S(1)} %get-tuple-element.32), channel_id=1, source_target_pairs={{0,1},{1,2},{2,3},{3,0},{4,5},{5,6},{6,7},{7,4},{8,9},{9,10},{10,1... | collective-permute-start | bytes 1572872 | tf_op jit(solution)/shard_map/ppermute | solution.py:391
  40.8 33.0 %all-to-all-start = ((bf16[4,128,2048]{2,1,0:T(8,128)(2,1)}), bf16[4,128,2048]{2,1,0:T(8,128)(2,1)S(1)}, u32[]{:S(2)}, u32[]{:S(2)}) async-start(bf16[4,128,2048]{2,1,0:T(8,128)(2,1)} %get-tuple-element.45), calls=%async_computation | async-start | bytes 4194304 | tf_op jit(solution)/shard_map/all_to_all | solution.py:421
  45.7 13.7 %collective-permute-start.9 = (bf16[16,1024]{1,0:T(8,128)(2,1)}, bf16[16,1024]{1,0:T(8,128)(2,1)S(1)}, u32[]{:S(2)}, u32[]{:S(2)}) collective-permute-start(bf16[16,1024]{1,0:T(8,128)(2,1)} %get-tuple-element.33), channel_id=1, source_target_pairs={{0,4},{4,8},{8,12},{12,16},{16,20},{20,24},{24,28},{28,32},{32,36}... | collective-permute-start | bytes 98312 | tf_op jit(solution)/shard_map/ppermute | solution.py:397
  47.6 11.8 %collective-permute-start.10 = (bf16[16,1024]{1,0:T(8,128)(2,1)}, bf16[16,1024]{1,0:T(8,128)(2,1)S(1)}, u32[]{:S(2)}, u32[]{:S(2)}) collective-permute-start(bf16[16,1024]{1,0:T(8,128)(2,1)} %get-tuple-element.34), channel_id=1, source_target_pairs={{4,0},{8,4},{12,8},{16,12},{20,16},{24,20},{28,24},{32,28},{36,32}... | collective-permute-start | bytes 98312 | tf_op jit(solution)/shard_map/ppermute | solution.py:397
  59.4 0.6 copy-start.5
  59.4 0.6 copy-start.7
  59.4 4.2 %copy-start.12 = (bf16[768,2048]{1,0:T(8,128)(2,1)S(1)}, bf16[768,2048]{1,0:T(8,128)(2,1)}, u32[]{:S(2)}) copy-start(bf16[768,2048]{1,0:T(8,128)(2,1)} %copy-done.11) | copy-start | bytes 9437188
  59.4 4.2 %copy-start.15 = (bf16[2048,256]{1,0:T(8,128)(2,1)S(1)}, bf16[2048,256]{1,0:T(8,128)(2,1)}, u32[]{:S(2)}) copy-start(bf16[2048,256]{1,0:T(8,128)(2,1)} %get-tuple-element.29.own) | copy-start | bytes 3145732
  60.0 2.1 %collective-permute-start.11 = (bf16[1024,256]{1,0:T(8,128)(2,1)}, bf16[1024,256]{1,0:T(8,128)(2,1)S(1)}, u32[]{:S(2)}, u32[]{:S(2)}) collective-permute-start(bf16[1024,256]{1,0:T(8,128)(2,1)} %get-tuple-element.36.a1), channel_id=1, source_target_pairs={{0,4},{4,0},{1,5},{5,1},{2,6},{6,2},{3,7},{7,3},{8,12},{12,8},{9,1... | collective-permute-start | bytes 1572872 | tf_op jit(solution)/shard_map/ppermute | solution.py:391
  60.0 2.9 %collective-permute-start.12 = (bf16[1024,256]{1,0:T(8,128)(2,1)}, bf16[1024,256]{1,0:T(8,128)(2,1)S(1)}, u32[]{:S(2)}, u32[]{:S(2)}) collective-permute-start(bf16[1024,256]{1,0:T(8,128)(2,1)} %get-tuple-element.37.a2), channel_id=1, source_target_pairs={{0,4},{4,0},{1,5},{5,1},{2,6},{6,2},{3,7},{7,3},{8,12},{12,8},{9,1... | collective-permute-start | bytes 1572872 | tf_op jit(solution)/shard_map/ppermute | solution.py:391
  60.5 3.1 %collective-permute-start.13 = (bf16[1024,256]{1,0:T(8,128)(2,1)}, bf16[1024,256]{1,0:T(8,128)(2,1)S(1)}, u32[]{:S(2)}, u32[]{:S(2)}) collective-permute-start(bf16[1024,256]{1,0:T(8,128)(2,1)} %get-tuple-element.38.a3), channel_id=1, source_target_pairs={{0,4},{4,0},{1,5},{5,1},{2,6},{6,2},{3,7},{7,3},{8,12},{12,8},{9,1... | collective-permute-start | bytes 1572872 | tf_op jit(solution)/shard_map/ppermute | solution.py:391
  70.0 21.2 %collective-permute-start.14 = (bf16[768,256]{1,0:T(8,128)(2,1)}, bf16[768,256]{1,0:T(8,128)(2,1)S(1)}, u32[]{:S(2)}, u32[]{:S(2)}) collective-permute-start(bf16[768,256]{1,0:T(8,128)(2,1)} %get-tuple-element.40), channel_id=1, source_target_pairs={{0,1},{1,2},{2,3},{3,0},{4,5},{5,6},{6,7},{7,4},{8,9},{9,10},{10,1... | collective-permute-start | bytes 1179656 | tf_op jit(solution)/shard_map/ppermute | solution.py:391
  71.1 20.1 %collective-permute-start.15 = (bf16[768,256]{1,0:T(8,128)(2,1)}, bf16[768,256]{1,0:T(8,128)(2,1)}, u32[]{:S(2)}, u32[]{:S(2)}) collective-permute-start(bf16[768,256]{1,0:T(8,128)(2,1)} %get-tuple-element.41), channel_id=1, source_target_pairs={{0,3},{1,0},{2,1},{3,2},{4,7},{5,4},{6,5},{7,6},{8,11},{9,8},{10,9... | collective-permute-start | bytes 1179656 | tf_op jit(solution)/shard_map/ppermute | solution.py:391
  73.3 17.9 %collective-permute-start.16 = (bf16[768,256]{1,0:T(8,128)(2,1)}, bf16[768,256]{1,0:T(8,128)(2,1)}, u32[]{:S(2)}, u32[]{:S(2)}) collective-permute-start(bf16[768,256]{1,0:T(8,128)(2,1)} %get-tuple-element.42), channel_id=1, source_target_pairs={{0,2},{1,3},{2,0},{3,1},{4,6},{5,7},{6,4},{7,5},{8,10},{9,11},{10,... | collective-permute-start | bytes 1179656 | tf_op jit(solution)/shard_map/ppermute | solution.py:391
  73.8 6.3 %copy-start.4 = (bf16[768,256]{1,0:T(8,128)(2,1)S(1)}, bf16[768,256]{1,0:T(8,128)(2,1)}, u32[]{:S(2)}) copy-start(bf16[768,256]{1,0:T(8,128)(2,1)} %copy-done.3) | copy-start | bytes 1179652
  73.8 6.3 %copy-start.6 = (bf16[16,1024]{1,0:T(8,128)(2,1)S(1)}, bf16[16,1024]{1,0:T(8,128)(2,1)}, u32[]{:S(2)}) copy-start(bf16[16,1024]{1,0:T(8,128)(2,1)} %copy-done.5) | copy-start | bytes 98308
  73.8 6.3 %copy-start.8 = (bf16[16,1024]{1,0:T(8,128)(2,1)S(1)}, bf16[16,1024]{1,0:T(8,128)(2,1)}, u32[]{:S(2)}) copy-start(bf16[16,1024]{1,0:T(8,128)(2,1)} %copy-done.7) | copy-start | bytes 98308
  75.0 22.2 %all-to-all-start.1 = ((bf16[8,16,2048]{2,1,0:T(8,128)(2,1)}), bf16[8,16,2048]{2,1,0:T(8,128)(2,1)S(1)}, u32[]{:S(2)}, u32[]{:S(2)}) async-start(bf16[8,16,2048]{2,1,0:T(8,128)(2,1)} %get-tuple-element.50), calls=%async_computation.1 | async-start | bytes 1048576 | tf_op jit(solution)/shard_map/all_to_all | solution.py:430
  80.2 2.2 %copy-start.13 = (bf16[2048,1024]{1,0:T(8,128)(2,1)S(1)}, bf16[2048,1024]{1,0:T(8,128)(2,1)}, u32[]{:S(2)}) copy-start(bf16[2048,1024]{1,0:T(8,128)(2,1)} %get-tuple-element.43.weights) | copy-start | bytes 12582916
  82.4 1.9 %copy-start.14 = (f32[6144,128]{1,0:T(8,128)S(1)}, f32[6144,128]{1,0:T(8,128)}, u32[]{:S(2)}) copy-start(f32[6144,128]{1,0:T(8,128)} %get-tuple-element.44.factor) | copy-start | bytes 9437188
  84.3 6.9 %copy-start.10 = (f32[768,256]{1,0:T(8,128)S(1)}, f32[768,256]{1,0:T(8,128)}, u32[]{:S(2)}) copy-start(f32[768,256]{1,0:T(8,128)} %get-tuple-element.39.own) | copy-start | bytes 2359300
